TPU v7x, 32 devices: a whole 2x2x4 slice. The times are simulated.
32 devices in a mesh: gx: 2 (over y), gy: 4 (over z), gz: 4 (over x, core).
Axes of the slice: x: 2, y: 2, z: 4, core: 2. Of those that a mesh axis runs over, the one named last changes fastest.
Arguments:
- e_adjoint: float32 [3, 64, 64, 1024], P(None, 'gx', 'gy', 'gz'), may hold values from -6 to 6
- h_adjoint: float32 [3, 64, 64, 1024], P(None, 'gx', 'gy', 'gz'), may hold values from -6 to 6
- snapshots: bfloat16 [3, 3, 64, 64, 1024], P(None, None, 'gx', 'gy', 'gz'), may hold values from -6 to 6
- material: int32 [64, 64, 1024], P('gx', 'gy', 'gz'), may hold values from 0 to 7
- permittivity: float32 [8], replicated, may hold values from 1 to 12
- design_mask: int32 [64, 64], P('gx', 'gy'), may hold values from 0 to 1
- ports: int32 [3], replicated, may hold values from 0 to 4194303
- amplitudes: float32 [2, 3], replicated, may hold values from -8 to 8
Outputs:
- e_final: float32 [3, 64, 64, 1024], P(None, 'gx', 'gy', 'gz')
- h_final: float32 [3, 64, 64, 1024], P(None, 'gx', 'gy', 'gz')
- gradient: float32 [64, 64], P('gx', ('gy', 'gz'))
All inputs are finite; a program needn't handle non-finite values.
Results may differ from a plain program's by a relative error of at most 0.0003.
Values sent between devices are 32-bit elements; how exact they have to be, the bound alone decides.
No kernel may reach another device: no remote copies, remote signals or barrier semaphores. Data moves between devices by JAX's collectives and lax.ppermute only.
A program may use at most 64 MiB of HBM per device.

v0:
```python
import jax
import jax.numpy as jnp
from jax import lax
from jax.sharding import PartitionSpec as P

STEPS = 2


magnetic_step = 0.5
electric_step = 0.5


def from_behind(array, axis, by):
    size = lax.axis_size(axis)
    pairs = [(i, i + by) for i in range(size) if 0 <= i + by < size]
    return lax.ppermute(array, axis, pairs)


def coordinates(anchor, sizes):
    return tuple((anchor[axis] + lax.broadcasted_iota(jnp.int32, sizes, axis) for axis in range(3)))


def port_source(anchor, sizes, port_cells, amp_row):
    cell_x, cell_y, cell_z = coordinates(anchor, sizes)
    source = jnp.zeros(sizes, jnp.float32)
    for port_no in range(port_cells[0].shape[0]):
        struck = (
            (cell_x == port_cells[0][port_no])
            & (cell_y == port_cells[1][port_no])
            & (cell_z == port_cells[2][port_no])
        )
        source = source + jnp.where(struck, amp_row[port_no], 0.0)
    return source


def split_step(electric, magnetic, coef, base, port_cells, amp_row):
    sizes = electric.shape[1:]
    from_x = from_behind(electric[1:3, 0:1], "gx", -1)
    from_y = from_behind(electric[0::2, :, 0:1], "gy", -1)
    from_z = from_behind(electric[0:2, :, :, 0:1], "gz", -1)
    ey_xp = jnp.concatenate([electric[1, 1:], from_x[0]], 0)
    ez_xp = jnp.concatenate([electric[2, 1:], from_x[1]], 0)
    ex_yp = jnp.concatenate([electric[0, :, 1:], from_y[0]], 1)
    ez_yp = jnp.concatenate([electric[2, :, 1:], from_y[1]], 1)
    ex_zp = jnp.concatenate([electric[0, :, :, 1:], from_z[0]], 2)
    ey_zp = jnp.concatenate([electric[1, :, :, 1:], from_z[1]], 2)
    magnetic = jnp.stack(
        [
            magnetic[0] - magnetic_step * (ez_yp - electric[2] - (ey_zp - electric[1])),
            magnetic[1] - magnetic_step * (ex_zp - electric[0] - (ez_xp - electric[2])),
            magnetic[2] - magnetic_step * (ey_xp - electric[1] - (ex_yp - electric[0])),
        ]
    )
    last_x = sizes[0] - 1
    last_y = sizes[1] - 1
    last_z = sizes[2] - 1
    to_x = from_behind(magnetic[1:3, last_x:], "gx", 1)
    to_y = from_behind(magnetic[0::2, :, last_y:], "gy", 1)
    to_z = from_behind(magnetic[0:2, :, :, last_z:], "gz", 1)
    hy_xm = jnp.concatenate([to_x[0], magnetic[1, :last_x]], 0)
    hz_xm = jnp.concatenate([to_x[1], magnetic[2, :last_x]], 0)
    hx_ym = jnp.concatenate([to_y[0], magnetic[0, :, :last_y]], 1)
    hz_ym = jnp.concatenate([to_y[1], magnetic[2, :, :last_y]], 1)
    hx_zm = jnp.concatenate([to_z[0], magnetic[0, :, :, :last_z]], 2)
    hy_zm = jnp.concatenate([to_z[1], magnetic[1, :, :, :last_z]], 2)
    source = port_source(base, sizes, port_cells, amp_row)
    electric = jnp.stack(
        [
            electric[0] + coef * (magnetic[2] - hz_ym - (magnetic[1] - hy_zm)),
            electric[1] + coef * (magnetic[0] - hx_zm - (magnetic[2] - hz_xm)),
            electric[2] + coef * (magnetic[1] - hy_xm - (magnetic[0] - hx_ym)) + source,
        ]
    )
    return (electric, magnetic)


def body(e_adjoint, h_adjoint, snapshots, material, permittivity, design_mask, ports, amplitudes):
    local_x, local_y, local_z = material.shape
    extent = (
        local_x * lax.axis_size("gx"),
        local_y * lax.axis_size("gy"),
        local_z * lax.axis_size("gz"),
    )
    base = (
        lax.axis_index("gx") * local_x,
        lax.axis_index("gy") * local_y,
        lax.axis_index("gz") * local_z,
    )
    plane = extent[1] * extent[2]
    port_cells = (ports // plane, ports // extent[2] % extent[1], ports % extent[2])
    coef = jnp.zeros(material.shape, jnp.float32)
    for material_no in range(permittivity.shape[0]):
        coef = coef + jnp.where(
            material == material_no, electric_step / permittivity[material_no], 0.0
        )
    corr = jnp.zeros(material.shape, jnp.float32)
    electric = e_adjoint
    magnetic = h_adjoint
    for step_no in range(STEPS):
        electric, magnetic = split_step(
            electric, magnetic, coef, base, port_cells, amplitudes[step_no]
        )
        change = snapshots[step_no].astype(jnp.float32) - snapshots[step_no + 1].astype(jnp.float32)
        corr = corr + jnp.sum(electric * change, axis=0)
    column = design_mask.astype(jnp.float32) * jnp.sum(corr, axis=2)
    gradient = lax.psum_scatter(column, "gz", scatter_dimension=1, tiled=True)
    return (electric, magnetic, gradient)


def solution(mesh):
    placed = (
        P(None, "gx", "gy", "gz"),
        P(None, "gx", "gy", "gz"),
        P(None, None, "gx", "gy", "gz"),
        P("gx", "gy", "gz"),
        P(),
        P("gx", "gy"),
        P(),
        P(),
    )
    return jax.shard_map(
        body,
        mesh=mesh,
        in_specs=placed,
        out_specs=(P(None, "gx", "gy", "gz"), P(None, "gx", "gy", "gz"), P("gx", ("gy", "gz"))),
        check_vma=False,
    )
```

profile of v0, /device:TPU:17, one launch (start us, length us, event | category | flops | bytes accessed | tf_op | source)
XLA Modules:
  0.0 120.0 jit_solution(1566137244136358882)
XLA Ops:
  0.6 0.9 slice.323
  1.5 1.3 %collective-permute-start = (f32[2,1,16,256]{3,2,1,0:T(8,128)S(1)}, f32[2,1,16,256]{3,2,1,0:T(8,128)S(1)}, u32[]{:S(2)}, u32[]{:S(2)}) collective-permute-start(f32[2,1,16,256]{3,2,1,0:T(8,128)S(1)} %slice.323), channel_id=1, source_target_pairs={{16,0},{17,1},{18,2},{19,3},{20,4},{21,5},{22,6},{23,7},{24,8},{25... | collective-permute-start | bytes 98312 | tf_op jit(solution)/shard_map/ppermute | solution.py:16
  2.8 1.1 slice.327
  3.9 2.1 %collective-permute-start.1 = (f32[2,32,1,256]{3,1,2,0:T(8,128)S(1)}, f32[2,32,1,256]{3,1,2,0:T(8,128)S(1)}, u32[]{:S(2)}, u32[]{:S(2)}) collective-permute-start(f32[2,32,1,256]{3,1,2,0:T(8,128)S(1)} %copy.478), channel_id=1, source_target_pairs={{4,0},{8,4},{12,8},{5,1},{9,5},{13,9},{6,2},{10,6},{14,10},{7,3},{... | collective-permute-start | bytes 196616 | tf_op jit(solution)/shard_map/ppermute | solution.py:16
  6.0 1.1 slice.334
  7.1 1.0 copy.483
  8.1 2.9 %collective-permute-start.2 = (f32[2,32,16,1]{3,1,2,0:T(8,128)}, f32[2,32,16,1]{3,1,2,0:T(8,128)}, u32[]{:S(2)}, u32[]{:S(2)}) collective-permute-start(f32[2,32,16,1]{3,1,2,0:T(8,128)} %copy.483), channel_id=1, source_target_pairs={{1,0},{2,1},{3,2},{5,4},{6,5},{7,6},{9,8},{10,9},{11,10},{13,12},{... | collective-permute-start | bytes 12296 | tf_op jit(solution)/shard_map/ppermute | solution.py:16
  10.9 0.9 fusion.72
  11.9 1.3 %fusion.74 = (f32[1,32,16,255]{3,2,1,0:T(8,128)}, f32[1,32,16,255]{3,2,1,0:T(8,128)}) fusion(f32[3,32,16,256]{3,2,1,0:T(8,128)S(1)} %copy-done.1), kind=kLoop, calls=%fused_computation.181 | loop fusion | bytes 2088960 | tf_op jit(solution)/shard_map/slice | solution.py:45
  13.2 0.9 fusion.73
  20.2 2.6 %fusion.70 = (f32[1,32,16,256]{3,2,1,0:T(8,128)}, f32[1,32,16,256]{3,2,1,0:T(8,128)}, f32[1,32,16,256]{3,2,1,0:T(8,128)S(1)}) fusion(f32[3,32,16,256]{3,2,1,0:T(8,128)} %param.9), kind=kLoop, calls=%fused_computation.177 | loop fusion | bytes 3145728 | tf_op jit(solution)/shard_map/slice | solution.py:51
  22.8 1.6 %fusion.69 = (bf16[1,3,32,16,256]{4,3,2,1,0:T(8,128)(2,1)}, bf16[1,3,32,16,256]{4,3,2,1,0:T(8,128)(2,1)}, bf16[1,3,32,16,256]{4,3,2,1,0:T(8,128)(2,1)}) fusion(bf16[3,3,32,16,256]{4,3,2,1,0:T(8,128)(2,1)S(1)} %copy-done.18), kind=kLoop, calls=%fused_computation.176 | loop fusion | bytes 4718592 | tf_op jit(solution)/shard_map/slice | solution.py:103
  25.0 1.3 %fusion.56 = (pred[256]{0:T(512)(128)(4,1)S(1)}, pred[256]{0:T(512)(128)(4,1)S(1)}) fusion(s32[]{:T(128)} %bitcast.50, s32[]{:T(128)S(6)} %mul.74, s32[]{:T(128)} %bitcast.46), kind=kLoop, calls=%fused_computation.147 | loop fusion | flops 768 | bytes 524 | tf_op jit(solution)/shard_map/eq | solution.py:30
  27.0 1.1 copy.556
  28.0 1.1 copy.477
  29.1 1.1 copy.555
  30.2 1.1 copy.480
  37.8 1.1 copy.554
  40.2 1.3 %slice_bitcast_fusion.38 = (f32[32,16,1]{2,0,1:T(8,128)S(1)}, f32[32,16,1]{2,0,1:T(8,128)S(1)}, f32[1,32,16,1]{3,1,2,0:T(8,128)S(1)}, f32[1,32,16,1]{3,1,2,0:T(8,128)S(1)}) fusion(f32[2,32,16,1]{3,1,2,0:T(8,128)} %collective-permute-done.2), kind=kLoop, calls=%fused_computation.170 | loop fusion | bytes 12288 | tf_op jit(solution)/shard_map/squeeze | solution.py:45
  41.7 3.6 %fusion.17 = (f32[1,32,16,256]{3,1,2,0:T(8,128)S(1)}, f32[1,32,16,256]{3,1,2,0:T(8,128)S(1)}, f32[1,32,16,256]{3,1,2,0:T(8,128)S(1)}) fusion(f32[1,1,16,256]{3,1,2,0:T(1,128)S(1)} %copy.435, f32[1,31,16,256]{3,1,2,0:T(8,128)S(1)} %copy.552, f32[1,32,1,256]{3,1,2,0:T(8,128)S(1)} %get-tuple-element.74, f32[1,32,15,256]{3,1,2,0:T(8,128)} %copy.477, ...), kind=kLoop, calls=%fused_computation.45 | loop fusion | flops 2752512 | bytes 7864320 | tf_op jit(solution)/shard_map/sub | solution.py:51
  46.0 3.1 %collective-permute-start.4 = (f32[2,32,16,1]{3,1,2,0:T(8,128)S(1)}, f32[2,32,16,1]{3,1,2,0:T(8,128)S(1)}, u32[]{:S(2)}, u32[]{:S(2)}) collective-permute-start(f32[2,32,16,1]{3,1,2,0:T(8,128)S(1)} %pad_maximum_fusion.6), channel_id=1, source_target_pairs={{0,1},{1,2},{2,3},{4,5},{5,6},{6,7},{8,9},{9,10},{10,11},{12,13},{... | collective-permute-start | bytes 12296 | tf_op jit(solution)/shard_map/ppermute | solution.py:16
  49.1 4.3 %collective-permute-start.5 = (f32[2,1,16,256]{3,1,2,0:T(1,128)S(1)}, f32[2,1,16,256]{3,1,2,0:T(1,128)S(1)}, u32[]{:S(2)}, u32[]{:S(2)}) collective-permute-start(f32[2,1,16,256]{3,1,2,0:T(1,128)S(1)} %pad_maximum_fusion.9), channel_id=1, source_target_pairs={{0,16},{1,17},{2,18},{3,19},{4,20},{5,21},{6,22},{7,23},{8,24},{9,... | collective-permute-start | bytes 98312 | tf_op jit(solution)/shard_map/ppermute | solution.py:16
  53.4 3.4 %collective-permute-start.3 = (f32[2,32,1,256]{3,1,2,0:T(8,128)S(1)}, f32[2,32,1,256]{3,1,2,0:T(8,128)S(1)}, u32[]{:S(2)}, u32[]{:S(2)}) collective-permute-start(f32[2,32,1,256]{3,1,2,0:T(8,128)S(1)} %slice.341), channel_id=1, source_target_pairs={{0,4},{4,8},{8,12},{1,5},{5,9},{9,13},{2,6},{6,10},{10,14},{3,7},{... | collective-permute-start | bytes 196616 | tf_op jit(solution)/shard_map/ppermute | solution.py:16
  56.9 2.7 %fusion.29 = (f32[32,16,256]{2,0,1:T(8,128)S(1)}, f32[32,16,256]{2,0,1:T(8,128)S(1)}, f32[32,16,256]{2,0,1:T(8,128)S(1)}) fusion(f32[32,16,255]{2,0,1:T(8,128)S(1)} %get-tuple-element.116, f32[32,16,1]{2,0,1:T(8,128)S(1)} %get-tuple-element.55, f32[31,16,256]{2,0,1:T(8,128)S(1)} %get-tuple-element.115, f32[1,16,256]{2,0,1:T(1,128)S(1)} %get-tuple-element.80, ...), kind=kLoop, calls=%fused_computation.65 | loop fusion | flops 5767168 | bytes 7864352 | tf_op jit(solution)/shard_map/add | solution.py:70
  60.3 1.0 slice_bitcast_fusion.6
  61.4 0.9 slice_bitcast_fusion.8
  62.3 1.8 %fusion.20 = (f32[32,16,256]{2,0,1:T(8,128)S(1)}, f32[32,16,256]{2,0,1:T(8,128)S(1)}) fusion(f32[32,16,256]{2,0,1:T(8,128)S(1)} %get-tuple-element.21, f32[32,15,256]{2,0,1:T(8,128)S(1)} %get-tuple-element.119, f32[32,1,256]{2,0,1:T(8,128)S(1)} %get-tuple-element.70, f32[32,16,255]{2,0,1:T(8,128)S(1)} %get-tuple-element.117, ...), kind=kLoop, calls=%fused_computation.50 | loop fusion | flops 4849664 | bytes 5767200 | tf_op jit(solution)/shard_map/add | solution.py:69
  64.2 3.1 %fusion.33 = f32[32,16,256]{2,0,1:T(8,128)S(1)} fusion(f32[32,16,256]{2,0,1:T(8,128)S(1)} %get-tuple-element.24, f32[31,16,256]{2,0,1:T(8,128)S(1)} %get-tuple-element.114, f32[1,16,256]{2,0,1:T(1,128)S(1)} %get-tuple-element.79, f32[32,16,256]{2,0,1:T(8,128)S(1)} %get-tuple-element.22, f32[32,15,256]{2,0,1:T(8,128)S(1)} %get-tuple-element.118, ...), kind=kLoop, calls=%fused_computation.71 | loop fusion | flops 5505024 | bytes 3670972 | tf_op jit(solution)/shard_map/add | solution.py:71
  67.3 0.8 slice_bitcast_fusion.14
  68.2 0.9 slice_bitcast_fusion.4
  69.6 0.8 slice_bitcast_fusion.15
  70.5 1.0 slice_bitcast_fusion.5
  71.7 1.9 %collective-permute-start.8 = (f32[2,32,16,1]{3,2,1,0:T(8,128)S(1)}, f32[2,32,16,1]{3,2,1,0:T(8,128)S(1)}, u32[]{:S(2)}, u32[]{:S(2)}) collective-permute-start(f32[2,32,16,1]{3,2,1,0:T(8,128)S(1)} %pad_maximum_fusion.5), channel_id=1, source_target_pairs={{1,0},{2,1},{3,2},{5,4},{6,5},{7,6},{9,8},{10,9},{11,10},{13,12},{... | collective-permute-start | bytes 12296 | tf_op jit(solution)/shard_map/ppermute | solution.py:16
  74.2 1.3 %collective-permute-start.6 = (f32[2,1,16,256]{3,1,2,0:T(1,128)}, f32[2,1,16,256]{3,1,2,0:T(1,128)}, u32[]{:S(2)}, u32[]{:S(2)}) collective-permute-start(f32[2,1,16,256]{3,1,2,0:T(1,128)} %pad_maximum_fusion.8), channel_id=1, source_target_pairs={{16,0},{17,1},{18,2},{19,3},{20,4},{21,5},{22,6},{23,7},{24,8},{25... | collective-permute-start | bytes 98312 | tf_op jit(solution)/shard_map/ppermute | solution.py:16
  75.5 2.1 %collective-permute-start.7 = (f32[2,32,1,256]{3,1,2,0:T(8,128)S(1)}, f32[2,32,1,256]{3,1,2,0:T(8,128)S(1)}, u32[]{:S(2)}, u32[]{:S(2)}) collective-permute-start(f32[2,32,1,256]{3,1,2,0:T(8,128)S(1)} %slice.372), channel_id=1, source_target_pairs={{4,0},{8,4},{12,8},{5,1},{9,5},{13,9},{6,2},{10,6},{14,10},{7,3},{... | collective-permute-start | bytes 196616 | tf_op jit(solution)/shard_map/ppermute | solution.py:16
  77.6 4.7 %collective-permute-done.8 = f32[2,32,16,1]{3,2,1,0:T(8,128)S(1)} collective-permute-done((f32[2,32,16,1]{3,2,1,0:T(8,128)S(1)}, f32[2,32,16,1]{3,2,1,0:T(8,128)S(1)}, u32[]{:S(2)}, u32[]{:S(2)}) %collective-permute-start.8) | collective-permute-done | bytes 4128 | tf_op jit(solution)/shard_map/ppermute | solution.py:16
  83.0 1.1 copy.451
  84.5 0.9 copy.452
  86.2 3.1 %fusion.39 = (f32[32,16,256]{2,0,1:T(8,128)S(1)}, f32[32,16,256]{2,0,1:T(8,128)S(1)}, f32[32,16,256]{2,0,1:T(8,128)S(1)}) fusion(f32[32,16,256]{2,0,1:T(8,128)} %copy-done.9, f32[32,16,256]{2,0,1:T(8,128)S(1)} %fusion.33, f32[32,1,256]{2,0,1:T(8,128)S(1)} %get-tuple-element.67, f32[32,15,256]{2,0,1:T(8,128)} %slice_bitcast_fusion.14, ...), kind=kLoop, calls=%fused_computation.81 | loop fusion | flops 2752512 | bytes 7864320 | tf_op jit(solution)/shard_map/sub | solution.py:49
  90.0 1.9 %collective-permute-start.10 = (f32[2,32,16,1]{3,1,2,0:T(8,128)S(1)}, f32[2,32,16,1]{3,1,2,0:T(8,128)S(1)}, u32[]{:S(2)}, u32[]{:S(2)}) collective-permute-start(f32[2,32,16,1]{3,1,2,0:T(8,128)S(1)} %pad_maximum_fusion.4), channel_id=1, source_target_pairs={{0,1},{1,2},{2,3},{4,5},{5,6},{6,7},{8,9},{9,10},{10,11},{12,13},{... | collective-permute-start | bytes 12296 | tf_op jit(solution)/shard_map/ppermute | solution.py:16
  91.9 2.1 %copy.471 = f32[3,32,16,256]{3,2,1,0:T(8,128)} copy(f32[3,32,16,256]{3,1,2,0:T(8,128)S(1)} %pad_maximum_fusion.2) | data formatting | bytes 3145728
  94.0 3.6 %collective-permute-start.11 = (f32[2,1,16,256]{3,1,2,0:T(1,128)S(1)}, f32[2,1,16,256]{3,1,2,0:T(1,128)S(1)}, u32[]{:S(2)}, u32[]{:S(2)}) collective-permute-start(f32[2,1,16,256]{3,1,2,0:T(1,128)S(1)} %pad_maximum_fusion.7), channel_id=1, source_target_pairs={{0,16},{1,17},{2,18},{3,19},{4,20},{5,21},{6,22},{7,23},{8,24},{9,... | collective-permute-start | bytes 98312 | tf_op jit(solution)/shard_map/ppermute | solution.py:16
  97.6 3.1 %collective-permute-start.9 = (f32[2,32,1,256]{3,1,2,0:T(8,128)S(1)}, f32[2,32,1,256]{3,1,2,0:T(8,128)S(1)}, u32[]{:S(2)}, u32[]{:S(2)}) collective-permute-start(f32[2,32,1,256]{3,1,2,0:T(8,128)S(1)} %slice.383), channel_id=1, source_target_pairs={{0,4},{4,8},{8,12},{1,5},{5,9},{9,13},{2,6},{6,10},{10,14},{3,7},{... | collective-permute-start | bytes 196616 | tf_op jit(solution)/shard_map/ppermute | solution.py:16
  101.5 1.1 collective-permute-done.9
  103.5 2.8 %fusion.55 = f32[1,32,16,256]{3,1,2,0:T(8,128)S(1)} fusion(f32[32,16,256]{2,0,1:T(8,128)S(1)} %fusion.33, f32[32,16,256]{2,0,1:T(8,128)S(1)} %get-tuple-element.45, f32[31,16,256]{2,0,1:T(8,128)S(1)} %slice_bitcast_fusion, f32[1,16,256]{2,0,1:T(1,128)S(1)} %get-tuple-element.76, f32[32,16,256]{2,0,1:T(8,128)S(1)} %get-tuple-element.43, ...), kind=kLoop, calls=%fused_computation.105 | loop fusion | flops 5505024 | bytes 3670972 | tf_op jit(solution)/shard_map/stack | solution.py:67
  106.3 2.3 %fusion.5 = (f32[32,16,256]{2,0,1:T(8,128)S(1)}, f32[32,16,256]{2,0,1:T(8,128)S(1)}, f32[3,32,16,256]{3,1,2,0:T(8,128)}) fusion(bf16[1,3,32,16,256]{4,3,2,1,0:T(8,128)(2,1)S(1)} %copy-done.17, bf16[1,3,32,16,256]{4,3,2,1,0:T(8,128)(2,1)S(1)} %copy-done.16, f32[1,32,16,256]{3,1,2,0:T(8,128)S(1)} %fusion.55, f32[1,32,16,256]{3,1,2,0:T(8,128)S(1)} %fusion.50, ...), kind=kLoop, calls=%fused_computation.7 | loop fusion | flops 4849664 | bytes 8126464 | tf_op jit(solution)/shard_map/reduce_sum | solution.py:104
  108.9 7.0 %all-reduce = f32[32,16]{0,1:T(8,128)S(1)} all-reduce(f32[32,16]{0,1:T(8,128)S(1)} %convert_multiply_fusion), channel_id=2, replica_groups=mesh['gx'=2,'gy'=4,'gz'=4] {'gz'}, use_global_device_ids=true, to_apply=%region_3.4.clone | all-reduce | flops 512 | bytes 4096
  115.9 3.5 %copy.470 = f32[3,32,16,256]{3,2,1,0:T(8,128)} copy(f32[3,32,16,256]{3,1,2,0:T(8,128)} %get-tuple-element.28) | data formatting | bytes 3145728
  (169 shorter events, 16.6 us)
Async XLA Ops:
  0.6 10.3 %copy-start.1 = (f32[3,32,16,256]{3,2,1,0:T(8,128)S(1)}, f32[3,32,16,256]{3,2,1,0:T(8,128)}, u32[]{:S(2)}) copy-start(f32[3,32,16,256]{3,2,1,0:T(8,128)} %param.8) | copy-start | bytes 4718596
  1.5 40.0 %collective-permute-start = (f32[2,1,16,256]{3,2,1,0:T(8,128)S(1)}, f32[2,1,16,256]{3,2,1,0:T(8,128)S(1)}, u32[]{:S(2)}, u32[]{:S(2)}) collective-permute-start(f32[2,1,16,256]{3,2,1,0:T(8,128)S(1)} %slice.323), channel_id=1, source_target_pairs={{16,0},{17,1},{18,2},{19,3},{20,4},{21,5},{22,6},{23,7},{24,8},{25... | collective-permute-start | bytes 98312 | tf_op jit(solution)/shard_map/ppermute | solution.py:16
  3.9 37.7 %collective-permute-start.1 = (f32[2,32,1,256]{3,1,2,0:T(8,128)S(1)}, f32[2,32,1,256]{3,1,2,0:T(8,128)S(1)}, u32[]{:S(2)}, u32[]{:S(2)}) collective-permute-start(f32[2,32,1,256]{3,1,2,0:T(8,128)S(1)} %copy.478), channel_id=1, source_target_pairs={{4,0},{8,4},{12,8},{5,1},{9,5},{13,9},{6,2},{10,6},{14,10},{7,3},{... | collective-permute-start | bytes 196616 | tf_op jit(solution)/shard_map/ppermute | solution.py:16
  8.1 32.2 %collective-permute-start.2 = (f32[2,32,16,1]{3,1,2,0:T(8,128)}, f32[2,32,16,1]{3,1,2,0:T(8,128)}, u32[]{:S(2)}, u32[]{:S(2)}) collective-permute-start(f32[2,32,16,1]{3,1,2,0:T(8,128)} %copy.483), channel_id=1, source_target_pairs={{1,0},{2,1},{3,2},{5,4},{6,5},{7,6},{9,8},{10,9},{11,10},{13,12},{... | collective-permute-start | bytes 12296 | tf_op jit(solution)/shard_map/ppermute | solution.py:16
  13.2 5.6 %copy-start.25 = (f32[2,3]{1,0:T(2,128)S(1)}, f32[2,3]{1,0:T(2,128)}, u32[]{:S(2)}) copy-start(f32[2,3]{1,0:T(2,128)} %param.15) | copy-start | bytes 76
  13.2 6.3 %copy-start.24 = (f32[8]{0:T(128)S(1)}, f32[8]{0:T(128)}, u32[]{:S(2)}) copy-start(f32[8]{0:T(128)} %param.12) | copy-start | bytes 100
  16.1 48.0 %copy-start.31 = (pred[32]{0:T(512)(128)(4,1)}, pred[32]{0:T(512)(128)(4,1)S(1)}, u32[]{:S(2)}) copy-start(pred[32]{0:T(512)(128)(4,1)S(1)} %fusion.65) | copy-start | bytes 100
  16.8 47.3 %copy-start.33 = (pred[32]{0:T(512)(128)(4,1)}, pred[32]{0:T(512)(128)(4,1)S(1)}, u32[]{:S(2)}) copy-start(pred[32]{0:T(512)(128)(4,1)S(1)} %fusion.63) | copy-start | bytes 100
  17.5 46.6 %copy-start.35 = (pred[32]{0:T(512)(128)(4,1)}, pred[32]{0:T(512)(128)(4,1)S(1)}, u32[]{:S(2)}) copy-start(pred[32]{0:T(512)(128)(4,1)S(1)} %fusion.64) | copy-start | bytes 100
  18.1 46.0 %copy-start.37 = (pred[16]{0:T(512)(128)(4,1)}, pred[16]{0:T(512)(128)(4,1)S(1)}, u32[]{:S(2)}) copy-start(pred[16]{0:T(512)(128)(4,1)S(1)} %fusion.61) | copy-start | bytes 52
  18.9 45.3 %copy-start.39 = (pred[16]{0:T(512)(128)(4,1)}, pred[16]{0:T(512)(128)(4,1)S(1)}, u32[]{:S(2)}) copy-start(pred[16]{0:T(512)(128)(4,1)S(1)} %fusion.60) | copy-start | bytes 52
  20.2 2.6 %copy-start.18 = (bf16[3,3,32,16,256]{4,3,2,1,0:T(8,128)(2,1)S(1)}, bf16[3,3,32,16,256]{4,3,2,1,0:T(8,128)(2,1)}, u32[]{:S(2)}) copy-start(bf16[3,3,32,16,256]{4,3,2,1,0:T(8,128)(2,1)} %param.10) | copy-start | bytes 7077892
  22.8 18.8 %copy-start.7 = (f32[1,32,16,256]{3,2,1,0:T(8,128)}, f32[1,32,16,256]{3,2,1,0:T(8,128)S(1)}, u32[]{:S(2)}) copy-start(f32[1,32,16,256]{3,2,1,0:T(8,128)S(1)} %get-tuple-element.31) | copy-start | bytes 1572868
  25.0 39.2 %copy-start.41 = (pred[256]{0:T(512)(128)(4,1)}, pred[256]{0:T(512)(128)(4,1)S(1)}, u32[]{:S(2)}) copy-start(pred[256]{0:T(512)(128)(4,1)S(1)} %fusion.58) | copy-start | bytes 772
  26.3 37.9 %copy-start.27 = (pred[256]{0:T(512)(128)(4,1)}, pred[256]{0:T(512)(128)(4,1)S(1)}, u32[]{:S(2)}) copy-start(pred[256]{0:T(512)(128)(4,1)S(1)} %get-tuple-element.120) | copy-start | bytes 772
  26.3 37.9 %copy-start.29 = (pred[256]{0:T(512)(128)(4,1)}, pred[256]{0:T(512)(128)(4,1)S(1)}, u32[]{:S(2)}) copy-start(pred[256]{0:T(512)(128)(4,1)S(1)} %get-tuple-element.121) | copy-start | bytes 772
  26.9 37.2 %copy-start.43 = (pred[16]{0:T(512)(128)(4,1)}, pred[16]{0:T(512)(128)(4,1)S(1)}, u32[]{:S(2)}) copy-start(pred[16]{0:T(512)(128)(4,1)S(1)} %fusion.62) | copy-start | bytes 52
  28.0 8.7 %copy-start.21 = (f32[1,31,16,256]{3,2,1,0:T(8,128)S(1)}, f32[1,31,16,256]{3,2,1,0:T(8,128)}, u32[]{:S(2)}) copy-start(f32[1,31,16,256]{3,2,1,0:T(8,128)} %get-tuple-element.34) | copy-start | bytes 1523716
  30.2 7.2 %copy-start.20 = (f32[1,32,16,255]{3,2,1,0:T(8,128)S(1)}, f32[1,32,16,255]{3,2,1,0:T(8,128)}, u32[]{:S(2)}) copy-start(f32[1,32,16,255]{3,2,1,0:T(8,128)} %get-tuple-element.39) | copy-start | bytes 1566724
  32.0 5.8 %copy-start.19 = (f32[1,32,16,255]{3,2,1,0:T(8,128)S(1)}, f32[1,32,16,255]{3,2,1,0:T(8,128)}, u32[]{:S(2)}) copy-start(f32[1,32,16,255]{3,2,1,0:T(8,128)} %get-tuple-element.40) | copy-start | bytes 1566724
  37.1 1.8 %copy-start.46 = (u32[32]{0:T(128)S(1)}, u32[32]{0:T(128)}, u32[]{:S(2)}) copy-start(u32[32]{0:T(128)} %constant.98) | copy-start | bytes 388
  37.4 4.3 %copy-start.3 = (f32[1,31,16,256]{3,1,2,0:T(8,128)}, f32[1,31,16,256]{3,1,2,0:T(8,128)S(1)}, u32[]{:S(2)}) copy-start(f32[1,31,16,256]{3,1,2,0:T(8,128)S(1)} %copy.551) | copy-start | bytes 1523716
  37.7 7.5 %copy-start.5 = (f32[1,32,16,255]{3,1,2,0:T(8,128)}, f32[1,32,16,255]{3,1,2,0:T(8,128)S(1)}, u32[]{:S(2)}) copy-start(f32[1,32,16,255]{3,1,2,0:T(8,128)S(1)} %copy.553) | copy-start | bytes 1566724
  40.2 1.5 %copy-start.10 = (f32[1,32,16,255]{3,1,2,0:T(8,128)S(1)}, f32[1,32,16,255]{3,1,2,0:T(8,128)}, u32[]{:S(2)}) copy-start(f32[1,32,16,255]{3,1,2,0:T(8,128)} %copy.554) | copy-start | bytes 1566724
  40.2 1.5 %copy-start.12 = (f32[1,32,16,256]{3,2,1,0:T(8,128)S(1)}, f32[1,32,16,256]{3,2,1,0:T(8,128)}, u32[]{:S(2)}) copy-start(f32[1,32,16,256]{3,2,1,0:T(8,128)} %get-tuple-element.29) | copy-start | bytes 1572868
  45.9 11.0 %copy-start = (s32[32,16,256]{2,1,0:T(8,128)S(1)}, s32[32,16,256]{2,1,0:T(8,128)}, u32[]{:S(2)}) copy-start(s32[32,16,256]{2,1,0:T(8,128)} %param.11) | copy-start | bytes 1572868
  45.9 11.0 %copy-start.13 = (f32[1,32,16,256]{3,2,1,0:T(8,128)S(1)}, f32[1,32,16,256]{3,2,1,0:T(8,128)}, u32[]{:S(2)}) copy-start(f32[1,32,16,256]{3,2,1,0:T(8,128)} %get-tuple-element.30) | copy-start | bytes 1572868
  45.9 11.0 %copy-start.22 = (f32[1,32,15,256]{3,1,2,0:T(8,128)S(1)}, f32[1,32,15,256]{3,1,2,0:T(8,128)}, u32[]{:S(2)}) copy-start(f32[1,32,15,256]{3,1,2,0:T(8,128)} %copy.556) | copy-start | bytes 1474564
  45.9 11.0 %copy-start.23 = (f32[1,32,15,256]{3,1,2,0:T(8,128)S(1)}, f32[1,32,15,256]{3,1,2,0:T(8,128)}, u32[]{:S(2)}) copy-start(f32[1,32,15,256]{3,1,2,0:T(8,128)} %copy.555) | copy-start | bytes 1474564
  46.0 10.9 %collective-permute-start.4 = (f32[2,32,16,1]{3,1,2,0:T(8,128)S(1)}, f32[2,32,16,1]{3,1,2,0:T(8,128)S(1)}, u32[]{:S(2)}, u32[]{:S(2)}) collective-permute-start(f32[2,32,16,1]{3,1,2,0:T(8,128)S(1)} %pad_maximum_fusion.6), channel_id=1, source_target_pairs={{0,1},{1,2},{2,3},{4,5},{5,6},{6,7},{8,9},{9,10},{10,11},{12,13},{... | collective-permute-start | bytes 12296 | tf_op jit(solution)/shard_map/ppermute | solution.py:16
  49.1 7.7 %collective-permute-start.5 = (f32[2,1,16,256]{3,1,2,0:T(1,128)S(1)}, f32[2,1,16,256]{3,1,2,0:T(1,128)S(1)}, u32[]{:S(2)}, u32[]{:S(2)}) collective-permute-start(f32[2,1,16,256]{3,1,2,0:T(1,128)S(1)} %pad_maximum_fusion.9), channel_id=1, source_target_pairs={{0,16},{1,17},{2,18},{3,19},{4,20},{5,21},{6,22},{7,23},{8,24},{9,... | collective-permute-start | bytes 98312 | tf_op jit(solution)/shard_map/ppermute | solution.py:16
  53.4 8.8 %collective-permute-start.3 = (f32[2,32,1,256]{3,1,2,0:T(8,128)S(1)}, f32[2,32,1,256]{3,1,2,0:T(8,128)S(1)}, u32[]{:S(2)}, u32[]{:S(2)}) collective-permute-start(f32[2,32,1,256]{3,1,2,0:T(8,128)S(1)} %slice.341), channel_id=1, source_target_pairs={{0,4},{4,8},{8,12},{1,5},{5,9},{9,13},{2,6},{6,10},{10,14},{3,7},{... | collective-permute-start | bytes 196616 | tf_op jit(solution)/shard_map/ppermute | solution.py:16
  59.7 2.6 %copy-start.14 = (f32[32,16,256]{2,0,1:T(8,128)}, f32[32,16,256]{2,0,1:T(8,128)S(1)}, u32[]{:S(2)}) copy-start(f32[32,16,256]{2,0,1:T(8,128)S(1)} %get-tuple-element.21) | copy-start | bytes 1572868
  59.7 4.5 %copy-start.9 = (f32[32,16,256]{2,0,1:T(8,128)}, f32[32,16,256]{2,0,1:T(8,128)S(1)}, u32[]{:S(2)}) copy-start(f32[32,16,256]{2,0,1:T(8,128)S(1)} %get-tuple-element.22) | copy-start | bytes 1572868
  60.0 2.2 %copy-start.4 = (f32[1,31,16,256]{3,1,2,0:T(8,128)S(1)}, f32[1,31,16,256]{3,1,2,0:T(8,128)}, u32[]{:S(2)}) copy-start(f32[1,31,16,256]{3,1,2,0:T(8,128)} %copy-done.3) | copy-start | bytes 1523716
  60.0 2.2 %copy-start.6 = (f32[1,32,16,255]{3,1,2,0:T(8,128)S(1)}, f32[1,32,16,255]{3,1,2,0:T(8,128)}, u32[]{:S(2)}) copy-start(f32[1,32,16,255]{3,1,2,0:T(8,128)} %copy-done.5) | copy-start | bytes 1566724
  60.0 2.2 %copy-start.8 = (f32[1,32,16,256]{3,2,1,0:T(8,128)S(1)}, f32[1,32,16,256]{3,2,1,0:T(8,128)}, u32[]{:S(2)}) copy-start(f32[1,32,16,256]{3,2,1,0:T(8,128)} %copy-done.7) | copy-start | bytes 1572868
  64.1 3.2 %copy-start.2 = (f32[32,16,256]{2,0,1:T(8,128)}, f32[32,16,256]{2,0,1:T(8,128)S(1)}, u32[]{:S(2)}) copy-start(f32[32,16,256]{2,0,1:T(8,128)S(1)} %get-tuple-element.24) | copy-start | bytes 1572868
  71.7 10.6 %collective-permute-start.8 = (f32[2,32,16,1]{3,2,1,0:T(8,128)S(1)}, f32[2,32,16,1]{3,2,1,0:T(8,128)S(1)}, u32[]{:S(2)}, u32[]{:S(2)}) collective-permute-start(f32[2,32,16,1]{3,2,1,0:T(8,128)S(1)} %pad_maximum_fusion.5), channel_id=1, source_target_pairs={{1,0},{2,1},{3,2},{5,4},{6,5},{7,6},{9,8},{10,9},{11,10},{13,12},{... | collective-permute-start | bytes 12296 | tf_op jit(solution)/shard_map/ppermute | solution.py:16
  74.2 11.2 %collective-permute-start.6 = (f32[2,1,16,256]{3,1,2,0:T(1,128)}, f32[2,1,16,256]{3,1,2,0:T(1,128)}, u32[]{:S(2)}, u32[]{:S(2)}) collective-permute-start(f32[2,1,16,256]{3,1,2,0:T(1,128)} %pad_maximum_fusion.8), channel_id=1, source_target_pairs={{16,0},{17,1},{18,2},{19,3},{20,4},{21,5},{22,6},{23,7},{24,8},{25... | collective-permute-start | bytes 98312 | tf_op jit(solution)/shard_map/ppermute | solution.py:16
  75.5 10.6 %collective-permute-start.7 = (f32[2,32,1,256]{3,1,2,0:T(8,128)S(1)}, f32[2,32,1,256]{3,1,2,0:T(8,128)S(1)}, u32[]{:S(2)}, u32[]{:S(2)}) collective-permute-start(f32[2,32,1,256]{3,1,2,0:T(8,128)S(1)} %slice.372), channel_id=1, source_target_pairs={{4,0},{8,4},{12,8},{5,1},{9,5},{13,9},{6,2},{10,6},{14,10},{7,3},{... | collective-permute-start | bytes 196616 | tf_op jit(solution)/shard_map/ppermute | solution.py:16
  90.0 10.7 %collective-permute-start.10 = (f32[2,32,16,1]{3,1,2,0:T(8,128)S(1)}, f32[2,32,16,1]{3,1,2,0:T(8,128)S(1)}, u32[]{:S(2)}, u32[]{:S(2)}) collective-permute-start(f32[2,32,16,1]{3,1,2,0:T(8,128)S(1)} %pad_maximum_fusion.4), channel_id=1, source_target_pairs={{0,1},{1,2},{2,3},{4,5},{5,6},{6,7},{8,9},{9,10},{10,11},{12,13},{... | collective-permute-start | bytes 12296 | tf_op jit(solution)/shard_map/ppermute | solution.py:16
  94.0 6.8 %collective-permute-start.11 = (f32[2,1,16,256]{3,1,2,0:T(1,128)S(1)}, f32[2,1,16,256]{3,1,2,0:T(1,128)S(1)}, u32[]{:S(2)}, u32[]{:S(2)}) collective-permute-start(f32[2,1,16,256]{3,1,2,0:T(1,128)S(1)} %pad_maximum_fusion.7), channel_id=1, source_target_pairs={{0,16},{1,17},{2,18},{3,19},{4,20},{5,21},{6,22},{7,23},{8,24},{9,... | collective-permute-start | bytes 98312 | tf_op jit(solution)/shard_map/ppermute | solution.py:16
  97.6 5.0 %collective-permute-start.9 = (f32[2,32,1,256]{3,1,2,0:T(8,128)S(1)}, f32[2,32,1,256]{3,1,2,0:T(8,128)S(1)}, u32[]{:S(2)}, u32[]{:S(2)}) collective-permute-start(f32[2,32,1,256]{3,1,2,0:T(8,128)S(1)} %slice.383), channel_id=1, source_target_pairs={{0,4},{4,8},{8,12},{1,5},{5,9},{9,13},{2,6},{6,10},{10,14},{3,7},{... | collective-permute-start | bytes 196616 | tf_op jit(solution)/shard_map/ppermute | solution.py:16
  103.4 2.9 %copy-start.15 = (bf16[1,3,32,16,256]{4,3,2,1,0:T(8,128)(2,1)S(1)}, bf16[1,3,32,16,256]{4,3,2,1,0:T(8,128)(2,1)}, u32[]{:S(2)}) copy-start(bf16[1,3,32,16,256]{4,3,2,1,0:T(8,128)(2,1)} %get-tuple-element.25) | copy-start | bytes 2359300
  103.5 2.9 %copy-start.16 = (bf16[1,3,32,16,256]{4,3,2,1,0:T(8,128)(2,1)S(1)}, bf16[1,3,32,16,256]{4,3,2,1,0:T(8,128)(2,1)}, u32[]{:S(2)}) copy-start(bf16[1,3,32,16,256]{4,3,2,1,0:T(8,128)(2,1)} %get-tuple-element.26) | copy-start | bytes 2359300
  103.5 2.9 %copy-start.17 = (bf16[1,3,32,16,256]{4,3,2,1,0:T(8,128)(2,1)S(1)}, bf16[1,3,32,16,256]{4,3,2,1,0:T(8,128)(2,1)}, u32[]{:S(2)}) copy-start(bf16[1,3,32,16,256]{4,3,2,1,0:T(8,128)(2,1)} %get-tuple-element.27) | copy-start | bytes 2359300
  106.3 2.5 %copy-start.26 = (s32[32,16]{0,1:T(8,128)S(1)}, s32[32,16]{0,1:T(8,128)}, u32[]{:S(2)}) copy-start(s32[32,16]{0,1:T(8,128)} %param.13) | copy-start | bytes 6148
  (11 other events, 9.4 us)
where the time goes:
time: 122 us; the launch traced here: 120 us
  local copies, waits for them, and re-layouts  39.9 us (33%)
  starting transfers between devices  30.9 us (25%)
  other arithmetic  28.5 us (23%)
  between operations  7.94 us (7%)
  blocking collectives  7.04 us (6%)
  waiting for transfers between devices  5.75 us (5%)
    ppermute x12, starting transfers between devices, from_behind(): return lax.ppermute(array, axis, pairs)  30.9 us
    unnamed x104, local copies, waits for them, and re-layouts  12.3 us
    unnamed x1, blocking collectives  7.04 us
    ppermute x12, waiting for transfers between devices, from_behind(): return lax.ppermute(array, axis, pairs)  5.75 us
    another operation x6, other arithmetic, split_step(): jnp.stack([electric[0] + coef * (magnetic[2] - hz_ym - (magnetic[1] - hy_...  5.04 us
    sub x1, other arithmetic, split_step(): magnetic[2] - magnetic_step * (ey_xp - electric[1] - (ex_yp - electric[0]))  3.55 us
    sub x1, other arithmetic, split_step(): magnetic[0] - magnetic_step * (ez_yp - electric[2] - (ey_zp - electric[1]))  3.14 us
    add x1, other arithmetic, split_step(): electric[2] + coef * (magnetic[1] - hy_xm - (magnetic[0] - hx_ym)) + source  3.1 us
  transfers between devices with their start and end apart: 12, of which 2 were waited for; matrix products, arithmetic and copies ran while one was open for 33% of the time, Pallas kernels for 0%

commit v1 on v0

v1 whole, which is shorter than its diff:
```python
import functools

import jax
import jax.numpy as jnp
from jax import lax
from jax.experimental import pallas as pl
from jax.experimental.pallas import tpu as pltpu
from jax.sharding import PartitionSpec as P

STEPS = 2
FIELDS = 7
HALO = 8
HIGHEST = lax.Precision.HIGHEST

magnetic_step = 0.5
electric_step = 0.5

VM = pl.BlockSpec(memory_space=pltpu.VMEM)
SM = pl.BlockSpec(memory_space=pltpu.SMEM)


def in_vmem(array):
    return pltpu.with_memory_space_constraint(array, pltpu.VMEM)


def swap_table(size, odd):
    table = list(range(size))
    for i in range(odd, size - 1, 2):
        table[i], table[i + 1] = i + 1, i
    return table


def swaps(size):
    return [odd for odd in (0, 1) if odd + 1 < size]


def sends_up(index, odd):
    return lax.rem(index, 2) == odd


def has_partner(index, size, odd):
    up = sends_up(index, odd)
    return (up & (index + 1 < size)) | (jnp.logical_not(up) & (index >= 1))


def slots(axis):
    near = [(f, 0) for f in range(FIELDS)]
    far = [(f, 1) for f in range(3)] + [(3 + f, 1) for f in range(3) if f != axis]
    return near + far


def coef_of(material, perm_ref):
    count = perm_ref.shape[0]
    out = jnp.zeros(material.shape, jnp.float32)
    for i in range(count):
        value = electric_step / jnp.full((1, 1), perm_ref[i], jnp.float32)
        out = jnp.where(material == i, value, out)
    return out


def tiled(array):
    *lead, nx, ny, nz = array.shape
    n = len(lead)
    split = array.reshape(*lead, nx, ny // 8, 8, nz // 128, 128)
    order = tuple(range(n + 2)) + (n + 3, n + 2, n + 4)
    return split.transpose(order).reshape(*lead, nx * ny * nz // 128, 128)


def untiled(array, dims):
    nx, ny, nz = dims
    lead = array.shape[:-2]
    n = len(lead)
    split = array.reshape(*lead, nx, ny // 8, nz // 128, 8, 128)
    order = tuple(range(n + 2)) + (n + 3, n + 2, n + 4)
    return split.transpose(order).reshape(*lead, nx, ny, nz)


def pack_faces(dims, sizes, e_ref, h_ref, m_ref, perm_ref, *outs):
    nx, ny, nz = dims
    lanes = nz // 128
    plane = ny * lanes
    gx, gy = lax.axis_index("gx"), lax.axis_index("gy")
    xs, ys = swaps(sizes[0]), swaps(sizes[1])

    def rows(field, index):
        if field < 3:
            return e_ref[field, index, :]
        if field < 6:
            return h_ref[field - 3, index, :]
        return coef_of(m_ref[index, :], perm_ref)

    def y_row(y, z):
        return ((y // 8) * lanes + z) * 8 + y % 8

    def x_ends(odd):
        up = sends_up(gx, odd)
        return jnp.where(up, nx - 1, 0) * plane, jnp.where(up, nx - 2, 1) * plane

    def y_ends(odd, z):
        up = sends_up(gy, odd)
        return (
            jnp.where(up, y_row(ny - 1, z), y_row(0, z)),
            jnp.where(up, y_row(ny - 2, z), y_row(1, z)),
        )

    at = 0
    for odd in xs:
        place = x_ends(odd)
        for k, (f, far) in enumerate(slots(0)):
            outs[at][k] = rows(f, pl.ds(pl.multiple_of(place[far], 8), plane))
        at += 1
    for odd in ys:
        for z in range(lanes):
            place = y_ends(odd, z)
            for k, (f, far) in enumerate(slots(1)):
                outs[at][k, z] = rows(f, pl.ds(place[far], nx, stride=plane))
        at += 1
    for ox in xs:
        for oy in ys:
            px = x_ends(ox)
            for z in range(lanes):
                py = y_ends(oy, z)
                for f in range(FIELDS):
                    for k in range(4):
                        outs[at][z, pl.ds(4 * f + k, 1), :] = rows(f, pl.ds(px[k // 2] + py[k % 2], 1))
            at += 1


def gather_block(dims, sizes, e_ref, h_ref, m_ref, perm_ref, *refs):
    nx, ny, nz = dims
    lanes = nz // 128
    step = ny + HALO
    gx, gy = lax.axis_index("gx"), lax.axis_index("gy")
    xs, ys = swaps(sizes[0]), swaps(sizes[1])
    n_msgs = len(xs) + len(ys) + len(xs) * len(ys)
    msgs = refs[:n_msgs]
    ext, up_ref, down_ref, packed = refs[n_msgs:]

    def own_plane(x, carry):
        for f in range(FIELDS):
            for z in range(lanes):
                for t in range(ny // 8):
                    here = pl.ds(pl.multiple_of((x * (ny // 8) + t) * lanes * 8 + z * 8, 8), 8)
                    there = pl.ds(pl.multiple_of((x + 2) * step + t * 8, 8), 8)
                    if f < 3:
                        ext[f, z, there, :] = e_ref[f, here, :]
                    elif f < 6:
                        ext[f, z, there, :] = h_ref[f - 3, here, :]
                    else:
                        ext[f, z, there, :] = coef_of(m_ref[here, :], perm_ref)
                ext[f, z, pl.ds(pl.multiple_of((x + 2) * step + ny, 8), HALO), :] = jnp.zeros(
                    (HALO, 128), jnp.float32
                )
        return carry

    lax.fori_loop(0, nx, own_plane, 0)
    for f in range(FIELDS):
        for z in range(lanes):
            for p in (0, 1, nx + 2, nx + 3):
                ext[f, z, pl.ds(p * step, step), :] = jnp.zeros((step, 128), jnp.float32)

    def planes(odd):
        high = sends_up(gx, odd)
        return jnp.where(high, nx + 2, 1), jnp.where(high, nx + 3, 0)

    def lines(odd):
        high = sends_up(gy, odd)
        return jnp.where(high, ny, step - 1), jnp.where(high, ny + 1, step - 2)

    at = 0
    for odd in xs:
        ok = has_partner(gx, sizes[0], odd)
        place = planes(odd)
        for k, (f, far) in enumerate(slots(0)):
            for z in range(lanes):
                for t in range(ny // 8):
                    ext[f, z, pl.ds(pl.multiple_of(place[far] * step + t * 8, 8), 8), :] = jnp.where(
                        ok, msgs[at][k, pl.ds((t * lanes + z) * 8, 8), :], 0.0
                    )
        at += 1
    for odd in ys:
        ok = has_partner(gy, sizes[1], odd)
        place = lines(odd)
        for k, (f, far) in enumerate(slots(1)):
            for z in range(lanes):
                ext[f, z, pl.ds(2 * step + place[far], nx, stride=step), :] = jnp.where(
                    ok, msgs[at][k, z], 0.0
                )
        at += 1
    for ox in xs:
        for oy in ys:
            ok = has_partner(gx, sizes[0], ox) & has_partner(gy, sizes[1], oy)
            px, py = planes(ox), lines(oy)
            for z in range(lanes):
                for f in range(FIELDS):
                    for k in range(4):
                        ext[f, z, pl.ds(px[k // 2] * step + py[k % 2], 1), :] = jnp.where(
                            ok, msgs[at][z, pl.ds(4 * f + k, 1), :], 0.0
                        )
            at += 1

    total = (nx + 4) * step
    padded = packed.shape[0]
    lane = lax.broadcasted_iota(jnp.int32, (step, 128), 1)

    def pack_plane(p, carry):
        index = pl.ds(pl.multiple_of(p * step, 8), step)
        out = jnp.zeros((step, 128), jnp.float32)
        for f in range(FIELDS):
            both = jnp.where(lane < 64, ext[f, 0, index, :], ext[f, lanes - 1, index, :])
            turned = pltpu.roll(both, 4 * f + 2, 1)
            out = jnp.where((lane >= 4 * f) & (lane < 4 * f + 4), turned, out)
        packed[index, :] = out
        return carry

    lax.fori_loop(0, nx + 4, pack_plane, 0)
    if padded > total:
        packed[total:padded, :] = jnp.zeros((padded - total, 128), jnp.float32)
    for b in range(padded // 128):
        block = jnp.transpose(packed[b * 128 : (b + 1) * 128, :])
        for f in range(FIELDS):
            up_ref[f : f + 1, b * 128 : (b + 1) * 128] = block[4 * f + 1 : 4 * f + 2, :]
            up_ref[8 + f : 9 + f, b * 128 : (b + 1) * 128] = block[4 * f : 4 * f + 1, :]
            down_ref[f : f + 1, b * 128 : (b + 1) * 128] = block[4 * f + 2 : 4 * f + 3, :]
            down_ref[8 + f : 9 + f, b * 128 : (b + 1) * 128] = block[4 * f + 3 : 4 * f + 4, :]
    for row in (7, 15):
        up_ref[row : row + 1, :] = jnp.zeros((1, padded), jnp.float32)
        down_ref[row : row + 1, :] = jnp.zeros((1, padded), jnp.float32)


def march(
    dims, sizes, ext, low_ref, high_ref, snap_ref, mask_ref, ports_ref, amps_ref, *refs
):
    nx, ny, nz = dims
    step = ny + HALO
    lanes = nz // 128
    wide = nz + 128
    parts = sizes[2]
    e_out, h_out = refs[0], refs[1]
    grads = refs[2 : 2 + parts]
    ends, rows_ref, e1, h1, h2, half_ref, sums = refs[2 + parts :]
    gx, gy, gz = lax.axis_index("gx"), lax.axis_index("gy"), lax.axis_index("gz")
    padded = rows_ref.shape[1]

    rows_ref[...] = jnp.zeros(rows_ref.shape, jnp.float32)
    low_ok, high_ok = gz > 0, gz < sizes[2] - 1
    for f in range(FIELDS):
        rows_ref[4 * f : 4 * f + 1, :] = jnp.where(low_ok, low_ref[8 + f : 9 + f, :], 0.0)
        rows_ref[4 * f + 1 : 4 * f + 2, :] = jnp.where(low_ok, low_ref[f : f + 1, :], 0.0)
        rows_ref[4 * f + 2 : 4 * f + 3, :] = jnp.where(high_ok, high_ref[f : f + 1, :], 0.0)
        rows_ref[4 * f + 3 : 4 * f + 4, :] = jnp.where(high_ok, high_ref[8 + f : 9 + f, :], 0.0)
    for b in range(padded // 128):
        block = jnp.transpose(rows_ref[:, b * 128 : (b + 1) * 128])
        for f in range(FIELDS):
            ends[f, b * 128 : (b + 1) * 128, :] = pltpu.roll(block, 128 - (4 * f + 2), 1)

    row = lax.broadcasted_iota(jnp.int32, (step, wide), 0)
    lane = lax.broadcasted_iota(jnp.int32, (step, wide), 1)
    inside = (
        ((row < ny) | ((row < ny + 2) & (gy < sizes[1] - 1)) | ((row >= ny + 4) & (gy > 0)))
        & ((lane < nz) | ((lane < nz + 64) & high_ok) | ((lane >= nz + 64) & low_ok))
    )
    half_ref[...] = jnp.where(inside, magnetic_step, 0.0)

    plane_cells = (ny * sizes[1]) * (nz * sizes[2])
    line_cells = nz * sizes[2]
    spots = []
    for q in range(ports_ref.shape[0]):
        cell = ports_ref[q]
        sx = lax.div(cell, plane_cells) - gx * nx
        sy = lax.rem(lax.div(cell, line_cells), ny * sizes[1]) - gy * ny
        sz = lax.rem(cell, line_cells) - gz * nz
        near = (sy >= -2) & (sy < ny + 2) & (sz >= -2) & (sz < nz + 2)
        own = (sy >= 0) & (sy < ny) & (sz >= 0) & (sz < nz)
        spots.append(
            (sx + 2, jnp.where(sy < 0, sy + step, sy), jnp.where(sz < 0, sz + wide, sz), near, own)
        )

    def load(f, p):
        index = pl.ds(pl.multiple_of(p * step, 8), step)
        return jnp.concatenate(
            [ext[f, z, index, :] for z in range(lanes)] + [ends[f, index, :]], axis=1
        )

    def spot(x, t, z):
        return pl.ds(pl.multiple_of(((x * (ny // 8) + t) * lanes + z) * 8, 8), 8)

    def put(ref, f, x, v):
        for t in range(ny // 8):
            for z in range(lanes):
                ref[f, spot(x, t, z), :] = v[t * 8 : t * 8 + 8, z * 128 : z * 128 + 128]

    def take(ref, f, x):
        return jnp.concatenate(
            [
                jnp.concatenate([ref[f, spot(x, t, z), :] for z in range(lanes)], axis=1)
                for t in range(ny // 8)
            ],
            axis=0,
        )

    def y_up(v):
        return pltpu.roll(v, step - 1, 0)

    def y_down(v):
        return pltpu.roll(v, 1, 0)

    def z_up(v):
        return pltpu.roll(v, wide - 1, 1)

    def z_down(v):
        return pltpu.roll(v, 1, 1)

    def new_h(p, half, ex, ey, ez, ey_x, ez_x, hx, hy, hz):
        cx = (y_up(ez) - ez) - (z_up(ey) - ey)
        cy = (z_up(ex) - ex) - (ez_x - ez)
        cz = (ey_x - ey) - (y_up(ex) - ex)
        return hx - half * cx, hy - half * cy, hz - half * cz

    def new_e(coef, ex, ey, ez, hx, hy, hz, hy_x, hz_x):
        cx = (hz - y_down(hz)) - (hy - z_down(hy))
        cy = (hx - z_down(hx)) - (hz - hz_x)
        cz = (hy - hy_x) - (hx - y_down(hx))
        return ex + coef * cx, ey + coef * cy, ez + coef * cz

    def half_of(p):
        out = ((p < 2) & (gx == 0)) | ((p >= nx + 2) & (gx == sizes[0] - 1))
        return half_ref[...] * jnp.where(out, 0.0, 1.0)

    def first_h(p):
        e = [load(f, p) for f in range(3)]
        h = [load(3 + f, p) for f in range(3)]
        out = new_h(p, half_of(p), *e, load(1, p + 1), load(2, p + 1), *h)
        for f in range(3):
            h1[f, p] = out[f]

    def first_e(p):
        e = [load(f, p) for f in range(3)]
        h = [h1[f, p] for f in range(3)]
        out = new_e(load(6, p), *e, *h, h1[1, p - 1], h1[2, p - 1])
        for f in range(3):
            e1[f, p] = out[f]
        for q, (sx, sy, sz, near, own) in enumerate(spots):

            @pl.when(near & (sx == p))
            def _():
                e1[2, p] = e1[2, p] + jnp.where((row == sy) & (lane == sz), amps_ref[0, q], 0.0)

    def second_h(p):
        e = [e1[f, p] for f in range(3)]
        h = [h1[f, p] for f in range(3)]
        out = new_h(p, half_of(p), *e, e1[1, p + 1], e1[2, p + 1], *h)
        for f in range(3):
            h2[f, p] = out[f]
        return out

    def second_e(p):
        e = [e1[f, p] for f in range(3)]
        h = [h2[f, p] for f in range(3)]
        out = new_e(load(6, p), *e, *h, h2[1, p - 1], h2[2, p - 1])
        index = pl.ds(pl.multiple_of((p - 2) * ny, ny), ny)
        for f in range(3):
            put(e_out, f, p - 2, out[f])
            put(h_out, f, p - 2, h[f])
        for q, (sx, sy, sz, near, own) in enumerate(spots):

            @pl.when(own & (sx == p))
            def _():
                put(
                    e_out,
                    2,
                    p - 2,
                    take(e_out, 2, p - 2)
                    + jnp.where((row[:ny, :nz] == sy) & (lane[:ny, :nz] == sz), amps_ref[1, q], 0.0),
                )

        total = jnp.zeros((ny, nz), jnp.float32)
        for f in range(3):
            s = [snap_ref[t, f, index, :].astype(jnp.float32) for t in range(STEPS + 1)]
            total = total + e[f][:ny, :nz] * (s[0] - s[1])
            total = total + take(e_out, f, p - 2) * (s[1] - s[2])
        folded = total[:, 0:128]
        for at in range(128, nz, 128):
            folded = folded + total[:, at : at + 128]
        sums[index, :] = folded

    first_h(0)
    first_h(1)
    first_e(1)
    first_h(2)
    first_e(2)
    second_h(1)

    def body(p, carry):
        first_h(p)
        first_e(p)
        second_h(p - 1)
        second_e(p - 1)
        return carry

    lax.fori_loop(3, nx + 3, body, 0)

    cells = nx * ny
    nt = (((1,), (1,)), ((), ()))
    nn = (((1,), (0,)), ((), ()))
    lined = lax.dot_general(jnp.ones((8, 128), jnp.float32), sums[...], nt, precision=HIGHEST)
    spread = jnp.where(
        lax.broadcasted_iota(jnp.int32, (nx, cells), 1) // ny
        == lax.broadcasted_iota(jnp.int32, (nx, cells), 0),
        lined[0:1, :],
        0.0,
    )
    pick = (
        lax.rem(lax.broadcasted_iota(jnp.int32, (cells, ny), 0), ny)
        == lax.broadcasted_iota(jnp.int32, (cells, ny), 1)
    ).astype(jnp.float32)
    column = lax.dot_general(spread, pick, nn, precision=HIGHEST) * mask_ref[...].astype(jnp.float32)
    width = ny // parts
    for shift in range(parts):
        owner = lax.rem(gz + shift, parts)
        choose = (
            lax.broadcasted_iota(jnp.int32, (ny, width), 0)
            == owner * width + lax.broadcasted_iota(jnp.int32, (ny, width), 1)
        ).astype(jnp.float32)
        grads[shift][...] = lax.dot_general(column, choose, nn, precision=HIGHEST)


def params(limit=12):
    return pltpu.CompilerParams(vmem_limit_bytes=limit * 1024 * 1024)


def body(sizes, e_adjoint, h_adjoint, snapshots, material, permittivity, design_mask, ports, amplitudes):
    dims = material.shape
    nx, ny, nz = dims
    lanes = nz // 128
    step = ny + HALO
    total = (nx + 4) * step
    padded = -(-total // 128) * 128
    f32 = jnp.float32
    cells = nx * ny
    e = in_vmem(tiled(e_adjoint))
    h = in_vmem(tiled(h_adjoint))
    m = in_vmem(tiled(material))
    s = in_vmem(snapshots.reshape(STEPS + 1, 3, cells, nz))
    xs, ys = swaps(sizes[0]), swaps(sizes[1])

    shapes = [jax.ShapeDtypeStruct((len(slots(0)), ny * lanes, 128), f32) for _ in xs]
    shapes += [jax.ShapeDtypeStruct((len(slots(1)), lanes, nx, 128), f32) for _ in ys]
    shapes += [jax.ShapeDtypeStruct((lanes, 4 * FIELDS, 128), f32) for _ in xs for _ in ys]
    msgs = pl.pallas_call(
        functools.partial(pack_faces, dims, sizes),
        out_shape=shapes,
        in_specs=[VM, VM, VM, SM],
        out_specs=[VM] * len(shapes),
        compiler_params=params(),
        name="pack_faces",
    )(e, h, m, permittivity)

    both = ("gx", "gy")
    tables = [("gx", list(enumerate(swap_table(sizes[0], o)))) for o in xs]
    tables += [("gy", list(enumerate(swap_table(sizes[1], o)))) for o in ys]
    for ox in xs:
        for oy in ys:
            tx, ty = swap_table(sizes[0], ox), swap_table(sizes[1], oy)
            pairs = [
                (x * sizes[1] + y, tx[x] * sizes[1] + ty[y])
                for x in range(sizes[0])
                for y in range(sizes[1])
            ]
            tables.append((both, pairs))
    got = [lax.ppermute(msg, axis, pairs) for msg, (axis, pairs) in zip(msgs, tables)]

    ext, up, down = pl.pallas_call(
        functools.partial(gather_block, dims, sizes),
        out_shape=[
            pltpu.VMEM((FIELDS, lanes, total, 128), f32),
            jax.ShapeDtypeStruct((16, padded), f32),
            jax.ShapeDtypeStruct((16, padded), f32),
        ],
        in_specs=[VM, VM, VM, SM] + [VM] * len(got),
        out_specs=[VM] * 3,
        scratch_shapes=[pltpu.VMEM((padded, 128), f32)],
        compiler_params=params(),
        name="gather_block",
    )(e, h, m, permittivity, *got)

    parts = sizes[2]
    low = lax.ppermute(up, "gz", [(i, (i + 1) % parts) for i in range(parts)])
    high = lax.ppermute(down, "gz", [(i, (i - 1) % parts) for i in range(parts)])

    wide = nz + 128
    out = pl.pallas_call(
        functools.partial(march, dims, sizes),
        out_shape=[
            jax.ShapeDtypeStruct(e.shape, f32),
            jax.ShapeDtypeStruct(h.shape, f32),
        ]
        + [jax.ShapeDtypeStruct((nx, ny // parts), f32)] * parts,
        in_specs=[VM, VM, VM, VM, VM, SM, SM],
        out_specs=[VM] * (2 + parts),
        scratch_shapes=[
            pltpu.VMEM((FIELDS, padded, 128), f32),
            pltpu.VMEM((128, padded), f32),
            pltpu.VMEM((3, nx + 4, step, wide), f32),
            pltpu.VMEM((3, nx + 4, step, wide), f32),
            pltpu.VMEM((3, nx + 4, step, wide), f32),
            pltpu.VMEM((step, wide), f32),
            pltpu.VMEM((cells, 128), f32),
        ],
        compiler_params=params(30),
        name="march",
    )(in_vmem(ext), low, high, s, design_mask, ports, amplitudes)
    gradient = out[2]
    for shift in range(1, parts):
        gradient = gradient + lax.ppermute(
            out[2 + shift], "gz", [(i, (i + shift) % parts) for i in range(parts)]
        )
    return untiled(out[0], dims), untiled(out[1], dims), gradient


def solution(mesh):
    placed = (
        P(None, "gx", "gy", "gz"),
        P(None, "gx", "gy", "gz"),
        P(None, None, "gx", "gy", "gz"),
        P("gx", "gy", "gz"),
        P(),
        P("gx", "gy"),
        P(),
        P(),
    )
    sizes = tuple(mesh.shape[axis] for axis in ("gx", "gy", "gz"))
    return jax.shard_map(
        functools.partial(body, sizes),
        mesh=mesh,
        in_specs=placed,
        out_specs=(P(None, "gx", "gy", "gz"), P(None, "gx", "gy", "gz"), P("gx", ("gy", "gz"))),
        check_vma=False,
    )
```

time: 122 us -> 59.2 us (0.49); the launches traced: 120 us -> 58.9 us
  local copies, waits for them, and re-layouts: 39.9 us -> 10.6 us
  other arithmetic: 28.5 us -> 0.01 us
  Pallas kernels: 0 us -> 22.7 us
  starting transfers between devices: 30.9 us -> 10.3 us
  waiting for transfers between devices: 5.75 us -> 14.5 us
  between operations: 7.94 us -> 0.72 us
  blocking collectives: 7.04 us -> 0 us
    pallas_call x0 -> x3, Pallas kernels: none -> 22.7 us  [the longest x1 16 us: body(): pl.pallas_call(functools.partial(march, dims, sizes), out_shape=[jax.Shap...]
    ppermute x12 -> x10, starting transfers between devices: 30.9 us -> 10.3 us  [the longest x5 6.04 us: body(): lax.ppermute(msg, axis, pairs)]
    slice x21 -> x0, local copies, waits for them, and re-layouts: 15.2 us -> none  [the longest x1 2.6 us: split_step(): magnetic[2] - magnetic_step * (ey_xp - electric[1] - (ex_yp - electric[0]))]
    squeeze x34 -> x0, local copies, waits for them, and re-layouts: 11.1 us -> none  [the longest x3 3 us: split_step(): ey_zp = jnp.concatenate([electric[1, :, :, 1:], from_z[1]], 2)]
    ppermute x12 -> x10, waiting for transfers between devices: 5.75 us -> 14.5 us  [the longest x5 8.21 us: body(): lax.ppermute(msg, axis, pairs)]
    add x3 -> x1, other arithmetic: 7.64 us -> 0.01 us  [body(): gradient + lax.ppermute(out[2 + shift], 'gz', [(i, (i + shift) % parts) f...]
    unnamed x1 -> x0, blocking collectives: 7.04 us -> none
    sub x2 -> x0, other arithmetic: 6.7 us -> none  [the longest x1 3.55 us: split_step(): magnetic[2] - magnetic_step * (ey_xp - electric[1] - (ex_yp - electric[0]))]
  transfers between devices with their start and end apart: 12 -> 10, of which waited for: 2 -> 7; matrix products, arithmetic and copies ran while one was open for 33% -> 0% of each run, Pallas kernels for 0% -> 0%
where the time goes in v1:
time: 59.2 us; the launch traced here: 58.9 us
  Pallas kernels  22.7 us (38%)
  waiting for transfers between devices  14.5 us (24%)
  local copies, waits for them, and re-layouts  10.6 us (18%)
  starting transfers between devices  10.3 us (17%)
  between operations  0.72 us (1%)
    pallas_call x1, Pallas kernels, body(): pl.pallas_call(functools.partial(march, dims, sizes), out_shape=[jax.Shap...  16 us
    unnamed x22, local copies, waits for them, and re-layouts  10.6 us
    ppermute x5, waiting for transfers between devices, body(): lax.ppermute(msg, axis, pairs)  8.21 us
    ppermute x5, starting transfers between devices, body(): lax.ppermute(msg, axis, pairs)  6.04 us
    pallas_call x1, Pallas kernels, body(): pl.pallas_call(functools.partial(gather_block, dims, sizes), out_shape=[p...  5.18 us
    ppermute x1, starting transfers between devices, body(): low = lax.ppermute(up, 'gz', [(i, (i + 1) % parts) for i in range(parts)])  3.26 us
    ppermute x3, waiting for transfers between devices, body(): lax.ppermute(out[2 + shift], 'gz', [(i, (i + shift) % parts) for i in ran...  2.81 us
    ppermute x1, waiting for transfers between devices, body(): lax.ppermute(down, 'gz', [(i, (i - 1) % parts) for i in range(parts)])  2.35 us
  transfers between devices with their start and end apart: 10, of which 7 were waited for; matrix products, arithmetic and copies ran while one was open for 0% of the time, Pallas kernels for 0%

profile of v1, /device:TPU:17, one launch (start us, length us, event | category | flops | bytes accessed | tf_op | source)
XLA Modules:
  0.0 58.9 jit_solution(8905928779176703362)
XLA Ops:
  0.6 0.0 copy-start
  0.6 1.4 %copy-done = f32[3,32,16,256]{3,2,1,0:T(8,128)S(1)} copy-done((f32[3,32,16,256]{3,2,1,0:T(8,128)S(1)}, f32[3,32,16,256]{3,2,1,0:T(8,128)}, u32[]{:S(2)}) %copy-start) | copy-done | bytes 1572888
  2.0 0.0 copy-start.1
  2.0 1.4 %copy-done.1 = f32[3,32,16,256]{3,2,1,0:T(8,128)S(1)} copy-done((f32[3,32,16,256]{3,2,1,0:T(8,128)S(1)}, f32[3,32,16,256]{3,2,1,0:T(8,128)}, u32[]{:S(2)}) %copy-start.1) | copy-done | bytes 1572888
  3.4 0.0 copy-start.5
  3.5 1.0 %copy-done.5 = s32[32,16,256]{2,1,0:T(8,128)S(1)} copy-done((s32[32,16,256]{2,1,0:T(8,128)S(1)}, s32[32,16,256]{2,1,0:T(8,128)}, u32[]{:S(2)}) %copy-start.5) | copy-done | bytes 524312
  4.5 0.0 copy-start.6
  4.5 0.7 %copy-done.6 = f32[8]{0:T(128)S(1)} copy-done((f32[8]{0:T(128)S(1)}, f32[8]{0:T(128)}, u32[]{:S(2)}) %copy-start.6) | copy-done | bytes 56
  5.1 1.4 %pack_faces.1 = (f32[12,32,128]{2,1,0:T(8,128)S(1)}, f32[12,2,32,128]{3,2,1,0:T(8,128)S(1)}, f32[12,2,32,128]{3,2,1,0:T(8,128)S(1)}, f32[2,28,128]{2,1,0:T(8,128)S(1)}, f32[2,28,128]{2,1,0:T(8,128)S(1)}) custom-call(f32[3,1024,128]{2,1,0:T(8,128)S(1)} %bitcast.26, f32[3,1024,128]{2,1,0:T(8,128)S(1)} %bitcast.28, s32[1024,128]{1,0:T(8,128)S(1)} %bitcast.31, ...), custom_call_target="tpu_custom_call" | custom-call | tf_op jit(solution)/shard_map/pack_faces/pallas_call | solution.py:450
  6.6 1.4 %collective-permute-start.1 = (f32[12,2,32,128]{3,2,1,0:T(8,128)S(1)}, f32[12,2,32,128]{3,2,1,0:T(8,128)S(1)}, u32[]{:S(2)}, u32[]{:S(2)}) collective-permute-start(f32[12,2,32,128]{3,2,1,0:T(8,128)S(1)} %get-tuple-element.18), channel_id=1, source_target_pairs={{0,4},{4,0},{8,12},{12,8},{1,5},{5,1},{9,13},{13,9},{2,6},{6,2},{1... | collective-permute-start | bytes 1179656 | tf_op jit(solution)/shard_map/ppermute | solution.py:471
  8.0 1.9 %collective-permute-start.2 = (f32[12,2,32,128]{3,2,1,0:T(8,128)S(1)}, f32[12,2,32,128]{3,2,1,0:T(8,128)S(1)}, u32[]{:S(2)}, u32[]{:S(2)}) collective-permute-start(f32[12,2,32,128]{3,2,1,0:T(8,128)S(1)} %get-tuple-element.19), channel_id=1, source_target_pairs={{0,0},{4,8},{8,4},{12,12},{1,1},{5,9},{9,5},{13,13},{2,2},{6,10},{... | collective-permute-start | bytes 1179656 | tf_op jit(solution)/shard_map/ppermute | solution.py:471
  9.9 1.3 %collective-permute-start = (f32[12,32,128]{2,1,0:T(8,128)S(1)}, f32[12,32,128]{2,1,0:T(8,128)S(1)}, u32[]{:S(2)}, u32[]{:S(2)}) collective-permute-start(f32[12,32,128]{2,1,0:T(8,128)S(1)} %get-tuple-element.17), channel_id=1, source_target_pairs={{0,16},{16,0},{1,17},{17,1},{2,18},{18,2},{3,19},{19,3},{4,20},{20... | collective-permute-start | bytes 589832 | tf_op jit(solution)/shard_map/ppermute | solution.py:471
  11.2 0.0 collective-permute-start.3
  11.2 0.0 copy-start.9
  11.2 0.0 copy-start.4
  11.2 0.0 copy-start.7
  11.2 0.0 copy-start.8
  11.2 1.5 %collective-permute-start.4 = (f32[2,28,128]{2,1,0:T(8,128)S(1)}, f32[2,28,128]{2,1,0:T(8,128)S(1)}, u32[]{:S(2)}, u32[]{:S(2)}) collective-permute-start(f32[2,28,128]{2,1,0:T(8,128)S(1)} %get-tuple-element.21), channel_id=1, source_target_pairs={{0,16},{4,24},{8,20},{12,28},{16,0},{20,8},{24,4},{28,12},{1,17},{... | collective-permute-start | bytes 86024 | tf_op jit(solution)/shard_map/ppermute | solution.py:471
  12.7 5.3 %collective-permute-done.3.refs_3_ = f32[2,28,128]{2,1,0:T(8,128)S(1)} collective-permute-done((f32[2,28,128]{2,1,0:T(8,128)S(1)}, f32[2,28,128]{2,1,0:T(8,128)S(1)}, u32[]{:S(2)}, u32[]{:S(2)}) %collective-permute-start.3) | collective-permute-done | bytes 28704 | tf_op jit(solution)/shard_map/ppermute | solution.py:471
  18.0 2.9 %collective-permute-done.4.refs_4_ = f32[2,28,128]{2,1,0:T(8,128)S(1)} collective-permute-done((f32[2,28,128]{2,1,0:T(8,128)S(1)}, f32[2,28,128]{2,1,0:T(8,128)S(1)}, u32[]{:S(2)}, u32[]{:S(2)}) %collective-permute-start.4) | collective-permute-done | bytes 28704 | tf_op jit(solution)/shard_map/ppermute | solution.py:471
  20.9 0.0 collective-permute-done.refs_0_
  20.9 0.0 collective-permute-done.1.refs_1_
  20.9 0.0 collective-permute-done.2.refs_2_
  20.9 5.2 %gather_block.1 = (f32[7,2,864,128]{3,2,1,0:T(8,128)S(1)}, f32[16,896]{1,0:T(8,128)S(1)}, f32[16,896]{1,0:T(8,128)S(1)}) custom-call(f32[3,1024,128]{2,1,0:T(8,128)S(1)} %bitcast.27, f32[3,1024,128]{2,1,0:T(8,128)S(1)} %bitcast.29, s32[1024,128]{1,0:T(8,128)S(1)} %bitcast.32, f32[8]{0:T(128)S(1)} %copy-done.6, ...), custom_call_target="tpu_custom_call" | custom-call | tf_op jit(solution)/shard_map/gather_block/pallas_call | solution.py:473
  26.1 0.0 copy-start.2
  26.1 2.6 %copy-done.2 = f32[7,2,864,128]{3,2,1,0:T(8,128)} copy-done((f32[7,2,864,128]{3,2,1,0:T(8,128)}, f32[7,2,864,128]{3,2,1,0:T(8,128)S(1)}, u32[]{:S(2)}) %copy-start.2) | copy-done | bytes 6193176
  28.7 3.3 %collective-permute-start.5 = (f32[16,896]{1,0:T(8,128)S(1)}, f32[16,896]{1,0:T(8,128)S(1)}, u32[]{:S(2)}, u32[]{:S(2)}) collective-permute-start(f32[16,896]{1,0:T(8,128)S(1)} %get-tuple-element.23), channel_id=1, source_target_pairs={{0,1},{1,2},{2,3},{3,0},{4,5},{5,6},{6,7},{7,4},{8,9},{9,10},{10,1... | collective-permute-start | bytes 172040 | tf_op jit(solution)/shard_map/ppermute | solution.py:488
  32.0 0.0 collective-permute-start.6
  32.0 0.0 copy-done.9
  32.0 0.1 copy.11.mask_ref
  32.0 1.2 %collective-permute-done.5.low_ref = f32[16,896]{1,0:T(8,128)S(1)} collective-permute-done((f32[16,896]{1,0:T(8,128)S(1)}, f32[16,896]{1,0:T(8,128)S(1)}, u32[]{:S(2)}, u32[]{:S(2)}) %collective-permute-start.5) | collective-permute-done | bytes 57376 | tf_op jit(solution)/shard_map/ppermute | solution.py:488
  33.2 2.3 %collective-permute-done.6.high_ref = f32[16,896]{1,0:T(8,128)S(1)} collective-permute-done((f32[16,896]{1,0:T(8,128)S(1)}, f32[16,896]{1,0:T(8,128)S(1)}, u32[]{:S(2)}, u32[]{:S(2)}) %collective-permute-start.6) | collective-permute-done | bytes 57376 | tf_op jit(solution)/shard_map/ppermute | solution.py:489
  35.6 0.0 copy-done.4
  35.6 0.0 copy-done.7
  35.6 0.0 copy-done.8
  35.6 0.0 copy-start.3
  35.6 2.7 %copy-done.3 = f32[7,2,864,128]{3,2,1,0:T(8,128)S(1)} copy-done((f32[7,2,864,128]{3,2,1,0:T(8,128)S(1)}, f32[7,2,864,128]{3,2,1,0:T(8,128)}, u32[]{:S(2)}) %copy-start.3) | copy-done | bytes 6193176
  38.3 16.0 %march.1 = (f32[3,1024,128]{2,1,0:T(8,128)}, f32[3,1024,128]{2,1,0:T(8,128)}, f32[32,4]{1,0:T(8,128)S(1)}, f32[32,4]{1,0:T(8,128)S(1)}, f32[32,4]{1,0:T(8,128)S(1)}, /*index=5*/f32[32,4]{1,0:T(8,128)S(1)}) custom-call(f32[7,2,864,128]{3,2,1,0:T(8,128)S(1)} %copy-done.3, f32[16,896]{1,0:T(8,128)S(1)} %collective-permute-done.5.low_ref, ...), custom_call_target="tpu_custom_call" | custom-call | tf_op jit(solution)/shard_map/march/pallas_call | solution.py:492
  54.4 0.0 collective-permute-start.7
  54.4 0.3 collective-permute-start.8
  54.6 0.8 %collective-permute-start.9 = (f32[32,4]{1,0:T(8,128)S(1)}, f32[32,4]{1,0:T(8,128)S(1)}, u32[]{:S(2)}, u32[]{:S(2)}) collective-permute-start(f32[32,4]{1,0:T(8,128)S(1)} %get-tuple-element.30), channel_id=1, source_target_pairs={{0,3},{1,0},{2,1},{3,2},{4,7},{5,4},{6,5},{7,6},{8,11},{9,8},{10,9... | collective-permute-start | bytes 1544 | tf_op jit(solution)/shard_map/ppermute | solution.py:515
  55.4 0.1 collective-permute-done.7
  55.6 1.4 %collective-permute-done.8 = f32[32,4]{1,0:T(8,128)S(1)} collective-permute-done((f32[32,4]{1,0:T(8,128)S(1)}, f32[32,4]{1,0:T(8,128)S(1)}, u32[]{:S(2)}, u32[]{:S(2)}) %collective-permute-start.8) | collective-permute-done | bytes 544 | tf_op jit(solution)/shard_map/ppermute | solution.py:515
  57.0 1.3 %collective-permute-done.9 = f32[32,4]{1,0:T(8,128)S(1)} collective-permute-done((f32[32,4]{1,0:T(8,128)S(1)}, f32[32,4]{1,0:T(8,128)S(1)}, u32[]{:S(2)}, u32[]{:S(2)}) %collective-permute-start.9) | collective-permute-done | bytes 544 | tf_op jit(solution)/shard_map/ppermute | solution.py:515
  58.2 0.7 %copy.12 = f32[32,4]{0,1:T(4,128)} copy(f32[32,4]{1,0:T(8,128)S(1)} %add_add_fusion) | data formatting | bytes 1024
  (1 shorter events, 0.0 us)
Async XLA Ops:
  0.6 1.4 %copy-start = (f32[3,32,16,256]{3,2,1,0:T(8,128)S(1)}, f32[3,32,16,256]{3,2,1,0:T(8,128)}, u32[]{:S(2)}) copy-start(f32[3,32,16,256]{3,2,1,0:T(8,128)} %param.8) | copy-start | bytes 4718596
  2.0 1.4 %copy-start.1 = (f32[3,32,16,256]{3,2,1,0:T(8,128)S(1)}, f32[3,32,16,256]{3,2,1,0:T(8,128)}, u32[]{:S(2)}) copy-start(f32[3,32,16,256]{3,2,1,0:T(8,128)} %param.9) | copy-start | bytes 4718596
  3.4 1.0 %copy-start.5 = (s32[32,16,256]{2,1,0:T(8,128)S(1)}, s32[32,16,256]{2,1,0:T(8,128)}, u32[]{:S(2)}) copy-start(s32[32,16,256]{2,1,0:T(8,128)} %param.11) | copy-start | bytes 1572868
  4.5 0.7 %copy-start.6 = (f32[8]{0:T(128)S(1)}, f32[8]{0:T(128)}, u32[]{:S(2)}) copy-start(f32[8]{0:T(128)} %perm_ref.3) | copy-start | bytes 100
  6.6 14.3 %collective-permute-start.1 = (f32[12,2,32,128]{3,2,1,0:T(8,128)S(1)}, f32[12,2,32,128]{3,2,1,0:T(8,128)S(1)}, u32[]{:S(2)}, u32[]{:S(2)}) collective-permute-start(f32[12,2,32,128]{3,2,1,0:T(8,128)S(1)} %get-tuple-element.18), channel_id=1, source_target_pairs={{0,4},{4,0},{8,12},{12,8},{1,5},{5,1},{9,13},{13,9},{2,6},{6,2},{1... | collective-permute-start | bytes 1179656 | tf_op jit(solution)/shard_map/ppermute | solution.py:471
  8.0 12.9 %collective-permute-start.2 = (f32[12,2,32,128]{3,2,1,0:T(8,128)S(1)}, f32[12,2,32,128]{3,2,1,0:T(8,128)S(1)}, u32[]{:S(2)}, u32[]{:S(2)}) collective-permute-start(f32[12,2,32,128]{3,2,1,0:T(8,128)S(1)} %get-tuple-element.19), channel_id=1, source_target_pairs={{0,0},{4,8},{8,4},{12,12},{1,1},{5,9},{9,5},{13,13},{2,2},{6,10},{... | collective-permute-start | bytes 1179656 | tf_op jit(solution)/shard_map/ppermute | solution.py:471
  9.9 11.0 %collective-permute-start = (f32[12,32,128]{2,1,0:T(8,128)S(1)}, f32[12,32,128]{2,1,0:T(8,128)S(1)}, u32[]{:S(2)}, u32[]{:S(2)}) collective-permute-start(f32[12,32,128]{2,1,0:T(8,128)S(1)} %get-tuple-element.17), channel_id=1, source_target_pairs={{0,16},{16,0},{1,17},{17,1},{2,18},{18,2},{3,19},{19,3},{4,20},{20... | collective-permute-start | bytes 589832 | tf_op jit(solution)/shard_map/ppermute | solution.py:471
  11.2 6.8 %collective-permute-start.3 = (f32[2,28,128]{2,1,0:T(8,128)S(1)}, f32[2,28,128]{2,1,0:T(8,128)S(1)}, u32[]{:S(2)}, u32[]{:S(2)}) collective-permute-start(f32[2,28,128]{2,1,0:T(8,128)S(1)} %get-tuple-element.20), channel_id=1, source_target_pairs={{0,20},{4,16},{8,28},{12,24},{16,4},{20,0},{24,12},{28,8},{1,21},{... | collective-permute-start | bytes 86024 | tf_op jit(solution)/shard_map/ppermute | solution.py:471
  11.2 20.8 %copy-start.9 = (s32[32,16]{0,1:T(8,128)S(1)}, s32[32,16]{0,1:T(8,128)}, u32[]{:S(2)}) copy-start(s32[32,16]{0,1:T(8,128)} %param.13) | copy-start | bytes 6148
  11.2 24.4 %copy-start.4 = (bf16[3,3,32,16,256]{4,3,2,1,0:T(8,128)(2,1)S(1)}, bf16[3,3,32,16,256]{4,3,2,1,0:T(8,128)(2,1)}, u32[]{:S(2)}) copy-start(bf16[3,3,32,16,256]{4,3,2,1,0:T(8,128)(2,1)} %param.10) | copy-start | bytes 7077892
  11.2 24.4 %copy-start.7 = (f32[2,3]{1,0:T(2,128)S(1)}, f32[2,3]{1,0:T(2,128)}, u32[]{:S(2)}) copy-start(f32[2,3]{1,0:T(2,128)} %amps_ref.1) | copy-start | bytes 76
  11.2 24.4 %copy-start.8 = (s32[3]{0:T(128)S(1)}, s32[3]{0:T(128)}, u32[]{:S(2)}) copy-start(s32[3]{0:T(128)} %ports_ref.1) | copy-start | bytes 40
  11.2 9.7 %collective-permute-start.4 = (f32[2,28,128]{2,1,0:T(8,128)S(1)}, f32[2,28,128]{2,1,0:T(8,128)S(1)}, u32[]{:S(2)}, u32[]{:S(2)}) collective-permute-start(f32[2,28,128]{2,1,0:T(8,128)S(1)} %get-tuple-element.21), channel_id=1, source_target_pairs={{0,16},{4,24},{8,20},{12,28},{16,0},{20,8},{24,4},{28,12},{1,17},{... | collective-permute-start | bytes 86024 | tf_op jit(solution)/shard_map/ppermute | solution.py:471
  26.1 2.6 %copy-start.2 = (f32[7,2,864,128]{3,2,1,0:T(8,128)}, f32[7,2,864,128]{3,2,1,0:T(8,128)S(1)}, u32[]{:S(2)}) copy-start(f32[7,2,864,128]{3,2,1,0:T(8,128)S(1)} %get-tuple-element.22.ext) | copy-start | bytes 18579460
  28.7 4.5 %collective-permute-start.5 = (f32[16,896]{1,0:T(8,128)S(1)}, f32[16,896]{1,0:T(8,128)S(1)}, u32[]{:S(2)}, u32[]{:S(2)}) collective-permute-start(f32[16,896]{1,0:T(8,128)S(1)} %get-tuple-element.23), channel_id=1, source_target_pairs={{0,1},{1,2},{2,3},{3,0},{4,5},{5,6},{6,7},{7,4},{8,9},{9,10},{10,1... | collective-permute-start | bytes 172040 | tf_op jit(solution)/shard_map/ppermute | solution.py:488
  32.0 3.6 %collective-permute-start.6 = (f32[16,896]{1,0:T(8,128)S(1)}, f32[16,896]{1,0:T(8,128)S(1)}, u32[]{:S(2)}, u32[]{:S(2)}) collective-permute-start(f32[16,896]{1,0:T(8,128)S(1)} %get-tuple-element.24), channel_id=1, source_target_pairs={{0,3},{1,0},{2,1},{3,2},{4,7},{5,4},{6,5},{7,6},{8,11},{9,8},{10,9... | collective-permute-start | bytes 172040 | tf_op jit(solution)/shard_map/ppermute | solution.py:489
  35.6 2.8 %copy-start.3 = (f32[7,2,864,128]{3,2,1,0:T(8,128)S(1)}, f32[7,2,864,128]{3,2,1,0:T(8,128)}, u32[]{:S(2)}) copy-start(f32[7,2,864,128]{3,2,1,0:T(8,128)} %copy-done.2) | copy-start | bytes 18579460
  54.4 1.2 %collective-permute-start.7 = (f32[32,4]{1,0:T(8,128)S(1)}, f32[32,4]{1,0:T(8,128)S(1)}, u32[]{:S(2)}, u32[]{:S(2)}) collective-permute-start(f32[32,4]{1,0:T(8,128)S(1)} %get-tuple-element.28), channel_id=1, source_target_pairs={{0,1},{1,2},{2,3},{3,0},{4,5},{5,6},{6,7},{7,4},{8,9},{9,10},{10,1... | collective-permute-start | bytes 1544 | tf_op jit(solution)/shard_map/ppermute | solution.py:515
  54.4 2.6 %collective-permute-start.8 = (f32[32,4]{1,0:T(8,128)S(1)}, f32[32,4]{1,0:T(8,128)S(1)}, u32[]{:S(2)}, u32[]{:S(2)}) collective-permute-start(f32[32,4]{1,0:T(8,128)S(1)} %get-tuple-element.29), channel_id=1, source_target_pairs={{0,2},{1,3},{2,0},{3,1},{4,6},{5,7},{6,4},{7,5},{8,10},{9,11},{10,... | collective-permute-start | bytes 1544 | tf_op jit(solution)/shard_map/ppermute | solution.py:515
  54.6 3.6 %collective-permute-start.9 = (f32[32,4]{1,0:T(8,128)S(1)}, f32[32,4]{1,0:T(8,128)S(1)}, u32[]{:S(2)}, u32[]{:S(2)}) collective-permute-start(f32[32,4]{1,0:T(8,128)S(1)} %get-tuple-element.30), channel_id=1, source_target_pairs={{0,3},{1,0},{2,1},{3,2},{4,7},{5,4},{6,5},{7,6},{8,11},{9,8},{10,9... | collective-permute-start | bytes 1544 | tf_op jit(solution)/shard_map/ppermute | solution.py:515

commit v2 on v1

v2 whole, which is shorter than its diff:
```python
import functools

import jax
import jax.numpy as jnp
from jax import lax
from jax.experimental import pallas as pl
from jax.experimental.pallas import tpu as pltpu
from jax.sharding import PartitionSpec as P

STEPS = 2
FIELDS = 7
HALO = 8
HIGHEST = lax.Precision.HIGHEST

magnetic_step = 0.5
electric_step = 0.5

VM = pl.BlockSpec(memory_space=pltpu.VMEM)
SM = pl.BlockSpec(memory_space=pltpu.SMEM)
ANY = pl.BlockSpec(memory_space=pl.ANY)


HBM = pl.BlockSpec(memory_space=pltpu.HBM)


def in_hbm(array):
    return pltpu.with_memory_space_constraint(array, pltpu.HBM)


def in_vmem(array):
    return pltpu.with_memory_space_constraint(array, pltpu.VMEM)


def swap_table(size, odd):
    table = list(range(size))
    for i in range(odd, size - 1, 2):
        table[i], table[i + 1] = i + 1, i
    return table


def swaps(size):
    return [odd for odd in (0, 1) if odd + 1 < size]


def sends_up(index, odd):
    return lax.rem(index, 2) == odd


def has_partner(index, size, odd):
    up = sends_up(index, odd)
    return (up & (index + 1 < size)) | (jnp.logical_not(up) & (index >= 1))


def slots(axis):
    near = [(f, 0) for f in range(FIELDS)]
    far = [(f, 1) for f in range(3)] + [(3 + f, 1) for f in range(3) if f != axis]
    return near + far


def coef_table(perm_ref):
    return [
        electric_step / jnp.full((1, 1), perm_ref[i], jnp.float32) for i in range(perm_ref.shape[0])
    ]


def coef_of(material, table):
    out = jnp.zeros(material.shape, jnp.float32)
    for i, value in enumerate(table):
        out = jnp.where(material == i, value, out)
    return out


def tiled(array):
    *lead, nx, ny, nz = array.shape
    n = len(lead)
    split = array.reshape(*lead, nx, ny // 8, 8, nz // 128, 128)
    order = tuple(range(n + 2)) + (n + 3, n + 2, n + 4)
    return split.transpose(order).reshape(*lead, nx * ny * nz // 128, 128)


def untiled(array, dims):
    nx, ny, nz = dims
    lead = array.shape[:-2]
    n = len(lead)
    split = array.reshape(*lead, nx, ny // 8, nz // 128, 8, 128)
    order = tuple(range(n + 2)) + (n + 3, n + 2, n + 4)
    return split.transpose(order).reshape(*lead, nx, ny, nz)


def load_faces(dims, sizes, e_ref, h_ref, m_ref, perm_ref, e_v, h_v, m_v, *refs):
    nx, ny, nz = dims
    lanes = nz // 128
    plane = ny * lanes
    outs, sems = refs[:-1], refs[-1]
    gx, gy = lax.axis_index("gx"), lax.axis_index("gy")
    xs, ys = swaps(sizes[0]), swaps(sizes[1])
    copies = [pltpu.make_async_copy(e_ref.at[f], e_v.at[f], sems.at[f]) for f in range(3)]
    copies += [pltpu.make_async_copy(h_ref.at[f], h_v.at[f], sems.at[3 + f]) for f in range(3)]
    copies += [pltpu.make_async_copy(m_ref, m_v, sems.at[6])]
    for copy in copies:
        copy.start()
    table = coef_table(perm_ref)

    def rows(field, index):
        if field < 3:
            return e_v[field, index, :]
        if field < 6:
            return h_v[field - 3, index, :]
        return coef_of(m_v[index, :], table)

    def y_row(y, z):
        return ((y // 8) * lanes + z) * 8 + y % 8

    def x_ends(odd):
        up = sends_up(gx, odd)
        return jnp.where(up, nx - 1, 0) * plane, jnp.where(up, nx - 2, 1) * plane

    def y_ends(odd, z):
        up = sends_up(gy, odd)
        return (
            jnp.where(up, y_row(ny - 1, z), y_row(0, z)),
            jnp.where(up, y_row(ny - 2, z), y_row(1, z)),
        )

    for field in range(FIELDS):
        copies[field].wait()
        at = 0
        for odd in xs:
            place = x_ends(odd)
            for k, (f, far) in enumerate(slots(0)):
                if f == field:
                    outs[at][k] = rows(f, pl.ds(pl.multiple_of(place[far], 8), plane))
            at += 1
        for odd in ys:
            for z in range(lanes):
                place = y_ends(odd, z)
                for k, (f, far) in enumerate(slots(1)):
                    if f == field:
                        outs[at][k, z] = rows(f, pl.ds(place[far], nx, stride=plane))
            at += 1
        for ox in xs:
            for oy in ys:
                px = x_ends(ox)
                for z in range(lanes):
                    py = y_ends(oy, z)
                    for k in range(4):
                        outs[at][z, pl.ds(4 * field + k, 1), :] = rows(
                            field, pl.ds(px[k // 2] + py[k % 2], 1)
                        )
                at += 1


def turn_ends(parts, lane):
    out = None
    for f in range(FIELDS):
        first, last = parts(f)
        turned = pltpu.roll(jnp.where(lane < 64, first, last), 4 * f + 2, 1)
        out = turned if out is None else jnp.where(lane >= 4 * f, turned, out)
    return out


def own_ends(dims, e_v, h_v, m_v, perm_ref, coef_v, packed):
    nx, ny, nz = dims
    lanes = nz // 128
    step = ny + HALO
    table = coef_table(perm_ref)
    lane = lax.broadcasted_iota(jnp.int32, (8, 128), 1)
    tiles = ny // 8

    def one(x, carry):
        for t in range(tiles):
            index = [
                pl.ds(pl.multiple_of(((x * tiles + t) * lanes + z) * 8, 8), 8) for z in range(lanes)
            ]
            for z in range(lanes):
                coef_v[index[z], :] = coef_of(m_v[index[z], :], table)

            def parts(f):
                if f < 3:
                    return e_v[f, index[0], :], e_v[f, index[-1], :]
                if f < 6:
                    return h_v[f - 3, index[0], :], h_v[f - 3, index[-1], :]
                return coef_v[index[0], :], coef_v[index[-1], :]

            packed[pl.ds(pl.multiple_of((x + 2) * step + t * 8, 8), 8), :] = turn_ends(parts, lane)
        return carry

    lax.fori_loop(0, nx, one, 0)


def unpack_faces(dims, sizes, own_packed, *refs):
    nx, ny, nz = dims
    lanes = nz // 128
    tiles = ny // 8
    step = ny + HALO
    gx, gy = lax.axis_index("gx"), lax.axis_index("gy")
    xs, ys = swaps(sizes[0]), swaps(sizes[1])
    n_msgs = len(xs) + len(ys) + len(xs) * len(ys)
    msgs = refs[:n_msgs]
    xh, yh, up_ref, down_ref, packed = refs[n_msgs:]
    if len(xs) < 2:
        xh[...] = jnp.zeros(xh.shape, jnp.float32)
    for f in range(FIELDS):
        for z in range(lanes):
            if len(ys) < 2:
                yh[f, z] = jnp.zeros(yh.shape[2:], jnp.float32)
            else:
                for p in (0, 1, nx + 2, nx + 3):
                    yh[f, z, pl.ds(p * HALO, HALO), :] = jnp.zeros((HALO, 128), jnp.float32)

    def planes(odd):
        high = sends_up(gx, odd)
        return jnp.where(high, 2, 1), jnp.where(high, 3, 0)

    def lines(odd):
        high = sends_up(gy, odd)
        return jnp.where(high, 0, HALO - 1), jnp.where(high, 1, HALO - 2)

    at = 0
    for odd in xs:
        ok = has_partner(gx, sizes[0], odd)
        place = planes(odd)
        for k, (f, far) in enumerate(slots(0)):
            for z in range(lanes):
                for t in range(tiles):
                    xh[f, z, pl.ds(pl.multiple_of(place[far] * ny + t * 8, 8), 8), :] = jnp.where(
                        ok, msgs[at][k, pl.ds((t * lanes + z) * 8, 8), :], 0.0
                    )
        at += 1
    for odd in ys:
        ok = has_partner(gy, sizes[1], odd)
        place = lines(odd)
        for k, (f, far) in enumerate(slots(1)):
            for z in range(lanes):
                yh[f, z, pl.ds(2 * HALO + place[far], nx, stride=HALO), :] = jnp.where(
                    ok, msgs[at][k, z], 0.0
                )
        at += 1
    for ox in xs:
        for oy in ys:
            ok = has_partner(gx, sizes[0], ox) & has_partner(gy, sizes[1], oy)
            px, py = planes(ox), lines(oy)
            px = [jnp.where(q < 2, q, q + nx) for q in px]
            for z in range(lanes):
                for f in range(FIELDS):
                    for k in range(4):
                        yh[f, z, pl.ds(px[k // 2] * HALO + py[k % 2], 1), :] = jnp.where(
                            ok, msgs[at][z, pl.ds(4 * f + k, 1), :], 0.0
                        )
            at += 1

    lane = lax.broadcasted_iota(jnp.int32, (8, 128), 1)

    def one(p, carry):
        index = pl.ds(pl.multiple_of(p * HALO, 8), HALO)
        packed[pl.ds(pl.multiple_of(p * step + ny, 8), HALO), :] = turn_ends(
            lambda f: (yh[f, 0, index, :], yh[f, lanes - 1, index, :]), lane
        )
        return carry

    lax.fori_loop(0, nx + 4, one, 0, unroll=2)
    for q, p in enumerate((0, 1, nx + 2, nx + 3)):
        for t in range(tiles):
            index = pl.ds(q * ny + t * 8, 8)
            packed[pl.ds(p * step + t * 8, 8), :] = turn_ends(
                lambda f: (xh[f, 0, index, :], xh[f, lanes - 1, index, :]), lane
            )
    for x in range(nx):
        index = pl.ds((x + 2) * step, ny)
        packed[index, :] = own_packed[index, :]
    total = (nx + 4) * step
    padded = packed.shape[0]
    if padded > total:
        packed[total:padded, :] = jnp.zeros((padded - total, 128), jnp.float32)
    for b in range(padded // 128):
        here = pl.ds(b * 128, 128)
        block = jnp.transpose(packed[here, :])
        for f in range(FIELDS):
            up_ref[f : f + 1, here] = block[4 * f + 1 : 4 * f + 2, :]
            up_ref[8 + f : 9 + f, here] = block[4 * f : 4 * f + 1, :]
            down_ref[f : f + 1, here] = block[4 * f + 2 : 4 * f + 3, :]
            down_ref[8 + f : 9 + f, here] = block[4 * f + 3 : 4 * f + 4, :]
    for row in (7, 15):
        up_ref[row : row + 1, :] = jnp.zeros((1, padded), jnp.float32)
        down_ref[row : row + 1, :] = jnp.zeros((1, padded), jnp.float32)


def march(
    dims,
    sizes,
    e_v,
    h_v,
    coef_v,
    xh,
    yh,
    low_ref,
    high_ref,
    snap_ref,
    mask_ref,
    ports_ref,
    amps_ref,
    *refs,
):
    nx, ny, nz = dims
    lanes = nz // 128
    tiles = ny // 8
    plane = ny * lanes
    step = ny + HALO
    wide = nz + 128
    parts = sizes[2]
    e_out, h_out = refs[0], refs[1]
    grads = refs[2 : 2 + parts]
    (ends, rows_ref, e1, h1, h2, half_ref, struck, sums, turned, e_s, h_s, sems) = refs[2 + parts :]
    gx, gy, gz = lax.axis_index("gx"), lax.axis_index("gy"), lax.axis_index("gz")
    padded = rows_ref.shape[1]

    low_ok, high_ok = gz > 0, gz < sizes[2] - 1
    for f in range(FIELDS):
        rows_ref[4 * f : 4 * f + 1, :] = jnp.where(low_ok, low_ref[8 + f : 9 + f, :], 0.0)
        rows_ref[4 * f + 1 : 4 * f + 2, :] = jnp.where(low_ok, low_ref[f : f + 1, :], 0.0)
        rows_ref[4 * f + 2 : 4 * f + 3, :] = jnp.where(high_ok, high_ref[f : f + 1, :], 0.0)
        rows_ref[4 * f + 3 : 4 * f + 4, :] = jnp.where(high_ok, high_ref[8 + f : 9 + f, :], 0.0)
    rows_ref[4 * FIELDS :, :] = jnp.zeros((128 - 4 * FIELDS, padded), jnp.float32)
    for b in range(padded // 128):
        block = jnp.transpose(rows_ref[:, b * 128 : (b + 1) * 128])
        for f in range(FIELDS):
            ends[f, b * 128 : (b + 1) * 128, :] = pltpu.roll(block, 128 - (4 * f + 2), 1)

    row = lax.broadcasted_iota(jnp.int32, (step, wide), 0)
    lane = lax.broadcasted_iota(jnp.int32, (step, wide), 1)
    inside = (
        ((row < ny) | ((row < ny + 2) & (gy < sizes[1] - 1)) | ((row >= ny + 4) & (gy > 0)))
        & ((lane < nz) | ((lane < nz + 64) & high_ok) | ((lane >= nz + 64) & low_ok))
    )
    half_ref[...] = jnp.where(inside, magnetic_step, 0.0)

    plane_cells = (ny * sizes[1]) * (nz * sizes[2])
    line_cells = nz * sizes[2]
    planes_struck = []
    for q in range(ports_ref.shape[0]):
        cell = ports_ref[q]
        sx = lax.div(cell, plane_cells) - gx * nx
        sy = lax.rem(lax.div(cell, line_cells), ny * sizes[1]) - gy * ny
        sz = lax.rem(cell, line_cells) - gz * nz
        near = (sy >= -2) & (sy < ny + 2) & (sz >= -2) & (sz < nz + 2)
        sy = jnp.where(sy < 0, sy + step, sy)
        sz = jnp.where(sz < 0, sz + wide, sz)
        struck[q] = jnp.where((row == sy) & (lane == sz) & near, 1.0, 0.0)
        planes_struck.append(sx + 2)

    def sources(p, s, rows, columns):
        total = None
        for q, at in enumerate(planes_struck):
            one = struck[q, 0:rows, 0:columns] * jnp.where(at == p, amps_ref[s, q], 0.0)
            total = one if total is None else total + one
        return total

    def spot(x, t, z):
        index = ((x * tiles + t) * lanes + z) * 8
        return pl.ds(index if isinstance(index, int) else pl.multiple_of(index, 8), 8)

    def own_tile(f, p, t, z):
        if isinstance(p, int) and not 2 <= p < nx + 2:
            return xh[f, z, pl.ds((p if p < 2 else p - nx) * ny + t * 8, 8), :]
        if f < 3:
            return e_v[f, spot(p - 2, t, z), :]
        if f < 6:
            return h_v[f - 3, spot(p - 2, t, z), :]
        return coef_v[spot(p - 2, t, z), :]

    def aligned(index):
        return index if isinstance(index, int) else pl.multiple_of(index, 8)

    def load(f, p):
        columns = []
        for z in range(lanes):
            column = [own_tile(f, p, t, z) for t in range(tiles)]
            column.append(yh[f, z, pl.ds(aligned(p * HALO), HALO), :])
            columns.append(jnp.concatenate(column, axis=0))
        columns.append(ends[f, pl.ds(aligned(p * step), step), :])
        return jnp.concatenate(columns, axis=1)

    def load_own(f, p):
        return jnp.concatenate(
            [
                jnp.concatenate([own_tile(f, p, t, z) for t in range(tiles)], axis=0)
                for z in range(lanes)
            ],
            axis=1,
        )

    def put(ref, f, x, v):
        for t in range(tiles):
            for z in range(lanes):
                ref[f, spot(x, t, z), :] = v[t * 8 : t * 8 + 8, z * 128 : z * 128 + 128]

    def y_up(v):
        return pltpu.roll(v, step - 1, 0)

    def y_down(v):
        return pltpu.roll(v, 1, 0)

    def z_up(v):
        return pltpu.roll(v, wide - 1, 1)

    def z_down(v):
        return pltpu.roll(v, 1, 1)

    def new_h(half, ex, ey, ez, ey_x, ez_x, hx, hy, hz):
        cx = (y_up(ez) - ez) - (z_up(ey) - ey)
        cy = (z_up(ex) - ex) - (ez_x - ez)
        cz = (ey_x - ey) - (y_up(ex) - ex)
        return hx - half * cx, hy - half * cy, hz - half * cz

    def curl_h(hx, hy, hz, hy_x, hz_x):
        cx = (hz - y_down(hz)) - (hy - z_down(hy))
        cy = (hx - z_down(hx)) - (hz - hz_x)
        cz = (hy - hy_x) - (hx - y_down(hx))
        return cx, cy, cz

    def half_of(p):
        if isinstance(p, int) and p < 2:
            return half_ref[...] * jnp.where(gx == 0, 0.0, 1.0)
        if isinstance(p, int) and p >= nx + 2:
            return half_ref[...] * jnp.where(gx == sizes[0] - 1, 0.0, 1.0)
        return half_ref[...]

    def first_h(p):
        e = [load(f, p) for f in range(3)]
        h = [load(3 + f, p) for f in range(3)]
        out = new_h(half_of(p), *e, load(1, p + 1), load(2, p + 1), *h)
        for f in range(3):
            h1[f, p] = out[f]

    def first_e(p):
        e = [load(f, p) for f in range(3)]
        curl = curl_h(*[h1[f, p] for f in range(3)], h1[1, p - 1], h1[2, p - 1])
        coef = load(6, p)
        out = [e[f] + coef * curl[f] for f in range(3)]
        out[2] = out[2] + sources(p, 0, step, wide)
        for f in range(3):
            e1[f, p] = out[f]

    def second_h(p):
        e = [e1[f, p] for f in range(3)]
        h = [h1[f, p] for f in range(3)]
        out = new_h(half_of(p), *e, e1[1, p + 1], e1[2, p + 1], *h)
        for f in range(3):
            h2[f, p] = out[f]

    def second_e(p):
        h = [h2[f, p] for f in range(3)]
        curl = curl_h(*h, h2[1, p - 1], h2[2, p - 1])
        coef = load_own(6, p)
        old = [e1[f, p, 0:ny, 0:nz] for f in range(3)]
        new = [old[f] + coef * curl[f][:ny, :nz] for f in range(3)]
        new[2] = new[2] + sources(p, 1, ny, nz)
        x = p - 2
        index = pl.ds(aligned(x * ny), ny)
        total = None
        for f in range(3):
            put(e_s, f, x, new[f])
            put(h_s, f, x, h[f][:ny, :nz])
            s = [snap_ref[t, f, index, :].astype(jnp.float32) for t in range(STEPS + 1)]
            one = old[f] * (s[0] - s[1]) + new[f] * (s[1] - s[2])
            total = one if total is None else total + one
        folded = total[:, 0:128]
        for at in range(128, nz, 128):
            folded = folded + total[:, at : at + 128]
        sums[index, :] = folded

    def one(p):
        dynamic = not isinstance(p, int)
        if dynamic or 2 <= p - 4 <= nx + 1:
            second_e(p - 4)
        if dynamic or 1 <= p - 3 <= nx + 1:
            second_h(p - 3)
        if dynamic or 1 <= p - 1 <= nx + 2:
            first_e(p - 1)
        if dynamic or 0 <= p <= nx + 2:
            first_h(p)

    def body(p, carry):
        one(p)
        return carry

    for p in range(6):
        one(p)
    chunk = nx // 4
    copies = []
    for c in range(4):
        lax.fori_loop(6 + c * chunk, min(6 + (c + 1) * chunk, nx + 1), body, 0)
        if c == 3:
            for p in range(nx + 1, nx + 6):
                one(p)
        here = pl.ds(c * chunk * plane, chunk * plane)
        for k, (src, dst) in enumerate(((e_s, e_out), (h_s, h_out))):
            copy = pltpu.make_async_copy(src.at[:, here], dst.at[:, here], sems.at[2 * c + k])
            copy.start()
            copies.append(copy)

    cells = nx * ny
    nt = (((1,), (1,)), ((), ()))
    nn = (((1,), (0,)), ((), ()))
    lined = lax.dot_general(jnp.ones((8, 128), jnp.float32), sums[...], nt, precision=HIGHEST)
    spread = jnp.where(
        lax.rem(lax.broadcasted_iota(jnp.int32, (ny, cells), 1), ny)
        == lax.broadcasted_iota(jnp.int32, (ny, cells), 0),
        lined[0:1, :],
        0.0,
    )
    pick = (
        lax.div(lax.broadcasted_iota(jnp.int32, (cells, nx), 0), ny)
        == lax.broadcasted_iota(jnp.int32, (cells, nx), 1)
    ).astype(jnp.float32)
    turned[...] = lax.dot_general(spread, pick, nn, precision=HIGHEST) * mask_ref[...].astype(
        jnp.float32
    )
    width = ny // parts
    for shift in range(parts):
        owner = lax.rem(gz + shift, parts)
        grads[shift][...] = turned[pl.ds(owner * width, width), :]
    for copy in copies:
        copy.wait()


def params(limit=12):
    return pltpu.CompilerParams(vmem_limit_bytes=limit * 1024 * 1024)


def body(sizes, e_adjoint, h_adjoint, snapshots, material, permittivity, design_mask, ports, amplitudes):
    dims = material.shape
    nx, ny, nz = dims
    lanes = nz // 128
    step = ny + HALO
    total = (nx + 4) * step
    padded = -(-total // 128) * 128
    f32 = jnp.float32
    cells = nx * ny
    e = in_hbm(tiled(e_adjoint))
    h = in_hbm(tiled(h_adjoint))
    m = in_hbm(tiled(material))
    s = in_vmem(snapshots.reshape(STEPS + 1, 3, cells, nz))
    xs, ys = swaps(sizes[0]), swaps(sizes[1])

    block, cube = jax.ShapeDtypeStruct, pltpu.VMEM
    shapes = [block((len(slots(0)), ny * lanes, 128), f32) for _ in xs]
    shapes += [block((len(slots(1)), lanes, nx, 128), f32) for _ in ys]
    shapes += [block((lanes, 4 * FIELDS, 128), f32) for _ in xs for _ in ys]
    e_v, h_v, m_v, *msgs = pl.pallas_call(
        functools.partial(load_faces, dims, sizes),
        out_shape=[cube(e.shape, f32), cube(h.shape, f32), cube(m.shape, jnp.int32)] + shapes,
        in_specs=[HBM, HBM, HBM, SM],
        out_specs=[VM] * (3 + len(shapes)),
        scratch_shapes=[pltpu.SemaphoreType.DMA((FIELDS,))],
        compiler_params=params(),
        name="load_faces",
    )(e, h, m, permittivity)
    coef_v, own_packed = pl.pallas_call(
        functools.partial(own_ends, dims),
        out_shape=[cube(m.shape, f32), cube((padded, 128), f32)],
        in_specs=[VM, VM, VM, SM],
        out_specs=[VM] * 2,
        compiler_params=params(),
        cost_estimate=pl.CostEstimate(flops=10**7, bytes_accessed=4 * 10**6, transcendentals=0),
        name="own_ends",
    )(e_v, h_v, m_v, permittivity)

    both = ("gx", "gy")
    tables = [("gx", list(enumerate(swap_table(sizes[0], o)))) for o in xs]
    tables += [("gy", list(enumerate(swap_table(sizes[1], o)))) for o in ys]
    for ox in xs:
        for oy in ys:
            tx, ty = swap_table(sizes[0], ox), swap_table(sizes[1], oy)
            pairs = [
                (x * sizes[1] + y, tx[x] * sizes[1] + ty[y])
                for x in range(sizes[0])
                for y in range(sizes[1])
            ]
            tables.append((both, pairs))
    got = [lax.ppermute(msg, axis, pairs) for msg, (axis, pairs) in zip(msgs, tables)]

    xh, yh, up, down = pl.pallas_call(
        functools.partial(unpack_faces, dims, sizes),
        out_shape=[
            cube((FIELDS, lanes, 4 * ny, 128), f32),
            cube((FIELDS, lanes, (nx + 4) * HALO, 128), f32),
            block((16, padded), f32),
            block((16, padded), f32),
        ],
        in_specs=[VM] * (1 + len(got)),
        out_specs=[VM] * 4,
        scratch_shapes=[pltpu.VMEM((padded, 128), f32)],
        compiler_params=params(),
        name="unpack_faces",
    )(own_packed, *got)

    parts = sizes[2]
    low = lax.ppermute(up, "gz", [(i, (i + 1) % parts) for i in range(parts)])
    high = lax.ppermute(down, "gz", [(i, (i - 1) % parts) for i in range(parts)])

    wide = nz + 128
    ported = ports.shape[0]
    out = pl.pallas_call(
        functools.partial(march, dims, sizes),
        out_shape=[block(e.shape, f32), block(h.shape, f32)]
        + [block((ny // parts, nx), f32)] * parts,
        in_specs=[VM] * 9 + [SM, SM],
        out_specs=[ANY, ANY] + [VM] * parts,
        scratch_shapes=[
            pltpu.VMEM((FIELDS, padded, 128), f32),
            pltpu.VMEM((128, padded), f32),
            pltpu.VMEM((3, nx + 4, step, wide), f32),
            pltpu.VMEM((3, nx + 4, step, wide), f32),
            pltpu.VMEM((3, nx + 4, step, wide), f32),
            pltpu.VMEM((step, wide), f32),
            pltpu.VMEM((ported, step, wide), f32),
            pltpu.VMEM((cells, 128), f32),
            pltpu.VMEM((ny, nx), f32),
            pltpu.VMEM(e.shape, f32),
            pltpu.VMEM(h.shape, f32),
            pltpu.SemaphoreType.DMA((8,)),
        ],
        compiler_params=params(32),
        name="march",
    )(e_v, h_v, coef_v, xh, yh, low, high, s, design_mask.T, ports, amplitudes)
    gradient = out[2]
    for shift in range(1, parts):
        gradient = gradient + lax.ppermute(
            out[2 + shift], "gz", [(i, (i + shift) % parts) for i in range(parts)]
        )
    return untiled(out[0], dims), untiled(out[1], dims), gradient.T


def solution(mesh):
    placed = (
        P(None, "gx", "gy", "gz"),
        P(None, "gx", "gy", "gz"),
        P(None, None, "gx", "gy", "gz"),
        P("gx", "gy", "gz"),
        P(),
        P("gx", "gy"),
        P(),
        P(),
    )
    sizes = tuple(mesh.shape[axis] for axis in ("gx", "gy", "gz"))
    return jax.shard_map(
        functools.partial(body, sizes),
        mesh=mesh,
        in_specs=placed,
        out_specs=(P(None, "gx", "gy", "gz"), P(None, "gx", "gy", "gz"), P("gx", ("gy", "gz"))),
        check_vma=False,
    )
```

time: 59.2 us -> 40.1 us (0.68)
  local copies, waits for them, and re-layouts: 10.6 us -> 0.66 us
  Pallas kernels: 22.7 us -> 16.4 us
  waiting for transfers between devices: 14.5 us -> 11.3 us
    unnamed x22 -> x10, local copies, waits for them, and re-layouts: 10.6 us -> 0.66 us
    pallas_call x3 -> x4, Pallas kernels: 22.7 us -> 16.4 us  [the longest x1 8.34 us: body(): pl.pallas_call(functools.partial(march, dims, sizes), out_shape=[block(e....]
    ppermute x5, waiting for transfers between devices: 8.21 us -> 5.03 us  [body(): lax.ppermute(msg, axis, pairs)]
  transfers between devices with their start and end apart: 10 -> 10, of which waited for: 7 -> 7; matrix products, arithmetic and copies ran while one was open for 0% -> 0% of each run, Pallas kernels for 0% -> 8%
where the time goes in v2:
time: 40.1 us; the launch traced here: 40 us
  Pallas kernels  16.4 us (41%)
  waiting for transfers between devices  11.3 us (28%)
  starting transfers between devices  10.4 us (26%)
  between operations  0.7 us (2%)
  local copies, waits for them, and re-layouts  0.66 us (2%)
  other arithmetic  0.58 us (1%)
    pallas_call x1, Pallas kernels, body(): pl.pallas_call(functools.partial(march, dims, sizes), out_shape=[block(e....  8.34 us
    ppermute x5, starting transfers between devices, body(): lax.ppermute(msg, axis, pairs)  5.97 us
    ppermute x5, waiting for transfers between devices, body(): lax.ppermute(msg, axis, pairs)  5.03 us
    ppermute x1, starting transfers between devices, body(): low = lax.ppermute(up, 'gz', [(i, (i + 1) % parts) for i in range(parts)])  3.31 us
    pallas_call x1, Pallas kernels, body(): pl.pallas_call(functools.partial(own_ends, dims), out_shape=[cube(m.shape...  3.25 us
    pallas_call x1, Pallas kernels, body(): pl.pallas_call(functools.partial(load_faces, dims, sizes), out_shape=[cub...  2.7 us
    ppermute x3, waiting for transfers between devices, body(): lax.ppermute(out[2 + shift], 'gz', [(i, (i + shift) % parts) for i in ran...  2.65 us
    ppermute x1, waiting for transfers between devices, body(): lax.ppermute(down, 'gz', [(i, (i - 1) % parts) for i in range(parts)])  2.35 us
  transfers between devices with their start and end apart: 10, of which 7 were waited for; matrix products, arithmetic and copies ran while one was open for 0% of the time, Pallas kernels for 8%

profile of v2, /device:TPU:17, one launch (start us, length us, event | category | flops | bytes accessed | tf_op | source)
XLA Modules:
  0.0 40.0 jit_solution(5587079303549395746)
XLA Ops:
  0.6 0.0 copy-start.2
  0.6 0.6 %copy-done.2 = f32[8]{0:T(128)S(1)} copy-done((f32[8]{0:T(128)S(1)}, f32[8]{0:T(128)}, u32[]{:S(2)}) %copy-start.2) | copy-done | bytes 56
  1.3 2.7 %load_faces.1 = (f32[3,1024,128]{2,1,0:T(8,128)S(1)}, f32[3,1024,128]{2,1,0:T(8,128)S(1)}, s32[1024,128]{1,0:T(8,128)S(1)}, f32[12,32,128]{2,1,0:T(8,128)S(1)}, ...) custom-call(f32[3,1024,128]{2,1,0:T(8,128)} %bitcast.31, ...), custom_call_target="tpu_custom_call" | custom-call | tf_op jit(solution)/shard_map/load_faces/pallas_call | solution.py:550
  4.0 1.4 %collective-permute-start.1 = (f32[12,2,32,128]{3,2,1,0:T(8,128)S(1)}, f32[12,2,32,128]{3,2,1,0:T(8,128)S(1)}, u32[]{:S(2)}, u32[]{:S(2)}) collective-permute-start(f32[12,2,32,128]{3,2,1,0:T(8,128)S(1)} %get-tuple-element.29), channel_id=1, source_target_pairs={{0,4},{4,0},{8,12},{12,8},{1,5},{5,1},{9,13},{13,9},{2,6},{6,2},{1... | collective-permute-start | bytes 1179656 | tf_op jit(solution)/shard_map/ppermute | solution.py:581
  5.4 1.9 %collective-permute-start.2 = (f32[12,2,32,128]{3,2,1,0:T(8,128)S(1)}, f32[12,2,32,128]{3,2,1,0:T(8,128)S(1)}, u32[]{:S(2)}, u32[]{:S(2)}) collective-permute-start(f32[12,2,32,128]{3,2,1,0:T(8,128)S(1)} %get-tuple-element.30), channel_id=1, source_target_pairs={{0,0},{4,8},{8,4},{12,12},{1,1},{5,9},{9,5},{13,13},{2,2},{6,10},{... | collective-permute-start | bytes 1179656 | tf_op jit(solution)/shard_map/ppermute | solution.py:581
  7.3 1.3 %collective-permute-start = (f32[12,32,128]{2,1,0:T(8,128)S(1)}, f32[12,32,128]{2,1,0:T(8,128)S(1)}, u32[]{:S(2)}, u32[]{:S(2)}) collective-permute-start(f32[12,32,128]{2,1,0:T(8,128)S(1)} %get-tuple-element.28), channel_id=1, source_target_pairs={{0,16},{16,0},{1,17},{17,1},{2,18},{18,2},{3,19},{19,3},{4,20},{20... | collective-permute-start | bytes 589832 | tf_op jit(solution)/shard_map/ppermute | solution.py:581
  8.6 0.0 collective-permute-start.3
  8.6 1.4 %collective-permute-start.4 = (f32[2,28,128]{2,1,0:T(8,128)S(1)}, f32[2,28,128]{2,1,0:T(8,128)S(1)}, u32[]{:S(2)}, u32[]{:S(2)}) collective-permute-start(f32[2,28,128]{2,1,0:T(8,128)S(1)} %get-tuple-element.32), channel_id=1, source_target_pairs={{0,16},{4,24},{8,20},{12,28},{16,0},{20,8},{24,4},{28,12},{1,17},{... | collective-permute-start | bytes 86024 | tf_op jit(solution)/shard_map/ppermute | solution.py:581
  10.0 0.0 copy-start
  10.0 0.0 copy-start.1
  10.0 0.0 copy-start.3
  10.0 0.0 copy-start.4
  10.0 3.2 %own_ends.1 = (f32[1024,128]{1,0:T(8,128)S(1)}, f32[896,128]{1,0:T(8,128)S(1)}) custom-call(f32[3,1024,128]{2,1,0:T(8,128)S(1)} %get-tuple-element.23.e_v, f32[3,1024,128]{2,1,0:T(8,128)S(1)} %get-tuple-element.24.h_v, s32[1024,128]{1,0:T(8,128)S(1)} %get-tuple-element.25.m_v, f32[8]{0:T(128)S(1)} %copy-done.2), custom_call_target="tpu_custom_call" | custom-call | flops 10000000 | bytes 4000000 | tf_op jit(solution)/shard_map/own_ends/pallas_call | solution.py:559
  13.2 2.2 %collective-permute-done.3.refs_3_ = f32[2,28,128]{2,1,0:T(8,128)S(1)} collective-permute-done((f32[2,28,128]{2,1,0:T(8,128)S(1)}, f32[2,28,128]{2,1,0:T(8,128)S(1)}, u32[]{:S(2)}, u32[]{:S(2)}) %collective-permute-start.3) | collective-permute-done | bytes 28704 | tf_op jit(solution)/shard_map/ppermute | solution.py:581
  15.4 2.9 %collective-permute-done.4.refs_4_ = f32[2,28,128]{2,1,0:T(8,128)S(1)} collective-permute-done((f32[2,28,128]{2,1,0:T(8,128)S(1)}, f32[2,28,128]{2,1,0:T(8,128)S(1)}, u32[]{:S(2)}, u32[]{:S(2)}) %collective-permute-start.4) | collective-permute-done | bytes 28704 | tf_op jit(solution)/shard_map/ppermute | solution.py:581
  18.3 0.0 collective-permute-done.refs_0_
  18.3 0.0 collective-permute-done.1.refs_1_
  18.3 0.0 collective-permute-done.2.refs_2_
  18.3 2.1 %unpack_faces.1 = (f32[7,2,64,128]{3,2,1,0:T(8,128)S(1)}, f32[7,2,288,128]{3,2,1,0:T(8,128)S(1)}, f32[16,896]{1,0:T(8,128)S(1)}, f32[16,896]{1,0:T(8,128)S(1)}) custom-call(f32[896,128]{1,0:T(8,128)S(1)} %get-tuple-element.27.own_packed, f32[12,32,128]{2,1,0:T(8,128)S(1)} %collective-permute-done.refs_0_, ...), custom_call_target="tpu_custom_call" | custom-call | tf_op jit(solution)/shard_map/unpack_faces/pallas_call | solution.py:583
  20.4 3.3 %collective-permute-start.5 = (f32[16,896]{1,0:T(8,128)S(1)}, f32[16,896]{1,0:T(8,128)S(1)}, u32[]{:S(2)}, u32[]{:S(2)}) collective-permute-start(f32[16,896]{1,0:T(8,128)S(1)} %get-tuple-element.35), channel_id=1, source_target_pairs={{0,1},{1,2},{2,3},{3,0},{4,5},{5,6},{6,7},{7,4},{8,9},{9,10},{10,1... | collective-permute-start | bytes 172040 | tf_op jit(solution)/shard_map/ppermute | solution.py:599
  23.7 0.0 collective-permute-start.6
  23.7 1.3 %collective-permute-done.5.low_ref = f32[16,896]{1,0:T(8,128)S(1)} collective-permute-done((f32[16,896]{1,0:T(8,128)S(1)}, f32[16,896]{1,0:T(8,128)S(1)}, u32[]{:S(2)}, u32[]{:S(2)}) %collective-permute-start.5) | collective-permute-done | bytes 57376 | tf_op jit(solution)/shard_map/ppermute | solution.py:599
  24.9 2.3 %collective-permute-done.6.high_ref = f32[16,896]{1,0:T(8,128)S(1)} collective-permute-done((f32[16,896]{1,0:T(8,128)S(1)}, f32[16,896]{1,0:T(8,128)S(1)}, u32[]{:S(2)}, u32[]{:S(2)}) %collective-permute-start.6) | collective-permute-done | bytes 57376 | tf_op jit(solution)/shard_map/ppermute | solution.py:600
  27.3 0.0 copy-done
  27.3 0.0 copy-done.1
  27.3 0.0 copy-done.3
  27.3 0.0 copy-done.4
  27.3 8.3 %march.1 = (f32[3,1024,128]{2,1,0:T(8,128)}, f32[3,1024,128]{2,1,0:T(8,128)}, f32[4,32]{1,0:T(4,128)S(1)}, f32[4,32]{1,0:T(4,128)S(1)}, f32[4,32]{1,0:T(4,128)S(1)}, /*index=5*/f32[4,32]{1,0:T(4,128)S(1)}) custom-call(f32[3,1024,128]{2,1,0:T(8,128)S(1)} %get-tuple-element.23.e_v, f32[3,1024,128]{2,1,0:T(8,128)S(1)} %get-tuple-element.24.h_v, ...), custom_call_target="tpu_custom_call" | custom-call | tf_op jit(solution)/shard_map/march/pallas_call | solution.py:604
  35.6 0.1 collective-permute-start.7
  35.7 0.3 collective-permute-start.8
  36.0 0.7 %collective-permute-start.9 = (f32[4,32]{1,0:T(4,128)S(1)}, f32[4,32]{1,0:T(4,128)S(1)}, u32[]{:S(2)}, u32[]{:S(2)}) collective-permute-start(f32[4,32]{1,0:T(4,128)S(1)} %get-tuple-element.42), channel_id=1, source_target_pairs={{0,3},{1,0},{2,1},{3,2},{4,7},{5,4},{6,5},{7,6},{8,11},{9,8},{10,9... | collective-permute-start | bytes 1544 | tf_op jit(solution)/shard_map/ppermute | solution.py:629
  36.7 0.1 collective-permute-done.7
  36.8 1.4 %collective-permute-done.8 = f32[4,32]{1,0:T(4,128)S(1)} collective-permute-done((f32[4,32]{1,0:T(4,128)S(1)}, f32[4,32]{1,0:T(4,128)S(1)}, u32[]{:S(2)}, u32[]{:S(2)}) %collective-permute-start.8) | collective-permute-done | bytes 544 | tf_op jit(solution)/shard_map/ppermute | solution.py:629
  38.2 1.2 %collective-permute-done.9 = f32[4,32]{1,0:T(4,128)S(1)} collective-permute-done((f32[4,32]{1,0:T(4,128)S(1)}, f32[4,32]{1,0:T(4,128)S(1)}, u32[]{:S(2)}, u32[]{:S(2)}) %collective-permute-start.9) | collective-permute-done | bytes 544 | tf_op jit(solution)/shard_map/ppermute | solution.py:629
  39.4 0.6 %add_bitcast_fusion = f32[32,4]{0,1:T(4,128)} fusion(f32[4,32]{1,0:T(4,128)S(1)} %collective-permute-done.9, f32[4,32]{1,0:T(4,128)S(1)} %collective-permute-done.8, f32[4,32]{1,0:T(4,128)S(1)} %get-tuple-element.39, f32[4,32]{1,0:T(4,128)S(1)} %collective-permute-done.7), kind=kLoop, calls=%fused_computation | loop fusion | flops 384 | bytes 2560 | tf_op jit(solution)/shard_map/transpose | solution.py:632
Async XLA Ops:
  0.6 0.7 %copy-start.2 = (f32[8]{0:T(128)S(1)}, f32[8]{0:T(128)}, u32[]{:S(2)}) copy-start(f32[8]{0:T(128)} %perm_ref.3) | copy-start | bytes 100
  4.0 14.3 %collective-permute-start.1 = (f32[12,2,32,128]{3,2,1,0:T(8,128)S(1)}, f32[12,2,32,128]{3,2,1,0:T(8,128)S(1)}, u32[]{:S(2)}, u32[]{:S(2)}) collective-permute-start(f32[12,2,32,128]{3,2,1,0:T(8,128)S(1)} %get-tuple-element.29), channel_id=1, source_target_pairs={{0,4},{4,0},{8,12},{12,8},{1,5},{5,1},{9,13},{13,9},{2,6},{6,2},{1... | collective-permute-start | bytes 1179656 | tf_op jit(solution)/shard_map/ppermute | solution.py:581
  5.4 12.9 %collective-permute-start.2 = (f32[12,2,32,128]{3,2,1,0:T(8,128)S(1)}, f32[12,2,32,128]{3,2,1,0:T(8,128)S(1)}, u32[]{:S(2)}, u32[]{:S(2)}) collective-permute-start(f32[12,2,32,128]{3,2,1,0:T(8,128)S(1)} %get-tuple-element.30), channel_id=1, source_target_pairs={{0,0},{4,8},{8,4},{12,12},{1,1},{5,9},{9,5},{13,13},{2,2},{6,10},{... | collective-permute-start | bytes 1179656 | tf_op jit(solution)/shard_map/ppermute | solution.py:581
  7.3 11.0 %collective-permute-start = (f32[12,32,128]{2,1,0:T(8,128)S(1)}, f32[12,32,128]{2,1,0:T(8,128)S(1)}, u32[]{:S(2)}, u32[]{:S(2)}) collective-permute-start(f32[12,32,128]{2,1,0:T(8,128)S(1)} %get-tuple-element.28), channel_id=1, source_target_pairs={{0,16},{16,0},{1,17},{17,1},{2,18},{18,2},{3,19},{19,3},{4,20},{20... | collective-permute-start | bytes 589832 | tf_op jit(solution)/shard_map/ppermute | solution.py:581
  8.6 6.8 %collective-permute-start.3 = (f32[2,28,128]{2,1,0:T(8,128)S(1)}, f32[2,28,128]{2,1,0:T(8,128)S(1)}, u32[]{:S(2)}, u32[]{:S(2)}) collective-permute-start(f32[2,28,128]{2,1,0:T(8,128)S(1)} %get-tuple-element.31), channel_id=1, source_target_pairs={{0,20},{4,16},{8,28},{12,24},{16,4},{20,0},{24,12},{28,8},{1,21},{... | collective-permute-start | bytes 86024 | tf_op jit(solution)/shard_map/ppermute | solution.py:581
  8.6 9.7 %collective-permute-start.4 = (f32[2,28,128]{2,1,0:T(8,128)S(1)}, f32[2,28,128]{2,1,0:T(8,128)S(1)}, u32[]{:S(2)}, u32[]{:S(2)}) collective-permute-start(f32[2,28,128]{2,1,0:T(8,128)S(1)} %get-tuple-element.32), channel_id=1, source_target_pairs={{0,16},{4,24},{8,20},{12,28},{16,0},{20,8},{24,4},{28,12},{1,17},{... | collective-permute-start | bytes 86024 | tf_op jit(solution)/shard_map/ppermute | solution.py:581
  10.0 17.3 %copy-start = (bf16[3,3,32,16,256]{4,3,2,1,0:T(8,128)(2,1)S(1)}, bf16[3,3,32,16,256]{4,3,2,1,0:T(8,128)(2,1)}, u32[]{:S(2)}) copy-start(bf16[3,3,32,16,256]{4,3,2,1,0:T(8,128)(2,1)} %param.10) | copy-start | bytes 7077892
  10.0 17.3 %copy-start.1 = (s32[32,16]{0,1:T(8,128)S(1)}, s32[32,16]{0,1:T(8,128)}, u32[]{:S(2)}) copy-start(s32[32,16]{0,1:T(8,128)} %param.13) | copy-start | bytes 6148
  10.0 17.3 %copy-start.3 = (f32[2,3]{1,0:T(2,128)S(1)}, f32[2,3]{1,0:T(2,128)}, u32[]{:S(2)}) copy-start(f32[2,3]{1,0:T(2,128)} %amps_ref.1) | copy-start | bytes 76
  10.0 17.3 %copy-start.4 = (s32[3]{0:T(128)S(1)}, s32[3]{0:T(128)}, u32[]{:S(2)}) copy-start(s32[3]{0:T(128)} %ports_ref.1) | copy-start | bytes 40
  20.4 4.6 %collective-permute-start.5 = (f32[16,896]{1,0:T(8,128)S(1)}, f32[16,896]{1,0:T(8,128)S(1)}, u32[]{:S(2)}, u32[]{:S(2)}) collective-permute-start(f32[16,896]{1,0:T(8,128)S(1)} %get-tuple-element.35), channel_id=1, source_target_pairs={{0,1},{1,2},{2,3},{3,0},{4,5},{5,6},{6,7},{7,4},{8,9},{9,10},{10,1... | collective-permute-start | bytes 172040 | tf_op jit(solution)/shard_map/ppermute | solution.py:599
  23.7 3.6 %collective-permute-start.6 = (f32[16,896]{1,0:T(8,128)S(1)}, f32[16,896]{1,0:T(8,128)S(1)}, u32[]{:S(2)}, u32[]{:S(2)}) collective-permute-start(f32[16,896]{1,0:T(8,128)S(1)} %get-tuple-element.36), channel_id=1, source_target_pairs={{0,3},{1,0},{2,1},{3,2},{4,7},{5,4},{6,5},{7,6},{8,11},{9,8},{10,9... | collective-permute-start | bytes 172040 | tf_op jit(solution)/shard_map/ppermute | solution.py:600
  35.6 1.2 %collective-permute-start.7 = (f32[4,32]{1,0:T(4,128)S(1)}, f32[4,32]{1,0:T(4,128)S(1)}, u32[]{:S(2)}, u32[]{:S(2)}) collective-permute-start(f32[4,32]{1,0:T(4,128)S(1)} %get-tuple-element.40), channel_id=1, source_target_pairs={{0,1},{1,2},{2,3},{3,0},{4,5},{5,6},{6,7},{7,4},{8,9},{9,10},{10,1... | collective-permute-start | bytes 1544 | tf_op jit(solution)/shard_map/ppermute | solution.py:629
  35.7 2.5 %collective-permute-start.8 = (f32[4,32]{1,0:T(4,128)S(1)}, f32[4,32]{1,0:T(4,128)S(1)}, u32[]{:S(2)}, u32[]{:S(2)}) collective-permute-start(f32[4,32]{1,0:T(4,128)S(1)} %get-tuple-element.41), channel_id=1, source_target_pairs={{0,2},{1,3},{2,0},{3,1},{4,6},{5,7},{6,4},{7,5},{8,10},{9,11},{10,... | collective-permute-start | bytes 1544 | tf_op jit(solution)/shard_map/ppermute | solution.py:629
  36.0 3.4 %collective-permute-start.9 = (f32[4,32]{1,0:T(4,128)S(1)}, f32[4,32]{1,0:T(4,128)S(1)}, u32[]{:S(2)}, u32[]{:S(2)}) collective-permute-start(f32[4,32]{1,0:T(4,128)S(1)} %get-tuple-element.42), channel_id=1, source_target_pairs={{0,3},{1,0},{2,1},{3,2},{4,7},{5,4},{6,5},{7,6},{8,11},{9,8},{10,9... | collective-permute-start | bytes 1544 | tf_op jit(solution)/shard_map/ppermute | solution.py:629

commit v3 on v2

--- a/solution.py
+++ b/solution.py
@@ -49,12 +49,6 @@
 def has_partner(index, size, odd):
     up = sends_up(index, odd)
     return (up & (index + 1 < size)) | (jnp.logical_not(up) & (index >= 1))
-
-
-def slots(axis):
-    near = [(f, 0) for f in range(FIELDS)]
-    far = [(f, 1) for f in range(3)] + [(3 + f, 1) for f in range(3) if f != axis]
-    return near + far
 
 
 def coef_table(perm_ref):
@@ -87,67 +81,134 @@
     return split.transpose(order).reshape(*lead, nx, ny, nz)
 
 
-def load_faces(dims, sizes, e_ref, h_ref, m_ref, perm_ref, e_v, h_v, m_v, *refs):
+def tiles_of(array):
+    *lead, nx, ny, nz = array.shape
+    return tiled(array).reshape(*lead, nx, ny // 8, nz // 128, 8, 128)
+
+
+def send_faces(dims, sizes, e_ref, h_ref, m_ref, perm_ref, *refs):
     nx, ny, nz = dims
     lanes = nz // 128
+    tiles = ny // 8
     plane = ny * lanes
-    outs, sems = refs[:-1], refs[-1]
     gx, gy = lax.axis_index("gx"), lax.axis_index("gy")
     xs, ys = swaps(sizes[0]), swaps(sizes[1])
-    copies = [pltpu.make_async_copy(e_ref.at[f], e_v.at[f], sems.at[f]) for f in range(3)]
-    copies += [pltpu.make_async_copy(h_ref.at[f], h_v.at[f], sems.at[3 + f]) for f in range(3)]
-    copies += [pltpu.make_async_copy(m_ref, m_v, sems.at[6])]
-    for copy in copies:
+    n_out = len(xs) + len(ys) + len(xs) * len(ys)
+    outs, refs = refs[:n_out], refs[n_out:]
+    x_bufs, refs = refs[: 2 * len(xs)], refs[2 * len(xs) :]
+    y_bufs, sems = refs[: 2 * len(ys)], refs[2 * len(ys)]
+
+    def source(f):
+        return e_ref.at[f] if f < 3 else h_ref.at[f - 3] if f < 6 else m_ref
+
+    copies = []
+
+    def start(src, dst):
+        copy = pltpu.make_async_copy(src, dst, sems.at[len(copies)])
         copy.start()
+        copies.append(copy)
+
+    for i, odd in enumerate(ys):
+        up = sends_up(gy, odd)
+        t, r = jnp.where(up, tiles - 1, 0), jnp.where(up, 6, 0)
+        for f in range(FIELDS):
+            buf = y_bufs[2 * i].at[f] if f < 6 else y_bufs[2 * i + 1]
+            for z in range(lanes):
+                start(
+                    source(f).at[:, t, z, pl.ds(r, 2), :],
+                    buf.at[z].reshape(nx, 8, 128).at[:, pl.ds(0, 2), :],
+                )
+    for i, odd in enumerate(xs):
+        first = jnp.where(sends_up(gx, odd), nx - 2, 0)
+        for f in range(FIELDS):
+            start(source(f).at[pl.ds(first, 2)], x_bufs[2 * i].at[f] if f < 6 else x_bufs[2 * i + 1])
+
     table = coef_table(perm_ref)
-
-    def rows(field, index):
-        if field < 3:
-            return e_v[field, index, :]
-        if field < 6:
-            return h_v[field - 3, index, :]
-        return coef_of(m_v[index, :], table)
-
-    def y_row(y, z):
-        return ((y // 8) * lanes + z) * 8 + y % 8
-
-    def x_ends(odd):
+    lane = lax.broadcasted_iota(jnp.int32, (8, 128), 1)
+    lane_n = lax.broadcasted_iota(jnp.int32, (nx, 128), 1)
+
+    def z_up(v, lane):
+        out = []
+        for z in range(lanes):
+            after = pltpu.roll(v[z + 1], 127, 1) if z + 1 < lanes else jnp.zeros_like(v[z])
+            out.append(jnp.where(lane < 127, pltpu.roll(v[z], 127, 1), after))
+        return out
+
+    def row_up(v):
+        rows = v.shape[0]
+        row = lax.broadcasted_iota(jnp.int32, v.shape, 0)
+        return jnp.where(row < rows - 1, pltpu.roll(v, rows - 1, 0), 0.0)
+
+    done = 0
+    for i, odd in enumerate(ys):
+        for copy in copies[done : done + FIELDS * lanes]:
+            copy.wait()
+        done += FIELDS * lanes
+        up = sends_up(gy, odd)
+        near, far = jnp.where(up, 1, 0), jnp.where(up, 0, 1)
+        down = jnp.where(up, 0.0, magnetic_step)
+        buf, mat, out = y_bufs[2 * i], y_bufs[2 * i + 1], outs[len(xs) + i]
+
+        def at(f, which):
+            return [buf[f, z, pl.ds(which, nx, stride=8), :] for z in range(lanes)]
+
+        ex_f, ey_f, ez_f = (at(f, far) for f in range(3))
+        hx_f, hz_f = at(3, far), at(5, far)
+        hx_n, hz_n = at(3, near), at(5, near)
+        ey_z = z_up(ey_f, lane_n)
+        for z in range(lanes):
+            for f in range(3):
+                out[f * lanes + z] = buf[f, z, pl.ds(near, nx, stride=8), :]
+            out[3 * lanes + z] = hx_n[z] - down * ez_f[z]
+            out[4 * lanes + z] = buf[4, z, pl.ds(near, nx, stride=8), :]
+            out[5 * lanes + z] = hz_n[z] + down * ex_f[z]
+            out[6 * lanes + z] = coef_of(mat[z, pl.ds(near, nx, stride=8), :], table)
+            out[7 * lanes + z] = hx_f[z] + magnetic_step * (ez_f[z] + (ey_z[z] - ey_f[z]))
+            out[8 * lanes + z] = hz_f[z] - magnetic_step * ((row_up(ey_f[z]) - ey_f[z]) + ex_f[z])
+        out[9 * lanes] = ey_f[0]
+    for i, odd in enumerate(xs):
+        for copy in copies[done : done + FIELDS]:
+            copy.wait()
+        done += FIELDS
         up = sends_up(gx, odd)
-        return jnp.where(up, nx - 1, 0) * plane, jnp.where(up, nx - 2, 1) * plane
-
-    def y_ends(odd, z):
-        up = sends_up(gy, odd)
-        return (
-            jnp.where(up, y_row(ny - 1, z), y_row(0, z)),
-            jnp.where(up, y_row(ny - 2, z), y_row(1, z)),
-        )
-
-    for field in range(FIELDS):
-        copies[field].wait()
-        at = 0
-        for odd in xs:
-            place = x_ends(odd)
-            for k, (f, far) in enumerate(slots(0)):
-                if f == field:
-                    outs[at][k] = rows(f, pl.ds(pl.multiple_of(place[far], 8), plane))
-            at += 1
-        for odd in ys:
+        near, far = jnp.where(up, 1, 0), jnp.where(up, 0, 1)
+        down = jnp.where(up, 0.0, magnetic_step)
+        buf, mat, out = x_bufs[2 * i], x_bufs[2 * i + 1], outs[i]
+
+        def put(k, t, z, v):
+            out[pl.ds(k * plane + (t * lanes + z) * 8, 8), :] = v
+
+        ex_y = [
+            row_up(jnp.concatenate([buf[0, far, t, z] for t in range(tiles)], axis=0))
+            for z in range(lanes)
+        ]
+        for t in range(tiles):
+            ex_z = z_up([buf[0, far, t, z] for z in range(lanes)], lane)
             for z in range(lanes):
-                place = y_ends(odd, z)
-                for k, (f, far) in enumerate(slots(1)):
-                    if f == field:
-                        outs[at][k, z] = rows(f, pl.ds(place[far], nx, stride=plane))
-            at += 1
-        for ox in xs:
-            for oy in ys:
-                px = x_ends(ox)
-                for z in range(lanes):
-                    py = y_ends(oy, z)
+                ex_f, ey_f, ez_f = (buf[f, far, t, z] for f in range(3))
+                for f in range(4):
+                    put(f, t, z, buf[f, near, t, z])
+                put(4, t, z, buf[4, near, t, z] + down * ez_f)
+                put(5, t, z, buf[5, near, t, z] - down * ey_f)
+                put(6, t, z, coef_of(mat[near, t, z], table))
+                put(7, t, z, buf[4, far, t, z] - magnetic_step * ((ex_z[z] - ex_f) + ez_f))
+                ex_up = ex_y[z][t * 8 : t * 8 + 8]
+                put(8, t, z, buf[5, far, t, z] + magnetic_step * (ey_f + (ex_up - ex_f)))
+            out[pl.ds(9 * plane + t * 8, 8), :] = buf[0, far, t, 0]
+        for j, odd_y in enumerate(ys):
+            up_y = sends_up(gy, odd_y)
+            t = jnp.where(up_y, tiles - 1, 0)
+            lines = (jnp.where(up_y, 7, 0), jnp.where(up_y, 6, 1))
+            out = outs[len(xs) + len(ys) + i * len(ys) + j]
+            for z in range(lanes):
+                for f in range(FIELDS):
                     for k in range(4):
-                        outs[at][z, pl.ds(4 * field + k, 1), :] = rows(
-                            field, pl.ds(px[k // 2] + py[k % 2], 1)
-                        )
-                at += 1
+                        where = (near, far)[k // 2], t, z, pl.ds(lines[k % 2], 1)
+                        if f < 6:
+                            line = buf[(f, *where)]
+                        else:
+                            line = coef_of(mat[where], table)
+                        out[z, pl.ds(4 * f + k, 1), :] = line
 
 
 def turn_ends(parts, lane):
@@ -159,10 +220,23 @@
     return out
 
 
-def own_ends(dims, e_v, h_v, m_v, perm_ref, coef_v, packed):
+def turn_rows(packed, blocks, up_ref, down_ref, offset):
+    for b in range(blocks):
+        block = jnp.transpose(packed[b * 128 : (b + 1) * 128, :])
+        here = pl.ds(offset + b * 128, 128)
+        for f in range(FIELDS):
+            up_ref[f : f + 1, here] = block[4 * f + 1 : 4 * f + 2, :]
+            up_ref[8 + f : 9 + f, here] = block[4 * f : 4 * f + 1, :]
+            down_ref[f : f + 1, here] = block[4 * f + 2 : 4 * f + 3, :]
+            down_ref[8 + f : 9 + f, here] = block[4 * f + 3 : 4 * f + 4, :]
+    for row in (7, 15):
+        up_ref[row : row + 1, pl.ds(offset, blocks * 128)] = jnp.zeros((1, blocks * 128), jnp.float32)
+        down_ref[row : row + 1, pl.ds(offset, blocks * 128)] = jnp.zeros((1, blocks * 128), jnp.float32)
+
+
+def own_ends(dims, e_v, h_v, m_v, perm_ref, coef_v, up_ref, down_ref, packed):
     nx, ny, nz = dims
     lanes = nz // 128
-    step = ny + HALO
     table = coef_table(perm_ref)
     lane = lax.broadcasted_iota(jnp.int32, (8, 128), 1)
     tiles = ny // 8
@@ -182,27 +256,30 @@
                     return h_v[f - 3, index[0], :], h_v[f - 3, index[-1], :]
                 return coef_v[index[0], :], coef_v[index[-1], :]
 
-            packed[pl.ds(pl.multiple_of((x + 2) * step + t * 8, 8), 8), :] = turn_ends(parts, lane)
+            packed[pl.ds(pl.multiple_of(x * ny + t * 8, 8), 8), :] = turn_ends(parts, lane)
         return carry
 
     lax.fori_loop(0, nx, one, 0)
-
-
-def unpack_faces(dims, sizes, own_packed, *refs):
+    turn_rows(packed, nx * ny // 128, up_ref, down_ref, 0)
+
+
+def unpack_faces(dims, sizes, own_up, own_down, *refs):
     nx, ny, nz = dims
     lanes = nz // 128
     tiles = ny // 8
-    step = ny + HALO
+    plane = ny * lanes
+    cells = nx * ny
     gx, gy = lax.axis_index("gx"), lax.axis_index("gy")
     xs, ys = swaps(sizes[0]), swaps(sizes[1])
     n_msgs = len(xs) + len(ys) + len(xs) * len(ys)
     msgs = refs[:n_msgs]
-    xh, yh, up_ref, down_ref, packed = refs[n_msgs:]
-    if len(xs) < 2:
-        xh[...] = jnp.zeros(xh.shape, jnp.float32)
+    xh, yh, up_ref, down_ref, packed, x_raw, y_raw = refs[n_msgs:]
+    xh[...] = jnp.zeros(xh.shape, jnp.float32)
+    x_raw[...] = jnp.zeros(x_raw.shape, jnp.float32)
+    y_raw[...] = jnp.zeros(y_raw.shape, jnp.float32)
     for f in range(FIELDS):
         for z in range(lanes):
-            if len(ys) < 2:
+            if len(ys) < 2 or f < 3:
                 yh[f, z] = jnp.zeros(yh.shape[2:], jnp.float32)
             else:
                 for p in (0, 1, nx + 2, nx + 3):
@@ -216,73 +293,74 @@
         high = sends_up(gy, odd)
         return jnp.where(high, 0, HALO - 1), jnp.where(high, 1, HALO - 2)
 
-    at = 0
-    for odd in xs:
+    for i, odd in enumerate(xs):
         ok = has_partner(gx, sizes[0], odd)
-        place = planes(odd)
-        for k, (f, far) in enumerate(slots(0)):
+        near, far = planes(odd)
+        msg = msgs[i]
+        for t in range(tiles):
             for z in range(lanes):
-                for t in range(tiles):
-                    xh[f, z, pl.ds(pl.multiple_of(place[far] * ny + t * 8, 8), 8), :] = jnp.where(
-                        ok, msgs[at][k, pl.ds((t * lanes + z) * 8, 8), :], 0.0
+                for k, f in enumerate((0, 1, 2, 3, 4, 5, 6, 4, 5)):
+                    q = near if k < FIELDS else far
+                    xh[f, z, pl.ds(pl.multiple_of(q * ny + t * 8, 8), 8), :] = jnp.where(
+                        ok, msg[pl.ds(k * plane + (t * lanes + z) * 8, 8), :], 0.0
                     )
-        at += 1
-    for odd in ys:
+            x_raw[pl.ds(pl.multiple_of(far * ny + t * 8, 8), 8), :] = jnp.where(
+                ok & (far == 0), msg[pl.ds(9 * plane + t * 8, 8), :], 0.0
+            )
+    for i, odd in enumerate(ys):
         ok = has_partner(gy, sizes[1], odd)
-        place = lines(odd)
-        for k, (f, far) in enumerate(slots(1)):
-            for z in range(lanes):
-                yh[f, z, pl.ds(2 * HALO + place[far], nx, stride=HALO), :] = jnp.where(
-                    ok, msgs[at][k, z], 0.0
+        near, far = lines(odd)
+        msg = msgs[len(xs) + i]
+        for z in range(lanes):
+            for k, f in enumerate((0, 1, 2, 3, 4, 5, 6, 3, 5)):
+                r = near if k < FIELDS else far
+                yh[f, z, pl.ds(2 * HALO + r, nx, stride=HALO), :] = jnp.where(
+                    ok, msg[k * lanes + z], 0.0
                 )
-        at += 1
-    for ox in xs:
-        for oy in ys:
+        y_raw[pl.ds(2 * HALO + far, nx, stride=HALO), :] = jnp.where(
+            ok & (far == HALO - 2), msg[9 * lanes], 0.0
+        )
+    for i, ox in enumerate(xs):
+        for j, oy in enumerate(ys):
             ok = has_partner(gx, sizes[0], ox) & has_partner(gy, sizes[1], oy)
             px, py = planes(ox), lines(oy)
             px = [jnp.where(q < 2, q, q + nx) for q in px]
+            msg = msgs[len(xs) + len(ys) + i * len(ys) + j]
             for z in range(lanes):
                 for f in range(FIELDS):
                     for k in range(4):
                         yh[f, z, pl.ds(px[k // 2] * HALO + py[k % 2], 1), :] = jnp.where(
-                            ok, msgs[at][z, pl.ds(4 * f + k, 1), :], 0.0
+                            ok, msg[z, pl.ds(4 * f + k, 1), :], 0.0
                         )
-            at += 1
 
     lane = lax.broadcasted_iota(jnp.int32, (8, 128), 1)
 
     def one(p, carry):
         index = pl.ds(pl.multiple_of(p * HALO, 8), HALO)
-        packed[pl.ds(pl.multiple_of(p * step + ny, 8), HALO), :] = turn_ends(
-            lambda f: (yh[f, 0, index, :], yh[f, lanes - 1, index, :]), lane
-        )
+
+        def parts(f):
+            first = yh[f, 0, index, :]
+            return first + y_raw[index, :] if f == 1 else first, yh[f, lanes - 1, index, :]
+
+        packed[index, :] = turn_ends(parts, lane)
         return carry
 
-    lax.fori_loop(0, nx + 4, one, 0, unroll=2)
-    for q, p in enumerate((0, 1, nx + 2, nx + 3)):
-        for t in range(tiles):
-            index = pl.ds(q * ny + t * 8, 8)
-            packed[pl.ds(p * step + t * 8, 8), :] = turn_ends(
-                lambda f: (xh[f, 0, index, :], xh[f, lanes - 1, index, :]), lane
-            )
-    for x in range(nx):
-        index = pl.ds((x + 2) * step, ny)
-        packed[index, :] = own_packed[index, :]
-    total = (nx + 4) * step
-    padded = packed.shape[0]
-    if padded > total:
-        packed[total:padded, :] = jnp.zeros((padded - total, 128), jnp.float32)
-    for b in range(padded // 128):
-        here = pl.ds(b * 128, 128)
-        block = jnp.transpose(packed[here, :])
-        for f in range(FIELDS):
-            up_ref[f : f + 1, here] = block[4 * f + 1 : 4 * f + 2, :]
-            up_ref[8 + f : 9 + f, here] = block[4 * f : 4 * f + 1, :]
-            down_ref[f : f + 1, here] = block[4 * f + 2 : 4 * f + 3, :]
-            down_ref[8 + f : 9 + f, here] = block[4 * f + 3 : 4 * f + 4, :]
-    for row in (7, 15):
-        up_ref[row : row + 1, :] = jnp.zeros((1, padded), jnp.float32)
-        down_ref[row : row + 1, :] = jnp.zeros((1, padded), jnp.float32)
+    lax.fori_loop(0, nx + 4, one, 0, unroll=4)
+    after = (nx + 4) * HALO
+    for r in range(0, 4 * ny, 8):
+        index = pl.ds(r, 8)
+
+        def parts(f):
+            first = xh[f, 0, index, :]
+            return first + x_raw[index, :] if f == 0 else first, xh[f, lanes - 1, index, :]
+
+        packed[pl.ds(after + r, 8), :] = turn_ends(parts, lane)
+    after += 4 * ny
+    if packed.shape[0] > after:
+        packed[after:, :] = jnp.zeros((packed.shape[0] - after, 128), jnp.float32)
+    up_ref[:, 0:cells] = own_up[...]
+    down_ref[:, 0:cells] = own_down[...]
+    turn_rows(packed, packed.shape[0] // 128, up_ref, down_ref, cells)
 
 
 def march(
@@ -305,12 +383,15 @@
     lanes = nz // 128
     tiles = ny // 8
     plane = ny * lanes
+    cells = nx * ny
     step = ny + HALO
     wide = nz + 128
     parts = sizes[2]
     e_out, h_out = refs[0], refs[1]
     grads = refs[2 : 2 + parts]
-    (ends, rows_ref, e1, h1, h2, half_ref, struck, sums, turned, e_s, h_s, sems) = refs[2 + parts :]
+    (ends, rows_ref, ends_t, e1, h1, h2, half_ref, struck, sums, turned, e_s, h_s, sems) = refs[
+        2 + parts :
+    ]
     gx, gy, gz = lax.axis_index("gx"), lax.axis_index("gy"), lax.axis_index("gz")
     padded = rows_ref.shape[1]
 
@@ -322,9 +403,7 @@
         rows_ref[4 * f + 3 : 4 * f + 4, :] = jnp.where(high_ok, high_ref[8 + f : 9 + f, :], 0.0)
     rows_ref[4 * FIELDS :, :] = jnp.zeros((128 - 4 * FIELDS, padded), jnp.float32)
     for b in range(padded // 128):
-        block = jnp.transpose(rows_ref[:, b * 128 : (b + 1) * 128])
-        for f in range(FIELDS):
-            ends[f, b * 128 : (b + 1) * 128, :] = pltpu.roll(block, 128 - (4 * f + 2), 1)
+        ends_t[b * 128 : (b + 1) * 128, :] = jnp.transpose(rows_ref[:, b * 128 : (b + 1) * 128])
 
     row = lax.broadcasted_iota(jnp.int32, (step, wide), 0)
     lane = lax.broadcasted_iota(jnp.int32, (step, wide), 1)
@@ -348,13 +427,6 @@
         struck[q] = jnp.where((row == sy) & (lane == sz) & near, 1.0, 0.0)
         planes_struck.append(sx + 2)
 
-    def sources(p, s, rows, columns):
-        total = None
-        for q, at in enumerate(planes_struck):
-            one = struck[q, 0:rows, 0:columns] * jnp.where(at == p, amps_ref[s, q], 0.0)
-            total = one if total is None else total + one
-        return total
-
     def spot(x, t, z):
         index = ((x * tiles + t) * lanes + z) * 8
         return pl.ds(index if isinstance(index, int) else pl.multiple_of(index, 8), 8)
@@ -377,8 +449,19 @@
             column = [own_tile(f, p, t, z) for t in range(tiles)]
             column.append(yh[f, z, pl.ds(aligned(p * HALO), HALO), :])
             columns.append(jnp.concatenate(column, axis=0))
-        columns.append(ends[f, pl.ds(aligned(p * step), step), :])
+        columns.append(ends[f, p])
         return jnp.concatenate(columns, axis=1)
+
+    def spread(p):
+        if isinstance(p, int) and not 2 <= p < nx + 2:
+            own = cells + (nx + 4) * HALO + (p if p < 2 else p - nx) * ny
+        else:
+            own = (p - 2) * ny
+        rows = [own + t * 8 for t in range(tiles)] + [cells + p * HALO]
+        for k, r in enumerate(rows):
+            v = ends_t[pl.ds(aligned(r), 8), :]
+            for f in range(FIELDS):
+                ends[f, p, k * 8 : k * 8 + 8, :] = pltpu.roll(v, 128 - (4 * f + 2), 1)
 
     def load_own(f, p):
         return jnp.concatenate(
@@ -437,7 +520,6 @@
         curl = curl_h(*[h1[f, p] for f in range(3)], h1[1, p - 1], h1[2, p - 1])
         coef = load(6, p)
         out = [e[f] + coef * curl[f] for f in range(3)]
-        out[2] = out[2] + sources(p, 0, step, wide)
         for f in range(3):
             e1[f, p] = out[f]
 
@@ -454,7 +536,6 @@
         coef = load_own(6, p)
         old = [e1[f, p, 0:ny, 0:nz] for f in range(3)]
         new = [old[f] + coef * curl[f][:ny, :nz] for f in range(3)]
-        new[2] = new[2] + sources(p, 1, ny, nz)
         x = p - 2
         index = pl.ds(aligned(x * ny), ny)
         total = None
@@ -469,6 +550,34 @@
             folded = folded + total[:, at : at + 128]
         sums[index, :] = folded
 
+    def strike(p):
+        dynamic = not isinstance(p, int)
+        first, second = p - 1, p - 4
+        hit = None
+        for at in planes_struck:
+            here = (at == first) | (at == second)
+            hit = here if hit is None else hit | here
+
+        @pl.when(hit)
+        def _():
+            for q, at in enumerate(planes_struck):
+                if dynamic or 1 <= first <= nx + 2:
+                    amp = jnp.where(at == first, amps_ref[0, q], 0.0)
+                    e1[2, first] = e1[2, first] + struck[q] * amp
+                if dynamic or 2 <= second <= nx + 1:
+                    x = second - 2
+                    amp = jnp.where(at == second, amps_ref[1, q], 0.0)
+                    index = pl.ds(aligned(x * ny), ny)
+                    s = [snap_ref[t, 2, index, :].astype(jnp.float32) for t in (1, 2)]
+                    folded = jnp.zeros((ny, 128), jnp.float32)
+                    for z in range(lanes):
+                        gain = struck[q, 0:ny, z * 128 : z * 128 + 128] * amp
+                        folded = folded + gain * (s[0] - s[1])[:, z * 128 : z * 128 + 128]
+                        for t in range(tiles):
+                            here = spot(x, t, z)
+                            e_s[2, here, :] = e_s[2, here, :] + gain[t * 8 : t * 8 + 8]
+                    sums[index, :] = sums[index, :] + folded
+
     def one(p):
         dynamic = not isinstance(p, int)
         if dynamic or 2 <= p - 4 <= nx + 1:
@@ -479,19 +588,24 @@
             first_e(p - 1)
         if dynamic or 0 <= p <= nx + 2:
             first_h(p)
+        if dynamic or p + 2 <= nx + 3:
+            spread(p + 2)
+        strike(p)
 
     def body(p, carry):
         one(p)
         return carry
 
+    spread(0)
+    spread(1)
     for p in range(6):
         one(p)
     chunk = nx // 4
     copies = []
     for c in range(4):
-        lax.fori_loop(6 + c * chunk, min(6 + (c + 1) * chunk, nx + 1), body, 0)
+        lax.fori_loop(6 + c * chunk, min(6 + (c + 1) * chunk, nx), body, 0)
         if c == 3:
-            for p in range(nx + 1, nx + 6):
+            for p in range(nx, nx + 6):
                 one(p)
         here = pl.ds(c * chunk * plane, chunk * plane)
         for k, (src, dst) in enumerate(((e_s, e_out), (h_s, h_out))):
@@ -499,7 +613,6 @@
             copy.start()
             copies.append(copy)
 
-    cells = nx * ny
     nt = (((1,), (1,)), ((), ()))
     nn = (((1,), (0,)), ((), ()))
     lined = lax.dot_general(jnp.ones((8, 128), jnp.float32), sums[...], nt, precision=HIGHEST)
@@ -529,38 +642,52 @@
 
 
 def body(sizes, e_adjoint, h_adjoint, snapshots, material, permittivity, design_mask, ports, amplitudes):
+    permittivity = in_hbm(permittivity)
+    permittivity = in_hbm(permittivity)
     dims = material.shape
     nx, ny, nz = dims
     lanes = nz // 128
+    tiles = ny // 8
+    plane = ny * lanes
+    cells = nx * ny
     step = ny + HALO
-    total = (nx + 4) * step
-    padded = -(-total // 128) * 128
-    f32 = jnp.float32
-    cells = nx * ny
-    e = in_hbm(tiled(e_adjoint))
-    h = in_hbm(tiled(h_adjoint))
-    m = in_hbm(tiled(material))
+    edge = -(-((nx + 4) * HALO + 4 * ny) // 128) * 128
+    padded = cells + edge
+    f32, i32 = jnp.float32, jnp.int32
+    xs, ys = swaps(sizes[0]), swaps(sizes[1])
+    block, cube = jax.ShapeDtypeStruct, pltpu.VMEM
+
+    shapes = [block((9 * plane + ny, 128), f32) for _ in xs]
+    shapes += [block((9 * lanes + 1, nx, 128), f32) for _ in ys]
+    shapes += [block((lanes, 4 * FIELDS, 128), f32) for _ in xs for _ in ys]
+    buffers = []
+    for _ in xs:
+        buffers += [cube((6, 2, tiles, lanes, 8, 128), f32), cube((2, tiles, lanes, 8, 128), i32)]
+    for _ in ys:
+        buffers += [cube((6, lanes, nx * 8, 128), f32), cube((lanes, nx * 8, 128), i32)]
+    n_copies = FIELDS * (len(xs) + lanes * len(ys))
+    msgs = pl.pallas_call(
+        functools.partial(send_faces, dims, sizes),
+        out_shape=shapes,
+        in_specs=[HBM, HBM, HBM, SM],
+        out_specs=[VM] * len(shapes),
+        scratch_shapes=buffers + [pltpu.SemaphoreType.DMA((n_copies,))],
+        compiler_params=params(),
+        name="send_faces",
+    )(
+        in_hbm(tiles_of(e_adjoint)),
+        in_hbm(tiles_of(h_adjoint)),
+        in_hbm(tiles_of(material)),
+        permittivity,
+    )
+    e_v, h_v, m_v = in_vmem(tiled(e_adjoint)), in_vmem(tiled(h_adjoint)), in_vmem(tiled(material))
     s = in_vmem(snapshots.reshape(STEPS + 1, 3, cells, nz))
-    xs, ys = swaps(sizes[0]), swaps(sizes[1])
-
-    block, cube = jax.ShapeDtypeStruct, pltpu.VMEM
-    shapes = [block((len(slots(0)), ny * lanes, 128), f32) for _ in xs]
-    shapes += [block((len(slots(1)), lanes, nx, 128), f32) for _ in ys]
-    shapes += [block((lanes, 4 * FIELDS, 128), f32) for _ in xs for _ in ys]
-    e_v, h_v, m_v, *msgs = pl.pallas_call(
-        functools.partial(load_faces, dims, sizes),
-        out_shape=[cube(e.shape, f32), cube(h.shape, f32), cube(m.shape, jnp.int32)] + shapes,
-        in_specs=[HBM, HBM, HBM, SM],
-        out_specs=[VM] * (3 + len(shapes)),
-        scratch_shapes=[pltpu.SemaphoreType.DMA((FIELDS,))],
-        compiler_params=params(),
-        name="load_faces",
-    )(e, h, m, permittivity)
-    coef_v, own_packed = pl.pallas_call(
+    coef_v, own_up, own_down = pl.pallas_call(
         functools.partial(own_ends, dims),
-        out_shape=[cube(m.shape, f32), cube((padded, 128), f32)],
+        out_shape=[cube(m_v.shape, f32), cube((16, cells), f32), cube((16, cells), f32)],
         in_specs=[VM, VM, VM, SM],
-        out_specs=[VM] * 2,
+        out_specs=[VM] * 3,
+        scratch_shapes=[pltpu.VMEM((cells, 128), f32)],
         compiler_params=params(),
         cost_estimate=pl.CostEstimate(flops=10**7, bytes_accessed=4 * 10**6, transcendentals=0),
         name="own_ends",
@@ -588,12 +715,16 @@
             block((16, padded), f32),
             block((16, padded), f32),
         ],
-        in_specs=[VM] * (1 + len(got)),
+        in_specs=[VM] * (2 + len(got)),
         out_specs=[VM] * 4,
-        scratch_shapes=[pltpu.VMEM((padded, 128), f32)],
+        scratch_shapes=[
+            pltpu.VMEM((edge, 128), f32),
+            pltpu.VMEM((4 * ny, 128), f32),
+            pltpu.VMEM(((nx + 4) * HALO, 128), f32),
+        ],
         compiler_params=params(),
         name="unpack_faces",
-    )(own_packed, *got)
+    )(own_up, own_down, *got)
 
     parts = sizes[2]
     low = lax.ppermute(up, "gz", [(i, (i + 1) % parts) for i in range(parts)])
@@ -603,13 +734,14 @@
     ported = ports.shape[0]
     out = pl.pallas_call(
         functools.partial(march, dims, sizes),
-        out_shape=[block(e.shape, f32), block(h.shape, f32)]
+        out_shape=[block(e_v.shape, f32), block(h_v.shape, f32)]
         + [block((ny // parts, nx), f32)] * parts,
         in_specs=[VM] * 9 + [SM, SM],
         out_specs=[ANY, ANY] + [VM] * parts,
         scratch_shapes=[
-            pltpu.VMEM((FIELDS, padded, 128), f32),
+            pltpu.VMEM((FIELDS, nx + 4, step, 128), f32),
             pltpu.VMEM((128, padded), f32),
+            pltpu.VMEM((padded, 128), f32),
             pltpu.VMEM((3, nx + 4, step, wide), f32),
             pltpu.VMEM((3, nx + 4, step, wide), f32),
             pltpu.VMEM((3, nx + 4, step, wide), f32),
@@ -617,8 +749,8 @@
             pltpu.VMEM((ported, step, wide), f32),
             pltpu.VMEM((cells, 128), f32),
             pltpu.VMEM((ny, nx), f32),
-            pltpu.VMEM(e.shape, f32),
-            pltpu.VMEM(h.shape, f32),
+            pltpu.VMEM(e_v.shape, f32),
+            pltpu.VMEM(h_v.shape, f32),
             pltpu.SemaphoreType.DMA((8,)),
         ],
         compiler_params=params(32),

time: 40.1 us -> 37.7 us (0.940)
  the two profiles are of different devices: /device:TPU:17 before, /device:TPU:0 now
where the time goes in v3:
time: 37.7 us; the launch traced here: 37.5 us
  starting transfers between devices  16.1 us (43%)
  Pallas kernels  16 us (42%)
  waiting for transfers between devices  4.03 us (11%)
  between operations  0.79 us (2%)
  other arithmetic  0.58 us (2%)
    ppermute x5, starting transfers between devices, body(): lax.ppermute(msg, axis, pairs)  11.2 us
    pallas_call x1, Pallas kernels, body(): pl.pallas_call(functools.partial(march, dims, sizes), out_shape=[block(e_...  8.21 us
    pallas_call x1, Pallas kernels, body(): pl.pallas_call(functools.partial(own_ends, dims), out_shape=[cube(m_v.sha...  3.65 us
    ppermute x3, starting transfers between devices, body(): lax.ppermute(out[2 + shift], 'gz', [(i, (i + shift) % parts) for i in ran...  3.08 us
    pallas_call x1, Pallas kernels, body(): pl.pallas_call(functools.partial(send_faces, dims, sizes), out_shape=shap...  2.78 us
    ppermute x3, waiting for transfers between devices, body(): lax.ppermute(out[2 + shift], 'gz', [(i, (i + shift) % parts) for i in ran...  2.16 us
    ppermute x1, waiting for transfers between devices, body(): low = lax.ppermute(up, 'gz', [(i, (i + 1) % parts) for i in range(parts)])  1.86 us
    ppermute x1, starting transfers between devices, body(): lax.ppermute(down, 'gz', [(i, (i - 1) % parts) for i in range(parts)])  1.73 us
  transfers between devices with their start and end apart: 10, of which 2 were waited for; matrix products, arithmetic and copies ran while one was open for 0% of the time, Pallas kernels for 10%

profile of v3, /device:TPU:0, one launch (start us, length us, event | category | flops | bytes accessed | tf_op | source)
XLA Modules:
  0.0 37.5 jit_solution(17837419898611961049)
XLA Ops:
  0.6 0.0 copy-start
  0.6 0.0 copy-start.1
  0.7 0.0 copy-start.3
  0.7 2.8 %send_faces.1 = (f32[304,128]{1,0:T(8,128)S(1)}, f32[19,32,128]{2,1,0:T(8,128)S(1)}, f32[19,32,128]{2,1,0:T(8,128)S(1)}, f32[2,28,128]{2,1,0:T(8,128)S(1)}, f32[2,28,128]{2,1,0:T(8,128)S(1)}) custom-call(f32[3,32,2,2,8,128]{5,4,3,2,1,0:T(8,128)} %bitcast.29, f32[3,32,2,2,8,128]{5,4,3,2,1,0:T(8,128)} %bitcast.32, s32[32,2,2,8,128]{4,3,2,1,0:T(8,128)} %bitcast.36, ...), custom_call_target="tpu_custom_call" | custom-call | tf_op jit(solution)/shard_map/send_faces/pallas_call | solution.py:669
  3.5 3.1 %collective-permute-start.1 = (f32[19,32,128]{2,1,0:T(8,128)S(1)}, f32[19,32,128]{2,1,0:T(8,128)S(1)}, u32[]{:S(2)}, u32[]{:S(2)}) collective-permute-start(f32[19,32,128]{2,1,0:T(8,128)S(1)} %get-tuple-element.25), channel_id=1, source_target_pairs={{0,4},{4,0},{8,12},{12,8},{1,5},{5,1},{9,13},{13,9},{2,6},{6,2},{1... | collective-permute-start | bytes 933896 | tf_op jit(solution)/shard_map/ppermute | solution.py:708
  6.5 0.7 %collective-permute-start.2 = (f32[19,32,128]{2,1,0:T(8,128)S(1)}, f32[19,32,128]{2,1,0:T(8,128)S(1)}, u32[]{:S(2)}, u32[]{:S(2)}) collective-permute-start(f32[19,32,128]{2,1,0:T(8,128)S(1)} %get-tuple-element.26), channel_id=1, source_target_pairs={{0,0},{4,8},{8,4},{12,12},{1,1},{5,9},{9,5},{13,13},{2,2},{6,10},{... | collective-permute-start | bytes 933896 | tf_op jit(solution)/shard_map/ppermute | solution.py:708
  7.2 1.6 %collective-permute-start = (f32[304,128]{1,0:T(8,128)S(1)}, f32[304,128]{1,0:T(8,128)S(1)}, u32[]{:S(2)}, u32[]{:S(2)}) collective-permute-start(f32[304,128]{1,0:T(8,128)S(1)} %get-tuple-element.24), channel_id=1, source_target_pairs={{0,16},{16,0},{1,17},{17,1},{2,18},{18,2},{3,19},{19,3},{4,20},{20... | collective-permute-start | bytes 466952 | tf_op jit(solution)/shard_map/ppermute | solution.py:708
  8.8 4.3 %collective-permute-start.3 = (f32[2,28,128]{2,1,0:T(8,128)S(1)}, f32[2,28,128]{2,1,0:T(8,128)S(1)}, u32[]{:S(2)}, u32[]{:S(2)}) collective-permute-start(f32[2,28,128]{2,1,0:T(8,128)S(1)} %get-tuple-element.27), channel_id=1, source_target_pairs={{0,20},{4,16},{8,28},{12,24},{16,4},{20,0},{24,12},{28,8},{1,21},{... | collective-permute-start | bytes 86024 | tf_op jit(solution)/shard_map/ppermute | solution.py:708
  13.1 1.5 %collective-permute-start.4 = (f32[2,28,128]{2,1,0:T(8,128)S(1)}, f32[2,28,128]{2,1,0:T(8,128)S(1)}, u32[]{:S(2)}, u32[]{:S(2)}) collective-permute-start(f32[2,28,128]{2,1,0:T(8,128)S(1)} %get-tuple-element.28), channel_id=1, source_target_pairs={{0,16},{4,24},{8,20},{12,28},{16,0},{20,8},{24,4},{28,12},{1,17},{... | collective-permute-start | bytes 86024 | tf_op jit(solution)/shard_map/ppermute | solution.py:708
  14.6 0.0 copy-done
  14.6 0.0 copy-done.1
  14.7 0.0 copy-done.3
  14.7 0.0 copy-start.2
  14.7 0.0 copy-start.4
  14.7 0.0 copy-start.5
  14.7 0.0 copy-start.6
  14.7 3.7 %own_ends.1 = (f32[1024,128]{1,0:T(8,128)S(1)}, f32[16,512]{1,0:T(8,128)S(1)}, f32[16,512]{1,0:T(8,128)S(1)}) custom-call(f32[3,1024,128]{2,1,0:T(8,128)S(1)} %bitcast.30, f32[3,1024,128]{2,1,0:T(8,128)S(1)} %bitcast.33, s32[1024,128]{1,0:T(8,128)S(1)} %bitcast.37, f32[8]{0:T(128)} %perm_ref.3), custom_call_target="tpu_custom_call" | custom-call | flops 10000000 | bytes 4000000 | tf_op jit(solution)/shard_map/own_ends/pallas_call | solution.py:685
  18.4 0.0 collective-permute-done.3.refs_3_
  18.4 0.0 collective-permute-done.4.refs_4_
  18.4 0.0 collective-permute-done.refs_0_
  18.4 0.0 collective-permute-done.1.refs_1_
  18.4 0.0 collective-permute-done.2.refs_2_
  18.4 1.4 %unpack_faces.1 = (f32[7,2,64,128]{3,2,1,0:T(8,128)S(1)}, f32[7,2,288,128]{3,2,1,0:T(8,128)S(1)}, f32[16,896]{1,0:T(8,128)S(1)}, f32[16,896]{1,0:T(8,128)S(1)}) custom-call(f32[16,512]{1,0:T(8,128)S(1)} %get-tuple-element.22.own_up, f32[16,512]{1,0:T(8,128)S(1)} %get-tuple-element.23.own_down, f32[304,128]{1,0:T(8,128)S(1)} %collective-permute-done.refs_0_, ...), custom_call_target="tpu_custom_call" | custom-call | tf_op jit(solution)/shard_map/unpack_faces/pallas_call | solution.py:710
  19.8 0.1 collective-permute-start.5
  19.9 1.7 %collective-permute-start.6 = (f32[16,896]{1,0:T(8,128)S(1)}, f32[16,896]{1,0:T(8,128)S(1)}, u32[]{:S(2)}, u32[]{:S(2)}) collective-permute-start(f32[16,896]{1,0:T(8,128)S(1)} %get-tuple-element.32), channel_id=1, source_target_pairs={{0,3},{1,0},{2,1},{3,2},{4,7},{5,4},{6,5},{7,6},{8,11},{9,8},{10,9... | collective-permute-start | bytes 172040 | tf_op jit(solution)/shard_map/ppermute | solution.py:731
  21.6 1.9 %collective-permute-done.5.low_ref = f32[16,896]{1,0:T(8,128)S(1)} collective-permute-done((f32[16,896]{1,0:T(8,128)S(1)}, f32[16,896]{1,0:T(8,128)S(1)}, u32[]{:S(2)}, u32[]{:S(2)}) %collective-permute-start.5) | collective-permute-done | bytes 57376 | tf_op jit(solution)/shard_map/ppermute | solution.py:730
  23.4 0.0 collective-permute-done.6.high_ref
  23.4 0.0 copy-done.2
  23.5 0.0 copy-done.4
  23.5 0.0 copy-done.5
  23.5 0.0 copy-done.6
  23.5 8.2 %march.1 = (f32[3,1024,128]{2,1,0:T(8,128)}, f32[3,1024,128]{2,1,0:T(8,128)}, f32[4,32]{1,0:T(4,128)S(1)}, f32[4,32]{1,0:T(4,128)S(1)}, f32[4,32]{1,0:T(4,128)S(1)}, /*index=5*/f32[4,32]{1,0:T(4,128)S(1)}) custom-call(f32[3,1024,128]{2,1,0:T(8,128)S(1)} %bitcast.31, f32[3,1024,128]{2,1,0:T(8,128)S(1)} %bitcast.34, f32[1024,128]{1,0:T(8,128)S(1)} %get-tuple-element.21.coef_v, ...), custom_call_target="tpu_custom_call" | custom-call | tf_op jit(solution)/shard_map/march/pallas_call | solution.py:735
  31.7 1.6 %collective-permute-start.7 = (f32[4,32]{1,0:T(4,128)S(1)}, f32[4,32]{1,0:T(4,128)S(1)}, u32[]{:S(2)}, u32[]{:S(2)}) collective-permute-start(f32[4,32]{1,0:T(4,128)S(1)} %get-tuple-element.36), channel_id=1, source_target_pairs={{0,1},{1,2},{2,3},{3,0},{4,5},{5,6},{6,7},{7,4},{8,9},{9,10},{10,1... | collective-permute-start | bytes 1544 | tf_op jit(solution)/shard_map/ppermute | solution.py:761
  33.3 0.5 %collective-permute-start.8 = (f32[4,32]{1,0:T(4,128)S(1)}, f32[4,32]{1,0:T(4,128)S(1)}, u32[]{:S(2)}, u32[]{:S(2)}) collective-permute-start(f32[4,32]{1,0:T(4,128)S(1)} %get-tuple-element.37), channel_id=1, source_target_pairs={{0,2},{1,3},{2,0},{3,1},{4,6},{5,7},{6,4},{7,5},{8,10},{9,11},{10,... | collective-permute-start | bytes 1544 | tf_op jit(solution)/shard_map/ppermute | solution.py:761
  33.9 0.9 %collective-permute-start.9 = (f32[4,32]{1,0:T(4,128)S(1)}, f32[4,32]{1,0:T(4,128)S(1)}, u32[]{:S(2)}, u32[]{:S(2)}) collective-permute-start(f32[4,32]{1,0:T(4,128)S(1)} %get-tuple-element.38), channel_id=1, source_target_pairs={{0,3},{1,0},{2,1},{3,2},{4,7},{5,4},{6,5},{7,6},{8,11},{9,8},{10,9... | collective-permute-start | bytes 1544 | tf_op jit(solution)/shard_map/ppermute | solution.py:761
  34.8 0.0 collective-permute-done.7
  34.8 2.2 %collective-permute-done.8 = f32[4,32]{1,0:T(4,128)S(1)} collective-permute-done((f32[4,32]{1,0:T(4,128)S(1)}, f32[4,32]{1,0:T(4,128)S(1)}, u32[]{:S(2)}, u32[]{:S(2)}) %collective-permute-start.8) | collective-permute-done | bytes 544 | tf_op jit(solution)/shard_map/ppermute | solution.py:761
  36.9 0.0 collective-permute-done.9
  36.9 0.6 %add_bitcast_fusion = f32[32,4]{0,1:T(4,128)} fusion(f32[4,32]{1,0:T(4,128)S(1)} %collective-permute-done.9, f32[4,32]{1,0:T(4,128)S(1)} %collective-permute-done.8, f32[4,32]{1,0:T(4,128)S(1)} %get-tuple-element.35, f32[4,32]{1,0:T(4,128)S(1)} %collective-permute-done.7), kind=kLoop, calls=%fused_computation | loop fusion | flops 384 | bytes 2560 | tf_op jit(solution)/shard_map/transpose | solution.py:764
Async XLA Ops:
  0.6 14.0 %copy-start = (f32[3,32,16,256]{3,2,1,0:T(8,128)S(1)}, f32[3,32,16,256]{3,2,1,0:T(8,128)}, u32[]{:S(2)}) copy-start(f32[3,32,16,256]{3,2,1,0:T(8,128)} %param.8) | copy-start | bytes 4718596
  0.6 14.0 %copy-start.1 = (f32[3,32,16,256]{3,2,1,0:T(8,128)S(1)}, f32[3,32,16,256]{3,2,1,0:T(8,128)}, u32[]{:S(2)}) copy-start(f32[3,32,16,256]{3,2,1,0:T(8,128)} %param.9) | copy-start | bytes 4718596
  0.7 14.0 %copy-start.3 = (s32[32,16,256]{2,1,0:T(8,128)S(1)}, s32[32,16,256]{2,1,0:T(8,128)}, u32[]{:S(2)}) copy-start(s32[32,16,256]{2,1,0:T(8,128)} %param.11) | copy-start | bytes 1572868
  3.5 14.9 %collective-permute-start.1 = (f32[19,32,128]{2,1,0:T(8,128)S(1)}, f32[19,32,128]{2,1,0:T(8,128)S(1)}, u32[]{:S(2)}, u32[]{:S(2)}) collective-permute-start(f32[19,32,128]{2,1,0:T(8,128)S(1)} %get-tuple-element.25), channel_id=1, source_target_pairs={{0,4},{4,0},{8,12},{12,8},{1,5},{5,1},{9,13},{13,9},{2,6},{6,2},{1... | collective-permute-start | bytes 933896 | tf_op jit(solution)/shard_map/ppermute | solution.py:708
  6.5 11.9 %collective-permute-start.2 = (f32[19,32,128]{2,1,0:T(8,128)S(1)}, f32[19,32,128]{2,1,0:T(8,128)S(1)}, u32[]{:S(2)}, u32[]{:S(2)}) collective-permute-start(f32[19,32,128]{2,1,0:T(8,128)S(1)} %get-tuple-element.26), channel_id=1, source_target_pairs={{0,0},{4,8},{8,4},{12,12},{1,1},{5,9},{9,5},{13,13},{2,2},{6,10},{... | collective-permute-start | bytes 933896 | tf_op jit(solution)/shard_map/ppermute | solution.py:708
  7.2 11.2 %collective-permute-start = (f32[304,128]{1,0:T(8,128)S(1)}, f32[304,128]{1,0:T(8,128)S(1)}, u32[]{:S(2)}, u32[]{:S(2)}) collective-permute-start(f32[304,128]{1,0:T(8,128)S(1)} %get-tuple-element.24), channel_id=1, source_target_pairs={{0,16},{16,0},{1,17},{17,1},{2,18},{18,2},{3,19},{19,3},{4,20},{20... | collective-permute-start | bytes 466952 | tf_op jit(solution)/shard_map/ppermute | solution.py:708
  8.8 9.6 %collective-permute-start.3 = (f32[2,28,128]{2,1,0:T(8,128)S(1)}, f32[2,28,128]{2,1,0:T(8,128)S(1)}, u32[]{:S(2)}, u32[]{:S(2)}) collective-permute-start(f32[2,28,128]{2,1,0:T(8,128)S(1)} %get-tuple-element.27), channel_id=1, source_target_pairs={{0,20},{4,16},{8,28},{12,24},{16,4},{20,0},{24,12},{28,8},{1,21},{... | collective-permute-start | bytes 86024 | tf_op jit(solution)/shard_map/ppermute | solution.py:708
  13.1 5.2 %collective-permute-start.4 = (f32[2,28,128]{2,1,0:T(8,128)S(1)}, f32[2,28,128]{2,1,0:T(8,128)S(1)}, u32[]{:S(2)}, u32[]{:S(2)}) collective-permute-start(f32[2,28,128]{2,1,0:T(8,128)S(1)} %get-tuple-element.28), channel_id=1, source_target_pairs={{0,16},{4,24},{8,20},{12,28},{16,0},{20,8},{24,4},{28,12},{1,17},{... | collective-permute-start | bytes 86024 | tf_op jit(solution)/shard_map/ppermute | solution.py:708
  14.7 8.8 %copy-start.2 = (bf16[3,3,32,16,256]{4,3,2,1,0:T(8,128)(2,1)S(1)}, bf16[3,3,32,16,256]{4,3,2,1,0:T(8,128)(2,1)}, u32[]{:S(2)}) copy-start(bf16[3,3,32,16,256]{4,3,2,1,0:T(8,128)(2,1)} %param.10) | copy-start | bytes 7077892
  14.7 8.8 %copy-start.4 = (s32[32,16]{0,1:T(8,128)S(1)}, s32[32,16]{0,1:T(8,128)}, u32[]{:S(2)}) copy-start(s32[32,16]{0,1:T(8,128)} %param.13) | copy-start | bytes 6148
  14.7 8.8 %copy-start.5 = (f32[2,3]{1,0:T(2,128)S(1)}, f32[2,3]{1,0:T(2,128)}, u32[]{:S(2)}) copy-start(f32[2,3]{1,0:T(2,128)} %amps_ref.1) | copy-start | bytes 76
  14.7 8.8 %copy-start.6 = (s32[3]{0:T(128)S(1)}, s32[3]{0:T(128)}, u32[]{:S(2)}) copy-start(s32[3]{0:T(128)} %ports_ref.1) | copy-start | bytes 40
  19.8 3.7 %collective-permute-start.5 = (f32[16,896]{1,0:T(8,128)S(1)}, f32[16,896]{1,0:T(8,128)S(1)}, u32[]{:S(2)}, u32[]{:S(2)}) collective-permute-start(f32[16,896]{1,0:T(8,128)S(1)} %get-tuple-element.31), channel_id=1, source_target_pairs={{0,1},{1,2},{2,3},{3,0},{4,5},{5,6},{6,7},{7,4},{8,9},{9,10},{10,1... | collective-permute-start | bytes 172040 | tf_op jit(solution)/shard_map/ppermute | solution.py:730
  19.9 3.6 %collective-permute-start.6 = (f32[16,896]{1,0:T(8,128)S(1)}, f32[16,896]{1,0:T(8,128)S(1)}, u32[]{:S(2)}, u32[]{:S(2)}) collective-permute-start(f32[16,896]{1,0:T(8,128)S(1)} %get-tuple-element.32), channel_id=1, source_target_pairs={{0,3},{1,0},{2,1},{3,2},{4,7},{5,4},{6,5},{7,6},{8,11},{9,8},{10,9... | collective-permute-start | bytes 172040 | tf_op jit(solution)/shard_map/ppermute | solution.py:731
  31.7 3.1 %collective-permute-start.7 = (f32[4,32]{1,0:T(4,128)S(1)}, f32[4,32]{1,0:T(4,128)S(1)}, u32[]{:S(2)}, u32[]{:S(2)}) collective-permute-start(f32[4,32]{1,0:T(4,128)S(1)} %get-tuple-element.36), channel_id=1, source_target_pairs={{0,1},{1,2},{2,3},{3,0},{4,5},{5,6},{6,7},{7,4},{8,9},{9,10},{10,1... | collective-permute-start | bytes 1544 | tf_op jit(solution)/shard_map/ppermute | solution.py:761
  33.3 3.6 %collective-permute-start.8 = (f32[4,32]{1,0:T(4,128)S(1)}, f32[4,32]{1,0:T(4,128)S(1)}, u32[]{:S(2)}, u32[]{:S(2)}) collective-permute-start(f32[4,32]{1,0:T(4,128)S(1)} %get-tuple-element.37), channel_id=1, source_target_pairs={{0,2},{1,3},{2,0},{3,1},{4,6},{5,7},{6,4},{7,5},{8,10},{9,11},{10,... | collective-permute-start | bytes 1544 | tf_op jit(solution)/shard_map/ppermute | solution.py:761
  33.9 3.1 %collective-permute-start.9 = (f32[4,32]{1,0:T(4,128)S(1)}, f32[4,32]{1,0:T(4,128)S(1)}, u32[]{:S(2)}, u32[]{:S(2)}) collective-permute-start(f32[4,32]{1,0:T(4,128)S(1)} %get-tuple-element.38), channel_id=1, source_target_pairs={{0,3},{1,0},{2,1},{3,2},{4,7},{5,4},{6,5},{7,6},{8,11},{9,8},{10,9... | collective-permute-start | bytes 1544 | tf_op jit(solution)/shard_map/ppermute | solution.py:761

commit v4 on v3

--- a/solution.py
+++ b/solution.py
@@ -211,69 +211,70 @@
                         out[z, pl.ds(4 * f + k, 1), :] = line
 
 
-def turn_ends(parts, lane):
+def turn_ends(parts, lane, count):
     out = None
-    for f in range(FIELDS):
-        first, last = parts(f)
-        turned = pltpu.roll(jnp.where(lane < 64, first, last), 4 * f + 2, 1)
-        out = turned if out is None else jnp.where(lane >= 4 * f, turned, out)
+    for k in range(count):
+        first, last = parts(k)
+        turned = pltpu.roll(jnp.where(lane < 64, first, last), 8 * k + 4, 1)
+        out = turned if out is None else jnp.where(lane >= 8 * k, turned, out)
     return out
 
 
-def turn_rows(packed, blocks, up_ref, down_ref, offset):
-    for b in range(blocks):
-        block = jnp.transpose(packed[b * 128 : (b + 1) * 128, :])
-        here = pl.ds(offset + b * 128, 128)
-        for f in range(FIELDS):
-            up_ref[f : f + 1, here] = block[4 * f + 1 : 4 * f + 2, :]
-            up_ref[8 + f : 9 + f, here] = block[4 * f : 4 * f + 1, :]
-            down_ref[f : f + 1, here] = block[4 * f + 2 : 4 * f + 3, :]
-            down_ref[8 + f : 9 + f, here] = block[4 * f + 3 : 4 * f + 4, :]
-    for row in (7, 15):
-        up_ref[row : row + 1, pl.ds(offset, blocks * 128)] = jnp.zeros((1, blocks * 128), jnp.float32)
-        down_ref[row : row + 1, pl.ds(offset, blocks * 128)] = jnp.zeros((1, blocks * 128), jnp.float32)
-
-
-def own_ends(dims, e_v, h_v, m_v, perm_ref, coef_v, up_ref, down_ref, packed):
+def own_ends(dims, e_v, h_v, m_v, snap_ref, perm_ref, coef_v, packed):
     nx, ny, nz = dims
     lanes = nz // 128
+    step = ny + HALO
     table = coef_table(perm_ref)
     lane = lax.broadcasted_iota(jnp.int32, (8, 128), 1)
     tiles = ny // 8
 
     def one(x, carry):
+        index = pl.ds(pl.multiple_of(x * ny, ny), ny)
+        change = []
+        for c in range(3):
+            s = [
+                [
+                    snap_ref[t, c, index, z * 128 : z * 128 + 128].astype(jnp.float32)
+                    for z in (0, lanes - 1)
+                ]
+                for t in range(STEPS + 1)
+            ]
+            change.append([[s[t][z] - s[t + 1][z] for z in range(2)] for t in range(STEPS)])
         for t in range(tiles):
-            index = [
+            here = [
                 pl.ds(pl.multiple_of(((x * tiles + t) * lanes + z) * 8, 8), 8) for z in range(lanes)
             ]
             for z in range(lanes):
-                coef_v[index[z], :] = coef_of(m_v[index[z], :], table)
-
-            def parts(f):
-                if f < 3:
-                    return e_v[f, index[0], :], e_v[f, index[-1], :]
-                if f < 6:
-                    return h_v[f - 3, index[0], :], h_v[f - 3, index[-1], :]
-                return coef_v[index[0], :], coef_v[index[-1], :]
-
-            packed[pl.ds(pl.multiple_of(x * ny + t * 8, 8), 8), :] = turn_ends(parts, lane)
+                coef_v[here[z], :] = coef_of(m_v[here[z], :], table)
+
+            def parts(k):
+                if k < 3:
+                    return e_v[k, here[0], :], e_v[k, here[-1], :]
+                if k < 6:
+                    return h_v[k - 3, here[0], :], h_v[k - 3, here[-1], :]
+                if k == 6:
+                    return coef_v[here[0], :], coef_v[here[-1], :]
+                pair = change[(k - FIELDS) % 3][1 - (k - FIELDS) // 3]
+                return tuple(v[t * 8 : t * 8 + 8] for v in pair)
+
+            row = pl.multiple_of((x + 2) * step + HALO + t * 8, 8)
+            packed[pl.ds(row, 8), :] = turn_ends(parts, lane, FIELDS + 6)
         return carry
 
-    lax.fori_loop(0, nx, one, 0)
-    turn_rows(packed, nx * ny // 128, up_ref, down_ref, 0)
-
-
-def unpack_faces(dims, sizes, own_up, own_down, *refs):
+    lax.fori_loop(0, nx, one, 0, unroll=2)
+
+
+def unpack_faces(dims, sizes, own_packed, *refs):
     nx, ny, nz = dims
     lanes = nz // 128
     tiles = ny // 8
     plane = ny * lanes
-    cells = nx * ny
+    step = ny + HALO
     gx, gy = lax.axis_index("gx"), lax.axis_index("gy")
     xs, ys = swaps(sizes[0]), swaps(sizes[1])
     n_msgs = len(xs) + len(ys) + len(xs) * len(ys)
     msgs = refs[:n_msgs]
-    xh, yh, up_ref, down_ref, packed, x_raw, y_raw = refs[n_msgs:]
+    xh, yh, own_t, up_ref, down_ref, packed, x_raw, y_raw = refs[n_msgs:]
     xh[...] = jnp.zeros(xh.shape, jnp.float32)
     x_raw[...] = jnp.zeros(x_raw.shape, jnp.float32)
     y_raw[...] = jnp.zeros(y_raw.shape, jnp.float32)
@@ -334,98 +335,114 @@
                         )
 
     lane = lax.broadcasted_iota(jnp.int32, (8, 128), 1)
+    upper = lax.broadcasted_iota(jnp.int32, (8, 128), 0) < HALO // 2
+
+    def halo_rows(p, before, here):
+        def tile(f, z):
+            if f == FIELDS:
+                return y_raw[here, :]
+            return jnp.where(upper, yh[f, z, before, :], yh[f, z, here, :])
+
+        packed[pl.ds(p * step if isinstance(p, int) else pl.multiple_of(p * step, 8), HALO), :] = (
+            turn_ends(lambda f: (tile(f, 0), tile(f, lanes - 1)), lane, FIELDS + 1)
+        )
 
     def one(p, carry):
-        index = pl.ds(pl.multiple_of(p * HALO, 8), HALO)
-
-        def parts(f):
-            first = yh[f, 0, index, :]
-            return first + y_raw[index, :] if f == 1 else first, yh[f, lanes - 1, index, :]
-
-        packed[index, :] = turn_ends(parts, lane)
+        halo_rows(
+            p,
+            pl.ds(pl.multiple_of((p - 1) * HALO, 8), HALO),
+            pl.ds(pl.multiple_of(p * HALO, 8), HALO),
+        )
         return carry
 
-    lax.fori_loop(0, nx + 4, one, 0, unroll=4)
-    after = (nx + 4) * HALO
-    for r in range(0, 4 * ny, 8):
-        index = pl.ds(r, 8)
-
-        def parts(f):
-            first = xh[f, 0, index, :]
-            return first + x_raw[index, :] if f == 0 else first, xh[f, lanes - 1, index, :]
-
-        packed[pl.ds(after + r, 8), :] = turn_ends(parts, lane)
-    after += 4 * ny
-    if packed.shape[0] > after:
-        packed[after:, :] = jnp.zeros((packed.shape[0] - after, 128), jnp.float32)
-    up_ref[:, 0:cells] = own_up[...]
-    down_ref[:, 0:cells] = own_down[...]
-    turn_rows(packed, packed.shape[0] // 128, up_ref, down_ref, cells)
-
-
-def march(
-    dims,
-    sizes,
-    e_v,
-    h_v,
-    coef_v,
-    xh,
-    yh,
-    low_ref,
-    high_ref,
-    snap_ref,
-    mask_ref,
-    ports_ref,
-    amps_ref,
-    *refs,
-):
+    halo_rows(0, pl.ds(0, HALO), pl.ds(0, HALO))
+    lax.fori_loop(1, nx + 4, one, 0, unroll=5)
+    last = pl.ds((nx + 3) * HALO, HALO)
+    halo_rows(nx + 4, last, last)
+    for q, p in enumerate((0, 1, nx + 2, nx + 3)):
+        for t in range(tiles):
+            index = pl.ds(q * ny + t * 8, 8)
+
+            def parts(f):
+                if f == FIELDS:
+                    return x_raw[index, :], x_raw[index, :]
+                return xh[f, 0, index, :], xh[f, lanes - 1, index, :]
+
+            packed[pl.ds(p * step + HALO + t * 8, 8), :] = turn_ends(parts, lane, FIELDS + 1)
+    for x in range(nx):
+        index = pl.ds((x + 2) * step + HALO, ny)
+        packed[index, :] = own_packed[index, :]
+    after = (nx + 4) * step + HALO
+    padded = packed.shape[0]
+    if padded > after:
+        packed[after:, :] = jnp.zeros((padded - after, 128), jnp.float32)
+    for b in range(padded // 128):
+        here = pl.ds(b * 128, 128)
+        block = jnp.transpose(packed[here, :])
+        own_t[:, here] = block
+        for f in range(FIELDS):
+            up_ref[f : f + 1, here] = block[8 * f + 3 : 8 * f + 4, :]
+            up_ref[8 + f : 9 + f, here] = block[8 * f + 2 : 8 * f + 3, :]
+            down = [block[8 * f + 4 + k : 8 * f + 5 + k, :] for k in range(2)]
+            if f < 2:
+                at = lax.broadcasted_iota(jnp.int32, (1, 128), 1) + b * 128
+                raw = (at >= HALO) & (at < step) if f == 0 else lax.rem(at, step) < HALO
+                tail = [block[8 * FIELDS + 4 + k : 8 * FIELDS + 5 + k, :] for k in range(2)]
+                down = [down[k] + jnp.where(raw, tail[k], 0.0) for k in range(2)]
+            down_ref[f : f + 1, here] = down[0]
+            down_ref[8 + f : 9 + f, here] = down[1]
+    for row in (7, 15):
+        up_ref[row : row + 1, :] = jnp.zeros((1, padded), jnp.float32)
+        down_ref[row : row + 1, :] = jnp.zeros((1, padded), jnp.float32)
+
+
+def columns_of(line, nx, ny, step, first, skip):
+    size = line.shape[1]
+    at = lax.broadcasted_iota(jnp.int32, (ny, size), 1) - first
+    y = lax.broadcasted_iota(jnp.int32, (ny, size), 0)
+    ok = (at >= 0) & (at < nx * step) & (lax.rem(at + skip, step) == y)
+    spread = jnp.where(ok, line, 0.0)
+    at = lax.broadcasted_iota(jnp.int32, (size, nx), 0) - first
+    x = lax.broadcasted_iota(jnp.int32, (size, nx), 1)
+    pick = ((at >= x * step) & (at < (x + 1) * step)).astype(jnp.float32)
+    return lax.dot_general(spread, pick, (((1,), (0,)), ((), ())), precision=HIGHEST)
+
+
+def find_ports(dims, sizes, ports_ref):
+    nx, ny, nz = dims
+    gx, gy, gz = lax.axis_index("gx"), lax.axis_index("gy"), lax.axis_index("gz")
+    plane_cells = (ny * sizes[1]) * (nz * sizes[2])
+    line_cells = nz * sizes[2]
+    found = []
+    for q in range(ports_ref.shape[0]):
+        cell = ports_ref[q]
+        x = lax.div(cell, plane_cells) - gx * nx
+        y = lax.rem(lax.div(cell, line_cells), ny * sizes[1]) - gy * ny
+        z = lax.rem(cell, line_cells) - gz * nz
+        found.append((x, y, z))
+    return found
+
+
+def march(dims, sizes, e_v, h_v, coef_v, xh, yh, snap_ref, ports_ref, amps_ref, *refs):
     nx, ny, nz = dims
     lanes = nz // 128
     tiles = ny // 8
-    plane = ny * lanes
-    cells = nx * ny
     step = ny + HALO
-    wide = nz + 128
-    parts = sizes[2]
-    e_out, h_out = refs[0], refs[1]
-    grads = refs[2 : 2 + parts]
-    (ends, rows_ref, ends_t, e1, h1, h2, half_ref, struck, sums, turned, e_s, h_s, sems) = refs[
-        2 + parts :
-    ]
-    gx, gy, gz = lax.axis_index("gx"), lax.axis_index("gy"), lax.axis_index("gz")
-    padded = rows_ref.shape[1]
-
-    low_ok, high_ok = gz > 0, gz < sizes[2] - 1
-    for f in range(FIELDS):
-        rows_ref[4 * f : 4 * f + 1, :] = jnp.where(low_ok, low_ref[8 + f : 9 + f, :], 0.0)
-        rows_ref[4 * f + 1 : 4 * f + 2, :] = jnp.where(low_ok, low_ref[f : f + 1, :], 0.0)
-        rows_ref[4 * f + 2 : 4 * f + 3, :] = jnp.where(high_ok, high_ref[f : f + 1, :], 0.0)
-        rows_ref[4 * f + 3 : 4 * f + 4, :] = jnp.where(high_ok, high_ref[8 + f : 9 + f, :], 0.0)
-    rows_ref[4 * FIELDS :, :] = jnp.zeros((128 - 4 * FIELDS, padded), jnp.float32)
-    for b in range(padded // 128):
-        ends_t[b * 128 : (b + 1) * 128, :] = jnp.transpose(rows_ref[:, b * 128 : (b + 1) * 128])
-
-    row = lax.broadcasted_iota(jnp.int32, (step, wide), 0)
-    lane = lax.broadcasted_iota(jnp.int32, (step, wide), 1)
-    inside = (
-        ((row < ny) | ((row < ny + 2) & (gy < sizes[1] - 1)) | ((row >= ny + 4) & (gy > 0)))
-        & ((lane < nz) | ((lane < nz + 64) & high_ok) | ((lane >= nz + 64) & low_ok))
-    )
+    e_s, h_s, column_ref, e1, h1, h2, half_ref, struck, clean, sums = refs
+    gx, gy = lax.axis_index("gx"), lax.axis_index("gy")
+    row = lax.broadcasted_iota(jnp.int32, (step, nz), 0)
+    lane = lax.broadcasted_iota(jnp.int32, (step, nz), 1)
+    inside = (row < ny) | ((row < ny + 2) & (gy < sizes[1] - 1)) | ((row >= ny + 4) & (gy > 0))
     half_ref[...] = jnp.where(inside, magnetic_step, 0.0)
-
-    plane_cells = (ny * sizes[1]) * (nz * sizes[2])
-    line_cells = nz * sizes[2]
+    for k in range(2):
+        clean[k] = jnp.where((lane[:ny] > k) & (lane[:ny] < nz - 1 - k), 1.0, 0.0)
+
     planes_struck = []
-    for q in range(ports_ref.shape[0]):
-        cell = ports_ref[q]
-        sx = lax.div(cell, plane_cells) - gx * nx
-        sy = lax.rem(lax.div(cell, line_cells), ny * sizes[1]) - gy * ny
-        sz = lax.rem(cell, line_cells) - gz * nz
-        near = (sy >= -2) & (sy < ny + 2) & (sz >= -2) & (sz < nz + 2)
-        sy = jnp.where(sy < 0, sy + step, sy)
-        sz = jnp.where(sz < 0, sz + wide, sz)
-        struck[q] = jnp.where((row == sy) & (lane == sz) & near, 1.0, 0.0)
-        planes_struck.append(sx + 2)
+    for q, (x, y, z) in enumerate(find_ports(dims, sizes, ports_ref)):
+        near = (y >= -2) & (y < ny + 2) & (z >= 0) & (z < nz)
+        at = jnp.where(y < 0, y + step, y)
+        struck[q] = jnp.where((row == at) & (lane == z) & near, 1.0, 0.0)
+        planes_struck.append(x + 2)
 
     def spot(x, t, z):
         index = ((x * tiles + t) * lanes + z) * 8
@@ -449,19 +466,7 @@
             column = [own_tile(f, p, t, z) for t in range(tiles)]
             column.append(yh[f, z, pl.ds(aligned(p * HALO), HALO), :])
             columns.append(jnp.concatenate(column, axis=0))
-        columns.append(ends[f, p])
         return jnp.concatenate(columns, axis=1)
-
-    def spread(p):
-        if isinstance(p, int) and not 2 <= p < nx + 2:
-            own = cells + (nx + 4) * HALO + (p if p < 2 else p - nx) * ny
-        else:
-            own = (p - 2) * ny
-        rows = [own + t * 8 for t in range(tiles)] + [cells + p * HALO]
-        for k, r in enumerate(rows):
-            v = ends_t[pl.ds(aligned(r), 8), :]
-            for f in range(FIELDS):
-                ends[f, p, k * 8 : k * 8 + 8, :] = pltpu.roll(v, 128 - (4 * f + 2), 1)
 
     def load_own(f, p):
         return jnp.concatenate(
@@ -484,7 +489,7 @@
         return pltpu.roll(v, 1, 0)
 
     def z_up(v):
-        return pltpu.roll(v, wide - 1, 1)
+        return pltpu.roll(v, nz - 1, 1)
 
     def z_down(v):
         return pltpu.roll(v, 1, 1)
@@ -543,8 +548,9 @@
             put(e_s, f, x, new[f])
             put(h_s, f, x, h[f][:ny, :nz])
             s = [snap_ref[t, f, index, :].astype(jnp.float32) for t in range(STEPS + 1)]
-            one = old[f] * (s[0] - s[1]) + new[f] * (s[1] - s[2])
-            total = one if total is None else total + one
+            one = [old[f] * (s[0] - s[1]), new[f] * (s[1] - s[2])]
+            total = one if total is None else [total[k] + one[k] for k in range(2)]
+        total = total[0] * clean[0] + total[1] * clean[1]
         folded = total[:, 0:128]
         for at in range(128, nz, 128):
             folded = folded + total[:, at : at + 128]
@@ -571,8 +577,9 @@
                     s = [snap_ref[t, 2, index, :].astype(jnp.float32) for t in (1, 2)]
                     folded = jnp.zeros((ny, 128), jnp.float32)
                     for z in range(lanes):
-                        gain = struck[q, 0:ny, z * 128 : z * 128 + 128] * amp
-                        folded = folded + gain * (s[0] - s[1])[:, z * 128 : z * 128 + 128]
+                        here = slice(z * 128, z * 128 + 128)
+                        gain = struck[q, 0:ny, here] * amp
+                        folded = folded + gain * clean[1, :, here] * (s[0] - s[1])[:, here]
                         for t in range(tiles):
                             here = spot(x, t, z)
                             e_s[2, here, :] = e_s[2, here, :] + gain[t * 8 : t * 8 + 8]
@@ -588,51 +595,144 @@
             first_e(p - 1)
         if dynamic or 0 <= p <= nx + 2:
             first_h(p)
-        if dynamic or p + 2 <= nx + 3:
-            spread(p + 2)
         strike(p)
 
     def body(p, carry):
         one(p)
         return carry
 
-    spread(0)
-    spread(1)
     for p in range(6):
         one(p)
-    chunk = nx // 4
-    copies = []
-    for c in range(4):
-        lax.fori_loop(6 + c * chunk, min(6 + (c + 1) * chunk, nx), body, 0)
-        if c == 3:
-            for p in range(nx, nx + 6):
-                one(p)
-        here = pl.ds(c * chunk * plane, chunk * plane)
-        for k, (src, dst) in enumerate(((e_s, e_out), (h_s, h_out))):
-            copy = pltpu.make_async_copy(src.at[:, here], dst.at[:, here], sems.at[2 * c + k])
-            copy.start()
-            copies.append(copy)
-
+    lax.fori_loop(6, nx + 1, body, 0)
+    for p in range(nx + 1, nx + 6):
+        one(p)
     nt = (((1,), (1,)), ((), ()))
-    nn = (((1,), (0,)), ((), ()))
-    lined = lax.dot_general(jnp.ones((8, 128), jnp.float32), sums[...], nt, precision=HIGHEST)
-    spread = jnp.where(
-        lax.rem(lax.broadcasted_iota(jnp.int32, (ny, cells), 1), ny)
-        == lax.broadcasted_iota(jnp.int32, (ny, cells), 0),
-        lined[0:1, :],
-        0.0,
-    )
-    pick = (
-        lax.div(lax.broadcasted_iota(jnp.int32, (cells, nx), 0), ny)
-        == lax.broadcasted_iota(jnp.int32, (cells, nx), 1)
-    ).astype(jnp.float32)
-    turned[...] = lax.dot_general(spread, pick, nn, precision=HIGHEST) * mask_ref[...].astype(
-        jnp.float32
-    )
+    line = lax.dot_general(jnp.ones((8, 128), jnp.float32), sums[...], nt, precision=HIGHEST)
+    column_ref[...] = columns_of(line[0:1, :], nx, ny, ny, 0, 0)
+
+
+def finish_ends(
+    dims, sizes, own_t, low_ref, high_ref, column_ref, mask_ref, ports_ref, amps_ref, *refs
+):
+    nx, ny, nz = dims
+    step = ny + HALO
+    parts = sizes[2]
+    ends_ref = refs[0]
+    grads = refs[1 : 1 + parts]
+    strips, turned, rows_ref = refs[1 + parts :]
+    gx, gy, gz = lax.axis_index("gx"), lax.axis_index("gy"), lax.axis_index("gz")
+    padded = own_t.shape[1]
+    row = lax.broadcasted_iota(jnp.int32, (8, padded), 0)
+    lane = lax.broadcasted_iota(jnp.int32, (8, padded), 1) - HALO
+    has_low, has_high = gz > 0, gz < sizes[2] - 1
+    for k, (msg, ok, far, near) in enumerate(((low_ref, has_low, 2, 3), (high_ref, has_high, 5, 4))):
+        for f in range(FIELDS):
+            strips[k, f] = own_t[8 * f : 8 * f + 8, :]
+            strips[k, f, far : far + 1, :] = jnp.where(ok, msg[8 + f : 9 + f, :], 0.0)
+            strips[k, f, near : near + 1, :] = jnp.where(ok, msg[f : f + 1, :], 0.0)
+
+    at = lane + 2
+    p, y = lax.div(at, step), lax.rem(at, step) - 2
+    inside = ((p >= 2) | (gx > 0)) & ((p < nx + 2) | (gx < sizes[0] - 1))
+    inside = inside & ((y >= 0) | (gy > 0)) & ((y < ny) | (gy < sizes[1] - 1))
+    found = find_ports(dims, sizes, ports_ref)
+
+    def x_up(v):
+        return pltpu.roll(v, padded - step, 1)
+
+    def x_down(v):
+        return pltpu.roll(v, step, 1)
+
+    def y_up(v):
+        return pltpu.roll(v, padded - 1, 1)
+
+    def y_down(v):
+        return pltpu.roll(v, 1, 1)
+
+    def z_up(v):
+        return pltpu.roll(v, 7, 0)
+
+    def z_down(v):
+        return pltpu.roll(v, 1, 0)
+
+    total = None
+    results = []
+    for k in range(2):
+        ex, ey, ez, hx, hy, hz, coef = (strips[k, f] for f in range(FIELDS))
+        first = -4 if k == 0 else nz - 4
+        good = ((row >= 4) | has_low) if k == 0 else ((row < 4) | has_high)
+        half = jnp.where(inside & good, magnetic_step, 0.0)
+        for s in range(STEPS):
+            cx = (y_up(ez) - ez) - (z_up(ey) - ey)
+            cy = (z_up(ex) - ex) - (x_up(ez) - ez)
+            cz = (x_up(ey) - ey) - (y_up(ex) - ex)
+            hx, hy, hz = hx - half * cx, hy - half * cy, hz - half * cz
+            cx = (hz - y_down(hz)) - (hy - z_down(hy))
+            cy = (hx - z_down(hx)) - (hz - x_down(hz))
+            cz = (hy - x_down(hy)) - (hx - y_down(hx))
+            ex, ey, ez = ex + coef * cx, ey + coef * cy, ez + coef * cz
+            for q, (sx, sy, sz) in enumerate(found):
+                near = (sx >= -2) & (sx < nx + 2) & (sy >= -2) & (sy < ny + 2)
+                hit = (row == sz - first) & (at == (sx + 2) * step + sy + 2) & near
+                ez = ez + jnp.where(hit, amps_ref[s, q], 0.0)
+            if k == 0:
+                mine = (row == 4) | ((row == 5) & (s == 1))
+            else:
+                mine = (row == 3) | ((row == 2) & (s == 1))
+            for c, e in enumerate((ex, ey, ez)):
+                tile = FIELDS + c + 3 * (1 - s)
+                one = jnp.where(mine, e * own_t[8 * tile : 8 * tile + 8, :], 0.0)
+                total = one if total is None else total + one
+        results.append((ex, ey, ez, hx, hy, hz))
+    for c in range(6):
+        rows_ref[8 * c : 8 * c + 8, :] = jnp.where(row < 4, results[1][c], results[0][c])
+    line = jnp.sum(total, axis=0, keepdims=True)
+    column = column_ref[...] + columns_of(line, nx, ny, step, 2 * step + HALO, 0)
+    turned[...] = column * mask_ref[...].astype(jnp.float32)
     width = ny // parts
     for shift in range(parts):
         owner = lax.rem(gz + shift, parts)
         grads[shift][...] = turned[pl.ds(owner * width, width), :]
+    ends_ref[...] = rows_ref[...]
+
+
+def write_out(dims, e_s, h_s, ends_ref, e_out, h_out, spare, e_v, h_v, ends_t, sems):
+    nx, ny, nz = dims
+    lanes = nz // 128
+    tiles = ny // 8
+    plane = ny * lanes
+    step = ny + HALO
+    lane = lax.broadcasted_iota(jnp.int32, (8, 128), 1)
+    spare[...] = jnp.zeros(spare.shape, jnp.float32)
+    spare[0 : ends_ref.shape[0], :] = ends_ref[...]
+    for b in range(spare.shape[1] // 128):
+        ends_t[b * 128 : (b + 1) * 128, :] = jnp.transpose(spare[:, b * 128 : (b + 1) * 128])
+
+    def one(x, carry):
+        for t in range(tiles):
+            v = ends_t[pl.ds(pl.multiple_of((x + 2) * step + HALO + t * 8, 8), 8), :]
+            for c in range(6):
+                src, dst = (e_s, e_v) if c < 3 else (h_s, h_v)
+                placed = pltpu.roll(v, 124 - 8 * c, 1)
+                for z in range(lanes):
+                    here = pl.ds(pl.multiple_of(((x * tiles + t) * lanes + z) * 8, 8), 8)
+                    out = src[c % 3, here, :]
+                    if z == 0:
+                        out = jnp.where(lane < 2, placed, out)
+                    if z == lanes - 1:
+                        out = jnp.where(lane >= 126, placed, out)
+                    dst[c % 3, here, :] = out
+        return carry
+
+    chunk = nx // 4
+    copies = []
+    for c in range(4):
+        lax.fori_loop(c * chunk, (c + 1) * chunk, one, 0, unroll=2)
+        here = pl.ds(c * chunk * plane, chunk * plane)
+        for k, (src, dst) in enumerate(((e_v, e_out), (h_v, h_out))):
+            copy = pltpu.make_async_copy(src.at[:, here], dst.at[:, here], sems.at[2 * c + k])
+            copy.start()
+            copies.append(copy)
     for copy in copies:
         copy.wait()
 
@@ -651,8 +751,7 @@
     plane = ny * lanes
     cells = nx * ny
     step = ny + HALO
-    edge = -(-((nx + 4) * HALO + 4 * ny) // 128) * 128
-    padded = cells + edge
+    padded = -(-((nx + 4) * step + HALO) // 128) * 128
     f32, i32 = jnp.float32, jnp.int32
     xs, ys = swaps(sizes[0]), swaps(sizes[1])
     block, cube = jax.ShapeDtypeStruct, pltpu.VMEM
@@ -682,16 +781,15 @@
     )
     e_v, h_v, m_v = in_vmem(tiled(e_adjoint)), in_vmem(tiled(h_adjoint)), in_vmem(tiled(material))
     s = in_vmem(snapshots.reshape(STEPS + 1, 3, cells, nz))
-    coef_v, own_up, own_down = pl.pallas_call(
+    coef_v, own_packed = pl.pallas_call(
         functools.partial(own_ends, dims),
-        out_shape=[cube(m_v.shape, f32), cube((16, cells), f32), cube((16, cells), f32)],
-        in_specs=[VM, VM, VM, SM],
-        out_specs=[VM] * 3,
-        scratch_shapes=[pltpu.VMEM((cells, 128), f32)],
+        out_shape=[cube(m_v.shape, f32), cube((padded, 128), f32)],
+        in_specs=[VM, VM, VM, VM, SM],
+        out_specs=[VM] * 2,
         compiler_params=params(),
         cost_estimate=pl.CostEstimate(flops=10**7, bytes_accessed=4 * 10**6, transcendentals=0),
         name="own_ends",
-    )(e_v, h_v, m_v, permittivity)
+    )(e_v, h_v, m_v, s, permittivity)
 
     both = ("gx", "gy")
     tables = [("gx", list(enumerate(swap_table(sizes[0], o)))) for o in xs]
@@ -707,61 +805,84 @@
             tables.append((both, pairs))
     got = [lax.ppermute(msg, axis, pairs) for msg, (axis, pairs) in zip(msgs, tables)]
 
-    xh, yh, up, down = pl.pallas_call(
+    xh, yh, own_t, up, down = pl.pallas_call(
         functools.partial(unpack_faces, dims, sizes),
         out_shape=[
             cube((FIELDS, lanes, 4 * ny, 128), f32),
             cube((FIELDS, lanes, (nx + 4) * HALO, 128), f32),
+            cube((128, padded), f32),
             block((16, padded), f32),
             block((16, padded), f32),
         ],
-        in_specs=[VM] * (2 + len(got)),
-        out_specs=[VM] * 4,
+        in_specs=[VM] * (1 + len(got)),
+        out_specs=[VM] * 5,
         scratch_shapes=[
-            pltpu.VMEM((edge, 128), f32),
+            pltpu.VMEM((padded, 128), f32),
             pltpu.VMEM((4 * ny, 128), f32),
             pltpu.VMEM(((nx + 4) * HALO, 128), f32),
         ],
         compiler_params=params(),
         name="unpack_faces",
-    )(own_up, own_down, *got)
+    )(own_packed, *got)
 
     parts = sizes[2]
     low = lax.ppermute(up, "gz", [(i, (i + 1) % parts) for i in range(parts)])
     high = lax.ppermute(down, "gz", [(i, (i - 1) % parts) for i in range(parts)])
 
-    wide = nz + 128
     ported = ports.shape[0]
-    out = pl.pallas_call(
+    e_s, h_s, column = pl.pallas_call(
         functools.partial(march, dims, sizes),
-        out_shape=[block(e_v.shape, f32), block(h_v.shape, f32)]
-        + [block((ny // parts, nx), f32)] * parts,
-        in_specs=[VM] * 9 + [SM, SM],
-        out_specs=[ANY, ANY] + [VM] * parts,
+        out_shape=[cube(e_v.shape, f32), cube(h_v.shape, f32), cube((ny, nx), f32)],
+        in_specs=[VM] * 6 + [SM, SM],
+        out_specs=[VM] * 3,
         scratch_shapes=[
-            pltpu.VMEM((FIELDS, nx + 4, step, 128), f32),
+            pltpu.VMEM((3, nx + 4, step, nz), f32),
+            pltpu.VMEM((3, nx + 4, step, nz), f32),
+            pltpu.VMEM((3, nx + 4, step, nz), f32),
+            pltpu.VMEM((step, nz), f32),
+            pltpu.VMEM((ported, step, nz), f32),
+            pltpu.VMEM((2, ny, nz), f32),
+            pltpu.VMEM((cells, 128), f32),
+        ],
+        compiler_params=params(24),
+        cost_estimate=pl.CostEstimate(flops=4 * 10**7, bytes_accessed=10**7, transcendentals=0),
+        name="march",
+    )(e_v, h_v, coef_v, xh, yh, s, ports, amplitudes)
+    ends, *chunks = pl.pallas_call(
+        functools.partial(finish_ends, dims, sizes),
+        out_shape=[cube((48, padded), f32)] + [block((ny // parts, nx), f32)] * parts,
+        in_specs=[VM] * 5 + [SM, SM],
+        out_specs=[VM] * (1 + parts),
+        scratch_shapes=[
+            pltpu.VMEM((2, FIELDS, 8, padded), f32),
+            pltpu.VMEM((ny, nx), f32),
+            pltpu.VMEM((48, padded), f32),
+        ],
+        compiler_params=params(),
+        name="finish_ends",
+    )(own_t, low, high, column, design_mask.T, ports, amplitudes)
+    e_out, h_out = pl.pallas_call(
+        functools.partial(write_out, dims),
+        out_shape=[block(e_v.shape, f32), block(h_v.shape, f32)],
+        in_specs=[VM] * 3,
+        out_specs=[HBM] * 2,
+        scratch_shapes=[
             pltpu.VMEM((128, padded), f32),
-            pltpu.VMEM((padded, 128), f32),
-            pltpu.VMEM((3, nx + 4, step, wide), f32),
-            pltpu.VMEM((3, nx + 4, step, wide), f32),
-            pltpu.VMEM((3, nx + 4, step, wide), f32),
-            pltpu.VMEM((step, wide), f32),
-            pltpu.VMEM((ported, step, wide), f32),
-            pltpu.VMEM((cells, 128), f32),
-            pltpu.VMEM((ny, nx), f32),
             pltpu.VMEM(e_v.shape, f32),
             pltpu.VMEM(h_v.shape, f32),
+            pltpu.VMEM((padded, 128), f32),
             pltpu.SemaphoreType.DMA((8,)),
         ],
-        compiler_params=params(32),
-        name="march",
-    )(e_v, h_v, coef_v, xh, yh, low, high, s, design_mask.T, ports, amplitudes)
-    gradient = out[2]
+        compiler_params=params(),
+        cost_estimate=pl.CostEstimate(flops=10**7, bytes_accessed=8 * 10**6, transcendentals=0),
+        name="write_out",
+    )(e_s, h_s, ends)
+    gradient = chunks[0]
     for shift in range(1, parts):
         gradient = gradient + lax.ppermute(
-            out[2 + shift], "gz", [(i, (i + shift) % parts) for i in range(parts)]
+            chunks[shift], "gz", [(i, (i + shift) % parts) for i in range(parts)]
         )
-    return untiled(out[0], dims), untiled(out[1], dims), gradient.T
+    return untiled(e_out, dims), untiled(h_out, dims), gradient.T
 
 
 def solution(mesh):

time: 37.7 us -> 36.3 us (0.963)
  waiting for transfers between devices: 4.03 us -> 0.03 us
  local copies, waits for them, and re-layouts: 0.04 us -> 1.69 us
  Pallas kernels: 16 us -> 17 us
    ppermute x3, waiting for transfers between devices: 2.16 us -> 0.01 us  [body(): lax.ppermute(chunks[shift], 'gz', [(i, (i + shift) % parts) for i in rang...]
    ppermute x1, waiting for transfers between devices: 1.86 us -> 0.01 us  [body(): low = lax.ppermute(up, 'gz', [(i, (i + 1) % parts) for i in range(parts)])]
    unnamed x14 -> x16, local copies, waits for them, and re-layouts: 0.04 us -> 1.69 us
    pallas_call x1 -> x3, Pallas kernels: 8.21 us -> 9.85 us  [the longest x1 5.78 us: body(): pl.pallas_call(functools.partial(march, dims, sizes), out_shape=[cube(e_v...]
    pallas_call x1, Pallas kernels: 3.65 us -> 2.81 us  [body(): pl.pallas_call(functools.partial(own_ends, dims), out_shape=[cube(m_v.sha...]
  transfers between devices with their start and end apart: 10 -> 10, of which waited for: 2 -> 0; matrix products, arithmetic and copies ran while one was open for 0% -> 0% of each run, Pallas kernels for 10% -> 31%
where the time goes in v4:
time: 36.3 us; the launch traced here: 36 us
  Pallas kernels  17 us (47%)
  starting transfers between devices  16 us (44%)
  local copies, waits for them, and re-layouts  1.69 us (5%)
  between operations  0.82 us (2%)
  other arithmetic  0.58 us (2%)
    ppermute x5, starting transfers between devices, body(): lax.ppermute(msg, axis, pairs)  11.2 us
    pallas_call x1, Pallas kernels, body(): pl.pallas_call(functools.partial(march, dims, sizes), out_shape=[cube(e_v...  5.78 us
    ppermute x3, starting transfers between devices, body(): lax.ppermute(chunks[shift], 'gz', [(i, (i + shift) % parts) for i in rang...  2.99 us
    pallas_call x1, Pallas kernels, body(): pl.pallas_call(functools.partial(own_ends, dims), out_shape=[cube(m_v.sha...  2.81 us
    pallas_call x1, Pallas kernels, body(): pl.pallas_call(functools.partial(send_faces, dims, sizes), out_shape=shap...  2.78 us
    pallas_call x1, Pallas kernels, body(): pl.pallas_call(functools.partial(write_out, dims), out_shape=[block(e_v.s...  2.64 us
    ppermute x1, starting transfers between devices, body(): lax.ppermute(down, 'gz', [(i, (i - 1) % parts) for i in range(parts)])  1.73 us
    unnamed x16, local copies, waits for them, and re-layouts  1.69 us
  transfers between devices with their start and end apart: 10, of which 0 were waited for; matrix products, arithmetic and copies ran while one was open for 0% of the time, Pallas kernels for 31%

profile of v4, /device:TPU:0, one launch (start us, length us, event | category | flops | bytes accessed | tf_op | source)
XLA Modules:
  0.0 36.0 jit_solution(11368226739242340825)
XLA Ops:
  0.6 0.0 copy-start
  0.6 0.0 copy-start.1
  0.7 0.0 copy-start.4
  0.7 2.8 %send_faces.1 = (f32[304,128]{1,0:T(8,128)S(1)}, f32[19,32,128]{2,1,0:T(8,128)S(1)}, f32[19,32,128]{2,1,0:T(8,128)S(1)}, f32[2,28,128]{2,1,0:T(8,128)S(1)}, f32[2,28,128]{2,1,0:T(8,128)S(1)}) custom-call(f32[3,32,2,2,8,128]{5,4,3,2,1,0:T(8,128)} %bitcast.29, f32[3,32,2,2,8,128]{5,4,3,2,1,0:T(8,128)} %bitcast.32, s32[32,2,2,8,128]{4,3,2,1,0:T(8,128)} %bitcast.37, ...), custom_call_target="tpu_custom_call" | custom-call | tf_op jit(solution)/shard_map/send_faces/pallas_call | solution.py:768
  3.5 3.1 %collective-permute-start.1 = (f32[19,32,128]{2,1,0:T(8,128)S(1)}, f32[19,32,128]{2,1,0:T(8,128)S(1)}, u32[]{:S(2)}, u32[]{:S(2)}) collective-permute-start(f32[19,32,128]{2,1,0:T(8,128)S(1)} %get-tuple-element.28), channel_id=1, source_target_pairs={{0,4},{4,0},{8,12},{12,8},{1,5},{5,1},{9,13},{13,9},{2,6},{6,2},{1... | collective-permute-start | bytes 933896 | tf_op jit(solution)/shard_map/ppermute | solution.py:806
  6.5 0.7 %collective-permute-start.2 = (f32[19,32,128]{2,1,0:T(8,128)S(1)}, f32[19,32,128]{2,1,0:T(8,128)S(1)}, u32[]{:S(2)}, u32[]{:S(2)}) collective-permute-start(f32[19,32,128]{2,1,0:T(8,128)S(1)} %get-tuple-element.29), channel_id=1, source_target_pairs={{0,0},{4,8},{8,4},{12,12},{1,1},{5,9},{9,5},{13,13},{2,2},{6,10},{... | collective-permute-start | bytes 933896 | tf_op jit(solution)/shard_map/ppermute | solution.py:806
  7.2 1.6 %collective-permute-start = (f32[304,128]{1,0:T(8,128)S(1)}, f32[304,128]{1,0:T(8,128)S(1)}, u32[]{:S(2)}, u32[]{:S(2)}) collective-permute-start(f32[304,128]{1,0:T(8,128)S(1)} %get-tuple-element.27), channel_id=1, source_target_pairs={{0,16},{16,0},{1,17},{17,1},{2,18},{18,2},{3,19},{19,3},{4,20},{20... | collective-permute-start | bytes 466952 | tf_op jit(solution)/shard_map/ppermute | solution.py:806
  8.8 4.3 %collective-permute-start.3 = (f32[2,28,128]{2,1,0:T(8,128)S(1)}, f32[2,28,128]{2,1,0:T(8,128)S(1)}, u32[]{:S(2)}, u32[]{:S(2)}) collective-permute-start(f32[2,28,128]{2,1,0:T(8,128)S(1)} %get-tuple-element.30), channel_id=1, source_target_pairs={{0,20},{4,16},{8,28},{12,24},{16,4},{20,0},{24,12},{28,8},{1,21},{... | collective-permute-start | bytes 86024 | tf_op jit(solution)/shard_map/ppermute | solution.py:806
  13.1 1.5 %collective-permute-start.4 = (f32[2,28,128]{2,1,0:T(8,128)S(1)}, f32[2,28,128]{2,1,0:T(8,128)S(1)}, u32[]{:S(2)}, u32[]{:S(2)}) collective-permute-start(f32[2,28,128]{2,1,0:T(8,128)S(1)} %get-tuple-element.31), channel_id=1, source_target_pairs={{0,16},{4,24},{8,20},{12,28},{16,0},{20,8},{24,4},{28,12},{1,17},{... | collective-permute-start | bytes 86024 | tf_op jit(solution)/shard_map/ppermute | solution.py:806
  14.6 0.0 copy-done
  14.6 0.0 copy-done.1
  14.7 0.0 copy-done.4
  14.7 0.0 copy-start.2
  14.7 1.7 %copy-done.2 = bf16[3,3,32,16,256]{4,3,2,1,0:T(8,128)(2,1)S(1)} copy-done((bf16[3,3,32,16,256]{4,3,2,1,0:T(8,128)(2,1)S(1)}, bf16[3,3,32,16,256]{4,3,2,1,0:T(8,128)(2,1)}, u32[]{:S(2)}) %copy-start.2) | copy-done | bytes 2359320
  16.3 0.0 copy-start.3
  16.3 0.0 copy-start.6
  16.3 0.0 copy-start.7
  16.3 2.8 %own_ends.1 = (f32[1024,128]{1,0:T(8,128)S(1)}, f32[896,128]{1,0:T(8,128)S(1)}) custom-call(f32[3,1024,128]{2,1,0:T(8,128)S(1)} %bitcast.30, f32[3,1024,128]{2,1,0:T(8,128)S(1)} %bitcast.33, s32[1024,128]{1,0:T(8,128)S(1)} %bitcast.38, bf16[3,3,512,256]{3,2,1,0:T(8,128)(2,1)S(1)} %bitcast.35, f32[8]{0:T(128)} %perm_ref.3), custom_call_target="tpu_custom_call" | custom-call | flops 10000000 | bytes 4000000 | tf_op jit(solution)/shard_map/own_ends/pallas_call | solution.py:784
  19.1 0.0 collective-permute-done.3.refs_3_
  19.2 0.0 collective-permute-done.4.refs_4_
  19.2 0.0 collective-permute-done.refs_0_
  19.2 0.0 collective-permute-done.1.refs_1_
  19.2 0.0 collective-permute-done.2.refs_2_
  19.2 1.5 %unpack_faces.1 = (f32[7,2,64,128]{3,2,1,0:T(8,128)S(1)}, f32[7,2,288,128]{3,2,1,0:T(8,128)S(1)}, f32[128,896]{1,0:T(8,128)S(1)}, f32[16,896]{1,0:T(8,128)S(1)}, f32[16,896]{1,0:T(8,128)S(1)}) custom-call(f32[896,128]{1,0:T(8,128)S(1)} %get-tuple-element.26.own_packed, f32[304,128]{1,0:T(8,128)S(1)} %collective-permute-done.refs_0_, ...), custom_call_target="tpu_custom_call" | custom-call | tf_op jit(solution)/shard_map/unpack_faces/pallas_call | solution.py:808
  20.7 0.1 collective-permute-start.5
  20.8 1.7 %collective-permute-start.6 = (f32[16,896]{1,0:T(8,128)S(1)}, f32[16,896]{1,0:T(8,128)S(1)}, u32[]{:S(2)}, u32[]{:S(2)}) collective-permute-start(f32[16,896]{1,0:T(8,128)S(1)} %get-tuple-element.38), channel_id=1, source_target_pairs={{0,3},{1,0},{2,1},{3,2},{4,7},{5,4},{6,5},{7,6},{8,11},{9,8},{10,9... | collective-permute-start | bytes 172040 | tf_op jit(solution)/shard_map/ppermute | solution.py:830
  22.5 0.0 copy-done.3
  22.5 0.0 copy-done.6
  22.5 0.0 copy-done.7
  22.5 0.0 copy-start.5
  22.5 5.8 %march.1 = (f32[3,1024,128]{2,1,0:T(8,128)S(1)}, f32[3,1024,128]{2,1,0:T(8,128)S(1)}, f32[16,32]{1,0:T(8,128)S(1)}) custom-call(f32[3,1024,128]{2,1,0:T(8,128)S(1)} %bitcast.31, f32[3,1024,128]{2,1,0:T(8,128)S(1)} %bitcast.34, f32[1024,128]{1,0:T(8,128)S(1)} %get-tuple-element.25.coef_v, f32[7,2,64,128]{3,2,1,0:T(8,128)S(1)} %get-tuple-element.32.xh, ...), custom_call_target="tpu_custom_call" | custom-call | flops 40000000 | bytes 10000000 | tf_op jit(solution)/shard_map/march/pallas_call | solution.py:833
  28.3 0.0 collective-permute-done.5.low_ref
  28.3 0.0 collective-permute-done.6.high_ref
  28.3 0.0 copy-done.5
  28.3 1.4 %finish_ends.1 = (f32[48,896]{1,0:T(8,128)S(1)}, f32[4,32]{1,0:T(4,128)S(1)}, f32[4,32]{1,0:T(4,128)S(1)}, f32[4,32]{1,0:T(4,128)S(1)}, f32[4,32]{1,0:T(4,128)S(1)}) custom-call(f32[128,896]{1,0:T(8,128)S(1)} %get-tuple-element.36.own_t, f32[16,896]{1,0:T(8,128)S(1)} %collective-permute-done.5.low_ref, f32[16,896]{1,0:T(8,128)S(1)} %collective-permute-done.6.high_ref, ...), custom_call_target="tpu_custom_call" | custom-call | tf_op jit(solution)/shard_map/finish_ends/pallas_call | solution.py:851
  29.8 0.0 collective-permute-start.7
  29.8 1.6 %collective-permute-start.8 = (f32[4,32]{1,0:T(4,128)S(1)}, f32[4,32]{1,0:T(4,128)S(1)}, u32[]{:S(2)}, u32[]{:S(2)}) collective-permute-start(f32[4,32]{1,0:T(4,128)S(1)} %get-tuple-element.45), channel_id=1, source_target_pairs={{0,2},{1,3},{2,0},{3,1},{4,6},{5,7},{6,4},{7,5},{8,10},{9,11},{10,... | collective-permute-start | bytes 1544 | tf_op jit(solution)/shard_map/ppermute | solution.py:882
  31.4 1.4 %collective-permute-start.9 = (f32[4,32]{1,0:T(4,128)S(1)}, f32[4,32]{1,0:T(4,128)S(1)}, u32[]{:S(2)}, u32[]{:S(2)}) collective-permute-start(f32[4,32]{1,0:T(4,128)S(1)} %get-tuple-element.46), channel_id=1, source_target_pairs={{0,3},{1,0},{2,1},{3,2},{4,7},{5,4},{6,5},{7,6},{8,11},{9,8},{10,9... | collective-permute-start | bytes 1544 | tf_op jit(solution)/shard_map/ppermute | solution.py:882
  32.8 2.6 %write_out.1 = (f32[3,1024,128]{2,1,0:T(8,128)}, f32[3,1024,128]{2,1,0:T(8,128)}) custom-call(f32[3,1024,128]{2,1,0:T(8,128)S(1)} %get-tuple-element.34.e_s, f32[3,1024,128]{2,1,0:T(8,128)S(1)} %get-tuple-element.35.h_s, f32[48,896]{1,0:T(8,128)S(1)} %get-tuple-element.40.ends_ref), custom_call_target="tpu_custom_call" | custom-call | flops 10000000 | bytes 8000000 | tf_op jit(solution)/shard_map/write_out/pallas_call | solution.py:864
  35.4 0.0 collective-permute-done.7
  35.4 0.0 collective-permute-done.8
  35.4 0.0 collective-permute-done.9
  35.5 0.6 %add_bitcast_fusion = f32[32,4]{0,1:T(4,128)} fusion(f32[4,32]{1,0:T(4,128)S(1)} %collective-permute-done.9, f32[4,32]{1,0:T(4,128)S(1)} %collective-permute-done.8, f32[4,32]{1,0:T(4,128)S(1)} %get-tuple-element.43, f32[4,32]{1,0:T(4,128)S(1)} %collective-permute-done.7), kind=kLoop, calls=%fused_computation | loop fusion | flops 384 | bytes 2560 | tf_op jit(solution)/shard_map/transpose | solution.py:885
Async XLA Ops:
  0.6 14.0 %copy-start = (f32[3,32,16,256]{3,2,1,0:T(8,128)S(1)}, f32[3,32,16,256]{3,2,1,0:T(8,128)}, u32[]{:S(2)}) copy-start(f32[3,32,16,256]{3,2,1,0:T(8,128)} %param.8) | copy-start | bytes 4718596
  0.6 14.0 %copy-start.1 = (f32[3,32,16,256]{3,2,1,0:T(8,128)S(1)}, f32[3,32,16,256]{3,2,1,0:T(8,128)}, u32[]{:S(2)}) copy-start(f32[3,32,16,256]{3,2,1,0:T(8,128)} %param.9) | copy-start | bytes 4718596
  0.7 14.0 %copy-start.4 = (s32[32,16,256]{2,1,0:T(8,128)S(1)}, s32[32,16,256]{2,1,0:T(8,128)}, u32[]{:S(2)}) copy-start(s32[32,16,256]{2,1,0:T(8,128)} %param.11) | copy-start | bytes 1572868
  3.5 15.7 %collective-permute-start.1 = (f32[19,32,128]{2,1,0:T(8,128)S(1)}, f32[19,32,128]{2,1,0:T(8,128)S(1)}, u32[]{:S(2)}, u32[]{:S(2)}) collective-permute-start(f32[19,32,128]{2,1,0:T(8,128)S(1)} %get-tuple-element.28), channel_id=1, source_target_pairs={{0,4},{4,0},{8,12},{12,8},{1,5},{5,1},{9,13},{13,9},{2,6},{6,2},{1... | collective-permute-start | bytes 933896 | tf_op jit(solution)/shard_map/ppermute | solution.py:806
  6.5 12.7 %collective-permute-start.2 = (f32[19,32,128]{2,1,0:T(8,128)S(1)}, f32[19,32,128]{2,1,0:T(8,128)S(1)}, u32[]{:S(2)}, u32[]{:S(2)}) collective-permute-start(f32[19,32,128]{2,1,0:T(8,128)S(1)} %get-tuple-element.29), channel_id=1, source_target_pairs={{0,0},{4,8},{8,4},{12,12},{1,1},{5,9},{9,5},{13,13},{2,2},{6,10},{... | collective-permute-start | bytes 933896 | tf_op jit(solution)/shard_map/ppermute | solution.py:806
  7.2 12.0 %collective-permute-start = (f32[304,128]{1,0:T(8,128)S(1)}, f32[304,128]{1,0:T(8,128)S(1)}, u32[]{:S(2)}, u32[]{:S(2)}) collective-permute-start(f32[304,128]{1,0:T(8,128)S(1)} %get-tuple-element.27), channel_id=1, source_target_pairs={{0,16},{16,0},{1,17},{17,1},{2,18},{18,2},{3,19},{19,3},{4,20},{20... | collective-permute-start | bytes 466952 | tf_op jit(solution)/shard_map/ppermute | solution.py:806
  8.8 10.4 %collective-permute-start.3 = (f32[2,28,128]{2,1,0:T(8,128)S(1)}, f32[2,28,128]{2,1,0:T(8,128)S(1)}, u32[]{:S(2)}, u32[]{:S(2)}) collective-permute-start(f32[2,28,128]{2,1,0:T(8,128)S(1)} %get-tuple-element.30), channel_id=1, source_target_pairs={{0,20},{4,16},{8,28},{12,24},{16,4},{20,0},{24,12},{28,8},{1,21},{... | collective-permute-start | bytes 86024 | tf_op jit(solution)/shard_map/ppermute | solution.py:806
  13.1 6.0 %collective-permute-start.4 = (f32[2,28,128]{2,1,0:T(8,128)S(1)}, f32[2,28,128]{2,1,0:T(8,128)S(1)}, u32[]{:S(2)}, u32[]{:S(2)}) collective-permute-start(f32[2,28,128]{2,1,0:T(8,128)S(1)} %get-tuple-element.31), channel_id=1, source_target_pairs={{0,16},{4,24},{8,20},{12,28},{16,0},{20,8},{24,4},{28,12},{1,17},{... | collective-permute-start | bytes 86024 | tf_op jit(solution)/shard_map/ppermute | solution.py:806
  14.7 1.7 %copy-start.2 = (bf16[3,3,32,16,256]{4,3,2,1,0:T(8,128)(2,1)S(1)}, bf16[3,3,32,16,256]{4,3,2,1,0:T(8,128)(2,1)}, u32[]{:S(2)}) copy-start(bf16[3,3,32,16,256]{4,3,2,1,0:T(8,128)(2,1)} %param.10) | copy-start | bytes 7077892
  16.3 6.2 %copy-start.3 = (bf16[3,3,32,16,256]{4,3,2,1,0:T(8,128)(2,1)S(1)}, bf16[3,3,32,16,256]{4,3,2,1,0:T(8,128)(2,1)}, u32[]{:S(2)}) copy-start(bf16[3,3,32,16,256]{4,3,2,1,0:T(8,128)(2,1)} %param.10) | copy-start | bytes 7077892
  16.3 6.2 %copy-start.6 = (f32[2,3]{1,0:T(2,128)S(1)}, f32[2,3]{1,0:T(2,128)}, u32[]{:S(2)}) copy-start(f32[2,3]{1,0:T(2,128)} %amps_ref.3) | copy-start | bytes 76
  16.3 6.2 %copy-start.7 = (s32[3]{0:T(128)S(1)}, s32[3]{0:T(128)}, u32[]{:S(2)}) copy-start(s32[3]{0:T(128)} %ports_ref.3) | copy-start | bytes 40
  20.7 7.6 %collective-permute-start.5 = (f32[16,896]{1,0:T(8,128)S(1)}, f32[16,896]{1,0:T(8,128)S(1)}, u32[]{:S(2)}, u32[]{:S(2)}) collective-permute-start(f32[16,896]{1,0:T(8,128)S(1)} %get-tuple-element.37), channel_id=1, source_target_pairs={{0,1},{1,2},{2,3},{3,0},{4,5},{5,6},{6,7},{7,4},{8,9},{9,10},{10,1... | collective-permute-start | bytes 172040 | tf_op jit(solution)/shard_map/ppermute | solution.py:829
  20.8 7.5 %collective-permute-start.6 = (f32[16,896]{1,0:T(8,128)S(1)}, f32[16,896]{1,0:T(8,128)S(1)}, u32[]{:S(2)}, u32[]{:S(2)}) collective-permute-start(f32[16,896]{1,0:T(8,128)S(1)} %get-tuple-element.38), channel_id=1, source_target_pairs={{0,3},{1,0},{2,1},{3,2},{4,7},{5,4},{6,5},{7,6},{8,11},{9,8},{10,9... | collective-permute-start | bytes 172040 | tf_op jit(solution)/shard_map/ppermute | solution.py:830
  22.5 5.8 %copy-start.5 = (s32[32,16]{0,1:T(8,128)S(1)}, s32[32,16]{0,1:T(8,128)}, u32[]{:S(2)}) copy-start(s32[32,16]{0,1:T(8,128)} %param.13) | copy-start | bytes 6148
  29.8 5.6 %collective-permute-start.7 = (f32[4,32]{1,0:T(4,128)S(1)}, f32[4,32]{1,0:T(4,128)S(1)}, u32[]{:S(2)}, u32[]{:S(2)}) collective-permute-start(f32[4,32]{1,0:T(4,128)S(1)} %get-tuple-element.44), channel_id=1, source_target_pairs={{0,1},{1,2},{2,3},{3,0},{4,5},{5,6},{6,7},{7,4},{8,9},{9,10},{10,1... | collective-permute-start | bytes 1544 | tf_op jit(solution)/shard_map/ppermute | solution.py:882
  29.8 5.6 %collective-permute-start.8 = (f32[4,32]{1,0:T(4,128)S(1)}, f32[4,32]{1,0:T(4,128)S(1)}, u32[]{:S(2)}, u32[]{:S(2)}) collective-permute-start(f32[4,32]{1,0:T(4,128)S(1)} %get-tuple-element.45), channel_id=1, source_target_pairs={{0,2},{1,3},{2,0},{3,1},{4,6},{5,7},{6,4},{7,5},{8,10},{9,11},{10,... | collective-permute-start | bytes 1544 | tf_op jit(solution)/shard_map/ppermute | solution.py:882
  31.4 4.1 %collective-permute-start.9 = (f32[4,32]{1,0:T(4,128)S(1)}, f32[4,32]{1,0:T(4,128)S(1)}, u32[]{:S(2)}, u32[]{:S(2)}) collective-permute-start(f32[4,32]{1,0:T(4,128)S(1)} %get-tuple-element.46), channel_id=1, source_target_pairs={{0,3},{1,0},{2,1},{3,2},{4,7},{5,4},{6,5},{7,6},{8,11},{9,8},{10,9... | collective-permute-start | bytes 1544 | tf_op jit(solution)/shard_map/ppermute | solution.py:882

commit v5 on v4

--- a/solution.py
+++ b/solution.py
@@ -10,7 +10,6 @@
 STEPS = 2
 FIELDS = 7
 HALO = 8
-HIGHEST = lax.Precision.HIGHEST
 
 magnetic_step = 0.5
 electric_step = 0.5
@@ -40,6 +39,12 @@
 
 def swaps(size):
     return [odd for odd in (0, 1) if odd + 1 < size]
+
+
+def partner_of(index, shift, size):
+    if size & (size - 1) == 0:
+        return index ^ shift
+    return (index + shift) % size
 
 
 def sends_up(index, odd):
@@ -95,12 +100,8 @@
     xs, ys = swaps(sizes[0]), swaps(sizes[1])
     n_out = len(xs) + len(ys) + len(xs) * len(ys)
     outs, refs = refs[:n_out], refs[n_out:]
-    x_bufs, refs = refs[: 2 * len(xs)], refs[2 * len(xs) :]
-    y_bufs, sems = refs[: 2 * len(ys)], refs[2 * len(ys)]
-
-    def source(f):
-        return e_ref.at[f] if f < 3 else h_ref.at[f - 3] if f < 6 else m_ref
-
+    x_bufs, refs = refs[: 3 * len(xs)], refs[3 * len(xs) :]
+    y_bufs, (perm_s, sems) = refs[: 3 * len(ys)], refs[3 * len(ys) :]
     copies = []
 
     def start(src, dst):
@@ -111,19 +112,18 @@
     for i, odd in enumerate(ys):
         up = sends_up(gy, odd)
         t, r = jnp.where(up, tiles - 1, 0), jnp.where(up, 6, 0)
-        for f in range(FIELDS):
-            buf = y_bufs[2 * i].at[f] if f < 6 else y_bufs[2 * i + 1]
-            for z in range(lanes):
-                start(
-                    source(f).at[:, t, z, pl.ds(r, 2), :],
-                    buf.at[z].reshape(nx, 8, 128).at[:, pl.ds(0, 2), :],
-                )
+        for k, ref in enumerate((e_ref, h_ref, m_ref)):
+            src = ref.at[:, t, :, pl.ds(r, 2), :] if k == 2 else ref.at[:, :, t, :, pl.ds(r, 2), :]
+            dst = y_bufs[3 * i + k]
+            dst = dst.reshape(*dst.shape[:-2], nx, lanes, 8, 128)
+            start(src, dst.at[:, :, pl.ds(0, 2), :] if k == 2 else dst.at[:, :, :, pl.ds(0, 2), :])
     for i, odd in enumerate(xs):
-        first = jnp.where(sends_up(gx, odd), nx - 2, 0)
-        for f in range(FIELDS):
-            start(source(f).at[pl.ds(first, 2)], x_bufs[2 * i].at[f] if f < 6 else x_bufs[2 * i + 1])
-
-    table = coef_table(perm_ref)
+        first = pl.ds(jnp.where(sends_up(gx, odd), nx - 2, 0), 2)
+        for k, ref in enumerate((e_ref, h_ref, m_ref)):
+            start(ref.at[first] if k == 2 else ref.at[:, first], x_bufs[3 * i + k])
+    start(perm_ref, perm_s)
+    copies.pop().wait()
+    table = coef_table(perm_s)
     lane = lax.broadcasted_iota(jnp.int32, (8, 128), 1)
     lane_n = lax.broadcasted_iota(jnp.int32, (nx, 128), 1)
 
@@ -139,96 +139,128 @@
         row = lax.broadcasted_iota(jnp.int32, v.shape, 0)
         return jnp.where(row < rows - 1, pltpu.roll(v, rows - 1, 0), 0.0)
 
-    done = 0
+    step = lanes * 8
     for i, odd in enumerate(ys):
-        for copy in copies[done : done + FIELDS * lanes]:
+        for copy in copies[3 * i : 3 * i + 3]:
             copy.wait()
-        done += FIELDS * lanes
         up = sends_up(gy, odd)
         near, far = jnp.where(up, 1, 0), jnp.where(up, 0, 1)
         down = jnp.where(up, 0.0, magnetic_step)
-        buf, mat, out = y_bufs[2 * i], y_bufs[2 * i + 1], outs[len(xs) + i]
-
-        def at(f, which):
-            return [buf[f, z, pl.ds(which, nx, stride=8), :] for z in range(lanes)]
-
-        ex_f, ey_f, ez_f = (at(f, far) for f in range(3))
-        hx_f, hz_f = at(3, far), at(5, far)
-        hx_n, hz_n = at(3, near), at(5, near)
+        e_b, h_b, m_b = y_bufs[3 * i : 3 * i + 3]
+        out = outs[len(xs) + i]
+
+        def at(ref, c, which):
+            return [ref[c, pl.ds(z * 8 + which, nx, stride=step), :] for z in range(lanes)]
+
+        e_n = [at(e_b, c, near) for c in range(3)]
+        h_n = [at(h_b, c, near) for c in range(3)]
+        ex_f, ey_f, ez_f = (at(e_b, c, far) for c in range(3))
+        hx_f, hz_f = at(h_b, 0, far), at(h_b, 2, far)
         ey_z = z_up(ey_f, lane_n)
         for z in range(lanes):
-            for f in range(3):
-                out[f * lanes + z] = buf[f, z, pl.ds(near, nx, stride=8), :]
-            out[3 * lanes + z] = hx_n[z] - down * ez_f[z]
-            out[4 * lanes + z] = buf[4, z, pl.ds(near, nx, stride=8), :]
-            out[5 * lanes + z] = hz_n[z] + down * ex_f[z]
-            out[6 * lanes + z] = coef_of(mat[z, pl.ds(near, nx, stride=8), :], table)
+            for c in range(3):
+                out[c * lanes + z] = e_n[c][z]
+            out[3 * lanes + z] = h_n[0][z] - down * ez_f[z]
+            out[4 * lanes + z] = h_n[1][z]
+            out[5 * lanes + z] = h_n[2][z] + down * ex_f[z]
+            out[6 * lanes + z] = coef_of(m_b[pl.ds(z * 8 + near, nx, stride=step), :], table)
             out[7 * lanes + z] = hx_f[z] + magnetic_step * (ez_f[z] + (ey_z[z] - ey_f[z]))
             out[8 * lanes + z] = hz_f[z] - magnetic_step * ((row_up(ey_f[z]) - ey_f[z]) + ex_f[z])
         out[9 * lanes] = ey_f[0]
     for i, odd in enumerate(xs):
-        for copy in copies[done : done + FIELDS]:
+        for copy in copies[3 * (len(ys) + i) : 3 * (len(ys) + i) + 3]:
             copy.wait()
-        done += FIELDS
         up = sends_up(gx, odd)
         near, far = jnp.where(up, 1, 0), jnp.where(up, 0, 1)
         down = jnp.where(up, 0.0, magnetic_step)
-        buf, mat, out = x_bufs[2 * i], x_bufs[2 * i + 1], outs[i]
+        e_b, h_b, m_b = x_bufs[3 * i : 3 * i + 3]
+        out = outs[i]
 
         def put(k, t, z, v):
             out[pl.ds(k * plane + (t * lanes + z) * 8, 8), :] = v
 
         ex_y = [
-            row_up(jnp.concatenate([buf[0, far, t, z] for t in range(tiles)], axis=0))
+            row_up(jnp.concatenate([e_b[0, far, t, z] for t in range(tiles)], axis=0))
             for z in range(lanes)
         ]
         for t in range(tiles):
-            ex_z = z_up([buf[0, far, t, z] for z in range(lanes)], lane)
+            ex_z = z_up([e_b[0, far, t, z] for z in range(lanes)], lane)
             for z in range(lanes):
-                ex_f, ey_f, ez_f = (buf[f, far, t, z] for f in range(3))
-                for f in range(4):
-                    put(f, t, z, buf[f, near, t, z])
-                put(4, t, z, buf[4, near, t, z] + down * ez_f)
-                put(5, t, z, buf[5, near, t, z] - down * ey_f)
-                put(6, t, z, coef_of(mat[near, t, z], table))
-                put(7, t, z, buf[4, far, t, z] - magnetic_step * ((ex_z[z] - ex_f) + ez_f))
+                ex_f, ey_f, ez_f = (e_b[c, far, t, z] for c in range(3))
+                for c in range(3):
+                    put(c, t, z, e_b[c, near, t, z])
+                put(3, t, z, h_b[0, near, t, z])
+                put(4, t, z, h_b[1, near, t, z] + down * ez_f)
+                put(5, t, z, h_b[2, near, t, z] - down * ey_f)
+                put(6, t, z, coef_of(m_b[near, t, z], table))
+                put(7, t, z, h_b[1, far, t, z] - magnetic_step * ((ex_z[z] - ex_f) + ez_f))
                 ex_up = ex_y[z][t * 8 : t * 8 + 8]
-                put(8, t, z, buf[5, far, t, z] + magnetic_step * (ey_f + (ex_up - ex_f)))
-            out[pl.ds(9 * plane + t * 8, 8), :] = buf[0, far, t, 0]
+                put(8, t, z, h_b[2, far, t, z] + magnetic_step * (ey_f + (ex_up - ex_f)))
+            out[pl.ds(9 * plane + t * 8, 8), :] = e_b[0, far, t, 0]
         for j, odd_y in enumerate(ys):
-            up_y = sends_up(gy, odd_y)
-            t = jnp.where(up_y, tiles - 1, 0)
-            lines = (jnp.where(up_y, 7, 0), jnp.where(up_y, 6, 1))
+            up = sends_up(gy, odd_y)
+            t = jnp.where(up, tiles - 1, 0)
+            rows = (jnp.where(up, 7, 0), jnp.where(up, 6, 1))
             out = outs[len(xs) + len(ys) + i * len(ys) + j]
             for z in range(lanes):
                 for f in range(FIELDS):
                     for k in range(4):
-                        where = (near, far)[k // 2], t, z, pl.ds(lines[k % 2], 1)
+                        where = (near, far)[k // 2], t, z, pl.ds(rows[k % 2], 1)
                         if f < 6:
-                            line = buf[(f, *where)]
+                            line = (e_b, h_b)[f // 3][(f % 3, *where)]
                         else:
-                            line = coef_of(mat[where], table)
+                            line = coef_of(m_b[where], table)
                         out[z, pl.ds(4 * f + k, 1), :] = line
 
 
-def turn_ends(parts, lane, count):
+def turn_ends(parts, lane, first_field, after_field):
     out = None
-    for k in range(count):
+    for k in range(first_field, after_field):
         first, last = parts(k)
         turned = pltpu.roll(jnp.where(lane < 64, first, last), 8 * k + 4, 1)
         out = turned if out is None else jnp.where(lane >= 8 * k, turned, out)
     return out
 
 
-def own_ends(dims, e_v, h_v, m_v, snap_ref, perm_ref, coef_v, packed):
+def own_ends(dims, e_v, h_v, m_v, snap_hbm, perm_ref, coef_v, packed, snap_ref, sems):
     nx, ny, nz = dims
     lanes = nz // 128
     step = ny + HALO
+    copies = []
+    for t in range(STEPS + 1):
+        for c in range(3):
+            copy = pltpu.make_async_copy(snap_hbm.at[t, c], snap_ref.at[t, c], sems.at[3 * t + c])
+            copy.start()
+            copies.append(copy)
     table = coef_table(perm_ref)
     lane = lax.broadcasted_iota(jnp.int32, (8, 128), 1)
     tiles = ny // 8
 
-    def one(x, carry):
+    def fields(x, carry):
+        for t in range(tiles):
+            here = [
+                pl.ds(pl.multiple_of(((x * tiles + t) * lanes + z) * 8, 8), 8) for z in range(lanes)
+            ]
+            for z in range(lanes):
+                coef_v[here[z], :] = coef_of(m_v[here[z], :], table)
+
+            def parts(k):
+                if k < 3:
+                    return e_v[k, here[0], :], e_v[k, here[-1], :]
+                if k < 6:
+                    return h_v[k - 3, here[0], :], h_v[k - 3, here[-1], :]
+                return coef_v[here[0], :], coef_v[here[-1], :]
+
+            row = pl.multiple_of((x + 2) * step + HALO + t * 8, 8)
+            packed[pl.ds(row, 8), :] = turn_ends(parts, lane, 0, FIELDS)
+        return carry
+
+    lax.fori_loop(0, nx, fields, 0, unroll=4)
+
+    for copy in copies:
+        copy.wait()
+
+    def changes(x, carry):
         index = pl.ds(pl.multiple_of(x * ny, ny), ny)
         change = []
         for c in range(3):
@@ -241,27 +273,17 @@
             ]
             change.append([[s[t][z] - s[t + 1][z] for z in range(2)] for t in range(STEPS)])
         for t in range(tiles):
-            here = [
-                pl.ds(pl.multiple_of(((x * tiles + t) * lanes + z) * 8, 8), 8) for z in range(lanes)
-            ]
-            for z in range(lanes):
-                coef_v[here[z], :] = coef_of(m_v[here[z], :], table)
 
             def parts(k):
-                if k < 3:
-                    return e_v[k, here[0], :], e_v[k, here[-1], :]
-                if k < 6:
-                    return h_v[k - 3, here[0], :], h_v[k - 3, here[-1], :]
-                if k == 6:
-                    return coef_v[here[0], :], coef_v[here[-1], :]
                 pair = change[(k - FIELDS) % 3][1 - (k - FIELDS) // 3]
                 return tuple(v[t * 8 : t * 8 + 8] for v in pair)
 
-            row = pl.multiple_of((x + 2) * step + HALO + t * 8, 8)
-            packed[pl.ds(row, 8), :] = turn_ends(parts, lane, FIELDS + 6)
+            here = pl.ds(pl.multiple_of((x + 2) * step + HALO + t * 8, 8), 8)
+            after = turn_ends(parts, lane, FIELDS, FIELDS + 6)
+            packed[here, :] = jnp.where(lane < 8 * FIELDS, packed[here, :], after)
         return carry
 
-    lax.fori_loop(0, nx, one, 0, unroll=2)
+    lax.fori_loop(0, nx, changes, 0, unroll=4)
 
 
 def unpack_faces(dims, sizes, own_packed, *refs):
@@ -344,7 +366,7 @@
             return jnp.where(upper, yh[f, z, before, :], yh[f, z, here, :])
 
         packed[pl.ds(p * step if isinstance(p, int) else pl.multiple_of(p * step, 8), HALO), :] = (
-            turn_ends(lambda f: (tile(f, 0), tile(f, lanes - 1)), lane, FIELDS + 1)
+            turn_ends(lambda f: (tile(f, 0), tile(f, lanes - 1)), lane, 0, FIELDS + 1)
         )
 
     def one(p, carry):
@@ -368,7 +390,7 @@
                     return x_raw[index, :], x_raw[index, :]
                 return xh[f, 0, index, :], xh[f, lanes - 1, index, :]
 
-            packed[pl.ds(p * step + HALO + t * 8, 8), :] = turn_ends(parts, lane, FIELDS + 1)
+            packed[pl.ds(p * step + HALO + t * 8, 8), :] = turn_ends(parts, lane, 0, FIELDS + 1)
     for x in range(nx):
         index = pl.ds((x + 2) * step + HALO, ny)
         packed[index, :] = own_packed[index, :]
@@ -396,16 +418,30 @@
         down_ref[row : row + 1, :] = jnp.zeros((1, padded), jnp.float32)
 
 
-def columns_of(line, nx, ny, step, first, skip):
-    size = line.shape[1]
-    at = lax.broadcasted_iota(jnp.int32, (ny, size), 1) - first
-    y = lax.broadcasted_iota(jnp.int32, (ny, size), 0)
-    ok = (at >= 0) & (at < nx * step) & (lax.rem(at + skip, step) == y)
-    spread = jnp.where(ok, line, 0.0)
-    at = lax.broadcasted_iota(jnp.int32, (size, nx), 0) - first
-    x = lax.broadcasted_iota(jnp.int32, (size, nx), 1)
-    pick = ((at >= x * step) & (at < (x + 1) * step)).astype(jnp.float32)
-    return lax.dot_general(spread, pick, (((1,), (0,)), ((), ())), precision=HIGHEST)
+def columns_of(lines, nx, ny):
+    spread, pick = [], []
+    for line, step, first in lines:
+        size = line.shape[1]
+        at = lax.broadcasted_iota(jnp.int32, (ny, size), 1) - first
+        y = lax.broadcasted_iota(jnp.int32, (ny, size), 0)
+        ok = (at >= 0) & (at < nx * step) & (lax.rem(at, step) == y)
+        spread.append(jnp.where(ok, line, 0.0))
+        at = lax.broadcasted_iota(jnp.int32, (nx, size), 1) - first
+        x = lax.broadcasted_iota(jnp.int32, (nx, size), 0) * step
+        pick.append(jnp.where((at >= x) & (at < x + step), 1.0, 0.0))
+    left = jnp.concatenate(spread, axis=1)
+    thirds = []
+    for _ in range(3):
+        part = left.astype(jnp.bfloat16)
+        left = left - part.astype(jnp.float32)
+        thirds.append(part)
+    out = lax.dot_general(
+        jnp.concatenate(thirds, axis=0),
+        jnp.concatenate(pick, axis=1).astype(jnp.bfloat16),
+        (((1,), (1,)), ((), ())),
+        preferred_element_type=jnp.float32,
+    )
+    return out[0:ny] + (out[ny : 2 * ny] + out[2 * ny : 3 * ny])
 
 
 def find_ports(dims, sizes, ports_ref):
@@ -428,7 +464,7 @@
     lanes = nz // 128
     tiles = ny // 8
     step = ny + HALO
-    e_s, h_s, column_ref, e1, h1, h2, half_ref, struck, clean, sums = refs
+    e_s, h_s, line_ref, e1, h1, h2, half_ref, struck, clean, sums = refs
     gx, gy = lax.axis_index("gx"), lax.axis_index("gy")
     row = lax.broadcasted_iota(jnp.int32, (step, nz), 0)
     lane = lax.broadcasted_iota(jnp.int32, (step, nz), 1)
@@ -603,16 +639,16 @@
 
     for p in range(6):
         one(p)
-    lax.fori_loop(6, nx + 1, body, 0)
+    lax.fori_loop(6, nx + 1, body, 0, unroll=3)
     for p in range(nx + 1, nx + 6):
         one(p)
-    nt = (((1,), (1,)), ((), ()))
-    line = lax.dot_general(jnp.ones((8, 128), jnp.float32), sums[...], nt, precision=HIGHEST)
-    column_ref[...] = columns_of(line[0:1, :], nx, ny, ny, 0, 0)
+    for b in range(nx * ny // 128):
+        here = pl.ds(b * 128, 128)
+        line_ref[:, here] = jnp.sum(jnp.transpose(sums[here, :]), axis=0, keepdims=True)
 
 
 def finish_ends(
-    dims, sizes, own_t, low_ref, high_ref, column_ref, mask_ref, ports_ref, amps_ref, *refs
+    dims, sizes, own_t, low_ref, high_ref, line_ref, mask_ref, ports_ref, amps_ref, *refs
 ):
     nx, ny, nz = dims
     step = ny + HALO
@@ -687,11 +723,11 @@
     for c in range(6):
         rows_ref[8 * c : 8 * c + 8, :] = jnp.where(row < 4, results[1][c], results[0][c])
     line = jnp.sum(total, axis=0, keepdims=True)
-    column = column_ref[...] + columns_of(line, nx, ny, step, 2 * step + HALO, 0)
+    column = columns_of([(line_ref[...], ny, 0), (line, step, 2 * step + HALO)], nx, ny)
     turned[...] = column * mask_ref[...].astype(jnp.float32)
     width = ny // parts
     for shift in range(parts):
-        owner = lax.rem(gz + shift, parts)
+        owner = partner_of(gz, shift, parts)
         grads[shift][...] = turned[pl.ds(owner * width, width), :]
     ends_ref[...] = rows_ref[...]
 
@@ -727,7 +763,7 @@
     chunk = nx // 4
     copies = []
     for c in range(4):
-        lax.fori_loop(c * chunk, (c + 1) * chunk, one, 0, unroll=2)
+        lax.fori_loop(c * chunk, (c + 1) * chunk, one, 0, unroll=4)
         here = pl.ds(c * chunk * plane, chunk * plane)
         for k, (src, dst) in enumerate(((e_v, e_out), (h_v, h_out))):
             copy = pltpu.make_async_copy(src.at[:, here], dst.at[:, here], sems.at[2 * c + k])
@@ -761,16 +797,19 @@
     shapes += [block((lanes, 4 * FIELDS, 128), f32) for _ in xs for _ in ys]
     buffers = []
     for _ in xs:
-        buffers += [cube((6, 2, tiles, lanes, 8, 128), f32), cube((2, tiles, lanes, 8, 128), i32)]
+        tile = (2, tiles, lanes, 8, 128)
+        buffers += [cube((3, *tile), f32), cube((3, *tile), f32), cube(tile, i32)]
     for _ in ys:
-        buffers += [cube((6, lanes, nx * 8, 128), f32), cube((lanes, nx * 8, 128), i32)]
-    n_copies = FIELDS * (len(xs) + lanes * len(ys))
+        tile = (nx * lanes * 8, 128)
+        buffers += [cube((3, *tile), f32), cube((3, *tile), f32), cube(tile, i32)]
+    n_copies = 3 * (len(xs) + len(ys)) + 1
     msgs = pl.pallas_call(
         functools.partial(send_faces, dims, sizes),
         out_shape=shapes,
-        in_specs=[HBM, HBM, HBM, SM],
+        in_specs=[HBM, HBM, HBM, HBM],
         out_specs=[VM] * len(shapes),
-        scratch_shapes=buffers + [pltpu.SemaphoreType.DMA((n_copies,))],
+        scratch_shapes=buffers
+        + [pltpu.SMEM(permittivity.shape, f32), pltpu.SemaphoreType.DMA((n_copies,))],
         compiler_params=params(),
         name="send_faces",
     )(
@@ -780,16 +819,17 @@
         permittivity,
     )
     e_v, h_v, m_v = in_vmem(tiled(e_adjoint)), in_vmem(tiled(h_adjoint)), in_vmem(tiled(material))
-    s = in_vmem(snapshots.reshape(STEPS + 1, 3, cells, nz))
-    coef_v, own_packed = pl.pallas_call(
+    snaps = in_hbm(snapshots.reshape(STEPS + 1, 3, cells, nz))
+    coef_v, own_packed, s = pl.pallas_call(
         functools.partial(own_ends, dims),
-        out_shape=[cube(m_v.shape, f32), cube((padded, 128), f32)],
-        in_specs=[VM, VM, VM, VM, SM],
-        out_specs=[VM] * 2,
+        out_shape=[cube(m_v.shape, f32), cube((padded, 128), f32), cube(snaps.shape, snaps.dtype)],
+        in_specs=[VM, VM, VM, HBM, SM],
+        out_specs=[VM] * 3,
+        scratch_shapes=[pltpu.SemaphoreType.DMA((3 * (STEPS + 1),))],
         compiler_params=params(),
         cost_estimate=pl.CostEstimate(flops=10**7, bytes_accessed=4 * 10**6, transcendentals=0),
         name="own_ends",
-    )(e_v, h_v, m_v, s, permittivity)
+    )(e_v, h_v, m_v, snaps, permittivity)
 
     both = ("gx", "gy")
     tables = [("gx", list(enumerate(swap_table(sizes[0], o)))) for o in xs]
@@ -830,9 +870,9 @@
     high = lax.ppermute(down, "gz", [(i, (i - 1) % parts) for i in range(parts)])
 
     ported = ports.shape[0]
-    e_s, h_s, column = pl.pallas_call(
+    e_s, h_s, line = pl.pallas_call(
         functools.partial(march, dims, sizes),
-        out_shape=[cube(e_v.shape, f32), cube(h_v.shape, f32), cube((ny, nx), f32)],
+        out_shape=[cube(e_v.shape, f32), cube(h_v.shape, f32), block((1, cells), f32)],
         in_specs=[VM] * 6 + [SM, SM],
         out_specs=[VM] * 3,
         scratch_shapes=[
@@ -860,7 +900,7 @@
         ],
         compiler_params=params(),
         name="finish_ends",
-    )(own_t, low, high, column, design_mask.T, ports, amplitudes)
+    )(own_t, low, high, line, design_mask.T, ports, amplitudes)
     e_out, h_out = pl.pallas_call(
         functools.partial(write_out, dims),
         out_shape=[block(e_v.shape, f32), block(h_v.shape, f32)],
@@ -880,7 +920,7 @@
     gradient = chunks[0]
     for shift in range(1, parts):
         gradient = gradient + lax.ppermute(
-            chunks[shift], "gz", [(i, (i + shift) % parts) for i in range(parts)]
+            chunks[shift], "gz", [(i, partner_of(i, shift, parts)) for i in range(parts)]
         )
     return untiled(e_out, dims), untiled(h_out, dims), gradient.T
 

time: 36.3 us -> 32.3 us (0.89)
  the two profiles are of different devices: /device:TPU:0 before, /device:TPU:17 now
where the time goes in v5:
time: 32.3 us; the launch traced here: 31.8 us
  Pallas kernels  15.4 us (48%)
  starting transfers between devices  11.6 us (36%)
  waiting for transfers between devices  3.41 us (11%)
  between operations  0.77 us (2%)
  other arithmetic  0.58 us (2%)
    ppermute x5, starting transfers between devices, body(): lax.ppermute(msg, axis, pairs)  5.97 us
    pallas_call x1, Pallas kernels, body(): pl.pallas_call(functools.partial(march, dims, sizes), out_shape=[cube(e_v...  5.23 us
    pallas_call x1, Pallas kernels, body(): pl.pallas_call(functools.partial(own_ends, dims), out_shape=[cube(m_v.sha...  3.44 us
    ppermute x1, starting transfers between devices, body(): low = lax.ppermute(up, 'gz', [(i, (i + 1) % parts) for i in range(parts)])  3.31 us
    ppermute x5, waiting for transfers between devices, body(): lax.ppermute(msg, axis, pairs)  3.06 us
    ppermute x3, starting transfers between devices, body(): lax.ppermute(chunks[shift], 'gz', [(i, partner_of(i, shift, parts)) for i...  2.34 us
    pallas_call x1, Pallas kernels, body(): pl.pallas_call(functools.partial(write_out, dims), out_shape=[block(e_v.s...  2.16 us
    pallas_call x1, Pallas kernels, body(): pl.pallas_call(functools.partial(send_faces, dims, sizes), out_shape=shap...  1.79 us
  transfers between devices with their start and end apart: 10, of which 3 were waited for; matrix products, arithmetic and copies ran while one was open for 0% of the time, Pallas kernels for 34%

profile of v5, /device:TPU:17, one launch (start us, length us, event | category | flops | bytes accessed | tf_op | source)
XLA Modules:
  0.0 31.8 jit_solution(1360392241506654794)
XLA Ops:
  0.6 0.0 copy-start
  0.6 0.0 copy-start.1
  0.7 0.0 copy-start.2
  0.7 1.8 %send_faces.1 = (f32[304,128]{1,0:T(8,128)S(1)}, f32[19,32,128]{2,1,0:T(8,128)S(1)}, f32[19,32,128]{2,1,0:T(8,128)S(1)}, f32[2,28,128]{2,1,0:T(8,128)S(1)}, f32[2,28,128]{2,1,0:T(8,128)S(1)}) custom-call(f32[3,32,2,2,8,128]{5,4,3,2,1,0:T(8,128)} %bitcast.29, f32[3,32,2,2,8,128]{5,4,3,2,1,0:T(8,128)} %bitcast.32, s32[32,2,2,8,128]{4,3,2,1,0:T(8,128)} %bitcast.35, ...), custom_call_target="tpu_custom_call" | custom-call | tf_op jit(solution)/shard_map/send_faces/pallas_call | solution.py:806
  2.5 1.4 %collective-permute-start.1 = (f32[19,32,128]{2,1,0:T(8,128)S(1)}, f32[19,32,128]{2,1,0:T(8,128)S(1)}, u32[]{:S(2)}, u32[]{:S(2)}) collective-permute-start(f32[19,32,128]{2,1,0:T(8,128)S(1)} %get-tuple-element.29), channel_id=1, source_target_pairs={{0,4},{4,0},{8,12},{12,8},{1,5},{5,1},{9,13},{13,9},{2,6},{6,2},{1... | collective-permute-start | bytes 933896 | tf_op jit(solution)/shard_map/ppermute | solution.py:846
  3.8 1.9 %collective-permute-start.2 = (f32[19,32,128]{2,1,0:T(8,128)S(1)}, f32[19,32,128]{2,1,0:T(8,128)S(1)}, u32[]{:S(2)}, u32[]{:S(2)}) collective-permute-start(f32[19,32,128]{2,1,0:T(8,128)S(1)} %get-tuple-element.30), channel_id=1, source_target_pairs={{0,0},{4,8},{8,4},{12,12},{1,1},{5,9},{9,5},{13,13},{2,2},{6,10},{... | collective-permute-start | bytes 933896 | tf_op jit(solution)/shard_map/ppermute | solution.py:846
  5.7 1.3 %collective-permute-start = (f32[304,128]{1,0:T(8,128)S(1)}, f32[304,128]{1,0:T(8,128)S(1)}, u32[]{:S(2)}, u32[]{:S(2)}) collective-permute-start(f32[304,128]{1,0:T(8,128)S(1)} %get-tuple-element.28), channel_id=1, source_target_pairs={{0,16},{16,0},{1,17},{17,1},{2,18},{18,2},{3,19},{19,3},{4,20},{20... | collective-permute-start | bytes 466952 | tf_op jit(solution)/shard_map/ppermute | solution.py:846
  7.0 0.0 collective-permute-start.3
  7.0 1.4 %collective-permute-start.4 = (f32[2,28,128]{2,1,0:T(8,128)S(1)}, f32[2,28,128]{2,1,0:T(8,128)S(1)}, u32[]{:S(2)}, u32[]{:S(2)}) collective-permute-start(f32[2,28,128]{2,1,0:T(8,128)S(1)} %get-tuple-element.32), channel_id=1, source_target_pairs={{0,16},{4,24},{8,20},{12,28},{16,0},{20,8},{24,4},{28,12},{1,17},{... | collective-permute-start | bytes 86024 | tf_op jit(solution)/shard_map/ppermute | solution.py:846
  8.4 0.0 copy-done
  8.4 0.0 copy-done.1
  8.4 0.0 copy-done.2
  8.5 0.0 copy-start.4
  8.5 0.0 copy-start.5
  8.5 3.4 %own_ends.1 = (f32[1024,128]{1,0:T(8,128)S(1)}, f32[896,128]{1,0:T(8,128)S(1)}, bf16[3,3,512,256]{3,2,1,0:T(8,128)(2,1)S(1)}) custom-call(f32[3,1024,128]{2,1,0:T(8,128)S(1)} %bitcast.30, f32[3,1024,128]{2,1,0:T(8,128)S(1)} %bitcast.33, s32[1024,128]{1,0:T(8,128)S(1)} %bitcast.36, bf16[3,3,512,256]{3,2,1,0:T(8,128)(2,1)} %bitcast.38, f32[8]{0:T(128)} %perm_ref.3), custom_call_target="tpu_custom_call" | custom-call | flops 10000000 | bytes 4000000 | tf_op jit(solution)/shard_map/own_ends/pallas_call | solution.py:823
  11.9 0.2 collective-permute-done.3.refs_3_
  12.1 2.9 %collective-permute-done.4.refs_4_ = f32[2,28,128]{2,1,0:T(8,128)S(1)} collective-permute-done((f32[2,28,128]{2,1,0:T(8,128)S(1)}, f32[2,28,128]{2,1,0:T(8,128)S(1)}, u32[]{:S(2)}, u32[]{:S(2)}) %collective-permute-start.4) | collective-permute-done | bytes 28704 | tf_op jit(solution)/shard_map/ppermute | solution.py:846
  15.0 0.0 collective-permute-done.refs_0_
  15.0 0.0 collective-permute-done.1.refs_1_
  15.0 0.0 collective-permute-done.2.refs_2_
  15.0 1.5 %unpack_faces.1 = (f32[7,2,64,128]{3,2,1,0:T(8,128)S(1)}, f32[7,2,288,128]{3,2,1,0:T(8,128)S(1)}, f32[128,896]{1,0:T(8,128)S(1)}, f32[16,896]{1,0:T(8,128)S(1)}, f32[16,896]{1,0:T(8,128)S(1)}) custom-call(f32[896,128]{1,0:T(8,128)S(1)} %get-tuple-element.27.own_packed, f32[304,128]{1,0:T(8,128)S(1)} %collective-permute-done.refs_0_, ...), custom_call_target="tpu_custom_call" | custom-call | tf_op jit(solution)/shard_map/unpack_faces/pallas_call | solution.py:848
  16.5 3.3 %collective-permute-start.5 = (f32[16,896]{1,0:T(8,128)S(1)}, f32[16,896]{1,0:T(8,128)S(1)}, u32[]{:S(2)}, u32[]{:S(2)}) collective-permute-start(f32[16,896]{1,0:T(8,128)S(1)} %get-tuple-element.39), channel_id=1, source_target_pairs={{0,1},{1,2},{2,3},{3,0},{4,5},{5,6},{6,7},{7,4},{8,9},{9,10},{10,1... | collective-permute-start | bytes 172040 | tf_op jit(solution)/shard_map/ppermute | solution.py:869
  19.8 0.0 collective-permute-start.6
  19.8 0.0 copy-done.4
  19.8 0.0 copy-done.5
  19.8 0.0 copy-start.3
  19.8 5.2 %march.1 = (f32[3,1024,128]{2,1,0:T(8,128)S(1)}, f32[3,1024,128]{2,1,0:T(8,128)S(1)}, f32[1,512]{1,0:T(1,128)S(1)}) custom-call(f32[3,1024,128]{2,1,0:T(8,128)S(1)} %bitcast.31, f32[3,1024,128]{2,1,0:T(8,128)S(1)} %bitcast.34, f32[1024,128]{1,0:T(8,128)S(1)} %get-tuple-element.26.coef_v, f32[7,2,64,128]{3,2,1,0:T(8,128)S(1)} %get-tuple-element.33.xh, ...), custom_call_target="tpu_custom_call" | custom-call | flops 40000000 | bytes 10000000 | tf_op jit(solution)/shard_map/march/pallas_call | solution.py:873
  25.1 0.0 collective-permute-done.5.low_ref
  25.1 0.0 collective-permute-done.6.high_ref
  25.1 0.0 copy-done.3
  25.1 1.2 %finish_ends.1 = (f32[48,896]{1,0:T(8,128)S(1)}, f32[4,32]{1,0:T(4,128)S(1)}, f32[4,32]{1,0:T(4,128)S(1)}, f32[4,32]{1,0:T(4,128)S(1)}, f32[4,32]{1,0:T(4,128)S(1)}) custom-call(f32[128,896]{1,0:T(8,128)S(1)} %get-tuple-element.38.own_t, f32[16,896]{1,0:T(8,128)S(1)} %collective-permute-done.5.low_ref, f32[16,896]{1,0:T(8,128)S(1)} %collective-permute-done.6.high_ref, ...), custom_call_target="tpu_custom_call" | custom-call | tf_op jit(solution)/shard_map/finish_ends/pallas_call | solution.py:891
  26.3 0.6 %collective-permute-start.7 = (f32[4,32]{1,0:T(4,128)S(1)}, f32[4,32]{1,0:T(4,128)S(1)}, u32[]{:S(2)}, u32[]{:S(2)}) collective-permute-start(f32[4,32]{1,0:T(4,128)S(1)} %get-tuple-element.46), channel_id=1, source_target_pairs={{0,1},{1,0},{2,3},{3,2},{4,5},{5,4},{6,7},{7,6},{8,9},{9,8},{10,11... | collective-permute-start | bytes 1544 | tf_op jit(solution)/shard_map/ppermute | solution.py:922
  27.0 1.2 %collective-permute-start.8 = (f32[4,32]{1,0:T(4,128)S(1)}, f32[4,32]{1,0:T(4,128)S(1)}, u32[]{:S(2)}, u32[]{:S(2)}) collective-permute-start(f32[4,32]{1,0:T(4,128)S(1)} %get-tuple-element.47), channel_id=1, source_target_pairs={{0,2},{1,3},{2,0},{3,1},{4,6},{5,7},{6,4},{7,5},{8,10},{9,11},{10,... | collective-permute-start | bytes 1544 | tf_op jit(solution)/shard_map/ppermute | solution.py:922
  28.2 0.5 %collective-permute-start.9 = (f32[4,32]{1,0:T(4,128)S(1)}, f32[4,32]{1,0:T(4,128)S(1)}, u32[]{:S(2)}, u32[]{:S(2)}) collective-permute-start(f32[4,32]{1,0:T(4,128)S(1)} %get-tuple-element.48), channel_id=1, source_target_pairs={{0,3},{1,2},{2,1},{3,0},{4,7},{5,6},{6,5},{7,4},{8,11},{9,10},{10,... | collective-permute-start | bytes 1544 | tf_op jit(solution)/shard_map/ppermute | solution.py:922
  28.7 2.2 %write_out.1 = (f32[3,1024,128]{2,1,0:T(8,128)}, f32[3,1024,128]{2,1,0:T(8,128)}) custom-call(f32[3,1024,128]{2,1,0:T(8,128)S(1)} %get-tuple-element.36.e_s, f32[3,1024,128]{2,1,0:T(8,128)S(1)} %get-tuple-element.37.h_s, f32[48,896]{1,0:T(8,128)S(1)} %get-tuple-element.42.ends_ref), custom_call_target="tpu_custom_call" | custom-call | flops 10000000 | bytes 8000000 | tf_op jit(solution)/shard_map/write_out/pallas_call | solution.py:904
  30.8 0.0 collective-permute-done.7
  30.9 0.0 collective-permute-done.8
  30.9 0.3 %collective-permute-done.9 = f32[4,32]{1,0:T(4,128)S(1)} collective-permute-done((f32[4,32]{1,0:T(4,128)S(1)}, f32[4,32]{1,0:T(4,128)S(1)}, u32[]{:S(2)}, u32[]{:S(2)}) %collective-permute-start.9) | collective-permute-done | bytes 544 | tf_op jit(solution)/shard_map/ppermute | solution.py:922
  31.2 0.6 %add_bitcast_fusion = f32[32,4]{0,1:T(4,128)} fusion(f32[4,32]{1,0:T(4,128)S(1)} %collective-permute-done.9, f32[4,32]{1,0:T(4,128)S(1)} %collective-permute-done.8, f32[4,32]{1,0:T(4,128)S(1)} %get-tuple-element.45, f32[4,32]{1,0:T(4,128)S(1)} %collective-permute-done.7), kind=kLoop, calls=%fused_computation | loop fusion | flops 384 | bytes 2560 | tf_op jit(solution)/shard_map/transpose | solution.py:925
Async XLA Ops:
  0.6 7.8 %copy-start = (f32[3,32,16,256]{3,2,1,0:T(8,128)S(1)}, f32[3,32,16,256]{3,2,1,0:T(8,128)}, u32[]{:S(2)}) copy-start(f32[3,32,16,256]{3,2,1,0:T(8,128)} %param.8) | copy-start | bytes 4718596
  0.6 7.8 %copy-start.1 = (f32[3,32,16,256]{3,2,1,0:T(8,128)S(1)}, f32[3,32,16,256]{3,2,1,0:T(8,128)}, u32[]{:S(2)}) copy-start(f32[3,32,16,256]{3,2,1,0:T(8,128)} %param.9) | copy-start | bytes 4718596
  0.7 7.8 %copy-start.2 = (s32[32,16,256]{2,1,0:T(8,128)S(1)}, s32[32,16,256]{2,1,0:T(8,128)}, u32[]{:S(2)}) copy-start(s32[32,16,256]{2,1,0:T(8,128)} %param.11) | copy-start | bytes 1572868
  2.5 12.5 %collective-permute-start.1 = (f32[19,32,128]{2,1,0:T(8,128)S(1)}, f32[19,32,128]{2,1,0:T(8,128)S(1)}, u32[]{:S(2)}, u32[]{:S(2)}) collective-permute-start(f32[19,32,128]{2,1,0:T(8,128)S(1)} %get-tuple-element.29), channel_id=1, source_target_pairs={{0,4},{4,0},{8,12},{12,8},{1,5},{5,1},{9,13},{13,9},{2,6},{6,2},{1... | collective-permute-start | bytes 933896 | tf_op jit(solution)/shard_map/ppermute | solution.py:846
  3.8 11.2 %collective-permute-start.2 = (f32[19,32,128]{2,1,0:T(8,128)S(1)}, f32[19,32,128]{2,1,0:T(8,128)S(1)}, u32[]{:S(2)}, u32[]{:S(2)}) collective-permute-start(f32[19,32,128]{2,1,0:T(8,128)S(1)} %get-tuple-element.30), channel_id=1, source_target_pairs={{0,0},{4,8},{8,4},{12,12},{1,1},{5,9},{9,5},{13,13},{2,2},{6,10},{... | collective-permute-start | bytes 933896 | tf_op jit(solution)/shard_map/ppermute | solution.py:846
  5.7 9.2 %collective-permute-start = (f32[304,128]{1,0:T(8,128)S(1)}, f32[304,128]{1,0:T(8,128)S(1)}, u32[]{:S(2)}, u32[]{:S(2)}) collective-permute-start(f32[304,128]{1,0:T(8,128)S(1)} %get-tuple-element.28), channel_id=1, source_target_pairs={{0,16},{16,0},{1,17},{17,1},{2,18},{18,2},{3,19},{19,3},{4,20},{20... | collective-permute-start | bytes 466952 | tf_op jit(solution)/shard_map/ppermute | solution.py:846
  7.0 5.1 %collective-permute-start.3 = (f32[2,28,128]{2,1,0:T(8,128)S(1)}, f32[2,28,128]{2,1,0:T(8,128)S(1)}, u32[]{:S(2)}, u32[]{:S(2)}) collective-permute-start(f32[2,28,128]{2,1,0:T(8,128)S(1)} %get-tuple-element.31), channel_id=1, source_target_pairs={{0,20},{4,16},{8,28},{12,24},{16,4},{20,0},{24,12},{28,8},{1,21},{... | collective-permute-start | bytes 86024 | tf_op jit(solution)/shard_map/ppermute | solution.py:846
  7.0 7.9 %collective-permute-start.4 = (f32[2,28,128]{2,1,0:T(8,128)S(1)}, f32[2,28,128]{2,1,0:T(8,128)S(1)}, u32[]{:S(2)}, u32[]{:S(2)}) collective-permute-start(f32[2,28,128]{2,1,0:T(8,128)S(1)} %get-tuple-element.32), channel_id=1, source_target_pairs={{0,16},{4,24},{8,20},{12,28},{16,0},{20,8},{24,4},{28,12},{1,17},{... | collective-permute-start | bytes 86024 | tf_op jit(solution)/shard_map/ppermute | solution.py:846
  8.5 11.4 %copy-start.4 = (f32[2,3]{1,0:T(2,128)S(1)}, f32[2,3]{1,0:T(2,128)}, u32[]{:S(2)}) copy-start(f32[2,3]{1,0:T(2,128)} %amps_ref.3) | copy-start | bytes 76
  8.5 11.4 %copy-start.5 = (s32[3]{0:T(128)S(1)}, s32[3]{0:T(128)}, u32[]{:S(2)}) copy-start(s32[3]{0:T(128)} %ports_ref.3) | copy-start | bytes 40
  16.5 8.6 %collective-permute-start.5 = (f32[16,896]{1,0:T(8,128)S(1)}, f32[16,896]{1,0:T(8,128)S(1)}, u32[]{:S(2)}, u32[]{:S(2)}) collective-permute-start(f32[16,896]{1,0:T(8,128)S(1)} %get-tuple-element.39), channel_id=1, source_target_pairs={{0,1},{1,2},{2,3},{3,0},{4,5},{5,6},{6,7},{7,4},{8,9},{9,10},{10,1... | collective-permute-start | bytes 172040 | tf_op jit(solution)/shard_map/ppermute | solution.py:869
  19.8 5.3 %collective-permute-start.6 = (f32[16,896]{1,0:T(8,128)S(1)}, f32[16,896]{1,0:T(8,128)S(1)}, u32[]{:S(2)}, u32[]{:S(2)}) collective-permute-start(f32[16,896]{1,0:T(8,128)S(1)} %get-tuple-element.40), channel_id=1, source_target_pairs={{0,3},{1,0},{2,1},{3,2},{4,7},{5,4},{6,5},{7,6},{8,11},{9,8},{10,9... | collective-permute-start | bytes 172040 | tf_op jit(solution)/shard_map/ppermute | solution.py:870
  19.8 5.3 %copy-start.3 = (s32[32,16]{0,1:T(8,128)S(1)}, s32[32,16]{0,1:T(8,128)}, u32[]{:S(2)}) copy-start(s32[32,16]{0,1:T(8,128)} %param.13) | copy-start | bytes 6148
  26.3 4.5 %collective-permute-start.7 = (f32[4,32]{1,0:T(4,128)S(1)}, f32[4,32]{1,0:T(4,128)S(1)}, u32[]{:S(2)}, u32[]{:S(2)}) collective-permute-start(f32[4,32]{1,0:T(4,128)S(1)} %get-tuple-element.46), channel_id=1, source_target_pairs={{0,1},{1,0},{2,3},{3,2},{4,5},{5,4},{6,7},{7,6},{8,9},{9,8},{10,11... | collective-permute-start | bytes 1544 | tf_op jit(solution)/shard_map/ppermute | solution.py:922
  27.0 3.9 %collective-permute-start.8 = (f32[4,32]{1,0:T(4,128)S(1)}, f32[4,32]{1,0:T(4,128)S(1)}, u32[]{:S(2)}, u32[]{:S(2)}) collective-permute-start(f32[4,32]{1,0:T(4,128)S(1)} %get-tuple-element.47), channel_id=1, source_target_pairs={{0,2},{1,3},{2,0},{3,1},{4,6},{5,7},{6,4},{7,5},{8,10},{9,11},{10,... | collective-permute-start | bytes 1544 | tf_op jit(solution)/shard_map/ppermute | solution.py:922
  28.2 3.0 %collective-permute-start.9 = (f32[4,32]{1,0:T(4,128)S(1)}, f32[4,32]{1,0:T(4,128)S(1)}, u32[]{:S(2)}, u32[]{:S(2)}) collective-permute-start(f32[4,32]{1,0:T(4,128)S(1)} %get-tuple-element.48), channel_id=1, source_target_pairs={{0,3},{1,2},{2,1},{3,0},{4,7},{5,6},{6,5},{7,4},{8,11},{9,10},{10,... | collective-permute-start | bytes 1544 | tf_op jit(solution)/shard_map/ppermute | solution.py:922

commit v6 on v5

--- a/solution.py
+++ b/solution.py
@@ -568,8 +568,9 @@
         e = [e1[f, p] for f in range(3)]
         h = [h1[f, p] for f in range(3)]
         out = new_h(half_of(p), *e, e1[1, p + 1], e1[2, p + 1], *h)
-        for f in range(3):
-            h2[f, p] = out[f]
+        h2[0, p] = out[0]
+        h2[1, p, 0:ny] = out[1][:ny]
+        h2[2, p] = out[2]
 
     def second_e(p):
         h = [h2[f, p] for f in range(3)]
@@ -592,29 +593,34 @@
             folded = folded + total[:, at : at + 128]
         sums[index, :] = folded
 
-    def strike(p):
-        dynamic = not isinstance(p, int)
-        first, second = p - 1, p - 4
+    group = 4
+    behind_e, behind_h, behind_last = group, 2 * group + 1, 3 * group + 1
+
+    def some(p, behind, least, most):
+        planes = [p - behind + i for i in range(group)]
+        return [q for q in planes if not isinstance(q, int) or least <= q <= most]
+
+    def strike(first, second):
         hit = None
         for at in planes_struck:
-            here = (at == first) | (at == second)
-            hit = here if hit is None else hit | here
+            for q in first + second:
+                hit = at == q if hit is None else hit | (at == q)
 
         @pl.when(hit)
         def _():
-            for q, at in enumerate(planes_struck):
-                if dynamic or 1 <= first <= nx + 2:
-                    amp = jnp.where(at == first, amps_ref[0, q], 0.0)
-                    e1[2, first] = e1[2, first] + struck[q] * amp
-                if dynamic or 2 <= second <= nx + 1:
-                    x = second - 2
-                    amp = jnp.where(at == second, amps_ref[1, q], 0.0)
+            for k, at in enumerate(planes_struck):
+                for p in first:
+                    amp = jnp.where(at == p, amps_ref[0, k], 0.0)
+                    e1[2, p] = e1[2, p] + struck[k] * amp
+                for p in second:
+                    x = p - 2
+                    amp = jnp.where(at == p, amps_ref[1, k], 0.0)
                     index = pl.ds(aligned(x * ny), ny)
                     s = [snap_ref[t, 2, index, :].astype(jnp.float32) for t in (1, 2)]
                     folded = jnp.zeros((ny, 128), jnp.float32)
                     for z in range(lanes):
                         here = slice(z * 128, z * 128 + 128)
-                        gain = struck[q, 0:ny, here] * amp
+                        gain = struck[k, 0:ny, here] * amp
                         folded = folded + gain * clean[1, :, here] * (s[0] - s[1])[:, here]
                         for t in range(tiles):
                             here = spot(x, t, z)
@@ -622,25 +628,29 @@
                     sums[index, :] = sums[index, :] + folded
 
     def one(p):
-        dynamic = not isinstance(p, int)
-        if dynamic or 2 <= p - 4 <= nx + 1:
-            second_e(p - 4)
-        if dynamic or 1 <= p - 3 <= nx + 1:
-            second_h(p - 3)
-        if dynamic or 1 <= p - 1 <= nx + 2:
-            first_e(p - 1)
-        if dynamic or 0 <= p <= nx + 2:
-            first_h(p)
-        strike(p)
-
-    def body(p, carry):
+        last = some(p, behind_last, 2, nx + 1)
+        first = some(p, behind_e, 1, nx + 2)
+        for q in last:
+            second_e(q)
+        for q in some(p, behind_h, 1, nx + 1):
+            second_h(q)
+        for q in first:
+            first_e(q)
+        for q in some(p, 0, 0, nx + 2):
+            first_h(q)
+        if first + last:
+            strike(first, last)
+
+    def body(k, carry):
+        one(start + k * group)
+        return carry
+
+    start = -(-(2 + behind_last) // group) * group
+    passes = (nx + 1 - group - start) // group + 1
+    for p in range(0, start, group):
         one(p)
-        return carry
-
-    for p in range(6):
-        one(p)
-    lax.fori_loop(6, nx + 1, body, 0, unroll=3)
-    for p in range(nx + 1, nx + 6):
+    lax.fori_loop(0, passes, body, 0)
+    for p in range(start + passes * group, nx + 2 + behind_last, group):
         one(p)
     for b in range(nx * ny // 128):
         here = pl.ds(b * 128, 128)
@@ -832,13 +842,19 @@
     )(e_v, h_v, m_v, snaps, permittivity)
 
     both = ("gx", "gy")
+
+    def meet(x, y, tx, ty):
+        if tx[x] == x or ty[y] == y:
+            return x * sizes[1] + y
+        return tx[x] * sizes[1] + ty[y]
+
     tables = [("gx", list(enumerate(swap_table(sizes[0], o)))) for o in xs]
     tables += [("gy", list(enumerate(swap_table(sizes[1], o)))) for o in ys]
     for ox in xs:
         for oy in ys:
             tx, ty = swap_table(sizes[0], ox), swap_table(sizes[1], oy)
             pairs = [
-                (x * sizes[1] + y, tx[x] * sizes[1] + ty[y])
+                (x * sizes[1] + y, meet(x, y, tx, ty))
                 for x in range(sizes[0])
                 for y in range(sizes[1])
             ]

time: 32.3 us -> 30.7 us (0.950); the launches traced: 31.8 us -> 30.6 us
  waiting for transfers between devices: 3.41 us -> 1.47 us
  starting transfers between devices: 11.6 us -> 13.5 us
  Pallas kernels: 15.4 us -> 14.2 us
    ppermute x5, waiting for transfers between devices: 3.06 us -> 1.12 us  [body(): lax.ppermute(msg, axis, pairs)]
    ppermute x5, starting transfers between devices: 5.97 us -> 7.87 us  [body(): lax.ppermute(msg, axis, pairs)]
    pallas_call x1, Pallas kernels: 5.23 us -> 4.03 us  [body(): pl.pallas_call(functools.partial(march, dims, sizes), out_shape=[cube(e_v...]
  transfers between devices with their start and end apart: 10 -> 10, of which waited for: 3 -> 2; matrix products, arithmetic and copies ran while one was open for 0% -> 0% of each run, Pallas kernels for 34% -> 31%
where the time goes in v6:
time: 30.7 us; the launch traced here: 30.6 us
  Pallas kernels  14.2 us (46%)
  starting transfers between devices  13.5 us (44%)
  waiting for transfers between devices  1.47 us (5%)
  between operations  0.81 us (3%)
  other arithmetic  0.58 us (2%)
    ppermute x5, starting transfers between devices, body(): lax.ppermute(msg, axis, pairs)  7.87 us
    pallas_call x1, Pallas kernels, body(): pl.pallas_call(functools.partial(march, dims, sizes), out_shape=[cube(e_v...  4.03 us
    pallas_call x1, Pallas kernels, body(): pl.pallas_call(functools.partial(own_ends, dims), out_shape=[cube(m_v.sha...  3.44 us
    ppermute x1, starting transfers between devices, body(): low = lax.ppermute(up, 'gz', [(i, (i + 1) % parts) for i in range(parts)])  3.31 us
    ppermute x3, starting transfers between devices, body(): lax.ppermute(chunks[shift], 'gz', [(i, partner_of(i, shift, parts)) for i...  2.34 us
    pallas_call x1, Pallas kernels, body(): pl.pallas_call(functools.partial(write_out, dims), out_shape=[block(e_v.s...  2.16 us
    pallas_call x1, Pallas kernels, body(): pl.pallas_call(functools.partial(send_faces, dims, sizes), out_shape=shap...  1.79 us
    pallas_call x1, Pallas kernels, body(): pl.pallas_call(functools.partial(unpack_faces, dims, sizes), out_shape=[c...  1.52 us
  transfers between devices with their start and end apart: 10, of which 2 were waited for; matrix products, arithmetic and copies ran while one was open for 0% of the time, Pallas kernels for 31%

profile of v6, /device:TPU:17, one launch (start us, length us, event | category | flops | bytes accessed | tf_op | source)
XLA Modules:
  0.0 30.6 jit_solution(5932667434996523016)
XLA Ops:
  0.6 0.0 copy-start
  0.6 0.0 copy-start.1
  0.7 0.0 copy-start.2
  0.7 1.8 %send_faces.1 = (f32[304,128]{1,0:T(8,128)S(1)}, f32[19,32,128]{2,1,0:T(8,128)S(1)}, f32[19,32,128]{2,1,0:T(8,128)S(1)}, f32[2,28,128]{2,1,0:T(8,128)S(1)}, f32[2,28,128]{2,1,0:T(8,128)S(1)}) custom-call(f32[3,32,2,2,8,128]{5,4,3,2,1,0:T(8,128)} %bitcast.29, f32[3,32,2,2,8,128]{5,4,3,2,1,0:T(8,128)} %bitcast.32, s32[32,2,2,8,128]{4,3,2,1,0:T(8,128)} %bitcast.35, ...), custom_call_target="tpu_custom_call" | custom-call | tf_op jit(solution)/shard_map/send_faces/pallas_call | solution.py:816
  2.5 1.4 %collective-permute-start.1 = (f32[19,32,128]{2,1,0:T(8,128)S(1)}, f32[19,32,128]{2,1,0:T(8,128)S(1)}, u32[]{:S(2)}, u32[]{:S(2)}) collective-permute-start(f32[19,32,128]{2,1,0:T(8,128)S(1)} %get-tuple-element.29), channel_id=1, source_target_pairs={{0,4},{4,0},{8,12},{12,8},{1,5},{5,1},{9,13},{13,9},{2,6},{6,2},{1... | collective-permute-start | bytes 933896 | tf_op jit(solution)/shard_map/ppermute | solution.py:862
  3.8 1.9 %collective-permute-start.2 = (f32[19,32,128]{2,1,0:T(8,128)S(1)}, f32[19,32,128]{2,1,0:T(8,128)S(1)}, u32[]{:S(2)}, u32[]{:S(2)}) collective-permute-start(f32[19,32,128]{2,1,0:T(8,128)S(1)} %get-tuple-element.30), channel_id=1, source_target_pairs={{0,0},{4,8},{8,4},{12,12},{1,1},{5,9},{9,5},{13,13},{2,2},{6,10},{... | collective-permute-start | bytes 933896 | tf_op jit(solution)/shard_map/ppermute | solution.py:862
  5.7 1.3 %collective-permute-start = (f32[304,128]{1,0:T(8,128)S(1)}, f32[304,128]{1,0:T(8,128)S(1)}, u32[]{:S(2)}, u32[]{:S(2)}) collective-permute-start(f32[304,128]{1,0:T(8,128)S(1)} %get-tuple-element.28), channel_id=1, source_target_pairs={{0,16},{16,0},{1,17},{17,1},{2,18},{18,2},{3,19},{19,3},{4,20},{20... | collective-permute-start | bytes 466952 | tf_op jit(solution)/shard_map/ppermute | solution.py:862
  7.0 0.0 collective-permute-start.3
  7.0 3.3 %collective-permute-start.4 = (f32[2,28,128]{2,1,0:T(8,128)S(1)}, f32[2,28,128]{2,1,0:T(8,128)S(1)}, u32[]{:S(2)}, u32[]{:S(2)}) collective-permute-start(f32[2,28,128]{2,1,0:T(8,128)S(1)} %get-tuple-element.32), channel_id=1, source_target_pairs={{0,0},{4,24},{8,20},{12,12},{16,16},{20,8},{24,4},{28,28},{1,1},{5... | collective-permute-start | bytes 86024 | tf_op jit(solution)/shard_map/ppermute | solution.py:862
  10.3 0.0 copy-done
  10.4 0.0 copy-done.1
  10.4 0.0 copy-done.2
  10.4 0.0 copy-start.4
  10.4 0.0 copy-start.5
  10.4 3.4 %own_ends.1 = (f32[1024,128]{1,0:T(8,128)S(1)}, f32[896,128]{1,0:T(8,128)S(1)}, bf16[3,3,512,256]{3,2,1,0:T(8,128)(2,1)S(1)}) custom-call(f32[3,1024,128]{2,1,0:T(8,128)S(1)} %bitcast.30, f32[3,1024,128]{2,1,0:T(8,128)S(1)} %bitcast.33, s32[1024,128]{1,0:T(8,128)S(1)} %bitcast.36, bf16[3,3,512,256]{3,2,1,0:T(8,128)(2,1)} %bitcast.38, f32[8]{0:T(128)} %perm_ref.3), custom_call_target="tpu_custom_call" | custom-call | flops 10000000 | bytes 4000000 | tf_op jit(solution)/shard_map/own_ends/pallas_call | solution.py:833
  13.9 0.0 collective-permute-done.3.refs_3_
  13.9 1.1 %collective-permute-done.4.refs_4_ = f32[2,28,128]{2,1,0:T(8,128)S(1)} collective-permute-done((f32[2,28,128]{2,1,0:T(8,128)S(1)}, f32[2,28,128]{2,1,0:T(8,128)S(1)}, u32[]{:S(2)}, u32[]{:S(2)}) %collective-permute-start.4) | collective-permute-done | bytes 28704 | tf_op jit(solution)/shard_map/ppermute | solution.py:862
  15.0 0.0 collective-permute-done.refs_0_
  15.0 0.0 collective-permute-done.1.refs_1_
  15.0 0.0 collective-permute-done.2.refs_2_
  15.0 1.5 %unpack_faces.1 = (f32[7,2,64,128]{3,2,1,0:T(8,128)S(1)}, f32[7,2,288,128]{3,2,1,0:T(8,128)S(1)}, f32[128,896]{1,0:T(8,128)S(1)}, f32[16,896]{1,0:T(8,128)S(1)}, f32[16,896]{1,0:T(8,128)S(1)}) custom-call(f32[896,128]{1,0:T(8,128)S(1)} %get-tuple-element.27.own_packed, f32[304,128]{1,0:T(8,128)S(1)} %collective-permute-done.refs_0_, ...), custom_call_target="tpu_custom_call" | custom-call | tf_op jit(solution)/shard_map/unpack_faces/pallas_call | solution.py:864
  16.5 3.3 %collective-permute-start.5 = (f32[16,896]{1,0:T(8,128)S(1)}, f32[16,896]{1,0:T(8,128)S(1)}, u32[]{:S(2)}, u32[]{:S(2)}) collective-permute-start(f32[16,896]{1,0:T(8,128)S(1)} %get-tuple-element.39), channel_id=1, source_target_pairs={{0,1},{1,2},{2,3},{3,0},{4,5},{5,6},{6,7},{7,4},{8,9},{9,10},{10,1... | collective-permute-start | bytes 172040 | tf_op jit(solution)/shard_map/ppermute | solution.py:885
  19.8 0.0 collective-permute-start.6
  19.8 0.0 copy-done.4
  19.8 0.0 copy-done.5
  19.8 0.0 copy-start.3
  19.8 4.0 %march.1 = (f32[3,1024,128]{2,1,0:T(8,128)S(1)}, f32[3,1024,128]{2,1,0:T(8,128)S(1)}, f32[1,512]{1,0:T(1,128)S(1)}) custom-call(f32[3,1024,128]{2,1,0:T(8,128)S(1)} %bitcast.31, f32[3,1024,128]{2,1,0:T(8,128)S(1)} %bitcast.34, f32[1024,128]{1,0:T(8,128)S(1)} %get-tuple-element.26.coef_v, f32[7,2,64,128]{3,2,1,0:T(8,128)S(1)} %get-tuple-element.33.xh, ...), custom_call_target="tpu_custom_call" | custom-call | flops 40000000 | bytes 10000000 | tf_op jit(solution)/shard_map/march/pallas_call | solution.py:889
  23.9 0.0 collective-permute-done.5.low_ref
  23.9 0.0 collective-permute-done.6.high_ref
  23.9 0.0 copy-done.3
  23.9 1.2 %finish_ends.1 = (f32[48,896]{1,0:T(8,128)S(1)}, f32[4,32]{1,0:T(4,128)S(1)}, f32[4,32]{1,0:T(4,128)S(1)}, f32[4,32]{1,0:T(4,128)S(1)}, f32[4,32]{1,0:T(4,128)S(1)}) custom-call(f32[128,896]{1,0:T(8,128)S(1)} %get-tuple-element.38.own_t, f32[16,896]{1,0:T(8,128)S(1)} %collective-permute-done.5.low_ref, f32[16,896]{1,0:T(8,128)S(1)} %collective-permute-done.6.high_ref, ...), custom_call_target="tpu_custom_call" | custom-call | tf_op jit(solution)/shard_map/finish_ends/pallas_call | solution.py:907
  25.1 0.6 %collective-permute-start.7 = (f32[4,32]{1,0:T(4,128)S(1)}, f32[4,32]{1,0:T(4,128)S(1)}, u32[]{:S(2)}, u32[]{:S(2)}) collective-permute-start(f32[4,32]{1,0:T(4,128)S(1)} %get-tuple-element.46), channel_id=1, source_target_pairs={{0,1},{1,0},{2,3},{3,2},{4,5},{5,4},{6,7},{7,6},{8,9},{9,8},{10,11... | collective-permute-start | bytes 1544 | tf_op jit(solution)/shard_map/ppermute | solution.py:938
  25.8 1.2 %collective-permute-start.8 = (f32[4,32]{1,0:T(4,128)S(1)}, f32[4,32]{1,0:T(4,128)S(1)}, u32[]{:S(2)}, u32[]{:S(2)}) collective-permute-start(f32[4,32]{1,0:T(4,128)S(1)} %get-tuple-element.47), channel_id=1, source_target_pairs={{0,2},{1,3},{2,0},{3,1},{4,6},{5,7},{6,4},{7,5},{8,10},{9,11},{10,... | collective-permute-start | bytes 1544 | tf_op jit(solution)/shard_map/ppermute | solution.py:938
  27.0 0.5 %collective-permute-start.9 = (f32[4,32]{1,0:T(4,128)S(1)}, f32[4,32]{1,0:T(4,128)S(1)}, u32[]{:S(2)}, u32[]{:S(2)}) collective-permute-start(f32[4,32]{1,0:T(4,128)S(1)} %get-tuple-element.48), channel_id=1, source_target_pairs={{0,3},{1,2},{2,1},{3,0},{4,7},{5,6},{6,5},{7,4},{8,11},{9,10},{10,... | collective-permute-start | bytes 1544 | tf_op jit(solution)/shard_map/ppermute | solution.py:938
  27.5 2.2 %write_out.1 = (f32[3,1024,128]{2,1,0:T(8,128)}, f32[3,1024,128]{2,1,0:T(8,128)}) custom-call(f32[3,1024,128]{2,1,0:T(8,128)S(1)} %get-tuple-element.36.e_s, f32[3,1024,128]{2,1,0:T(8,128)S(1)} %get-tuple-element.37.h_s, f32[48,896]{1,0:T(8,128)S(1)} %get-tuple-element.42.ends_ref), custom_call_target="tpu_custom_call" | custom-call | flops 10000000 | bytes 8000000 | tf_op jit(solution)/shard_map/write_out/pallas_call | solution.py:920
  29.6 0.0 collective-permute-done.7
  29.6 0.0 collective-permute-done.8
  29.7 0.3 %collective-permute-done.9 = f32[4,32]{1,0:T(4,128)S(1)} collective-permute-done((f32[4,32]{1,0:T(4,128)S(1)}, f32[4,32]{1,0:T(4,128)S(1)}, u32[]{:S(2)}, u32[]{:S(2)}) %collective-permute-start.9) | collective-permute-done | bytes 544 | tf_op jit(solution)/shard_map/ppermute | solution.py:938
  30.0 0.6 %add_bitcast_fusion = f32[32,4]{0,1:T(4,128)} fusion(f32[4,32]{1,0:T(4,128)S(1)} %collective-permute-done.9, f32[4,32]{1,0:T(4,128)S(1)} %collective-permute-done.8, f32[4,32]{1,0:T(4,128)S(1)} %get-tuple-element.45, f32[4,32]{1,0:T(4,128)S(1)} %collective-permute-done.7), kind=kLoop, calls=%fused_computation | loop fusion | flops 384 | bytes 2560 | tf_op jit(solution)/shard_map/transpose | solution.py:941
Async XLA Ops:
  0.6 9.7 %copy-start = (f32[3,32,16,256]{3,2,1,0:T(8,128)S(1)}, f32[3,32,16,256]{3,2,1,0:T(8,128)}, u32[]{:S(2)}) copy-start(f32[3,32,16,256]{3,2,1,0:T(8,128)} %param.8) | copy-start | bytes 4718596
  0.6 9.7 %copy-start.1 = (f32[3,32,16,256]{3,2,1,0:T(8,128)S(1)}, f32[3,32,16,256]{3,2,1,0:T(8,128)}, u32[]{:S(2)}) copy-start(f32[3,32,16,256]{3,2,1,0:T(8,128)} %param.9) | copy-start | bytes 4718596
  0.7 9.7 %copy-start.2 = (s32[32,16,256]{2,1,0:T(8,128)S(1)}, s32[32,16,256]{2,1,0:T(8,128)}, u32[]{:S(2)}) copy-start(s32[32,16,256]{2,1,0:T(8,128)} %param.11) | copy-start | bytes 1572868
  2.5 12.5 %collective-permute-start.1 = (f32[19,32,128]{2,1,0:T(8,128)S(1)}, f32[19,32,128]{2,1,0:T(8,128)S(1)}, u32[]{:S(2)}, u32[]{:S(2)}) collective-permute-start(f32[19,32,128]{2,1,0:T(8,128)S(1)} %get-tuple-element.29), channel_id=1, source_target_pairs={{0,4},{4,0},{8,12},{12,8},{1,5},{5,1},{9,13},{13,9},{2,6},{6,2},{1... | collective-permute-start | bytes 933896 | tf_op jit(solution)/shard_map/ppermute | solution.py:862
  3.8 11.2 %collective-permute-start.2 = (f32[19,32,128]{2,1,0:T(8,128)S(1)}, f32[19,32,128]{2,1,0:T(8,128)S(1)}, u32[]{:S(2)}, u32[]{:S(2)}) collective-permute-start(f32[19,32,128]{2,1,0:T(8,128)S(1)} %get-tuple-element.30), channel_id=1, source_target_pairs={{0,0},{4,8},{8,4},{12,12},{1,1},{5,9},{9,5},{13,13},{2,2},{6,10},{... | collective-permute-start | bytes 933896 | tf_op jit(solution)/shard_map/ppermute | solution.py:862
  5.7 9.2 %collective-permute-start = (f32[304,128]{1,0:T(8,128)S(1)}, f32[304,128]{1,0:T(8,128)S(1)}, u32[]{:S(2)}, u32[]{:S(2)}) collective-permute-start(f32[304,128]{1,0:T(8,128)S(1)} %get-tuple-element.28), channel_id=1, source_target_pairs={{0,16},{16,0},{1,17},{17,1},{2,18},{18,2},{3,19},{19,3},{4,20},{20... | collective-permute-start | bytes 466952 | tf_op jit(solution)/shard_map/ppermute | solution.py:862
  7.0 6.8 %collective-permute-start.3 = (f32[2,28,128]{2,1,0:T(8,128)S(1)}, f32[2,28,128]{2,1,0:T(8,128)S(1)}, u32[]{:S(2)}, u32[]{:S(2)}) collective-permute-start(f32[2,28,128]{2,1,0:T(8,128)S(1)} %get-tuple-element.31), channel_id=1, source_target_pairs={{0,20},{4,16},{8,28},{12,24},{16,4},{20,0},{24,12},{28,8},{1,21},{... | collective-permute-start | bytes 86024 | tf_op jit(solution)/shard_map/ppermute | solution.py:862
  7.0 7.9 %collective-permute-start.4 = (f32[2,28,128]{2,1,0:T(8,128)S(1)}, f32[2,28,128]{2,1,0:T(8,128)S(1)}, u32[]{:S(2)}, u32[]{:S(2)}) collective-permute-start(f32[2,28,128]{2,1,0:T(8,128)S(1)} %get-tuple-element.32), channel_id=1, source_target_pairs={{0,0},{4,24},{8,20},{12,12},{16,16},{20,8},{24,4},{28,28},{1,1},{5... | collective-permute-start | bytes 86024 | tf_op jit(solution)/shard_map/ppermute | solution.py:862
  10.4 9.4 %copy-start.4 = (f32[2,3]{1,0:T(2,128)S(1)}, f32[2,3]{1,0:T(2,128)}, u32[]{:S(2)}) copy-start(f32[2,3]{1,0:T(2,128)} %amps_ref.3) | copy-start | bytes 76
  10.4 9.4 %copy-start.5 = (s32[3]{0:T(128)S(1)}, s32[3]{0:T(128)}, u32[]{:S(2)}) copy-start(s32[3]{0:T(128)} %ports_ref.3) | copy-start | bytes 40
  16.5 7.4 %collective-permute-start.5 = (f32[16,896]{1,0:T(8,128)S(1)}, f32[16,896]{1,0:T(8,128)S(1)}, u32[]{:S(2)}, u32[]{:S(2)}) collective-permute-start(f32[16,896]{1,0:T(8,128)S(1)} %get-tuple-element.39), channel_id=1, source_target_pairs={{0,1},{1,2},{2,3},{3,0},{4,5},{5,6},{6,7},{7,4},{8,9},{9,10},{10,1... | collective-permute-start | bytes 172040 | tf_op jit(solution)/shard_map/ppermute | solution.py:885
  19.8 4.1 %collective-permute-start.6 = (f32[16,896]{1,0:T(8,128)S(1)}, f32[16,896]{1,0:T(8,128)S(1)}, u32[]{:S(2)}, u32[]{:S(2)}) collective-permute-start(f32[16,896]{1,0:T(8,128)S(1)} %get-tuple-element.40), channel_id=1, source_target_pairs={{0,3},{1,0},{2,1},{3,2},{4,7},{5,4},{6,5},{7,6},{8,11},{9,8},{10,9... | collective-permute-start | bytes 172040 | tf_op jit(solution)/shard_map/ppermute | solution.py:886
  19.8 4.1 %copy-start.3 = (s32[32,16]{0,1:T(8,128)S(1)}, s32[32,16]{0,1:T(8,128)}, u32[]{:S(2)}) copy-start(s32[32,16]{0,1:T(8,128)} %param.13) | copy-start | bytes 6148
  25.1 4.5 %collective-permute-start.7 = (f32[4,32]{1,0:T(4,128)S(1)}, f32[4,32]{1,0:T(4,128)S(1)}, u32[]{:S(2)}, u32[]{:S(2)}) collective-permute-start(f32[4,32]{1,0:T(4,128)S(1)} %get-tuple-element.46), channel_id=1, source_target_pairs={{0,1},{1,0},{2,3},{3,2},{4,5},{5,4},{6,7},{7,6},{8,9},{9,8},{10,11... | collective-permute-start | bytes 1544 | tf_op jit(solution)/shard_map/ppermute | solution.py:938
  25.8 3.9 %collective-permute-start.8 = (f32[4,32]{1,0:T(4,128)S(1)}, f32[4,32]{1,0:T(4,128)S(1)}, u32[]{:S(2)}, u32[]{:S(2)}) collective-permute-start(f32[4,32]{1,0:T(4,128)S(1)} %get-tuple-element.47), channel_id=1, source_target_pairs={{0,2},{1,3},{2,0},{3,1},{4,6},{5,7},{6,4},{7,5},{8,10},{9,11},{10,... | collective-permute-start | bytes 1544 | tf_op jit(solution)/shard_map/ppermute | solution.py:938
  27.0 3.0 %collective-permute-start.9 = (f32[4,32]{1,0:T(4,128)S(1)}, f32[4,32]{1,0:T(4,128)S(1)}, u32[]{:S(2)}, u32[]{:S(2)}) collective-permute-start(f32[4,32]{1,0:T(4,128)S(1)} %get-tuple-element.48), channel_id=1, source_target_pairs={{0,3},{1,2},{2,1},{3,0},{4,7},{5,6},{6,5},{7,4},{8,11},{9,10},{10,... | collective-permute-start | bytes 1544 | tf_op jit(solution)/shard_map/ppermute | solution.py:938

commit v7 on v6

--- a/solution.py
+++ b/solution.py
@@ -255,7 +255,7 @@
             packed[pl.ds(row, 8), :] = turn_ends(parts, lane, 0, FIELDS)
         return carry
 
-    lax.fori_loop(0, nx, fields, 0, unroll=4)
+    lax.fori_loop(0, nx, fields, 0, unroll=16)
 
     for copy in copies:
         copy.wait()
@@ -283,7 +283,7 @@
             packed[here, :] = jnp.where(lane < 8 * FIELDS, packed[here, :], after)
         return carry
 
-    lax.fori_loop(0, nx, changes, 0, unroll=4)
+    lax.fori_loop(0, nx, changes, 0, unroll=16)
 
 
 def unpack_faces(dims, sizes, own_packed, *refs):
@@ -378,7 +378,7 @@
         return carry
 
     halo_rows(0, pl.ds(0, HALO), pl.ds(0, HALO))
-    lax.fori_loop(1, nx + 4, one, 0, unroll=5)
+    lax.fori_loop(1, nx + 4, one, 0, unroll=True)
     last = pl.ds((nx + 3) * HALO, HALO)
     halo_rows(nx + 4, last, last)
     for q, p in enumerate((0, 1, nx + 2, nx + 3)):
@@ -773,7 +773,7 @@
     chunk = nx // 4
     copies = []
     for c in range(4):
-        lax.fori_loop(c * chunk, (c + 1) * chunk, one, 0, unroll=4)
+        lax.fori_loop(c * chunk, (c + 1) * chunk, one, 0, unroll=True)
         here = pl.ds(c * chunk * plane, chunk * plane)
         for k, (src, dst) in enumerate(((e_v, e_out), (h_v, h_out))):
             copy = pltpu.make_async_copy(src.at[:, here], dst.at[:, here], sems.at[2 * c + k])

time: 30.7 us -> 30.2 us (0.984)
  Pallas kernels: 14.2 us -> 13.1 us
  waiting for transfers between devices: 1.47 us -> 2.05 us
    pallas_call x1, Pallas kernels: 1.52 us -> 0.9 us  [body(): pl.pallas_call(functools.partial(unpack_faces, dims, sizes), out_shape=[c...]
    pallas_call x1, Pallas kernels: 3.44 us -> 3.01 us  [body(): pl.pallas_call(functools.partial(own_ends, dims), out_shape=[cube(m_v.sha...]
    ppermute x5, waiting for transfers between devices: 1.12 us -> 1.56 us  [body(): lax.ppermute(msg, axis, pairs)]
  transfers between devices with their start and end apart: 10 -> 10, of which waited for: 2 -> 2; matrix products, arithmetic and copies ran while one was open for 0% -> 0% of each run, Pallas kernels for 31% -> 30%
where the time goes in v7:
time: 30.2 us; the launch traced here: 30.1 us
  starting transfers between devices  13.5 us (45%)
  Pallas kernels  13.1 us (43%)
  waiting for transfers between devices  2.05 us (7%)
  between operations  0.81 us (3%)
  other arithmetic  0.58 us (2%)
    ppermute x5, starting transfers between devices, body(): lax.ppermute(msg, axis, pairs)  7.87 us
    pallas_call x1, Pallas kernels, body(): pl.pallas_call(functools.partial(march, dims, sizes), out_shape=[cube(e_v...  4.15 us
    ppermute x1, starting transfers between devices, body(): low = lax.ppermute(up, 'gz', [(i, (i + 1) % parts) for i in range(parts)])  3.31 us
    pallas_call x1, Pallas kernels, body(): pl.pallas_call(functools.partial(own_ends, dims), out_shape=[cube(m_v.sha...  3.01 us
    ppermute x3, starting transfers between devices, body(): lax.ppermute(chunks[shift], 'gz', [(i, partner_of(i, shift, parts)) for i...  2.34 us
    pallas_call x1, Pallas kernels, body(): pl.pallas_call(functools.partial(write_out, dims), out_shape=[block(e_v.s...  2.01 us
    pallas_call x1, Pallas kernels, body(): pl.pallas_call(functools.partial(send_faces, dims, sizes), out_shape=shap...  1.79 us
    ppermute x5, waiting for transfers between devices, body(): lax.ppermute(msg, axis, pairs)  1.56 us
  transfers between devices with their start and end apart: 10, of which 2 were waited for; matrix products, arithmetic and copies ran while one was open for 0% of the time, Pallas kernels for 30%

profile of v7, /device:TPU:17, one launch (start us, length us, event | category | flops | bytes accessed | tf_op | source)
XLA Modules:
  0.0 30.1 jit_solution(4766768359105078782)
XLA Ops:
  0.6 0.0 copy-start
  0.6 0.0 copy-start.1
  0.7 0.0 copy-start.2
  0.7 1.8 %send_faces.1 = (f32[304,128]{1,0:T(8,128)S(1)}, f32[19,32,128]{2,1,0:T(8,128)S(1)}, f32[19,32,128]{2,1,0:T(8,128)S(1)}, f32[2,28,128]{2,1,0:T(8,128)S(1)}, f32[2,28,128]{2,1,0:T(8,128)S(1)}) custom-call(f32[3,32,2,2,8,128]{5,4,3,2,1,0:T(8,128)} %bitcast.29, f32[3,32,2,2,8,128]{5,4,3,2,1,0:T(8,128)} %bitcast.32, s32[32,2,2,8,128]{4,3,2,1,0:T(8,128)} %bitcast.35, ...), custom_call_target="tpu_custom_call" | custom-call | tf_op jit(solution)/shard_map/send_faces/pallas_call | solution.py:816
  2.5 1.4 %collective-permute-start.1 = (f32[19,32,128]{2,1,0:T(8,128)S(1)}, f32[19,32,128]{2,1,0:T(8,128)S(1)}, u32[]{:S(2)}, u32[]{:S(2)}) collective-permute-start(f32[19,32,128]{2,1,0:T(8,128)S(1)} %get-tuple-element.29), channel_id=1, source_target_pairs={{0,4},{4,0},{8,12},{12,8},{1,5},{5,1},{9,13},{13,9},{2,6},{6,2},{1... | collective-permute-start | bytes 933896 | tf_op jit(solution)/shard_map/ppermute | solution.py:862
  3.8 1.9 %collective-permute-start.2 = (f32[19,32,128]{2,1,0:T(8,128)S(1)}, f32[19,32,128]{2,1,0:T(8,128)S(1)}, u32[]{:S(2)}, u32[]{:S(2)}) collective-permute-start(f32[19,32,128]{2,1,0:T(8,128)S(1)} %get-tuple-element.30), channel_id=1, source_target_pairs={{0,0},{4,8},{8,4},{12,12},{1,1},{5,9},{9,5},{13,13},{2,2},{6,10},{... | collective-permute-start | bytes 933896 | tf_op jit(solution)/shard_map/ppermute | solution.py:862
  5.7 1.3 %collective-permute-start = (f32[304,128]{1,0:T(8,128)S(1)}, f32[304,128]{1,0:T(8,128)S(1)}, u32[]{:S(2)}, u32[]{:S(2)}) collective-permute-start(f32[304,128]{1,0:T(8,128)S(1)} %get-tuple-element.28), channel_id=1, source_target_pairs={{0,16},{16,0},{1,17},{17,1},{2,18},{18,2},{3,19},{19,3},{4,20},{20... | collective-permute-start | bytes 466952 | tf_op jit(solution)/shard_map/ppermute | solution.py:862
  7.0 0.0 collective-permute-start.3
  7.0 3.3 %collective-permute-start.4 = (f32[2,28,128]{2,1,0:T(8,128)S(1)}, f32[2,28,128]{2,1,0:T(8,128)S(1)}, u32[]{:S(2)}, u32[]{:S(2)}) collective-permute-start(f32[2,28,128]{2,1,0:T(8,128)S(1)} %get-tuple-element.32), channel_id=1, source_target_pairs={{0,0},{4,24},{8,20},{12,12},{16,16},{20,8},{24,4},{28,28},{1,1},{5... | collective-permute-start | bytes 86024 | tf_op jit(solution)/shard_map/ppermute | solution.py:862
  10.3 0.0 copy-done
  10.4 0.0 copy-done.1
  10.4 0.0 copy-done.2
  10.4 0.0 copy-start.4
  10.4 0.0 copy-start.5
  10.4 3.0 %own_ends.1 = (f32[1024,128]{1,0:T(8,128)S(1)}, f32[896,128]{1,0:T(8,128)S(1)}, bf16[3,3,512,256]{3,2,1,0:T(8,128)(2,1)S(1)}) custom-call(f32[3,1024,128]{2,1,0:T(8,128)S(1)} %bitcast.30, f32[3,1024,128]{2,1,0:T(8,128)S(1)} %bitcast.33, s32[1024,128]{1,0:T(8,128)S(1)} %bitcast.36, bf16[3,3,512,256]{3,2,1,0:T(8,128)(2,1)} %bitcast.38, f32[8]{0:T(128)} %perm_ref.3), custom_call_target="tpu_custom_call" | custom-call | flops 10000000 | bytes 4000000 | tf_op jit(solution)/shard_map/own_ends/pallas_call | solution.py:833
  13.4 0.0 collective-permute-done.3.refs_3_
  13.4 1.5 %collective-permute-done.4.refs_4_ = f32[2,28,128]{2,1,0:T(8,128)S(1)} collective-permute-done((f32[2,28,128]{2,1,0:T(8,128)S(1)}, f32[2,28,128]{2,1,0:T(8,128)S(1)}, u32[]{:S(2)}, u32[]{:S(2)}) %collective-permute-start.4) | collective-permute-done | bytes 28704 | tf_op jit(solution)/shard_map/ppermute | solution.py:862
  15.0 0.0 collective-permute-done.refs_0_
  15.0 0.0 collective-permute-done.1.refs_1_
  15.0 0.0 collective-permute-done.2.refs_2_
  15.0 0.9 %unpack_faces.1 = (f32[7,2,64,128]{3,2,1,0:T(8,128)S(1)}, f32[7,2,288,128]{3,2,1,0:T(8,128)S(1)}, f32[128,896]{1,0:T(8,128)S(1)}, f32[16,896]{1,0:T(8,128)S(1)}, f32[16,896]{1,0:T(8,128)S(1)}) custom-call(f32[896,128]{1,0:T(8,128)S(1)} %get-tuple-element.27.own_packed, f32[304,128]{1,0:T(8,128)S(1)} %collective-permute-done.refs_0_, ...), custom_call_target="tpu_custom_call" | custom-call | tf_op jit(solution)/shard_map/unpack_faces/pallas_call | solution.py:864
  15.9 3.3 %collective-permute-start.5 = (f32[16,896]{1,0:T(8,128)S(1)}, f32[16,896]{1,0:T(8,128)S(1)}, u32[]{:S(2)}, u32[]{:S(2)}) collective-permute-start(f32[16,896]{1,0:T(8,128)S(1)} %get-tuple-element.39), channel_id=1, source_target_pairs={{0,1},{1,2},{2,3},{3,0},{4,5},{5,6},{6,7},{7,4},{8,9},{9,10},{10,1... | collective-permute-start | bytes 172040 | tf_op jit(solution)/shard_map/ppermute | solution.py:885
  19.2 0.0 collective-permute-start.6
  19.2 0.0 copy-done.4
  19.2 0.0 copy-done.5
  19.2 0.0 copy-start.3
  19.2 4.1 %march.1 = (f32[3,1024,128]{2,1,0:T(8,128)S(1)}, f32[3,1024,128]{2,1,0:T(8,128)S(1)}, f32[1,512]{1,0:T(1,128)S(1)}) custom-call(f32[3,1024,128]{2,1,0:T(8,128)S(1)} %bitcast.31, f32[3,1024,128]{2,1,0:T(8,128)S(1)} %bitcast.34, f32[1024,128]{1,0:T(8,128)S(1)} %get-tuple-element.26.coef_v, f32[7,2,64,128]{3,2,1,0:T(8,128)S(1)} %get-tuple-element.33.xh, ...), custom_call_target="tpu_custom_call" | custom-call | flops 40000000 | bytes 10000000 | tf_op jit(solution)/shard_map/march/pallas_call | solution.py:889
  23.4 0.0 collective-permute-done.5.low_ref
  23.4 0.0 collective-permute-done.6.high_ref
  23.4 0.0 copy-done.3
  23.4 1.2 %finish_ends.1 = (f32[48,896]{1,0:T(8,128)S(1)}, f32[4,32]{1,0:T(4,128)S(1)}, f32[4,32]{1,0:T(4,128)S(1)}, f32[4,32]{1,0:T(4,128)S(1)}, f32[4,32]{1,0:T(4,128)S(1)}) custom-call(f32[128,896]{1,0:T(8,128)S(1)} %get-tuple-element.38.own_t, f32[16,896]{1,0:T(8,128)S(1)} %collective-permute-done.5.low_ref, f32[16,896]{1,0:T(8,128)S(1)} %collective-permute-done.6.high_ref, ...), custom_call_target="tpu_custom_call" | custom-call | tf_op jit(solution)/shard_map/finish_ends/pallas_call | solution.py:907
  24.6 0.6 %collective-permute-start.7 = (f32[4,32]{1,0:T(4,128)S(1)}, f32[4,32]{1,0:T(4,128)S(1)}, u32[]{:S(2)}, u32[]{:S(2)}) collective-permute-start(f32[4,32]{1,0:T(4,128)S(1)} %get-tuple-element.46), channel_id=1, source_target_pairs={{0,1},{1,0},{2,3},{3,2},{4,5},{5,4},{6,7},{7,6},{8,9},{9,8},{10,11... | collective-permute-start | bytes 1544 | tf_op jit(solution)/shard_map/ppermute | solution.py:938
  25.3 1.2 %collective-permute-start.8 = (f32[4,32]{1,0:T(4,128)S(1)}, f32[4,32]{1,0:T(4,128)S(1)}, u32[]{:S(2)}, u32[]{:S(2)}) collective-permute-start(f32[4,32]{1,0:T(4,128)S(1)} %get-tuple-element.47), channel_id=1, source_target_pairs={{0,2},{1,3},{2,0},{3,1},{4,6},{5,7},{6,4},{7,5},{8,10},{9,11},{10,... | collective-permute-start | bytes 1544 | tf_op jit(solution)/shard_map/ppermute | solution.py:938
  26.5 0.5 %collective-permute-start.9 = (f32[4,32]{1,0:T(4,128)S(1)}, f32[4,32]{1,0:T(4,128)S(1)}, u32[]{:S(2)}, u32[]{:S(2)}) collective-permute-start(f32[4,32]{1,0:T(4,128)S(1)} %get-tuple-element.48), channel_id=1, source_target_pairs={{0,3},{1,2},{2,1},{3,0},{4,7},{5,6},{6,5},{7,4},{8,11},{9,10},{10,... | collective-permute-start | bytes 1544 | tf_op jit(solution)/shard_map/ppermute | solution.py:938
  27.0 2.0 %write_out.1 = (f32[3,1024,128]{2,1,0:T(8,128)}, f32[3,1024,128]{2,1,0:T(8,128)}) custom-call(f32[3,1024,128]{2,1,0:T(8,128)S(1)} %get-tuple-element.36.e_s, f32[3,1024,128]{2,1,0:T(8,128)S(1)} %get-tuple-element.37.h_s, f32[48,896]{1,0:T(8,128)S(1)} %get-tuple-element.42.ends_ref), custom_call_target="tpu_custom_call" | custom-call | flops 10000000 | bytes 8000000 | tf_op jit(solution)/shard_map/write_out/pallas_call | solution.py:920
  29.0 0.0 collective-permute-done.7
  29.0 0.0 collective-permute-done.8
  29.0 0.5 %collective-permute-done.9 = f32[4,32]{1,0:T(4,128)S(1)} collective-permute-done((f32[4,32]{1,0:T(4,128)S(1)}, f32[4,32]{1,0:T(4,128)S(1)}, u32[]{:S(2)}, u32[]{:S(2)}) %collective-permute-start.9) | collective-permute-done | bytes 544 | tf_op jit(solution)/shard_map/ppermute | solution.py:938
  29.5 0.6 %add_bitcast_fusion = f32[32,4]{0,1:T(4,128)} fusion(f32[4,32]{1,0:T(4,128)S(1)} %collective-permute-done.9, f32[4,32]{1,0:T(4,128)S(1)} %collective-permute-done.8, f32[4,32]{1,0:T(4,128)S(1)} %get-tuple-element.45, f32[4,32]{1,0:T(4,128)S(1)} %collective-permute-done.7), kind=kLoop, calls=%fused_computation | loop fusion | flops 384 | bytes 2560 | tf_op jit(solution)/shard_map/transpose | solution.py:941
Async XLA Ops:
  0.6 9.7 %copy-start = (f32[3,32,16,256]{3,2,1,0:T(8,128)S(1)}, f32[3,32,16,256]{3,2,1,0:T(8,128)}, u32[]{:S(2)}) copy-start(f32[3,32,16,256]{3,2,1,0:T(8,128)} %param.8) | copy-start | bytes 4718596
  0.6 9.7 %copy-start.1 = (f32[3,32,16,256]{3,2,1,0:T(8,128)S(1)}, f32[3,32,16,256]{3,2,1,0:T(8,128)}, u32[]{:S(2)}) copy-start(f32[3,32,16,256]{3,2,1,0:T(8,128)} %param.9) | copy-start | bytes 4718596
  0.7 9.7 %copy-start.2 = (s32[32,16,256]{2,1,0:T(8,128)S(1)}, s32[32,16,256]{2,1,0:T(8,128)}, u32[]{:S(2)}) copy-start(s32[32,16,256]{2,1,0:T(8,128)} %param.11) | copy-start | bytes 1572868
  2.5 12.5 %collective-permute-start.1 = (f32[19,32,128]{2,1,0:T(8,128)S(1)}, f32[19,32,128]{2,1,0:T(8,128)S(1)}, u32[]{:S(2)}, u32[]{:S(2)}) collective-permute-start(f32[19,32,128]{2,1,0:T(8,128)S(1)} %get-tuple-element.29), channel_id=1, source_target_pairs={{0,4},{4,0},{8,12},{12,8},{1,5},{5,1},{9,13},{13,9},{2,6},{6,2},{1... | collective-permute-start | bytes 933896 | tf_op jit(solution)/shard_map/ppermute | solution.py:862
  3.8 11.2 %collective-permute-start.2 = (f32[19,32,128]{2,1,0:T(8,128)S(1)}, f32[19,32,128]{2,1,0:T(8,128)S(1)}, u32[]{:S(2)}, u32[]{:S(2)}) collective-permute-start(f32[19,32,128]{2,1,0:T(8,128)S(1)} %get-tuple-element.30), channel_id=1, source_target_pairs={{0,0},{4,8},{8,4},{12,12},{1,1},{5,9},{9,5},{13,13},{2,2},{6,10},{... | collective-permute-start | bytes 933896 | tf_op jit(solution)/shard_map/ppermute | solution.py:862
  5.7 9.2 %collective-permute-start = (f32[304,128]{1,0:T(8,128)S(1)}, f32[304,128]{1,0:T(8,128)S(1)}, u32[]{:S(2)}, u32[]{:S(2)}) collective-permute-start(f32[304,128]{1,0:T(8,128)S(1)} %get-tuple-element.28), channel_id=1, source_target_pairs={{0,16},{16,0},{1,17},{17,1},{2,18},{18,2},{3,19},{19,3},{4,20},{20... | collective-permute-start | bytes 466952 | tf_op jit(solution)/shard_map/ppermute | solution.py:862
  7.0 6.4 %collective-permute-start.3 = (f32[2,28,128]{2,1,0:T(8,128)S(1)}, f32[2,28,128]{2,1,0:T(8,128)S(1)}, u32[]{:S(2)}, u32[]{:S(2)}) collective-permute-start(f32[2,28,128]{2,1,0:T(8,128)S(1)} %get-tuple-element.31), channel_id=1, source_target_pairs={{0,20},{4,16},{8,28},{12,24},{16,4},{20,0},{24,12},{28,8},{1,21},{... | collective-permute-start | bytes 86024 | tf_op jit(solution)/shard_map/ppermute | solution.py:862
  7.0 7.9 %collective-permute-start.4 = (f32[2,28,128]{2,1,0:T(8,128)S(1)}, f32[2,28,128]{2,1,0:T(8,128)S(1)}, u32[]{:S(2)}, u32[]{:S(2)}) collective-permute-start(f32[2,28,128]{2,1,0:T(8,128)S(1)} %get-tuple-element.32), channel_id=1, source_target_pairs={{0,0},{4,24},{8,20},{12,12},{16,16},{20,8},{24,4},{28,28},{1,1},{5... | collective-permute-start | bytes 86024 | tf_op jit(solution)/shard_map/ppermute | solution.py:862
  10.4 8.8 %copy-start.4 = (f32[2,3]{1,0:T(2,128)S(1)}, f32[2,3]{1,0:T(2,128)}, u32[]{:S(2)}) copy-start(f32[2,3]{1,0:T(2,128)} %amps_ref.3) | copy-start | bytes 76
  10.4 8.8 %copy-start.5 = (s32[3]{0:T(128)S(1)}, s32[3]{0:T(128)}, u32[]{:S(2)}) copy-start(s32[3]{0:T(128)} %ports_ref.3) | copy-start | bytes 40
  15.9 7.5 %collective-permute-start.5 = (f32[16,896]{1,0:T(8,128)S(1)}, f32[16,896]{1,0:T(8,128)S(1)}, u32[]{:S(2)}, u32[]{:S(2)}) collective-permute-start(f32[16,896]{1,0:T(8,128)S(1)} %get-tuple-element.39), channel_id=1, source_target_pairs={{0,1},{1,2},{2,3},{3,0},{4,5},{5,6},{6,7},{7,4},{8,9},{9,10},{10,1... | collective-permute-start | bytes 172040 | tf_op jit(solution)/shard_map/ppermute | solution.py:885
  19.2 4.2 %collective-permute-start.6 = (f32[16,896]{1,0:T(8,128)S(1)}, f32[16,896]{1,0:T(8,128)S(1)}, u32[]{:S(2)}, u32[]{:S(2)}) collective-permute-start(f32[16,896]{1,0:T(8,128)S(1)} %get-tuple-element.40), channel_id=1, source_target_pairs={{0,3},{1,0},{2,1},{3,2},{4,7},{5,4},{6,5},{7,6},{8,11},{9,8},{10,9... | collective-permute-start | bytes 172040 | tf_op jit(solution)/shard_map/ppermute | solution.py:886
  19.2 4.2 %copy-start.3 = (s32[32,16]{0,1:T(8,128)S(1)}, s32[32,16]{0,1:T(8,128)}, u32[]{:S(2)}) copy-start(s32[32,16]{0,1:T(8,128)} %param.13) | copy-start | bytes 6148
  24.6 4.4 %collective-permute-start.7 = (f32[4,32]{1,0:T(4,128)S(1)}, f32[4,32]{1,0:T(4,128)S(1)}, u32[]{:S(2)}, u32[]{:S(2)}) collective-permute-start(f32[4,32]{1,0:T(4,128)S(1)} %get-tuple-element.46), channel_id=1, source_target_pairs={{0,1},{1,0},{2,3},{3,2},{4,5},{5,4},{6,7},{7,6},{8,9},{9,8},{10,11... | collective-permute-start | bytes 1544 | tf_op jit(solution)/shard_map/ppermute | solution.py:938
  25.3 3.7 %collective-permute-start.8 = (f32[4,32]{1,0:T(4,128)S(1)}, f32[4,32]{1,0:T(4,128)S(1)}, u32[]{:S(2)}, u32[]{:S(2)}) collective-permute-start(f32[4,32]{1,0:T(4,128)S(1)} %get-tuple-element.47), channel_id=1, source_target_pairs={{0,2},{1,3},{2,0},{3,1},{4,6},{5,7},{6,4},{7,5},{8,10},{9,11},{10,... | collective-permute-start | bytes 1544 | tf_op jit(solution)/shard_map/ppermute | solution.py:938
  26.5 3.0 %collective-permute-start.9 = (f32[4,32]{1,0:T(4,128)S(1)}, f32[4,32]{1,0:T(4,128)S(1)}, u32[]{:S(2)}, u32[]{:S(2)}) collective-permute-start(f32[4,32]{1,0:T(4,128)S(1)} %get-tuple-element.48), channel_id=1, source_target_pairs={{0,3},{1,2},{2,1},{3,0},{4,7},{5,6},{6,5},{7,4},{8,11},{9,10},{10,... | collective-permute-start | bytes 1544 | tf_op jit(solution)/shard_map/ppermute | solution.py:938

commit v8 on v7

--- a/solution.py
+++ b/solution.py
@@ -15,8 +15,6 @@
 electric_step = 0.5
 
 VM = pl.BlockSpec(memory_space=pltpu.VMEM)
-SM = pl.BlockSpec(memory_space=pltpu.SMEM)
-ANY = pl.BlockSpec(memory_space=pl.ANY)
 
 
 HBM = pl.BlockSpec(memory_space=pltpu.HBM)
@@ -99,7 +97,7 @@
     gx, gy = lax.axis_index("gx"), lax.axis_index("gy")
     xs, ys = swaps(sizes[0]), swaps(sizes[1])
     n_out = len(xs) + len(ys) + len(xs) * len(ys)
-    outs, refs = refs[:n_out], refs[n_out:]
+    outs, table_ref, refs = refs[:n_out], refs[n_out], refs[n_out + 1 :]
     x_bufs, refs = refs[: 3 * len(xs)], refs[3 * len(xs) :]
     y_bufs, (perm_s, sems) = refs[: 3 * len(ys)], refs[3 * len(ys) :]
     copies = []
@@ -124,6 +122,8 @@
     start(perm_ref, perm_s)
     copies.pop().wait()
     table = coef_table(perm_s)
+    for k, value in enumerate(table):
+        table_ref[k : k + 1, :] = jnp.broadcast_to(value, (1, 128))
     lane = lax.broadcasted_iota(jnp.int32, (8, 128), 1)
     lane_n = lax.broadcasted_iota(jnp.int32, (nx, 128), 1)
 
@@ -222,7 +222,7 @@
     return out
 
 
-def own_ends(dims, e_v, h_v, m_v, snap_hbm, perm_ref, coef_v, packed, snap_ref, sems):
+def own_ends(dims, e_v, h_v, m_v, snap_hbm, table_ref, coef_v, packed, snap_ref, sems):
     nx, ny, nz = dims
     lanes = nz // 128
     step = ny + HALO
@@ -232,7 +232,7 @@
             copy = pltpu.make_async_copy(snap_hbm.at[t, c], snap_ref.at[t, c], sems.at[3 * t + c])
             copy.start()
             copies.append(copy)
-    table = coef_table(perm_ref)
+    table = [table_ref[k : k + 1, :] for k in range(table_ref.shape[0])]
     lane = lax.broadcasted_iota(jnp.int32, (8, 128), 1)
     tiles = ny // 8
 
@@ -418,13 +418,23 @@
         down_ref[row : row + 1, :] = jnp.zeros((1, padded), jnp.float32)
 
 
+def split_index(index, size):
+    if size & (size - 1) == 0:
+        return lax.shift_right_logical(index, size.bit_length() - 1), index & (size - 1)
+    return lax.div(index, size), lax.rem(index, size)
+
+
+def steps_in(index, step):
+    return ((index.astype(jnp.float32) + 0.5) * (1.0 / step)).astype(jnp.int32)
+
+
 def columns_of(lines, nx, ny):
     spread, pick = [], []
     for line, step, first in lines:
         size = line.shape[1]
         at = lax.broadcasted_iota(jnp.int32, (ny, size), 1) - first
         y = lax.broadcasted_iota(jnp.int32, (ny, size), 0)
-        ok = (at >= 0) & (at < nx * step) & (lax.rem(at, step) == y)
+        ok = (at >= 0) & (at < nx * step) & (at - steps_in(at, step) * step == y)
         spread.append(jnp.where(ok, line, 0.0))
         at = lax.broadcasted_iota(jnp.int32, (nx, size), 1) - first
         x = lax.broadcasted_iota(jnp.int32, (nx, size), 0) * step
@@ -447,15 +457,11 @@
 def find_ports(dims, sizes, ports_ref):
     nx, ny, nz = dims
     gx, gy, gz = lax.axis_index("gx"), lax.axis_index("gy"), lax.axis_index("gz")
-    plane_cells = (ny * sizes[1]) * (nz * sizes[2])
-    line_cells = nz * sizes[2]
     found = []
     for q in range(ports_ref.shape[0]):
-        cell = ports_ref[q]
-        x = lax.div(cell, plane_cells) - gx * nx
-        y = lax.rem(lax.div(cell, line_cells), ny * sizes[1]) - gy * ny
-        z = lax.rem(cell, line_cells) - gz * nz
-        found.append((x, y, z))
+        line, z = split_index(ports_ref[q], nz * sizes[2])
+        x, y = split_index(line, ny * sizes[1])
+        found.append((x - gx * nx, y - gy * ny, z - gz * nz))
     return found
 
 
@@ -464,7 +470,14 @@
     lanes = nz // 128
     tiles = ny // 8
     step = ny + HALO
-    e_s, h_s, line_ref, e1, h1, h2, half_ref, struck, clean, sums = refs
+    e_s, h_s, line_ref, spots_ref, gains_ref, e1, h1, h2, half_ref, struck, clean, sums = refs[:12]
+    ports_s, amps_s, sems = refs[12:]
+    copies = [
+        pltpu.make_async_copy(ports_ref, ports_s, sems.at[0]),
+        pltpu.make_async_copy(amps_ref, amps_s, sems.at[1]),
+    ]
+    for copy in copies:
+        copy.start()
     gx, gy = lax.axis_index("gx"), lax.axis_index("gy")
     row = lax.broadcasted_iota(jnp.int32, (step, nz), 0)
     lane = lax.broadcasted_iota(jnp.int32, (step, nz), 1)
@@ -474,11 +487,21 @@
         clean[k] = jnp.where((lane[:ny] > k) & (lane[:ny] < nz - 1 - k), 1.0, 0.0)
 
     planes_struck = []
-    for q, (x, y, z) in enumerate(find_ports(dims, sizes, ports_ref)):
-        near = (y >= -2) & (y < ny + 2) & (z >= 0) & (z < nz)
-        at = jnp.where(y < 0, y + step, y)
-        struck[q] = jnp.where((row == at) & (lane == z) & near, 1.0, 0.0)
-        planes_struck.append(x + 2)
+
+    def place_ports():
+        for copy in copies:
+            copy.wait()
+        for q, (x, y, z) in enumerate(find_ports(dims, sizes, ports_s)):
+            near = (y >= -2) & (y < ny + 2) & (z >= 0) & (z < nz)
+            at = jnp.where(y < 0, y + step, y)
+            struck[q] = jnp.where((row == at) & (lane == z) & near, 1.0, 0.0)
+            planes_struck.append(x + 2)
+            for k, v in enumerate((x, y, z)):
+                spots_ref[3 * q + k : 3 * q + k + 1, :] = jnp.full((1, 128), v, jnp.int32)
+            for k in range(STEPS):
+                gains_ref[STEPS * q + k : STEPS * q + k + 1, :] = jnp.full(
+                    (1, 128), amps_s[k, q], jnp.float32
+                )
 
     def spot(x, t, z):
         index = ((x * tiles + t) * lanes + z) * 8
@@ -603,18 +626,20 @@
     def strike(first, second):
         hit = None
         for at in planes_struck:
-            for q in first + second:
-                hit = at == q if hit is None else hit | (at == q)
+            for planes in (first, second):
+                if planes:
+                    here = (at >= planes[0]) & (at <= planes[-1])
+                    hit = here if hit is None else hit | here
 
         @pl.when(hit)
         def _():
             for k, at in enumerate(planes_struck):
                 for p in first:
-                    amp = jnp.where(at == p, amps_ref[0, k], 0.0)
+                    amp = jnp.where(at == p, amps_s[0, k], 0.0)
                     e1[2, p] = e1[2, p] + struck[k] * amp
                 for p in second:
                     x = p - 2
-                    amp = jnp.where(at == p, amps_ref[1, k], 0.0)
+                    amp = jnp.where(at == p, amps_s[1, k], 0.0)
                     index = pl.ds(aligned(x * ny), ny)
                     s = [snap_ref[t, 2, index, :].astype(jnp.float32) for t in (1, 2)]
                     folded = jnp.zeros((ny, 128), jnp.float32)
@@ -639,6 +664,8 @@
         for q in some(p, 0, 0, nx + 2):
             first_h(q)
         if first + last:
+            if not planes_struck:
+                place_ports()
             strike(first, last)
 
     def body(k, carry):
@@ -658,7 +685,7 @@
 
 
 def finish_ends(
-    dims, sizes, own_t, low_ref, high_ref, line_ref, mask_ref, ports_ref, amps_ref, *refs
+    dims, sizes, own_t, low_ref, high_ref, line_ref, mask_ref, spots_ref, gains_ref, *refs
 ):
     nx, ny, nz = dims
     step = ny + HALO
@@ -678,10 +705,14 @@
             strips[k, f, near : near + 1, :] = jnp.where(ok, msg[f : f + 1, :], 0.0)
 
     at = lane + 2
-    p, y = lax.div(at, step), lax.rem(at, step) - 2
+    p = steps_in(at, step)
+    y = at - p * step - 2
     inside = ((p >= 2) | (gx > 0)) & ((p < nx + 2) | (gx < sizes[0] - 1))
     inside = inside & ((y >= 0) | (gy > 0)) & ((y < ny) | (gy < sizes[1] - 1))
-    found = find_ports(dims, sizes, ports_ref)
+    found = [
+        tuple(spots_ref[3 * q + k : 3 * q + k + 1, 0:1] for k in range(3))
+        for q in range(spots_ref.shape[0] // 3)
+    ]
 
     def x_up(v):
         return pltpu.roll(v, padded - step, 1)
@@ -720,7 +751,7 @@
             for q, (sx, sy, sz) in enumerate(found):
                 near = (sx >= -2) & (sx < nx + 2) & (sy >= -2) & (sy < ny + 2)
                 hit = (row == sz - first) & (at == (sx + 2) * step + sy + 2) & near
-                ez = ez + jnp.where(hit, amps_ref[s, q], 0.0)
+                ez = ez + jnp.where(hit, gains_ref[STEPS * q + s : STEPS * q + s + 1, 0:1], 0.0)
             if k == 0:
                 mine = (row == 4) | ((row == 5) & (s == 1))
             else:
@@ -813,7 +844,8 @@
         tile = (nx * lanes * 8, 128)
         buffers += [cube((3, *tile), f32), cube((3, *tile), f32), cube(tile, i32)]
     n_copies = 3 * (len(xs) + len(ys)) + 1
-    msgs = pl.pallas_call(
+    shapes += [block((permittivity.shape[0], 128), f32)]
+    *msgs, table = pl.pallas_call(
         functools.partial(send_faces, dims, sizes),
         out_shape=shapes,
         in_specs=[HBM, HBM, HBM, HBM],
@@ -833,13 +865,13 @@
     coef_v, own_packed, s = pl.pallas_call(
         functools.partial(own_ends, dims),
         out_shape=[cube(m_v.shape, f32), cube((padded, 128), f32), cube(snaps.shape, snaps.dtype)],
-        in_specs=[VM, VM, VM, HBM, SM],
+        in_specs=[VM, VM, VM, HBM, VM],
         out_specs=[VM] * 3,
         scratch_shapes=[pltpu.SemaphoreType.DMA((3 * (STEPS + 1),))],
         compiler_params=params(),
         cost_estimate=pl.CostEstimate(flops=10**7, bytes_accessed=4 * 10**6, transcendentals=0),
         name="own_ends",
-    )(e_v, h_v, m_v, snaps, permittivity)
+    )(e_v, h_v, m_v, snaps, table)
 
     both = ("gx", "gy")
 
@@ -886,11 +918,12 @@
     high = lax.ppermute(down, "gz", [(i, (i - 1) % parts) for i in range(parts)])
 
     ported = ports.shape[0]
-    e_s, h_s, line = pl.pallas_call(
+    e_s, h_s, line, spots, gains = pl.pallas_call(
         functools.partial(march, dims, sizes),
-        out_shape=[cube(e_v.shape, f32), cube(h_v.shape, f32), block((1, cells), f32)],
-        in_specs=[VM] * 6 + [SM, SM],
-        out_specs=[VM] * 3,
+        out_shape=[cube(e_v.shape, f32), cube(h_v.shape, f32), block((1, cells), f32)]
+        + [block((3 * ported, 128), i32), block((STEPS * ported, 128), f32)],
+        in_specs=[VM] * 6 + [HBM, HBM],
+        out_specs=[VM] * 5,
         scratch_shapes=[
             pltpu.VMEM((3, nx + 4, step, nz), f32),
             pltpu.VMEM((3, nx + 4, step, nz), f32),
@@ -899,15 +932,18 @@
             pltpu.VMEM((ported, step, nz), f32),
             pltpu.VMEM((2, ny, nz), f32),
             pltpu.VMEM((cells, 128), f32),
+            pltpu.SMEM(ports.shape, i32),
+            pltpu.SMEM(amplitudes.shape, f32),
+            pltpu.SemaphoreType.DMA((2,)),
         ],
         compiler_params=params(24),
         cost_estimate=pl.CostEstimate(flops=4 * 10**7, bytes_accessed=10**7, transcendentals=0),
         name="march",
-    )(e_v, h_v, coef_v, xh, yh, s, ports, amplitudes)
+    )(e_v, h_v, coef_v, xh, yh, s, in_hbm(ports), in_hbm(amplitudes))
     ends, *chunks = pl.pallas_call(
         functools.partial(finish_ends, dims, sizes),
         out_shape=[cube((48, padded), f32)] + [block((ny // parts, nx), f32)] * parts,
-        in_specs=[VM] * 5 + [SM, SM],
+        in_specs=[VM] * 7,
         out_specs=[VM] * (1 + parts),
         scratch_shapes=[
             pltpu.VMEM((2, FIELDS, 8, padded), f32),
@@ -916,7 +952,7 @@
         ],
         compiler_params=params(),
         name="finish_ends",
-    )(own_t, low, high, line, design_mask.T, ports, amplitudes)
+    )(own_t, low, high, line, design_mask.T, spots, gains)
     e_out, h_out = pl.pallas_call(
         functools.partial(write_out, dims),
         out_shape=[block(e_v.shape, f32), block(h_v.shape, f32)],

time: 30.2 us -> 29.3 us (0.970)
  Pallas kernels: 13.1 us -> 11.3 us
  waiting for transfers between devices: 2.05 us -> 2.88 us
    ppermute x5, waiting for transfers between devices: 1.56 us -> 2.37 us  [body(): lax.ppermute(msg, axis, pairs)]
    pallas_call x1, Pallas kernels: 3.01 us -> 2.22 us  [body(): pl.pallas_call(functools.partial(own_ends, dims), out_shape=[cube(m_v.sha...]
    pallas_call x1, Pallas kernels: 1.22 us -> 0.66 us  [body(): pl.pallas_call(functools.partial(finish_ends, dims, sizes), out_shape=[cu...]
    pallas_call x1, Pallas kernels: 4.15 us -> 3.71 us  [body(): pl.pallas_call(functools.partial(march, dims, sizes), out_shape=[cube(e_v...]
  transfers between devices with their start and end apart: 10 -> 10, of which waited for: 2 -> 2; matrix products, arithmetic and copies ran while one was open for 0% -> 0% of each run, Pallas kernels for 30% -> 27%
where the time goes in v8:
time: 29.3 us; the launch traced here: 29.1 us
  starting transfers between devices  13.5 us (46%)
  Pallas kernels  11.3 us (39%)
  waiting for transfers between devices  2.88 us (10%)
  between operations  0.78 us (3%)
  other arithmetic  0.58 us (2%)
    ppermute x5, starting transfers between devices, body(): lax.ppermute(msg, axis, pairs)  7.87 us
    pallas_call x1, Pallas kernels, body(): pl.pallas_call(functools.partial(march, dims, sizes), out_shape=[cube(e_v...  3.71 us
    ppermute x1, starting transfers between devices, body(): low = lax.ppermute(up, 'gz', [(i, (i + 1) % parts) for i in range(parts)])  3.31 us
    ppermute x5, waiting for transfers between devices, body(): lax.ppermute(msg, axis, pairs)  2.37 us
    ppermute x3, starting transfers between devices, body(): lax.ppermute(chunks[shift], 'gz', [(i, partner_of(i, shift, parts)) for i...  2.35 us
    pallas_call x1, Pallas kernels, body(): pl.pallas_call(functools.partial(own_ends, dims), out_shape=[cube(m_v.sha...  2.22 us
    pallas_call x1, Pallas kernels, body(): pl.pallas_call(functools.partial(write_out, dims), out_shape=[block(e_v.s...  2.01 us
    pallas_call x1, Pallas kernels, body(): pl.pallas_call(functools.partial(send_faces, dims, sizes), out_shape=shap...  1.79 us
  transfers between devices with their start and end apart: 10, of which 2 were waited for; matrix products, arithmetic and copies ran while one was open for 0% of the time, Pallas kernels for 27%

profile of v8, /device:TPU:17, one launch (start us, length us, event | category | flops | bytes accessed | tf_op | source)
XLA Modules:
  0.0 29.1 jit_solution(9049804552352527933)
XLA Ops:
  0.6 0.0 copy-start
  0.6 0.0 copy-start.1
  0.7 0.0 copy-start.2
  0.7 1.8 %send_faces.1 = (f32[304,128]{1,0:T(8,128)S(1)}, f32[19,32,128]{2,1,0:T(8,128)S(1)}, f32[19,32,128]{2,1,0:T(8,128)S(1)}, f32[2,28,128]{2,1,0:T(8,128)S(1)}, f32[...) custom-call(f32[3,32,2,2,8,128]{5,4,3,2,1,0:T(8,128)} %bitcast.29, f32[3,32,2,2,8,128]{5,4,3,2,1,0:T(8,128)} %bitcast.32, ...), custom_call_target="tpu_custom_call" | custom-call | tf_op jit(solution)/shard_map/send_faces/pallas_call | solution.py:848
  2.5 1.4 %collective-permute-start.1 = (f32[19,32,128]{2,1,0:T(8,128)S(1)}, f32[19,32,128]{2,1,0:T(8,128)S(1)}, u32[]{:S(2)}, u32[]{:S(2)}) collective-permute-start(f32[19,32,128]{2,1,0:T(8,128)S(1)} %get-tuple-element.33), channel_id=1, source_target_pairs={{0,4},{4,0},{8,12},{12,8},{1,5},{5,1},{9,13},{13,9},{2,6},{6,2},{1... | collective-permute-start | bytes 933896 | tf_op jit(solution)/shard_map/ppermute | solution.py:894
  3.8 1.9 %collective-permute-start.2 = (f32[19,32,128]{2,1,0:T(8,128)S(1)}, f32[19,32,128]{2,1,0:T(8,128)S(1)}, u32[]{:S(2)}, u32[]{:S(2)}) collective-permute-start(f32[19,32,128]{2,1,0:T(8,128)S(1)} %get-tuple-element.34), channel_id=1, source_target_pairs={{0,0},{4,8},{8,4},{12,12},{1,1},{5,9},{9,5},{13,13},{2,2},{6,10},{... | collective-permute-start | bytes 933896 | tf_op jit(solution)/shard_map/ppermute | solution.py:894
  5.7 1.3 %collective-permute-start = (f32[304,128]{1,0:T(8,128)S(1)}, f32[304,128]{1,0:T(8,128)S(1)}, u32[]{:S(2)}, u32[]{:S(2)}) collective-permute-start(f32[304,128]{1,0:T(8,128)S(1)} %get-tuple-element.32), channel_id=1, source_target_pairs={{0,16},{16,0},{1,17},{17,1},{2,18},{18,2},{3,19},{19,3},{4,20},{20... | collective-permute-start | bytes 466952 | tf_op jit(solution)/shard_map/ppermute | solution.py:894
  7.0 0.0 collective-permute-start.3
  7.0 3.3 %collective-permute-start.4 = (f32[2,28,128]{2,1,0:T(8,128)S(1)}, f32[2,28,128]{2,1,0:T(8,128)S(1)}, u32[]{:S(2)}, u32[]{:S(2)}) collective-permute-start(f32[2,28,128]{2,1,0:T(8,128)S(1)} %get-tuple-element.36), channel_id=1, source_target_pairs={{0,0},{4,24},{8,20},{12,12},{16,16},{20,8},{24,4},{28,28},{1,1},{5... | collective-permute-start | bytes 86024 | tf_op jit(solution)/shard_map/ppermute | solution.py:894
  10.3 0.0 copy-done
  10.4 0.0 copy-done.1
  10.4 0.0 copy-done.2
  10.4 2.2 %own_ends.1 = (f32[1024,128]{1,0:T(8,128)S(1)}, f32[896,128]{1,0:T(8,128)S(1)}, bf16[3,3,512,256]{3,2,1,0:T(8,128)(2,1)S(1)}) custom-call(f32[3,1024,128]{2,1,0:T(8,128)S(1)} %bitcast.30, f32[3,1024,128]{2,1,0:T(8,128)S(1)} %bitcast.33, s32[1024,128]{1,0:T(8,128)S(1)} %bitcast.36, bf16[3,3,512,256]{3,2,1,0:T(8,128)(2,1)} %bitcast.38, ...), custom_call_target="tpu_custom_call" | custom-call | flops 10000000 | bytes 4000000 | tf_op jit(solution)/shard_map/own_ends/pallas_call | solution.py:865
  12.6 0.0 collective-permute-done.3.refs_3_
  12.6 2.4 %collective-permute-done.4.refs_4_ = f32[2,28,128]{2,1,0:T(8,128)S(1)} collective-permute-done((f32[2,28,128]{2,1,0:T(8,128)S(1)}, f32[2,28,128]{2,1,0:T(8,128)S(1)}, u32[]{:S(2)}, u32[]{:S(2)}) %collective-permute-start.4) | collective-permute-done | bytes 28704 | tf_op jit(solution)/shard_map/ppermute | solution.py:894
  15.0 0.0 collective-permute-done.refs_0_
  15.0 0.0 collective-permute-done.1.refs_1_
  15.0 0.0 collective-permute-done.2.refs_2_
  15.0 0.9 %unpack_faces.1 = (f32[7,2,64,128]{3,2,1,0:T(8,128)S(1)}, f32[7,2,288,128]{3,2,1,0:T(8,128)S(1)}, f32[128,896]{1,0:T(8,128)S(1)}, f32[16,896]{1,0:T(8,128)S(1)}, f32[16,896]{1,0:T(8,128)S(1)}) custom-call(f32[896,128]{1,0:T(8,128)S(1)} %get-tuple-element.31.own_packed, f32[304,128]{1,0:T(8,128)S(1)} %collective-permute-done.refs_0_, ...), custom_call_target="tpu_custom_call" | custom-call | tf_op jit(solution)/shard_map/unpack_faces/pallas_call | solution.py:896
  15.9 3.3 %collective-permute-start.5 = (f32[16,896]{1,0:T(8,128)S(1)}, f32[16,896]{1,0:T(8,128)S(1)}, u32[]{:S(2)}, u32[]{:S(2)}) collective-permute-start(f32[16,896]{1,0:T(8,128)S(1)} %get-tuple-element.43), channel_id=1, source_target_pairs={{0,1},{1,2},{2,3},{3,0},{4,5},{5,6},{6,7},{7,4},{8,9},{9,10},{10,1... | collective-permute-start | bytes 172040 | tf_op jit(solution)/shard_map/ppermute | solution.py:917
  19.2 0.0 collective-permute-start.6
  19.2 0.0 copy-start.3
  19.2 3.7 %march.1 = (f32[3,1024,128]{2,1,0:T(8,128)S(1)}, f32[3,1024,128]{2,1,0:T(8,128)S(1)}, f32[1,512]{1,0:T(1,128)S(1)}, s32[9,128]{1,0:T(8,128)S(1)}, f32[6,128]{1,0:T(8,128)S(1)}) custom-call(f32[3,1024,128]{2,1,0:T(8,128)S(1)} %bitcast.31, f32[3,1024,128]{2,1,0:T(8,128)S(1)} %bitcast.34, f32[1024,128]{1,0:T(8,128)S(1)} %get-tuple-element.30.coef_v, ...), custom_call_target="tpu_custom_call" | custom-call | flops 40000000 | bytes 10000000 | tf_op jit(solution)/shard_map/march/pallas_call | solution.py:921
  22.9 0.0 collective-permute-done.5.low_ref
  22.9 0.0 collective-permute-done.6.high_ref
  22.9 0.0 copy-done.3
  23.0 0.7 %finish_ends.1 = (f32[48,896]{1,0:T(8,128)S(1)}, f32[4,32]{1,0:T(4,128)S(1)}, f32[4,32]{1,0:T(4,128)S(1)}, f32[4,32]{1,0:T(4,128)S(1)}, f32[4,32]{1,0:T(4,128)S(1)}) custom-call(f32[128,896]{1,0:T(8,128)S(1)} %get-tuple-element.42.own_t, f32[16,896]{1,0:T(8,128)S(1)} %collective-permute-done.5.low_ref, f32[16,896]{1,0:T(8,128)S(1)} %collective-permute-done.6.high_ref, ...), custom_call_target="tpu_custom_call" | custom-call | tf_op jit(solution)/shard_map/finish_ends/pallas_call | solution.py:943
  23.6 0.7 %collective-permute-start.7 = (f32[4,32]{1,0:T(4,128)S(1)}, f32[4,32]{1,0:T(4,128)S(1)}, u32[]{:S(2)}, u32[]{:S(2)}) collective-permute-start(f32[4,32]{1,0:T(4,128)S(1)} %get-tuple-element.52), channel_id=1, source_target_pairs={{0,1},{1,0},{2,3},{3,2},{4,5},{5,4},{6,7},{7,6},{8,9},{9,8},{10,11... | collective-permute-start | bytes 1544 | tf_op jit(solution)/shard_map/ppermute | solution.py:974
  24.3 1.2 %collective-permute-start.8 = (f32[4,32]{1,0:T(4,128)S(1)}, f32[4,32]{1,0:T(4,128)S(1)}, u32[]{:S(2)}, u32[]{:S(2)}) collective-permute-start(f32[4,32]{1,0:T(4,128)S(1)} %get-tuple-element.53), channel_id=1, source_target_pairs={{0,2},{1,3},{2,0},{3,1},{4,6},{5,7},{6,4},{7,5},{8,10},{9,11},{10,... | collective-permute-start | bytes 1544 | tf_op jit(solution)/shard_map/ppermute | solution.py:974
  25.5 0.5 %collective-permute-start.9 = (f32[4,32]{1,0:T(4,128)S(1)}, f32[4,32]{1,0:T(4,128)S(1)}, u32[]{:S(2)}, u32[]{:S(2)}) collective-permute-start(f32[4,32]{1,0:T(4,128)S(1)} %get-tuple-element.54), channel_id=1, source_target_pairs={{0,3},{1,2},{2,1},{3,0},{4,7},{5,6},{6,5},{7,4},{8,11},{9,10},{10,... | collective-permute-start | bytes 1544 | tf_op jit(solution)/shard_map/ppermute | solution.py:974
  26.0 2.0 %write_out.1 = (f32[3,1024,128]{2,1,0:T(8,128)}, f32[3,1024,128]{2,1,0:T(8,128)}) custom-call(f32[3,1024,128]{2,1,0:T(8,128)S(1)} %get-tuple-element.40.e_s, f32[3,1024,128]{2,1,0:T(8,128)S(1)} %get-tuple-element.41.h_s, f32[48,896]{1,0:T(8,128)S(1)} %get-tuple-element.48.ends_ref), custom_call_target="tpu_custom_call" | custom-call | flops 10000000 | bytes 8000000 | tf_op jit(solution)/shard_map/write_out/pallas_call | solution.py:956
  28.0 0.0 collective-permute-done.7
  28.0 0.0 collective-permute-done.8
  28.0 0.5 %collective-permute-done.9 = f32[4,32]{1,0:T(4,128)S(1)} collective-permute-done((f32[4,32]{1,0:T(4,128)S(1)}, f32[4,32]{1,0:T(4,128)S(1)}, u32[]{:S(2)}, u32[]{:S(2)}) %collective-permute-start.9) | collective-permute-done | bytes 544 | tf_op jit(solution)/shard_map/ppermute | solution.py:974
  28.5 0.6 %add_bitcast_fusion = f32[32,4]{0,1:T(4,128)} fusion(f32[4,32]{1,0:T(4,128)S(1)} %collective-permute-done.9, f32[4,32]{1,0:T(4,128)S(1)} %collective-permute-done.8, f32[4,32]{1,0:T(4,128)S(1)} %get-tuple-element.51, f32[4,32]{1,0:T(4,128)S(1)} %collective-permute-done.7), kind=kLoop, calls=%fused_computation | loop fusion | flops 384 | bytes 2560 | tf_op jit(solution)/shard_map/transpose | solution.py:977
Async XLA Ops:
  0.6 9.7 %copy-start = (f32[3,32,16,256]{3,2,1,0:T(8,128)S(1)}, f32[3,32,16,256]{3,2,1,0:T(8,128)}, u32[]{:S(2)}) copy-start(f32[3,32,16,256]{3,2,1,0:T(8,128)} %param.8) | copy-start | bytes 4718596
  0.6 9.7 %copy-start.1 = (f32[3,32,16,256]{3,2,1,0:T(8,128)S(1)}, f32[3,32,16,256]{3,2,1,0:T(8,128)}, u32[]{:S(2)}) copy-start(f32[3,32,16,256]{3,2,1,0:T(8,128)} %param.9) | copy-start | bytes 4718596
  0.7 9.7 %copy-start.2 = (s32[32,16,256]{2,1,0:T(8,128)S(1)}, s32[32,16,256]{2,1,0:T(8,128)}, u32[]{:S(2)}) copy-start(s32[32,16,256]{2,1,0:T(8,128)} %param.11) | copy-start | bytes 1572868
  2.5 12.5 %collective-permute-start.1 = (f32[19,32,128]{2,1,0:T(8,128)S(1)}, f32[19,32,128]{2,1,0:T(8,128)S(1)}, u32[]{:S(2)}, u32[]{:S(2)}) collective-permute-start(f32[19,32,128]{2,1,0:T(8,128)S(1)} %get-tuple-element.33), channel_id=1, source_target_pairs={{0,4},{4,0},{8,12},{12,8},{1,5},{5,1},{9,13},{13,9},{2,6},{6,2},{1... | collective-permute-start | bytes 933896 | tf_op jit(solution)/shard_map/ppermute | solution.py:894
  3.8 11.2 %collective-permute-start.2 = (f32[19,32,128]{2,1,0:T(8,128)S(1)}, f32[19,32,128]{2,1,0:T(8,128)S(1)}, u32[]{:S(2)}, u32[]{:S(2)}) collective-permute-start(f32[19,32,128]{2,1,0:T(8,128)S(1)} %get-tuple-element.34), channel_id=1, source_target_pairs={{0,0},{4,8},{8,4},{12,12},{1,1},{5,9},{9,5},{13,13},{2,2},{6,10},{... | collective-permute-start | bytes 933896 | tf_op jit(solution)/shard_map/ppermute | solution.py:894
  5.7 9.2 %collective-permute-start = (f32[304,128]{1,0:T(8,128)S(1)}, f32[304,128]{1,0:T(8,128)S(1)}, u32[]{:S(2)}, u32[]{:S(2)}) collective-permute-start(f32[304,128]{1,0:T(8,128)S(1)} %get-tuple-element.32), channel_id=1, source_target_pairs={{0,16},{16,0},{1,17},{17,1},{2,18},{18,2},{3,19},{19,3},{4,20},{20... | collective-permute-start | bytes 466952 | tf_op jit(solution)/shard_map/ppermute | solution.py:894
  7.0 5.6 %collective-permute-start.3 = (f32[2,28,128]{2,1,0:T(8,128)S(1)}, f32[2,28,128]{2,1,0:T(8,128)S(1)}, u32[]{:S(2)}, u32[]{:S(2)}) collective-permute-start(f32[2,28,128]{2,1,0:T(8,128)S(1)} %get-tuple-element.35), channel_id=1, source_target_pairs={{0,20},{4,16},{8,28},{12,24},{16,4},{20,0},{24,12},{28,8},{1,21},{... | collective-permute-start | bytes 86024 | tf_op jit(solution)/shard_map/ppermute | solution.py:894
  7.0 7.9 %collective-permute-start.4 = (f32[2,28,128]{2,1,0:T(8,128)S(1)}, f32[2,28,128]{2,1,0:T(8,128)S(1)}, u32[]{:S(2)}, u32[]{:S(2)}) collective-permute-start(f32[2,28,128]{2,1,0:T(8,128)S(1)} %get-tuple-element.36), channel_id=1, source_target_pairs={{0,0},{4,24},{8,20},{12,12},{16,16},{20,8},{24,4},{28,28},{1,1},{5... | collective-permute-start | bytes 86024 | tf_op jit(solution)/shard_map/ppermute | solution.py:894
  15.9 7.0 %collective-permute-start.5 = (f32[16,896]{1,0:T(8,128)S(1)}, f32[16,896]{1,0:T(8,128)S(1)}, u32[]{:S(2)}, u32[]{:S(2)}) collective-permute-start(f32[16,896]{1,0:T(8,128)S(1)} %get-tuple-element.43), channel_id=1, source_target_pairs={{0,1},{1,2},{2,3},{3,0},{4,5},{5,6},{6,7},{7,4},{8,9},{9,10},{10,1... | collective-permute-start | bytes 172040 | tf_op jit(solution)/shard_map/ppermute | solution.py:917
  19.2 3.7 %collective-permute-start.6 = (f32[16,896]{1,0:T(8,128)S(1)}, f32[16,896]{1,0:T(8,128)S(1)}, u32[]{:S(2)}, u32[]{:S(2)}) collective-permute-start(f32[16,896]{1,0:T(8,128)S(1)} %get-tuple-element.44), channel_id=1, source_target_pairs={{0,3},{1,0},{2,1},{3,2},{4,7},{5,4},{6,5},{7,6},{8,11},{9,8},{10,9... | collective-permute-start | bytes 172040 | tf_op jit(solution)/shard_map/ppermute | solution.py:918
  19.2 3.7 %copy-start.3 = (s32[32,16]{0,1:T(8,128)S(1)}, s32[32,16]{0,1:T(8,128)}, u32[]{:S(2)}) copy-start(s32[32,16]{0,1:T(8,128)} %param.13) | copy-start | bytes 6148
  23.6 4.4 %collective-permute-start.7 = (f32[4,32]{1,0:T(4,128)S(1)}, f32[4,32]{1,0:T(4,128)S(1)}, u32[]{:S(2)}, u32[]{:S(2)}) collective-permute-start(f32[4,32]{1,0:T(4,128)S(1)} %get-tuple-element.52), channel_id=1, source_target_pairs={{0,1},{1,0},{2,3},{3,2},{4,5},{5,4},{6,7},{7,6},{8,9},{9,8},{10,11... | collective-permute-start | bytes 1544 | tf_op jit(solution)/shard_map/ppermute | solution.py:974
  24.3 3.7 %collective-permute-start.8 = (f32[4,32]{1,0:T(4,128)S(1)}, f32[4,32]{1,0:T(4,128)S(1)}, u32[]{:S(2)}, u32[]{:S(2)}) collective-permute-start(f32[4,32]{1,0:T(4,128)S(1)} %get-tuple-element.53), channel_id=1, source_target_pairs={{0,2},{1,3},{2,0},{3,1},{4,6},{5,7},{6,4},{7,5},{8,10},{9,11},{10,... | collective-permute-start | bytes 1544 | tf_op jit(solution)/shard_map/ppermute | solution.py:974
  25.5 3.0 %collective-permute-start.9 = (f32[4,32]{1,0:T(4,128)S(1)}, f32[4,32]{1,0:T(4,128)S(1)}, u32[]{:S(2)}, u32[]{:S(2)}) collective-permute-start(f32[4,32]{1,0:T(4,128)S(1)} %get-tuple-element.54), channel_id=1, source_target_pairs={{0,3},{1,2},{2,1},{3,0},{4,7},{5,6},{6,5},{7,4},{8,11},{9,10},{10,... | collective-permute-start | bytes 1544 | tf_op jit(solution)/shard_map/ppermute | solution.py:974

commit v9 on v8

--- a/solution.py
+++ b/solution.py
@@ -152,6 +152,9 @@
         def at(ref, c, which):
             return [ref[c, pl.ds(z * 8 + which, nx, stride=step), :] for z in range(lanes)]
 
+        def put(k, z, v):
+            out[pl.ds((k * lanes + z) * nx, nx), :] = v
+
         e_n = [at(e_b, c, near) for c in range(3)]
         h_n = [at(h_b, c, near) for c in range(3)]
         ex_f, ey_f, ez_f = (at(e_b, c, far) for c in range(3))
@@ -159,14 +162,15 @@
         ey_z = z_up(ey_f, lane_n)
         for z in range(lanes):
             for c in range(3):
-                out[c * lanes + z] = e_n[c][z]
-            out[3 * lanes + z] = h_n[0][z] - down * ez_f[z]
-            out[4 * lanes + z] = h_n[1][z]
-            out[5 * lanes + z] = h_n[2][z] + down * ex_f[z]
-            out[6 * lanes + z] = coef_of(m_b[pl.ds(z * 8 + near, nx, stride=step), :], table)
-            out[7 * lanes + z] = hx_f[z] + magnetic_step * (ez_f[z] + (ey_z[z] - ey_f[z]))
-            out[8 * lanes + z] = hz_f[z] - magnetic_step * ((row_up(ey_f[z]) - ey_f[z]) + ex_f[z])
-        out[9 * lanes] = ey_f[0]
+                put(c, z, e_n[c][z])
+            put(3, z, h_n[0][z] - down * ez_f[z])
+            put(4, z, h_n[1][z])
+            put(5, z, h_n[2][z] + down * ex_f[z])
+            put(6, z, coef_of(m_b[pl.ds(z * 8 + near, nx, stride=step), :], table))
+            put(7, z, hx_f[z] + magnetic_step * (ez_f[z] + (ey_z[z] - ey_f[z])))
+            put(8, z, hz_f[z] - magnetic_step * ((row_up(ey_f[z]) - ey_f[z]) + ex_f[z]))
+        first = jnp.concatenate([ey_f[0], jnp.zeros((128 - nx, 128), jnp.float32)], axis=0)
+        out[pl.ds(9 * lanes * nx, 8), :] = jnp.transpose(first)[0:8]
     for i, odd in enumerate(xs):
         for copy in copies[3 * (len(ys) + i) : 3 * (len(ys) + i) + 3]:
             copy.wait()
@@ -338,11 +342,11 @@
             for k, f in enumerate((0, 1, 2, 3, 4, 5, 6, 3, 5)):
                 r = near if k < FIELDS else far
                 yh[f, z, pl.ds(2 * HALO + r, nx, stride=HALO), :] = jnp.where(
-                    ok, msg[k * lanes + z], 0.0
+                    ok, msg[pl.ds((k * lanes + z) * nx, nx), :], 0.0
                 )
-        y_raw[pl.ds(2 * HALO + far, nx, stride=HALO), :] = jnp.where(
-            ok & (far == HALO - 2), msg[9 * lanes], 0.0
-        )
+        raw = jnp.where(ok & (far == HALO - 2), msg[pl.ds(9 * lanes * nx, 8), :], 0.0)
+        raw = jnp.concatenate([raw, jnp.zeros((120, 128), jnp.float32)], axis=0)
+        y_raw[pl.ds(2 * HALO + far, nx, stride=HALO), :] = jnp.transpose(raw)[0:nx]
     for i, ox in enumerate(xs):
         for j, oy in enumerate(ys):
             ok = has_partner(gx, sizes[0], ox) & has_partner(gy, sizes[1], oy)
@@ -834,7 +838,7 @@
     block, cube = jax.ShapeDtypeStruct, pltpu.VMEM
 
     shapes = [block((9 * plane + ny, 128), f32) for _ in xs]
-    shapes += [block((9 * lanes + 1, nx, 128), f32) for _ in ys]
+    shapes += [block((9 * lanes * nx + 8, 128), f32) for _ in ys]
     shapes += [block((lanes, 4 * FIELDS, 128), f32) for _ in xs for _ in ys]
     buffers = []
     for _ in xs:

time: 29.3 us -> 28.9 us (0.986)
  no operation moved by 1% of the time
where the time goes in v9:
time: 28.9 us; the launch traced here: 28.7 us
  starting transfers between devices  13.5 us (47%)
  Pallas kernels  11.2 us (39%)
  waiting for transfers between devices  2.62 us (9%)
  between operations  0.79 us (3%)
  other arithmetic  0.58 us (2%)
    ppermute x5, starting transfers between devices, body(): lax.ppermute(msg, axis, pairs)  7.87 us
    pallas_call x1, Pallas kernels, body(): pl.pallas_call(functools.partial(march, dims, sizes), out_shape=[cube(e_v...  3.63 us
    ppermute x1, starting transfers between devices, body(): low = lax.ppermute(up, 'gz', [(i, (i + 1) % parts) for i in range(parts)])  3.31 us
    ppermute x3, starting transfers between devices, body(): lax.ppermute(chunks[shift], 'gz', [(i, partner_of(i, shift, parts)) for i...  2.35 us
    pallas_call x1, Pallas kernels, body(): pl.pallas_call(functools.partial(own_ends, dims), out_shape=[cube(m_v.sha...  2.22 us
    ppermute x5, waiting for transfers between devices, body(): lax.ppermute(msg, axis, pairs)  2.11 us
    pallas_call x1, Pallas kernels, body(): pl.pallas_call(functools.partial(write_out, dims), out_shape=[block(e_v.s...  2.01 us
    pallas_call x1, Pallas kernels, body(): pl.pallas_call(functools.partial(send_faces, dims, sizes), out_shape=shap...  1.8 us
  transfers between devices with their start and end apart: 10, of which 2 were waited for; matrix products, arithmetic and copies ran while one was open for 0% of the time, Pallas kernels for 27%

profile of v9, /device:TPU:17, one launch (start us, length us, event | category | flops | bytes accessed | tf_op | source)
XLA Modules:
  0.0 28.7 jit_solution(10943602041730408348)
XLA Ops:
  0.6 0.0 copy-start
  0.6 0.0 copy-start.1
  0.7 0.0 copy-start.2
  0.7 1.8 %send_faces.1 = (f32[304,128]{1,0:T(8,128)S(1)}, f32[584,128]{1,0:T(8,128)S(1)}, f32[584,128]{1,0:T(8,128)S(1)}, f32[2,28,128]{2,1,0:T(8,128)S(1)}, f32[2,28,128]{2,1,0:T(8,128)S(1)}, /*index=5*/f32[8,128]{1,0:T(8,128)S(1)}) custom-call(f32[3,32,2,2,8,128]{5,4,3,2,1,0:T(8,128)} %bitcast.29, f32[3,32,2,2,8,128]{5,4,3,2,1,0:T(8,128)} %bitcast.32, ...), custom_call_target="tpu_custom_call" | custom-call | tf_op jit(solution)/shard_map/send_faces/pallas_call | solution.py:852
  2.5 1.4 %collective-permute-start.1 = (f32[584,128]{1,0:T(8,128)S(1)}, f32[584,128]{1,0:T(8,128)S(1)}, u32[]{:S(2)}, u32[]{:S(2)}) collective-permute-start(f32[584,128]{1,0:T(8,128)S(1)} %get-tuple-element.33), channel_id=1, source_target_pairs={{0,4},{4,0},{8,12},{12,8},{1,5},{5,1},{9,13},{13,9},{2,6},{6,2},{1... | collective-permute-start | bytes 897032 | tf_op jit(solution)/shard_map/ppermute | solution.py:898
  3.8 1.9 %collective-permute-start.2 = (f32[584,128]{1,0:T(8,128)S(1)}, f32[584,128]{1,0:T(8,128)S(1)}, u32[]{:S(2)}, u32[]{:S(2)}) collective-permute-start(f32[584,128]{1,0:T(8,128)S(1)} %get-tuple-element.34), channel_id=1, source_target_pairs={{0,0},{4,8},{8,4},{12,12},{1,1},{5,9},{9,5},{13,13},{2,2},{6,10},{... | collective-permute-start | bytes 897032 | tf_op jit(solution)/shard_map/ppermute | solution.py:898
  5.7 1.3 %collective-permute-start = (f32[304,128]{1,0:T(8,128)S(1)}, f32[304,128]{1,0:T(8,128)S(1)}, u32[]{:S(2)}, u32[]{:S(2)}) collective-permute-start(f32[304,128]{1,0:T(8,128)S(1)} %get-tuple-element.32), channel_id=1, source_target_pairs={{0,16},{16,0},{1,17},{17,1},{2,18},{18,2},{3,19},{19,3},{4,20},{20... | collective-permute-start | bytes 466952 | tf_op jit(solution)/shard_map/ppermute | solution.py:898
  7.1 0.0 collective-permute-start.3
  7.1 3.3 %collective-permute-start.4 = (f32[2,28,128]{2,1,0:T(8,128)S(1)}, f32[2,28,128]{2,1,0:T(8,128)S(1)}, u32[]{:S(2)}, u32[]{:S(2)}) collective-permute-start(f32[2,28,128]{2,1,0:T(8,128)S(1)} %get-tuple-element.36), channel_id=1, source_target_pairs={{0,0},{4,24},{8,20},{12,12},{16,16},{20,8},{24,4},{28,28},{1,1},{5... | collective-permute-start | bytes 86024 | tf_op jit(solution)/shard_map/ppermute | solution.py:898
  10.4 0.0 copy-done
  10.4 0.0 copy-done.1
  10.4 0.0 copy-done.2
  10.4 2.2 %own_ends.1 = (f32[1024,128]{1,0:T(8,128)S(1)}, f32[896,128]{1,0:T(8,128)S(1)}, bf16[3,3,512,256]{3,2,1,0:T(8,128)(2,1)S(1)}) custom-call(f32[3,1024,128]{2,1,0:T(8,128)S(1)} %bitcast.30, f32[3,1024,128]{2,1,0:T(8,128)S(1)} %bitcast.33, s32[1024,128]{1,0:T(8,128)S(1)} %bitcast.36, bf16[3,3,512,256]{3,2,1,0:T(8,128)(2,1)} %bitcast.38, ...), custom_call_target="tpu_custom_call" | custom-call | flops 10000000 | bytes 4000000 | tf_op jit(solution)/shard_map/own_ends/pallas_call | solution.py:869
  12.6 0.0 collective-permute-done.3.refs_3_
  12.6 2.1 %collective-permute-done.4.refs_4_ = f32[2,28,128]{2,1,0:T(8,128)S(1)} collective-permute-done((f32[2,28,128]{2,1,0:T(8,128)S(1)}, f32[2,28,128]{2,1,0:T(8,128)S(1)}, u32[]{:S(2)}, u32[]{:S(2)}) %collective-permute-start.4) | collective-permute-done | bytes 28704 | tf_op jit(solution)/shard_map/ppermute | solution.py:898
  14.7 0.0 collective-permute-done.refs_0_
  14.7 0.0 collective-permute-done.1.refs_1_
  14.7 0.0 collective-permute-done.2.refs_2_
  14.7 0.9 %unpack_faces.1 = (f32[7,2,64,128]{3,2,1,0:T(8,128)S(1)}, f32[7,2,288,128]{3,2,1,0:T(8,128)S(1)}, f32[128,896]{1,0:T(8,128)S(1)}, f32[16,896]{1,0:T(8,128)S(1)}, f32[16,896]{1,0:T(8,128)S(1)}) custom-call(f32[896,128]{1,0:T(8,128)S(1)} %get-tuple-element.31.own_packed, f32[304,128]{1,0:T(8,128)S(1)} %collective-permute-done.refs_0_, ...), custom_call_target="tpu_custom_call" | custom-call | tf_op jit(solution)/shard_map/unpack_faces/pallas_call | solution.py:900
  15.6 3.3 %collective-permute-start.5 = (f32[16,896]{1,0:T(8,128)S(1)}, f32[16,896]{1,0:T(8,128)S(1)}, u32[]{:S(2)}, u32[]{:S(2)}) collective-permute-start(f32[16,896]{1,0:T(8,128)S(1)} %get-tuple-element.43), channel_id=1, source_target_pairs={{0,1},{1,2},{2,3},{3,0},{4,5},{5,6},{6,7},{7,4},{8,9},{9,10},{10,1... | collective-permute-start | bytes 172040 | tf_op jit(solution)/shard_map/ppermute | solution.py:921
  18.9 0.0 collective-permute-start.6
  18.9 0.0 copy-start.3
  18.9 3.6 %march.1 = (f32[3,1024,128]{2,1,0:T(8,128)S(1)}, f32[3,1024,128]{2,1,0:T(8,128)S(1)}, f32[1,512]{1,0:T(1,128)S(1)}, s32[9,128]{1,0:T(8,128)S(1)}, f32[6,128]{1,0:T(8,128)S(1)}) custom-call(f32[3,1024,128]{2,1,0:T(8,128)S(1)} %bitcast.31, f32[3,1024,128]{2,1,0:T(8,128)S(1)} %bitcast.34, f32[1024,128]{1,0:T(8,128)S(1)} %get-tuple-element.30.coef_v, ...), custom_call_target="tpu_custom_call" | custom-call | flops 40000000 | bytes 10000000 | tf_op jit(solution)/shard_map/march/pallas_call | solution.py:925
  22.6 0.0 collective-permute-done.5.low_ref
  22.6 0.0 collective-permute-done.6.high_ref
  22.6 0.0 copy-done.3
  22.6 0.7 %finish_ends.1 = (f32[48,896]{1,0:T(8,128)S(1)}, f32[4,32]{1,0:T(4,128)S(1)}, f32[4,32]{1,0:T(4,128)S(1)}, f32[4,32]{1,0:T(4,128)S(1)}, f32[4,32]{1,0:T(4,128)S(1)}) custom-call(f32[128,896]{1,0:T(8,128)S(1)} %get-tuple-element.42.own_t, f32[16,896]{1,0:T(8,128)S(1)} %collective-permute-done.5.low_ref, f32[16,896]{1,0:T(8,128)S(1)} %collective-permute-done.6.high_ref, ...), custom_call_target="tpu_custom_call" | custom-call | tf_op jit(solution)/shard_map/finish_ends/pallas_call | solution.py:947
  23.2 0.7 %collective-permute-start.7 = (f32[4,32]{1,0:T(4,128)S(1)}, f32[4,32]{1,0:T(4,128)S(1)}, u32[]{:S(2)}, u32[]{:S(2)}) collective-permute-start(f32[4,32]{1,0:T(4,128)S(1)} %get-tuple-element.52), channel_id=1, source_target_pairs={{0,1},{1,0},{2,3},{3,2},{4,5},{5,4},{6,7},{7,6},{8,9},{9,8},{10,11... | collective-permute-start | bytes 1544 | tf_op jit(solution)/shard_map/ppermute | solution.py:978
  23.9 1.2 %collective-permute-start.8 = (f32[4,32]{1,0:T(4,128)S(1)}, f32[4,32]{1,0:T(4,128)S(1)}, u32[]{:S(2)}, u32[]{:S(2)}) collective-permute-start(f32[4,32]{1,0:T(4,128)S(1)} %get-tuple-element.53), channel_id=1, source_target_pairs={{0,2},{1,3},{2,0},{3,1},{4,6},{5,7},{6,4},{7,5},{8,10},{9,11},{10,... | collective-permute-start | bytes 1544 | tf_op jit(solution)/shard_map/ppermute | solution.py:978
  25.1 0.5 %collective-permute-start.9 = (f32[4,32]{1,0:T(4,128)S(1)}, f32[4,32]{1,0:T(4,128)S(1)}, u32[]{:S(2)}, u32[]{:S(2)}) collective-permute-start(f32[4,32]{1,0:T(4,128)S(1)} %get-tuple-element.54), channel_id=1, source_target_pairs={{0,3},{1,2},{2,1},{3,0},{4,7},{5,6},{6,5},{7,4},{8,11},{9,10},{10,... | collective-permute-start | bytes 1544 | tf_op jit(solution)/shard_map/ppermute | solution.py:978
  25.6 2.0 %write_out.1 = (f32[3,1024,128]{2,1,0:T(8,128)}, f32[3,1024,128]{2,1,0:T(8,128)}) custom-call(f32[3,1024,128]{2,1,0:T(8,128)S(1)} %get-tuple-element.40.e_s, f32[3,1024,128]{2,1,0:T(8,128)S(1)} %get-tuple-element.41.h_s, f32[48,896]{1,0:T(8,128)S(1)} %get-tuple-element.48.ends_ref), custom_call_target="tpu_custom_call" | custom-call | flops 10000000 | bytes 8000000 | tf_op jit(solution)/shard_map/write_out/pallas_call | solution.py:960
  27.6 0.0 collective-permute-done.7
  27.6 0.0 collective-permute-done.8
  27.6 0.5 %collective-permute-done.9 = f32[4,32]{1,0:T(4,128)S(1)} collective-permute-done((f32[4,32]{1,0:T(4,128)S(1)}, f32[4,32]{1,0:T(4,128)S(1)}, u32[]{:S(2)}, u32[]{:S(2)}) %collective-permute-start.9) | collective-permute-done | bytes 544 | tf_op jit(solution)/shard_map/ppermute | solution.py:978
  28.1 0.6 %add_bitcast_fusion = f32[32,4]{0,1:T(4,128)} fusion(f32[4,32]{1,0:T(4,128)S(1)} %collective-permute-done.9, f32[4,32]{1,0:T(4,128)S(1)} %collective-permute-done.8, f32[4,32]{1,0:T(4,128)S(1)} %get-tuple-element.51, f32[4,32]{1,0:T(4,128)S(1)} %collective-permute-done.7), kind=kLoop, calls=%fused_computation | loop fusion | flops 384 | bytes 2560 | tf_op jit(solution)/shard_map/transpose | solution.py:981
Async XLA Ops:
  0.6 9.7 %copy-start = (f32[3,32,16,256]{3,2,1,0:T(8,128)S(1)}, f32[3,32,16,256]{3,2,1,0:T(8,128)}, u32[]{:S(2)}) copy-start(f32[3,32,16,256]{3,2,1,0:T(8,128)} %param.8) | copy-start | bytes 4718596
  0.6 9.7 %copy-start.1 = (f32[3,32,16,256]{3,2,1,0:T(8,128)S(1)}, f32[3,32,16,256]{3,2,1,0:T(8,128)}, u32[]{:S(2)}) copy-start(f32[3,32,16,256]{3,2,1,0:T(8,128)} %param.9) | copy-start | bytes 4718596
  0.7 9.7 %copy-start.2 = (s32[32,16,256]{2,1,0:T(8,128)S(1)}, s32[32,16,256]{2,1,0:T(8,128)}, u32[]{:S(2)}) copy-start(s32[32,16,256]{2,1,0:T(8,128)} %param.11) | copy-start | bytes 1572868
  2.5 12.3 %collective-permute-start.1 = (f32[584,128]{1,0:T(8,128)S(1)}, f32[584,128]{1,0:T(8,128)S(1)}, u32[]{:S(2)}, u32[]{:S(2)}) collective-permute-start(f32[584,128]{1,0:T(8,128)S(1)} %get-tuple-element.33), channel_id=1, source_target_pairs={{0,4},{4,0},{8,12},{12,8},{1,5},{5,1},{9,13},{13,9},{2,6},{6,2},{1... | collective-permute-start | bytes 897032 | tf_op jit(solution)/shard_map/ppermute | solution.py:898
  3.8 10.9 %collective-permute-start.2 = (f32[584,128]{1,0:T(8,128)S(1)}, f32[584,128]{1,0:T(8,128)S(1)}, u32[]{:S(2)}, u32[]{:S(2)}) collective-permute-start(f32[584,128]{1,0:T(8,128)S(1)} %get-tuple-element.34), channel_id=1, source_target_pairs={{0,0},{4,8},{8,4},{12,12},{1,1},{5,9},{9,5},{13,13},{2,2},{6,10},{... | collective-permute-start | bytes 897032 | tf_op jit(solution)/shard_map/ppermute | solution.py:898
  5.7 9.0 %collective-permute-start = (f32[304,128]{1,0:T(8,128)S(1)}, f32[304,128]{1,0:T(8,128)S(1)}, u32[]{:S(2)}, u32[]{:S(2)}) collective-permute-start(f32[304,128]{1,0:T(8,128)S(1)} %get-tuple-element.32), channel_id=1, source_target_pairs={{0,16},{16,0},{1,17},{17,1},{2,18},{18,2},{3,19},{19,3},{4,20},{20... | collective-permute-start | bytes 466952 | tf_op jit(solution)/shard_map/ppermute | solution.py:898
  7.1 5.6 %collective-permute-start.3 = (f32[2,28,128]{2,1,0:T(8,128)S(1)}, f32[2,28,128]{2,1,0:T(8,128)S(1)}, u32[]{:S(2)}, u32[]{:S(2)}) collective-permute-start(f32[2,28,128]{2,1,0:T(8,128)S(1)} %get-tuple-element.35), channel_id=1, source_target_pairs={{0,20},{4,16},{8,28},{12,24},{16,4},{20,0},{24,12},{28,8},{1,21},{... | collective-permute-start | bytes 86024 | tf_op jit(solution)/shard_map/ppermute | solution.py:898
  7.1 7.7 %collective-permute-start.4 = (f32[2,28,128]{2,1,0:T(8,128)S(1)}, f32[2,28,128]{2,1,0:T(8,128)S(1)}, u32[]{:S(2)}, u32[]{:S(2)}) collective-permute-start(f32[2,28,128]{2,1,0:T(8,128)S(1)} %get-tuple-element.36), channel_id=1, source_target_pairs={{0,0},{4,24},{8,20},{12,12},{16,16},{20,8},{24,4},{28,28},{1,1},{5... | collective-permute-start | bytes 86024 | tf_op jit(solution)/shard_map/ppermute | solution.py:898
  15.6 7.0 %collective-permute-start.5 = (f32[16,896]{1,0:T(8,128)S(1)}, f32[16,896]{1,0:T(8,128)S(1)}, u32[]{:S(2)}, u32[]{:S(2)}) collective-permute-start(f32[16,896]{1,0:T(8,128)S(1)} %get-tuple-element.43), channel_id=1, source_target_pairs={{0,1},{1,2},{2,3},{3,0},{4,5},{5,6},{6,7},{7,4},{8,9},{9,10},{10,1... | collective-permute-start | bytes 172040 | tf_op jit(solution)/shard_map/ppermute | solution.py:921
  18.9 3.7 %collective-permute-start.6 = (f32[16,896]{1,0:T(8,128)S(1)}, f32[16,896]{1,0:T(8,128)S(1)}, u32[]{:S(2)}, u32[]{:S(2)}) collective-permute-start(f32[16,896]{1,0:T(8,128)S(1)} %get-tuple-element.44), channel_id=1, source_target_pairs={{0,3},{1,0},{2,1},{3,2},{4,7},{5,4},{6,5},{7,6},{8,11},{9,8},{10,9... | collective-permute-start | bytes 172040 | tf_op jit(solution)/shard_map/ppermute | solution.py:922
  18.9 3.7 %copy-start.3 = (s32[32,16]{0,1:T(8,128)S(1)}, s32[32,16]{0,1:T(8,128)}, u32[]{:S(2)}) copy-start(s32[32,16]{0,1:T(8,128)} %param.13) | copy-start | bytes 6148
  23.2 4.4 %collective-permute-start.7 = (f32[4,32]{1,0:T(4,128)S(1)}, f32[4,32]{1,0:T(4,128)S(1)}, u32[]{:S(2)}, u32[]{:S(2)}) collective-permute-start(f32[4,32]{1,0:T(4,128)S(1)} %get-tuple-element.52), channel_id=1, source_target_pairs={{0,1},{1,0},{2,3},{3,2},{4,5},{5,4},{6,7},{7,6},{8,9},{9,8},{10,11... | collective-permute-start | bytes 1544 | tf_op jit(solution)/shard_map/ppermute | solution.py:978
  23.9 3.7 %collective-permute-start.8 = (f32[4,32]{1,0:T(4,128)S(1)}, f32[4,32]{1,0:T(4,128)S(1)}, u32[]{:S(2)}, u32[]{:S(2)}) collective-permute-start(f32[4,32]{1,0:T(4,128)S(1)} %get-tuple-element.53), channel_id=1, source_target_pairs={{0,2},{1,3},{2,0},{3,1},{4,6},{5,7},{6,4},{7,5},{8,10},{9,11},{10,... | collective-permute-start | bytes 1544 | tf_op jit(solution)/shard_map/ppermute | solution.py:978
  25.1 3.0 %collective-permute-start.9 = (f32[4,32]{1,0:T(4,128)S(1)}, f32[4,32]{1,0:T(4,128)S(1)}, u32[]{:S(2)}, u32[]{:S(2)}) collective-permute-start(f32[4,32]{1,0:T(4,128)S(1)} %get-tuple-element.54), channel_id=1, source_target_pairs={{0,3},{1,2},{2,1},{3,0},{4,7},{5,6},{6,5},{7,4},{8,11},{9,10},{10,... | collective-permute-start | bytes 1544 | tf_op jit(solution)/shard_map/ppermute | solution.py:978

commit v10 on v9

--- a/solution.py
+++ b/solution.py
@@ -113,8 +113,9 @@
         for k, ref in enumerate((e_ref, h_ref, m_ref)):
             src = ref.at[:, t, :, pl.ds(r, 2), :] if k == 2 else ref.at[:, :, t, :, pl.ds(r, 2), :]
             dst = y_bufs[3 * i + k]
-            dst = dst.reshape(*dst.shape[:-2], nx, lanes, 8, 128)
-            start(src, dst.at[:, :, pl.ds(0, 2), :] if k == 2 else dst.at[:, :, :, pl.ds(0, 2), :])
+            dst = dst.reshape(*dst.shape[:-2], nx + 1, lanes, 8, 128)
+            here = (pl.ds(0, nx), slice(None), pl.ds(0, 2), slice(None))
+            start(src, dst.at[here] if k == 2 else dst.at[(slice(None), *here)])
     for i, odd in enumerate(xs):
         first = pl.ds(jnp.where(sends_up(gx, odd), nx - 2, 0), 2)
         for k, ref in enumerate((e_ref, h_ref, m_ref)):
@@ -769,7 +770,8 @@
         rows_ref[8 * c : 8 * c + 8, :] = jnp.where(row < 4, results[1][c], results[0][c])
     line = jnp.sum(total, axis=0, keepdims=True)
     column = columns_of([(line_ref[...], ny, 0), (line, step, 2 * step + HALO)], nx, ny)
-    turned[...] = column * mask_ref[...].astype(jnp.float32)
+    turned[0:ny, :] = column * mask_ref[...].astype(jnp.float32)
+    turned[ny:, :] = jnp.zeros((8, nx), jnp.float32)
     width = ny // parts
     for shift in range(parts):
         owner = partner_of(gz, shift, parts)
@@ -845,7 +847,7 @@
         tile = (2, tiles, lanes, 8, 128)
         buffers += [cube((3, *tile), f32), cube((3, *tile), f32), cube(tile, i32)]
     for _ in ys:
-        tile = (nx * lanes * 8, 128)
+        tile = ((nx + 1) * lanes * 8, 128)
         buffers += [cube((3, *tile), f32), cube((3, *tile), f32), cube(tile, i32)]
     n_copies = 3 * (len(xs) + len(ys)) + 1
     shapes += [block((permittivity.shape[0], 128), f32)]
@@ -951,7 +953,7 @@
         out_specs=[VM] * (1 + parts),
         scratch_shapes=[
             pltpu.VMEM((2, FIELDS, 8, padded), f32),
-            pltpu.VMEM((ny, nx), f32),
+            pltpu.VMEM((ny + 8, nx), f32),
             pltpu.VMEM((48, padded), f32),
         ],
         compiler_params=params(),

time: 28.9 us -> 28.9 us (level)
  transfers between devices with their start and end apart: 10 -> 10, of which waited for: 2 -> 3; matrix products, arithmetic and copies ran while one was open for 0% -> 0% of each run, Pallas kernels for 27% -> 27%
where the time goes in v10:
time: 28.9 us; the launch traced here: 28.6 us
  starting transfers between devices  13.5 us (47%)
  Pallas kernels  11.1 us (38%)
  waiting for transfers between devices  2.68 us (9%)
  between operations  0.77 us (3%)
  other arithmetic  0.58 us (2%)
    ppermute x5, starting transfers between devices, body(): lax.ppermute(msg, axis, pairs)  7.87 us
    pallas_call x1, Pallas kernels, body(): pl.pallas_call(functools.partial(march, dims, sizes), out_shape=[cube(e_v...  3.52 us
    ppermute x1, starting transfers between devices, body(): low = lax.ppermute(up, 'gz', [(i, (i + 1) % parts) for i in range(parts)])  3.31 us
    ppermute x3, starting transfers between devices, body(): lax.ppermute(chunks[shift], 'gz', [(i, partner_of(i, shift, parts)) for i...  2.3 us
    pallas_call x1, Pallas kernels, body(): pl.pallas_call(functools.partial(own_ends, dims), out_shape=[cube(m_v.sha...  2.22 us
    ppermute x5, waiting for transfers between devices, body(): lax.ppermute(msg, axis, pairs)  2.11 us
    pallas_call x1, Pallas kernels, body(): pl.pallas_call(functools.partial(write_out, dims), out_shape=[block(e_v.s...  2.01 us
    pallas_call x1, Pallas kernels, body(): pl.pallas_call(functools.partial(send_faces, dims, sizes), out_shape=shap...  1.8 us
  transfers between devices with their start and end apart: 10, of which 3 were waited for; matrix products, arithmetic and copies ran while one was open for 0% of the time, Pallas kernels for 27%

profile of v10, /device:TPU:17, one launch (start us, length us, event | category | flops | bytes accessed | tf_op | source)
XLA Modules:
  0.0 28.6 jit_solution(2446506302997600414)
XLA Ops:
  0.6 0.0 copy-start
  0.6 0.0 copy-start.1
  0.7 0.0 copy-start.2
  0.7 1.8 %send_faces.1 = (f32[304,128]{1,0:T(8,128)S(1)}, f32[584,128]{1,0:T(8,128)S(1)}, f32[584,128]{1,0:T(8,128)S(1)}, f32[2,28,128]{2,1,0:T(8,128)S(1)}, f32[2,28,128]{2,1,0:T(8,128)S(1)}, /*index=5*/f32[8,128]{1,0:T(8,128)S(1)}) custom-call(f32[3,32,2,2,8,128]{5,4,3,2,1,0:T(8,128)} %bitcast.29, f32[3,32,2,2,8,128]{5,4,3,2,1,0:T(8,128)} %bitcast.32, ...), custom_call_target="tpu_custom_call" | custom-call | tf_op jit(solution)/shard_map/send_faces/pallas_call | solution.py:854
  2.5 1.4 %collective-permute-start.1 = (f32[584,128]{1,0:T(8,128)S(1)}, f32[584,128]{1,0:T(8,128)S(1)}, u32[]{:S(2)}, u32[]{:S(2)}) collective-permute-start(f32[584,128]{1,0:T(8,128)S(1)} %get-tuple-element.33), channel_id=1, source_target_pairs={{0,4},{4,0},{8,12},{12,8},{1,5},{5,1},{9,13},{13,9},{2,6},{6,2},{1... | collective-permute-start | bytes 897032 | tf_op jit(solution)/shard_map/ppermute | solution.py:900
  3.8 1.9 %collective-permute-start.2 = (f32[584,128]{1,0:T(8,128)S(1)}, f32[584,128]{1,0:T(8,128)S(1)}, u32[]{:S(2)}, u32[]{:S(2)}) collective-permute-start(f32[584,128]{1,0:T(8,128)S(1)} %get-tuple-element.34), channel_id=1, source_target_pairs={{0,0},{4,8},{8,4},{12,12},{1,1},{5,9},{9,5},{13,13},{2,2},{6,10},{... | collective-permute-start | bytes 897032 | tf_op jit(solution)/shard_map/ppermute | solution.py:900
  5.7 1.3 %collective-permute-start = (f32[304,128]{1,0:T(8,128)S(1)}, f32[304,128]{1,0:T(8,128)S(1)}, u32[]{:S(2)}, u32[]{:S(2)}) collective-permute-start(f32[304,128]{1,0:T(8,128)S(1)} %get-tuple-element.32), channel_id=1, source_target_pairs={{0,16},{16,0},{1,17},{17,1},{2,18},{18,2},{3,19},{19,3},{4,20},{20... | collective-permute-start | bytes 466952 | tf_op jit(solution)/shard_map/ppermute | solution.py:900
  7.1 0.0 collective-permute-start.3
  7.1 3.3 %collective-permute-start.4 = (f32[2,28,128]{2,1,0:T(8,128)S(1)}, f32[2,28,128]{2,1,0:T(8,128)S(1)}, u32[]{:S(2)}, u32[]{:S(2)}) collective-permute-start(f32[2,28,128]{2,1,0:T(8,128)S(1)} %get-tuple-element.36), channel_id=1, source_target_pairs={{0,0},{4,24},{8,20},{12,12},{16,16},{20,8},{24,4},{28,28},{1,1},{5... | collective-permute-start | bytes 86024 | tf_op jit(solution)/shard_map/ppermute | solution.py:900
  10.4 0.0 copy-done
  10.4 0.0 copy-done.1
  10.4 0.0 copy-done.2
  10.4 2.2 %own_ends.1 = (f32[1024,128]{1,0:T(8,128)S(1)}, f32[896,128]{1,0:T(8,128)S(1)}, bf16[3,3,512,256]{3,2,1,0:T(8,128)(2,1)S(1)}) custom-call(f32[3,1024,128]{2,1,0:T(8,128)S(1)} %bitcast.30, f32[3,1024,128]{2,1,0:T(8,128)S(1)} %bitcast.33, s32[1024,128]{1,0:T(8,128)S(1)} %bitcast.36, bf16[3,3,512,256]{3,2,1,0:T(8,128)(2,1)} %bitcast.38, ...), custom_call_target="tpu_custom_call" | custom-call | flops 10000000 | bytes 4000000 | tf_op jit(solution)/shard_map/own_ends/pallas_call | solution.py:871
  12.6 0.0 collective-permute-done.3.refs_3_
  12.6 2.1 %collective-permute-done.4.refs_4_ = f32[2,28,128]{2,1,0:T(8,128)S(1)} collective-permute-done((f32[2,28,128]{2,1,0:T(8,128)S(1)}, f32[2,28,128]{2,1,0:T(8,128)S(1)}, u32[]{:S(2)}, u32[]{:S(2)}) %collective-permute-start.4) | collective-permute-done | bytes 28704 | tf_op jit(solution)/shard_map/ppermute | solution.py:900
  14.7 0.0 collective-permute-done.refs_0_
  14.7 0.0 collective-permute-done.1.refs_1_
  14.7 0.0 collective-permute-done.2.refs_2_
  14.7 0.9 %unpack_faces.1 = (f32[7,2,64,128]{3,2,1,0:T(8,128)S(1)}, f32[7,2,288,128]{3,2,1,0:T(8,128)S(1)}, f32[128,896]{1,0:T(8,128)S(1)}, f32[16,896]{1,0:T(8,128)S(1)}, f32[16,896]{1,0:T(8,128)S(1)}) custom-call(f32[896,128]{1,0:T(8,128)S(1)} %get-tuple-element.31.own_packed, f32[304,128]{1,0:T(8,128)S(1)} %collective-permute-done.refs_0_, ...), custom_call_target="tpu_custom_call" | custom-call | tf_op jit(solution)/shard_map/unpack_faces/pallas_call | solution.py:902
  15.6 3.3 %collective-permute-start.5 = (f32[16,896]{1,0:T(8,128)S(1)}, f32[16,896]{1,0:T(8,128)S(1)}, u32[]{:S(2)}, u32[]{:S(2)}) collective-permute-start(f32[16,896]{1,0:T(8,128)S(1)} %get-tuple-element.43), channel_id=1, source_target_pairs={{0,1},{1,2},{2,3},{3,0},{4,5},{5,6},{6,7},{7,4},{8,9},{9,10},{10,1... | collective-permute-start | bytes 172040 | tf_op jit(solution)/shard_map/ppermute | solution.py:923
  18.9 0.0 collective-permute-start.6
  18.9 0.0 copy-start.3
  18.9 3.5 %march.1 = (f32[3,1024,128]{2,1,0:T(8,128)S(1)}, f32[3,1024,128]{2,1,0:T(8,128)S(1)}, f32[1,512]{1,0:T(1,128)S(1)}, s32[9,128]{1,0:T(8,128)S(1)}, f32[6,128]{1,0:T(8,128)S(1)}) custom-call(f32[3,1024,128]{2,1,0:T(8,128)S(1)} %bitcast.31, f32[3,1024,128]{2,1,0:T(8,128)S(1)} %bitcast.34, f32[1024,128]{1,0:T(8,128)S(1)} %get-tuple-element.30.coef_v, ...), custom_call_target="tpu_custom_call" | custom-call | flops 40000000 | bytes 10000000 | tf_op jit(solution)/shard_map/march/pallas_call | solution.py:927
  22.4 0.0 collective-permute-done.5.low_ref
  22.5 0.1 collective-permute-done.6.high_ref
  22.5 0.0 copy-done.3
  22.5 0.7 %finish_ends.1 = (f32[48,896]{1,0:T(8,128)S(1)}, f32[4,32]{1,0:T(4,128)S(1)}, f32[4,32]{1,0:T(4,128)S(1)}, f32[4,32]{1,0:T(4,128)S(1)}, f32[4,32]{1,0:T(4,128)S(1)}) custom-call(f32[128,896]{1,0:T(8,128)S(1)} %get-tuple-element.42.own_t, f32[16,896]{1,0:T(8,128)S(1)} %collective-permute-done.5.low_ref, f32[16,896]{1,0:T(8,128)S(1)} %collective-permute-done.6.high_ref, ...), custom_call_target="tpu_custom_call" | custom-call | tf_op jit(solution)/shard_map/finish_ends/pallas_call | solution.py:949
  23.2 0.6 %collective-permute-start.7 = (f32[4,32]{1,0:T(4,128)S(1)}, f32[4,32]{1,0:T(4,128)S(1)}, u32[]{:S(2)}, u32[]{:S(2)}) collective-permute-start(f32[4,32]{1,0:T(4,128)S(1)} %get-tuple-element.52), channel_id=1, source_target_pairs={{0,1},{1,0},{2,3},{3,2},{4,5},{5,4},{6,7},{7,6},{8,9},{9,8},{10,11... | collective-permute-start | bytes 1544 | tf_op jit(solution)/shard_map/ppermute | solution.py:980
  23.8 1.2 %collective-permute-start.8 = (f32[4,32]{1,0:T(4,128)S(1)}, f32[4,32]{1,0:T(4,128)S(1)}, u32[]{:S(2)}, u32[]{:S(2)}) collective-permute-start(f32[4,32]{1,0:T(4,128)S(1)} %get-tuple-element.53), channel_id=1, source_target_pairs={{0,2},{1,3},{2,0},{3,1},{4,6},{5,7},{6,4},{7,5},{8,10},{9,11},{10,... | collective-permute-start | bytes 1544 | tf_op jit(solution)/shard_map/ppermute | solution.py:980
  25.0 0.5 %collective-permute-start.9 = (f32[4,32]{1,0:T(4,128)S(1)}, f32[4,32]{1,0:T(4,128)S(1)}, u32[]{:S(2)}, u32[]{:S(2)}) collective-permute-start(f32[4,32]{1,0:T(4,128)S(1)} %get-tuple-element.54), channel_id=1, source_target_pairs={{0,3},{1,2},{2,1},{3,0},{4,7},{5,6},{6,5},{7,4},{8,11},{9,10},{10,... | collective-permute-start | bytes 1544 | tf_op jit(solution)/shard_map/ppermute | solution.py:980
  25.5 2.0 %write_out.1 = (f32[3,1024,128]{2,1,0:T(8,128)}, f32[3,1024,128]{2,1,0:T(8,128)}) custom-call(f32[3,1024,128]{2,1,0:T(8,128)S(1)} %get-tuple-element.40.e_s, f32[3,1024,128]{2,1,0:T(8,128)S(1)} %get-tuple-element.41.h_s, f32[48,896]{1,0:T(8,128)S(1)} %get-tuple-element.48.ends_ref), custom_call_target="tpu_custom_call" | custom-call | flops 10000000 | bytes 8000000 | tf_op jit(solution)/shard_map/write_out/pallas_call | solution.py:962
  27.5 0.0 collective-permute-done.7
  27.5 0.0 collective-permute-done.8
  27.5 0.5 %collective-permute-done.9 = f32[4,32]{1,0:T(4,128)S(1)} collective-permute-done((f32[4,32]{1,0:T(4,128)S(1)}, f32[4,32]{1,0:T(4,128)S(1)}, u32[]{:S(2)}, u32[]{:S(2)}) %collective-permute-start.9) | collective-permute-done | bytes 544 | tf_op jit(solution)/shard_map/ppermute | solution.py:980
  28.0 0.6 %add_bitcast_fusion = f32[32,4]{0,1:T(4,128)} fusion(f32[4,32]{1,0:T(4,128)S(1)} %collective-permute-done.9, f32[4,32]{1,0:T(4,128)S(1)} %collective-permute-done.8, f32[4,32]{1,0:T(4,128)S(1)} %get-tuple-element.51, f32[4,32]{1,0:T(4,128)S(1)} %collective-permute-done.7), kind=kLoop, calls=%fused_computation | loop fusion | flops 384 | bytes 2560 | tf_op jit(solution)/shard_map/transpose | solution.py:983
Async XLA Ops:
  0.6 9.7 %copy-start = (f32[3,32,16,256]{3,2,1,0:T(8,128)S(1)}, f32[3,32,16,256]{3,2,1,0:T(8,128)}, u32[]{:S(2)}) copy-start(f32[3,32,16,256]{3,2,1,0:T(8,128)} %param.8) | copy-start | bytes 4718596
  0.6 9.7 %copy-start.1 = (f32[3,32,16,256]{3,2,1,0:T(8,128)S(1)}, f32[3,32,16,256]{3,2,1,0:T(8,128)}, u32[]{:S(2)}) copy-start(f32[3,32,16,256]{3,2,1,0:T(8,128)} %param.9) | copy-start | bytes 4718596
  0.7 9.7 %copy-start.2 = (s32[32,16,256]{2,1,0:T(8,128)S(1)}, s32[32,16,256]{2,1,0:T(8,128)}, u32[]{:S(2)}) copy-start(s32[32,16,256]{2,1,0:T(8,128)} %param.11) | copy-start | bytes 1572868
  2.5 12.3 %collective-permute-start.1 = (f32[584,128]{1,0:T(8,128)S(1)}, f32[584,128]{1,0:T(8,128)S(1)}, u32[]{:S(2)}, u32[]{:S(2)}) collective-permute-start(f32[584,128]{1,0:T(8,128)S(1)} %get-tuple-element.33), channel_id=1, source_target_pairs={{0,4},{4,0},{8,12},{12,8},{1,5},{5,1},{9,13},{13,9},{2,6},{6,2},{1... | collective-permute-start | bytes 897032 | tf_op jit(solution)/shard_map/ppermute | solution.py:900
  3.8 10.9 %collective-permute-start.2 = (f32[584,128]{1,0:T(8,128)S(1)}, f32[584,128]{1,0:T(8,128)S(1)}, u32[]{:S(2)}, u32[]{:S(2)}) collective-permute-start(f32[584,128]{1,0:T(8,128)S(1)} %get-tuple-element.34), channel_id=1, source_target_pairs={{0,0},{4,8},{8,4},{12,12},{1,1},{5,9},{9,5},{13,13},{2,2},{6,10},{... | collective-permute-start | bytes 897032 | tf_op jit(solution)/shard_map/ppermute | solution.py:900
  5.7 9.0 %collective-permute-start = (f32[304,128]{1,0:T(8,128)S(1)}, f32[304,128]{1,0:T(8,128)S(1)}, u32[]{:S(2)}, u32[]{:S(2)}) collective-permute-start(f32[304,128]{1,0:T(8,128)S(1)} %get-tuple-element.32), channel_id=1, source_target_pairs={{0,16},{16,0},{1,17},{17,1},{2,18},{18,2},{3,19},{19,3},{4,20},{20... | collective-permute-start | bytes 466952 | tf_op jit(solution)/shard_map/ppermute | solution.py:900
  7.1 5.6 %collective-permute-start.3 = (f32[2,28,128]{2,1,0:T(8,128)S(1)}, f32[2,28,128]{2,1,0:T(8,128)S(1)}, u32[]{:S(2)}, u32[]{:S(2)}) collective-permute-start(f32[2,28,128]{2,1,0:T(8,128)S(1)} %get-tuple-element.35), channel_id=1, source_target_pairs={{0,20},{4,16},{8,28},{12,24},{16,4},{20,0},{24,12},{28,8},{1,21},{... | collective-permute-start | bytes 86024 | tf_op jit(solution)/shard_map/ppermute | solution.py:900
  7.1 7.7 %collective-permute-start.4 = (f32[2,28,128]{2,1,0:T(8,128)S(1)}, f32[2,28,128]{2,1,0:T(8,128)S(1)}, u32[]{:S(2)}, u32[]{:S(2)}) collective-permute-start(f32[2,28,128]{2,1,0:T(8,128)S(1)} %get-tuple-element.36), channel_id=1, source_target_pairs={{0,0},{4,24},{8,20},{12,12},{16,16},{20,8},{24,4},{28,28},{1,1},{5... | collective-permute-start | bytes 86024 | tf_op jit(solution)/shard_map/ppermute | solution.py:900
  15.6 6.8 %collective-permute-start.5 = (f32[16,896]{1,0:T(8,128)S(1)}, f32[16,896]{1,0:T(8,128)S(1)}, u32[]{:S(2)}, u32[]{:S(2)}) collective-permute-start(f32[16,896]{1,0:T(8,128)S(1)} %get-tuple-element.43), channel_id=1, source_target_pairs={{0,1},{1,2},{2,3},{3,0},{4,5},{5,6},{6,7},{7,4},{8,9},{9,10},{10,1... | collective-permute-start | bytes 172040 | tf_op jit(solution)/shard_map/ppermute | solution.py:923
  18.9 3.6 %collective-permute-start.6 = (f32[16,896]{1,0:T(8,128)S(1)}, f32[16,896]{1,0:T(8,128)S(1)}, u32[]{:S(2)}, u32[]{:S(2)}) collective-permute-start(f32[16,896]{1,0:T(8,128)S(1)} %get-tuple-element.44), channel_id=1, source_target_pairs={{0,3},{1,0},{2,1},{3,2},{4,7},{5,4},{6,5},{7,6},{8,11},{9,8},{10,9... | collective-permute-start | bytes 172040 | tf_op jit(solution)/shard_map/ppermute | solution.py:924
  18.9 3.6 %copy-start.3 = (s32[32,16]{0,1:T(8,128)S(1)}, s32[32,16]{0,1:T(8,128)}, u32[]{:S(2)}) copy-start(s32[32,16]{0,1:T(8,128)} %param.13) | copy-start | bytes 6148
  23.2 4.3 %collective-permute-start.7 = (f32[4,32]{1,0:T(4,128)S(1)}, f32[4,32]{1,0:T(4,128)S(1)}, u32[]{:S(2)}, u32[]{:S(2)}) collective-permute-start(f32[4,32]{1,0:T(4,128)S(1)} %get-tuple-element.52), channel_id=1, source_target_pairs={{0,1},{1,0},{2,3},{3,2},{4,5},{5,4},{6,7},{7,6},{8,9},{9,8},{10,11... | collective-permute-start | bytes 1544 | tf_op jit(solution)/shard_map/ppermute | solution.py:980
  23.8 3.7 %collective-permute-start.8 = (f32[4,32]{1,0:T(4,128)S(1)}, f32[4,32]{1,0:T(4,128)S(1)}, u32[]{:S(2)}, u32[]{:S(2)}) collective-permute-start(f32[4,32]{1,0:T(4,128)S(1)} %get-tuple-element.53), channel_id=1, source_target_pairs={{0,2},{1,3},{2,0},{3,1},{4,6},{5,7},{6,4},{7,5},{8,10},{9,11},{10,... | collective-permute-start | bytes 1544 | tf_op jit(solution)/shard_map/ppermute | solution.py:980
  25.0 3.0 %collective-permute-start.9 = (f32[4,32]{1,0:T(4,128)S(1)}, f32[4,32]{1,0:T(4,128)S(1)}, u32[]{:S(2)}, u32[]{:S(2)}) collective-permute-start(f32[4,32]{1,0:T(4,128)S(1)} %get-tuple-element.54), channel_id=1, source_target_pairs={{0,3},{1,2},{2,1},{3,0},{4,7},{5,6},{6,5},{7,4},{8,11},{9,10},{10,... | collective-permute-start | bytes 1544 | tf_op jit(solution)/shard_map/ppermute | solution.py:980
